TPU v7x, 32 devices: a whole 2x2x4 slice. The times are simulated.
32 devices in a mesh: dp: 8 (over z, y), tensor: 4 (over x, core).
Axes of the slice: x: 2, y: 2, z: 4, core: 2. Of those that a mesh axis runs over, the one named last changes fastest.
Arguments:
- attn_heads: bfloat16 [1024, 8192], P('dp', 'tensor'), may hold values from -6 to 6
- residual: bfloat16 [1024, 8192], P('dp', 'tensor'), may hold values from -6 to 6
- low_hidden: bfloat16 [1024, 8192], P('dp', 'tensor'), may hold values from -6 to 6
- mid_hidden: bfloat16 [1024, 8192], P('dp', 'tensor'), may hold values from -6 to 6
- out_weight: bfloat16 [8192, 8192], P('tensor', 'dp'), may hold values from -0.0625 to 0.0625
- join_weight: bfloat16 [3, 8192, 8192], P(None, 'tensor', 'dp'), may hold values from -0.0390625 to 0.0390625
- join_gain: float32 [8192], replicated, may hold values from 0.1 to 1.9
Outputs:
- joined_state: bfloat16 [1024, 8192], P(('dp', 'tensor'))
All inputs are finite; a program needn't handle non-finite values.
Results may differ from a plain program's by a relative error of at most 0.0039.
Values may be sent and summed in bfloat16 or wider, within the bound.
No kernel may reach another device: no remote copies, remote signals or barrier semaphores. Data moves between devices by JAX's collectives and lax.ppermute only.
A program may use at most 128 MiB of HBM per device.

v0:
```python
import jax
import jax.numpy as jnp
from jax import lax
from jax.sharding import PartitionSpec as P


def depth_product(weights, portion):
    return jnp.einsum("dtf,dfc->tc", portion, weights, preferred_element_type=jnp.float32)


def local(attn_heads, residual, low_hidden, mid_hidden, out_weight, join_weight, join_gain):
    group_tokens = attn_heads.shape[0]
    owner_count = lax.axis_size("tensor")
    group_count = lax.axis_size("dp")
    column_width = join_weight.shape[2]
    head_partial = jnp.dot(
        attn_heads,
        lax.all_gather(out_weight, "dp", axis=1, tiled=True),
        preferred_element_type=jnp.float32,
    )
    head_sum = lax.psum_scatter(head_partial, "tensor", scatter_dimension=1, tiled=True)
    top_hidden = (residual.astype(jnp.float32) + head_sum).astype(jnp.bfloat16)
    stacked = jnp.stack([low_hidden, mid_hidden, top_hidden])
    joined_partial = depth_product(join_weight, lax.all_gather(stacked, "dp", axis=1, tiled=True))
    blocked = joined_partial.reshape(
        group_count, owner_count, group_tokens // owner_count, column_width
    )
    moved_partials = lax.all_to_all(blocked, "dp", split_axis=0, concat_axis=3, tiled=True)
    owned_rows = lax.psum_scatter(moved_partials, "tensor", scatter_dimension=1, tiled=True)
    joined_sum = owned_rows.reshape(group_tokens // owner_count, column_width * group_count)
    inverse_rms = lax.rsqrt(jnp.mean(joined_sum * joined_sum, axis=1, keepdims=True) + 1e-05)
    return (joined_sum * inverse_rms * join_gain).astype(jnp.bfloat16)


def solution(mesh):
    return jax.shard_map(
        local,
        mesh=mesh,
        in_specs=(
            P("dp", "tensor"),
            P("dp", "tensor"),
            P("dp", "tensor"),
            P("dp", "tensor"),
            P("tensor", "dp"),
            P(None, "tensor", "dp"),
            P(),
        ),
        out_specs=P(("dp", "tensor"), None),
        check_vma=False,
    )
```

profile of v0, /device:TPU:0, one launch (start us, length us, event | category | flops | bytes accessed | tf_op | source)
XLA Modules:
  0.0 1059.6 jit_solution(815088074883037789)
XLA Ops:
  6.5 0.0 copy-start
  6.5 0.0 all-gather.3.cloned.1.call-start
  6.5 0.7 all-gather.3.cloned.1.call-update
  7.3 0.0 reduce-scatter.3.cloned.1.call-start
  7.3 642.1 %all-gather.3.cloned.1.call-done = bf16[2048,8192]{1,0:T(8,128)(2,1)} async-done(((bf16[2048,1024]{1,0:T(8,128)(2,1)}), bf16[2048,8192]{1,0:T(8,128)(2,1)}) %all-gather.3.cloned.1.call-update) | async-done | bytes 33554448 | tf_op jit(solution)/shard_map/all_gather | solution.py:18
  649.4 0.0 copy-done
  649.4 17.1 %fusion.4 = f32[128,8192]{1,0:T(8,128)} fusion(bf16[128,2048]{1,0:T(8,128)(2,1)S(1)} %copy-done, bf16[2048,8192]{1,0:T(8,128)(2,1)} %all-gather.3.cloned.1.call-done), kind=kOutput, calls=%fused_computation.9 | convolution fusion | flops 4294967296 | bytes 38273024 | tf_op jit(solution)/shard_map/dot_general | solution.py:16
  666.5 0.0 reduce-scatter.3.cloned.1.call-update
  666.5 0.0 all-gather.5.cloned.1.call-start
  666.6 44.6 %reduce-scatter.3.cloned.1.call-done = f32[128,2048]{1,0:T(8,128)} async-done(((f32[128,8192]{1,0:T(8,128)}), f32[128,2048]{1,0:T(8,128)}) %reduce-scatter.3.cloned.1.call-update) | async-done | bytes 1048592 | tf_op jit(solution)/shard_map/reduce_scatter | solution.py:21
  711.2 1.3 fusion.3
  712.5 0.0 copy-done.3
  712.5 0.0 copy-done.4
  712.5 1.3 pad_maximum_fusion
  713.9 0.0 all-gather.5.cloned.1.call-update
  713.9 0.0 reduce-scatter.5.cloned.1.call-start
  713.9 176.5 %all-gather.5.cloned.1.call-done = bf16[3,1024,2048]{2,1,0:T(8,128)(2,1)} async-done(((bf16[3,128,2048]{2,1,0:T(8,128)(2,1)}), bf16[3,1024,2048]{2,1,0:T(8,128)(2,1)}) %all-gather.5.cloned.1.call-update) | async-done | bytes 12582928 | tf_op jit(solution)/shard_map/all_gather | solution.py:24
  890.5 17.2 %fusion.5 = f32[1024,1024,1]{1,0,2:T(8,128)S(1)} fusion(bf16[3,1024,2048]{2,1,0:T(8,128)(2,1)} %all-gather.5.cloned.1.call-done, bf16[3,2048,1024]{2,1,0:T(8,128)(2,1)} %param.12), kind=kOutput, calls=%fused_computation.10 | convolution fusion | flops 12884901888 | bytes 29360128 | tf_op jit(solution)/shard_map/dtf,dfc->tc/dot_general | solution.py:8
  907.6 95.9 %all_to_all.18 = f32[8,4,32,1024]{3,2,1,0:T(8,128)S(1)} all-to-all(f32[8,4,32,1024]{3,2,1,0:T(8,128)S(1)} %bitcast.27), channel_id=1, replica_groups=mesh['dp'=8,'tensor'=4] {'dp'}, dimensions={0} | all-to-all | bytes 8388608 | tf_op jit(solution)/shard_map/all_to_all | solution.py:28
  1003.5 2.3 copy.9
  1005.8 0.0 reduce-scatter.5.cloned.1.call-update
  1005.8 43.7 %reduce-scatter.5.cloned.1.call-done = f32[1,1,32,8192]{3,2,1,0:T(8,128)} async-done(((f32[1,4,32,8192]{3,2,1,0:T(8,128)}), f32[1,1,32,8192]{3,2,1,0:T(8,128)}) %reduce-scatter.5.cloned.1.call-update) | async-done | bytes 1048592 | tf_op jit(solution)/shard_map/reduce_scatter | solution.py:29
  1049.4 1.4 fusion
  1050.9 2.2 fusion.2
  (9 shorter events, 0.0 us)
Async XLA Ops:
  6.5 642.8 %copy-start = (bf16[128,2048]{1,0:T(8,128)(2,1)S(1)}, bf16[128,2048]{1,0:T(8,128)(2,1)}, u32[]{:S(2)}) copy-start(bf16[128,2048]{1,0:T(8,128)(2,1)} %param.7) | copy-start | bytes 1572868
  6.5 642.8 %all-gather.3.cloned.1.call-start = ((), (), s32[]{:S(2)}) async-start(), calls=%async_computation.3 | async-start | bytes 37748736 | tf_op jit(solution)/shard_map/all_gather | solution.py:18
  7.3 703.9 %reduce-scatter.3.cloned.1.call-start = ((), (), s32[]{:S(2)}) async-start(), calls=%async_computation.4 | async-start | bytes 5242880 | tf_op jit(solution)/shard_map/reduce_scatter | solution.py:21
  666.5 44.7 %copy-start.2 = (bf16[128,2048]{1,0:T(8,128)(2,1)S(1)}, bf16[128,2048]{1,0:T(8,128)(2,1)}, u32[]{:S(2)}) copy-start(bf16[128,2048]{1,0:T(8,128)(2,1)} %param.8) | copy-start | bytes 1572868
  666.5 46.0 %copy-start.3 = (bf16[128,2048]{1,0:T(8,128)(2,1)S(1)}, bf16[128,2048]{1,0:T(8,128)(2,1)}, u32[]{:S(2)}) copy-start(bf16[128,2048]{1,0:T(8,128)(2,1)} %param.10) | copy-start | bytes 1572868
  666.5 46.0 %copy-start.4 = (bf16[128,2048]{1,0:T(8,128)(2,1)S(1)}, bf16[128,2048]{1,0:T(8,128)(2,1)}, u32[]{:S(2)}) copy-start(bf16[128,2048]{1,0:T(8,128)(2,1)} %param.9) | copy-start | bytes 1572868
  666.5 223.9 %all-gather.5.cloned.1.call-start = ((), (), s32[]{:S(2)}) async-start(), calls=%async_computation.5 | async-start | bytes 14155776 | tf_op jit(solution)/shard_map/all_gather | solution.py:24
  713.9 335.6 %reduce-scatter.5.cloned.1.call-start = ((), (), s32[]{:S(2)}) async-start(), calls=%async_computation.6 | async-start | bytes 5242880 | tf_op jit(solution)/shard_map/reduce_scatter | solution.py:29
  1003.5 49.6 %copy-start.1 = (bf16[128,2048]{1,0:T(8,128)(2,1)S(1)}, bf16[128,2048]{1,0:T(8,128)(2,1)}, u32[]{:S(2)}) copy-start(bf16[128,2048]{1,0:T(8,128)(2,1)} %param.7) | copy-start | bytes 1572868
  1005.8 45.1 %copy-start.5 = (f32[8192]{0:T(1024)S(1)}, f32[8192]{0:T(1024)}, u32[]{:S(2)}) copy-start(f32[8192]{0:T(1024)} %param.13) | copy-start | bytes 98308
Sparse Core Ops, SparseCore 0:
  8.9 640.4 all-gather.2
  666.6 44.4 reduce-scatter.2
  714.0 176.4 all-gather.4
  1005.9 43.4 reduce-scatter.4
where the time goes:
time: 1060 us
  waiting for transfers between devices  908 us (86%)
  blocking collectives  95.9 us (9%)
  matrix products  34.3 us (3%)
  between operations  13.2 us (1%)
    all_gather x1, waiting for transfers between devices, local(): lax.all_gather(out_weight, 'dp', axis=1, tiled=True)  642 us
    all_gather x1, waiting for transfers between devices, local(): lax.all_gather(stacked, 'dp', axis=1, tiled=True)  177 us
    all_to_all x1, blocking collectives, local(): lax.all_to_all(blocked, 'dp', split_axis=0, concat_axis=3, tiled=True)  95.9 us
    reduce_scatter x1, waiting for transfers between devices, local(): lax.psum_scatter(head_partial, 'tensor', scatter_dimension=1, tiled=True)  44.6 us
    reduce_scatter x1, waiting for transfers between devices, local(): lax.psum_scatter(moved_partials, 'tensor', scatter_dimension=1, tiled=True)  43.7 us
  transfers between devices with their start and end apart: 4, of which 4 were waited for; matrix products, arithmetic and copies ran while one was open for 0% of the time, Pallas kernels for 0%

commit v1 on v0

v1 whole, which is shorter than its diff:
```python
import jax
import jax.numpy as jnp
import numpy as np
from jax import lax
from jax.sharding import PartitionSpec as P


def ring_of(groups):
    half = groups // 2
    return [2 * q for q in range(half)] + [2 * q + 1 for q in reversed(range(half))]


def ring_gather(forward, backward):
    ring = ring_of(lax.axis_size("dp"))
    count = len(ring)
    up = [(ring[q], ring[(q + 1) % count]) for q in range(count)]
    down = [(target, source) for source, target in up]
    above, below = [forward], [backward]
    for _ in range(count - 1):
        above.append(lax.ppermute(above[-1], "dp", up))
        below.append(lax.ppermute(below[-1], "dp", down))
    return above, below


def swap(values, bit):
    return lax.ppermute(values, "tensor", [(t, t ^ bit) for t in range(lax.axis_size("tensor"))])


def pick(values, index, axis=0):
    return lax.dynamic_index_in_dim(values, index, axis, keepdims=False)


def reduce_over_x(pieces, x):
    while pieces.shape[0] > 1:
        half = pieces.shape[0] // 2
        pieces = pieces.reshape((2, half) + pieces.shape[1:])
        side = lax.rem(lax.div(x, half), 2)
        sent = pick(pieces, 1 - side).astype(jnp.bfloat16)
        pieces = pick(pieces, side) + swap(sent, 2 * half).astype(jnp.float32)
    return pieces[0]


def local(attn_heads, residual, low_hidden, mid_hidden, out_weight, join_weight, join_gain):
    groups, owners = lax.axis_size("dp"), lax.axis_size("tensor")
    tokens, features = attn_heads.shape
    width = out_weight.shape[1]
    xs = owners // 2
    side_rows = tokens // 2
    rows = tokens // owners
    per_owner = groups // owners
    rounds = 2 * per_owner

    ring = np.array(ring_of(groups))
    place_of = np.argsort(ring)
    dp, tensor = lax.axis_index("dp"), lax.axis_index("tensor")
    x, core = lax.div(tensor, 2), lax.rem(tensor, 2)
    place = jnp.asarray(place_of, jnp.int32)[dp]

    def sides(values):
        split = values.reshape((xs, 2, rows) + values.shape[1:])
        return [split[:, s].reshape((side_rows,) + values.shape[1:]) for s in range(2)]

    def slot_of(q):
        return jnp.where(core == 0, lax.rem(place - q + groups, groups), lax.rem(q - place + groups, groups))

    attn_up, attn_down = ring_gather(*sides(attn_heads))
    low_sides, mid_sides = sides(low_hidden), sides(mid_hidden)
    depth_sides = [jnp.stack([low_sides[s], mid_sides[s]]) for s in range(2)]
    depth_sides[0], depth_sides[1], last_up, last_down = lax.optimization_barrier(
        (depth_sides[0], depth_sides[1], attn_up[-1], attn_down[-1])
    )
    attn_up[-1], attn_down[-1] = last_up, last_down
    depth_up, depth_down = ring_gather(*depth_sides)

    attn_all = jnp.concatenate(attn_up + attn_down, axis=0)
    head_partial = jnp.dot(attn_all, out_weight, preferred_element_type=jnp.float32)
    head_partial = head_partial.reshape(2, groups, side_rows, width)
    head_core = pick(head_partial, core) + swap(pick(head_partial, 1 - core), 1)
    by_place = jnp.stack([pick(head_core, slot_of(q)) for q in range(groups)])
    held = reduce_over_x(by_place.reshape(xs, rounds, side_rows, width), x).astype(jnp.bfloat16)

    shift = 2 * lax.rem(dp, per_owner) + core
    arrived = []
    for k in range(rounds):
        moves = []
        for d in range(groups):
            for t in range(owners):
                q = (t // 2) * rounds + (k - 2 * (d % per_owner) - t % 2) % rounds
                moves.append((d * owners + t, int(ring[q]) * owners + d // per_owner))
        piece = pick(held, lax.rem(k - shift + 2 * rounds, rounds))
        arrived.append(lax.ppermute(piece, ("dp", "tensor"), moves))
    arrived = jnp.stack(arrived)
    top_sides = []
    for s, rest in enumerate(sides(residual)):
        blocks = [pick(arrived, lax.rem(place + 2 * j + s, rounds)) for j in range(per_owner)]
        head_sum = jnp.concatenate(blocks, axis=1).astype(jnp.float32)
        top_sides.append((rest.astype(jnp.float32) + head_sum).astype(jnp.bfloat16))
    top_up, top_down = ring_gather(*top_sides)

    depth_all = jnp.concatenate(depth_up + depth_down, axis=1)
    top_all = jnp.concatenate(top_up + top_down, axis=0)
    joined = jnp.dot(depth_all[0], join_weight[0], preferred_element_type=jnp.float32)
    joined = joined + jnp.dot(depth_all[1], join_weight[1], preferred_element_type=jnp.float32)
    joined = joined + jnp.dot(top_all, join_weight[2], preferred_element_type=jnp.float32)
    joined = joined.reshape(2, groups, side_rows, width)
    joined_core = pick(joined, core) + swap(pick(joined, 1 - core), 1)
    by_owner = jnp.moveaxis(joined_core.reshape(groups, xs, rows, width), 1, 0)
    owned = reduce_over_x(by_owner, x)
    by_group = jnp.stack([pick(owned, slot_of(int(place_of[g]))) for g in range(groups)]).astype(jnp.bfloat16)
    moved = lax.all_to_all(by_group, "dp", split_axis=0, concat_axis=0, tiled=True)
    joined_sum = jnp.moveaxis(moved, 0, 1).reshape(rows, groups * width).astype(jnp.float32)
    inverse_rms = lax.rsqrt(jnp.mean(joined_sum * joined_sum, axis=1, keepdims=True) + 1e-05)
    return (joined_sum * inverse_rms * join_gain).astype(jnp.bfloat16)


def solution(mesh):
    return jax.shard_map(
        local,
        mesh=mesh,
        in_specs=(
            P("dp", "tensor"),
            P("dp", "tensor"),
            P("dp", "tensor"),
            P("dp", "tensor"),
            P("tensor", "dp"),
            P(None, "tensor", "dp"),
            P(),
        ),
        out_specs=P(("dp", "tensor"), None),
        check_vma=False,
    )
```

time: 1060 us -> 317 us (0.30)
  waiting for transfers between devices: 908 us -> 171 us
  blocking collectives: 95.9 us -> 17.6 us
  starting transfers between devices: 0.13 us -> 58.4 us
  local copies, waits for them, and re-layouts: 2.28 us -> 32.2 us
  matrix products: 34.3 us -> 20 us
    all_gather x2 -> x0, waiting for transfers between devices: 819 us -> none  [the longest x1 642 us: local(): lax.all_gather(out_weight, 'dp', axis=1, tiled=True)]
    ppermute x0 -> x50, waiting for transfers between devices: none -> 171 us  [the longest x21 110 us: ring_gather(): above.append(lax.ppermute(above[-1], 'dp', up))]
    reduce_scatter x2 -> x0, waiting for transfers between devices: 88.2 us -> none  [the longest x1 44.6 us: local(): lax.psum_scatter(head_partial, 'tensor', scatter_dimension=1, tiled=True)]
    all_to_all x1, blocking collectives: 95.9 us -> 17.6 us  [local(): lax.all_to_all(by_group, 'dp', split_axis=0, concat_axis=0, tiled=True)]
    ppermute x0 -> x50, starting transfers between devices: none -> 58.4 us  [the longest x21 31.1 us: ring_gather(): above.append(lax.ppermute(above[-1], 'dp', up))]
    unnamed x12 -> x79, local copies, waits for them, and re-layouts: 0.02 us -> 24 us
    dot_general x2 -> x4, matrix products: 34.3 us -> 20 us  [the longest x1 6.38 us: local(): jnp.dot(attn_all, out_weight, preferred_element_type=jnp.float32)]
  transfers between devices with their start and end apart: 4 -> 50, of which waited for: 4 -> 32; matrix products, arithmetic and copies ran while one was open for 0% -> 10% of each run, Pallas kernels for 0% -> 0%
where the time goes in v1:
time: 317 us; the launch traced here: 316 us
  waiting for transfers between devices  171 us (54%)
  starting transfers between devices  58.4 us (18%)
  local copies, waits for them, and re-layouts  32.2 us (10%)
  matrix products  20 us (6%)
  blocking collectives  17.6 us (6%)
  between operations  11.6 us (4%)
  other arithmetic  5.44 us (2%)
    ppermute x21, waiting for transfers between devices, ring_gather(): above.append(lax.ppermute(above[-1], 'dp', up))  110 us
    ppermute x21, waiting for transfers between devices, ring_gather(): below.append(lax.ppermute(below[-1], 'dp', down))  41.2 us
    ppermute x21, starting transfers between devices, ring_gather(): above.append(lax.ppermute(above[-1], 'dp', up))  31.1 us
    unnamed x79, local copies, waits for them, and re-layouts  24 us
    ppermute x4, waiting for transfers between devices, swap(): lax.ppermute(values, 'tensor', [(t, t ^ bit) for t in range(lax.axis_size...  19.5 us
    all_to_all x1, blocking collectives, local(): lax.all_to_all(by_group, 'dp', split_axis=0, concat_axis=0, tiled=True)  17.6 us
    ppermute x21, starting transfers between devices, ring_gather(): below.append(lax.ppermute(below[-1], 'dp', down))  15.9 us
    ppermute x4, starting transfers between devices, local(): arrived.append(lax.ppermute(piece, ('dp', 'tensor'), moves))  9.85 us
  transfers between devices with their start and end apart: 50, of which 32 were waited for; matrix products, arithmetic and copies ran while one was open for 10% of the time, Pallas kernels for 0%

profile of v1, /device:TPU:0, one launch (start us, length us, event | category | flops | bytes accessed | tf_op | source)
XLA Modules:
  0.0 316.1 jit_solution(3948794366978370193)
XLA Ops:
  4.2 6.2 %collective-permute-done = bf16[64,2048]{1,0:T(8,128)(2,1)S(1)} collective-permute-done((bf16[64,2048]{1,0:T(8,128)(2,1)S(1)}, bf16[64,2048]{1,0:T(8,128)(2,1)S(1)}, u32[]{:S(2)}, u32[]{:S(2)}) %collective-permute-start) | collective-permute-done | bytes 262176 | tf_op jit(solution)/shard_map/ppermute | solution.py:20
  13.5 4.4 %collective-permute-done.1 = bf16[64,2048]{1,0:T(8,128)(2,1)S(1)} collective-permute-done((bf16[64,2048]{1,0:T(8,128)(2,1)S(1)}, bf16[64,2048]{1,0:T(8,128)(2,1)S(1)}, u32[]{:S(2)}, u32[]{:S(2)}) %collective-permute-start.1) | collective-permute-done | bytes 262176 | tf_op jit(solution)/shard_map/ppermute | solution.py:20
  27.4 4.6 %collective-permute-done.3 = bf16[64,2048]{1,0:T(8,128)(2,1)} collective-permute-done((bf16[64,2048]{1,0:T(8,128)(2,1)}, bf16[64,2048]{1,0:T(8,128)(2,1)}, u32[]{:S(2)}, u32[]{:S(2)}) %collective-permute-start.3) | collective-permute-done | bytes 262176 | tf_op jit(solution)/shard_map/ppermute | solution.py:20
  64.5 6.4 %fusion.27 = f32[1024,1024]{1,0:T(8,128)S(1)} fusion(bf16[1024,2048]{1,0:T(8,128)(2,1)} %constant_dynamic-update-slice_fusion.16, bf16[2048,1024]{1,0:T(8,128)(2,1)S(1)} %copy-done.6), kind=kOutput, calls=%fused_computation.127 | convolution fusion | flops 4294967296 | bytes 12582912 | tf_op jit(solution)/shard_map/dot_general | solution.py:76
  76.6 12.4 %collective-permute-done.14 = bf16[2,64,2048]{2,1,0:T(8,128)(2,1)} collective-permute-done((bf16[2,64,2048]{2,1,0:T(8,128)(2,1)S(1)}, bf16[2,64,2048]{2,1,0:T(8,128)(2,1)}, u32[]{:S(2)}, u32[]{:S(2)}) %collective-permute-start.14) | collective-permute-done | bytes 524320 | tf_op jit(solution)/shard_map/ppermute | solution.py:20
  121.7 5.7 %collective-permute-start.33 = (bf16[64,1024]{1,0:T(8,128)(2,1)S(1)}, bf16[64,1024]{1,0:T(8,128)(2,1)S(1)}, u32[]{:S(2)}, u32[]{:S(2)}) collective-permute-start(bf16[64,1024]{1,0:T(8,128)(2,1)S(1)} %get-tuple-element.20), channel_id=1, source_target_pairs={{0,24},{1,16},{2,4},{3,12},{4,8},{5,0},{6,20},{7,28},{8,25},{9,17}... | collective-permute-start | bytes 393224 | tf_op jit(solution)/shard_map/ppermute | solution.py:91
  141.4 10.5 %collective-permute-done.18 = bf16[2,64,2048]{2,1,0:T(8,128)(2,1)S(1)} collective-permute-done((bf16[2,64,2048]{2,1,0:T(8,128)(2,1)S(1)}, bf16[2,64,2048]{2,1,0:T(8,128)(2,1)S(1)}, u32[]{:S(2)}, u32[]{:S(2)}) %collective-permute-start.18) | collective-permute-done | bytes 524320 | tf_op jit(solution)/shard_map/ppermute | solution.py:20
  157.6 11.2 %collective-permute-done.19 = bf16[2,64,2048]{2,1,0:T(8,128)(2,1)S(1)} collective-permute-done((bf16[2,64,2048]{2,1,0:T(8,128)(2,1)S(1)}, bf16[2,64,2048]{2,1,0:T(8,128)(2,1)S(1)}, u32[]{:S(2)}, u32[]{:S(2)}) %collective-permute-start.19) | collective-permute-done | bytes 524320 | tf_op jit(solution)/shard_map/ppermute | solution.py:20
  168.7 5.6 %collective-permute-done.35 = bf16[64,2048]{1,0:T(8,128)(2,1)S(1)} collective-permute-done((bf16[64,2048]{1,0:T(8,128)(2,1)S(1)}, bf16[64,2048]{1,0:T(8,128)(2,1)S(1)}, u32[]{:S(2)}, u32[]{:S(2)}) %collective-permute-start.35) | collective-permute-done | bytes 262176 | tf_op jit(solution)/shard_map/ppermute | solution.py:20
  176.5 13.7 %collective-permute-done.36 = bf16[64,2048]{1,0:T(8,128)(2,1)S(1)} collective-permute-done((bf16[64,2048]{1,0:T(8,128)(2,1)S(1)}, bf16[64,2048]{1,0:T(8,128)(2,1)S(1)}, u32[]{:S(2)}, u32[]{:S(2)}) %collective-permute-start.36) | collective-permute-done | bytes 262176 | tf_op jit(solution)/shard_map/ppermute | solution.py:20
  190.3 7.2 %collective-permute-done.37 = bf16[64,2048]{1,0:T(8,128)(2,1)S(1)} collective-permute-done((bf16[64,2048]{1,0:T(8,128)(2,1)S(1)}, bf16[64,2048]{1,0:T(8,128)(2,1)S(1)}, u32[]{:S(2)}, u32[]{:S(2)}) %collective-permute-start.37) | collective-permute-done | bytes 262176 | tf_op jit(solution)/shard_map/ppermute | solution.py:20
  208.8 3.9 %collective-permute-done.39 = bf16[64,2048]{1,0:T(8,128)(2,1)S(1)} collective-permute-done((bf16[64,2048]{1,0:T(8,128)(2,1)S(1)}, bf16[64,2048]{1,0:T(8,128)(2,1)S(1)}, u32[]{:S(2)}, u32[]{:S(2)}) %collective-permute-start.39) | collective-permute-done | bytes 262176 | tf_op jit(solution)/shard_map/ppermute | solution.py:20
  215.2 4.0 %collective-permute-done.40 = bf16[64,2048]{1,0:T(8,128)(2,1)S(1)} collective-permute-done((bf16[64,2048]{1,0:T(8,128)(2,1)S(1)}, bf16[64,2048]{1,0:T(8,128)(2,1)S(1)}, u32[]{:S(2)}, u32[]{:S(2)}) %collective-permute-start.40) | collective-permute-done | bytes 262176 | tf_op jit(solution)/shard_map/ppermute | solution.py:20
  220.6 6.4 %collective-permute-done.41 = bf16[64,2048]{1,0:T(8,128)(2,1)S(1)} collective-permute-done((bf16[64,2048]{1,0:T(8,128)(2,1)S(1)}, bf16[64,2048]{1,0:T(8,128)(2,1)S(1)}, u32[]{:S(2)}, u32[]{:S(2)}) %collective-permute-start.41) | collective-permute-done | bytes 262176 | tf_op jit(solution)/shard_map/ppermute | solution.py:21
  228.8 6.8 %collective-permute-done.42 = bf16[64,2048]{1,0:T(8,128)(2,1)S(1)} collective-permute-done((bf16[64,2048]{1,0:T(8,128)(2,1)S(1)}, bf16[64,2048]{1,0:T(8,128)(2,1)S(1)}, u32[]{:S(2)}, u32[]{:S(2)}) %collective-permute-start.42) | collective-permute-done | bytes 262176 | tf_op jit(solution)/shard_map/ppermute | solution.py:21
  237.8 4.5 %fusion.1 = f32[1024,1024]{1,0:T(8,128)S(1)} fusion(bf16[2,1024,2048]{2,1,0:T(8,128)(2,1)S(1)} %constant_dynamic-update-slice_fusion, bf16[3,2048,1024]{2,1,0:T(8,128)(2,1)S(1)} %bitcast.141), kind=kOutput, calls=%fused_computation.3 | convolution fusion | flops 4294967296 | bytes 12582912 | tf_op jit(solution)/shard_map/dot_general | solution.py:102
  245.9 4.5 %fusion = f32[1024,1024]{1,0:T(8,128)S(1)} fusion(bf16[2,1024,2048]{2,1,0:T(8,128)(2,1)S(1)} %constant_dynamic-update-slice_fusion, bf16[3,2048,1024]{2,1,0:T(8,128)(2,1)S(1)} %bitcast.141), kind=kOutput, calls=%fused_computation.1 | convolution fusion | flops 4294967296 | bytes 12582912 | tf_op jit(solution)/shard_map/dot_general | solution.py:103
  253.3 7.1 %collective-permute-done.45 = bf16[64,2048]{1,0:T(8,128)(2,1)S(1)} collective-permute-done((bf16[64,2048]{1,0:T(8,128)(2,1)S(1)}, bf16[64,2048]{1,0:T(8,128)(2,1)S(1)}, u32[]{:S(2)}, u32[]{:S(2)}) %collective-permute-start.45) | collective-permute-done | bytes 262176 | tf_op jit(solution)/shard_map/ppermute | solution.py:21
  260.7 6.0 %collective-permute-done.46 = bf16[64,2048]{1,0:T(8,128)(2,1)S(1)} collective-permute-done((bf16[64,2048]{1,0:T(8,128)(2,1)S(1)}, bf16[64,2048]{1,0:T(8,128)(2,1)S(1)}, u32[]{:S(2)}, u32[]{:S(2)}) %collective-permute-start.46) | collective-permute-done | bytes 262176 | tf_op jit(solution)/shard_map/ppermute | solution.py:21
  267.2 5.9 %collective-permute-done.47 = bf16[64,2048]{1,0:T(8,128)(2,1)S(1)} collective-permute-done((bf16[64,2048]{1,0:T(8,128)(2,1)S(1)}, bf16[64,2048]{1,0:T(8,128)(2,1)S(1)}, u32[]{:S(2)}, u32[]{:S(2)}) %collective-permute-start.47) | collective-permute-done | bytes 262176 | tf_op jit(solution)/shard_map/ppermute | solution.py:21
  273.2 4.5 %add_add_fusion = f32[1024,1024]{1,0:T(8,128)S(1)} fusion(f32[1024,1024]{1,0:T(8,128)S(1)} %fusion.1, f32[1024,1024]{1,0:T(8,128)S(1)} %fusion, bf16[1024,2048]{1,0:T(8,128)(2,1)S(1)} %constant_dynamic-update-slice_fusion.32, bf16[3,2048,1024]{2,1,0:T(8,128)(2,1)S(1)} %bitcast.141), kind=kOutput, calls=%fused_computation.9 | convolution fusion | flops 4297064448 | bytes 20971520 | tf_op jit(solution)/shard_map/dot_general | solution.py:104
  277.9 4.1 %collective-permute-done.48 = f32[8,64,1024]{2,1,0:T(8,128)S(1)} collective-permute-done((f32[8,64,1024]{2,1,0:T(8,128)S(1)}, f32[8,64,1024]{2,1,0:T(8,128)S(1)}, u32[]{:S(2)}, u32[]{:S(2)}) %collective-permute-start.48) | collective-permute-done | bytes 2097184 | tf_op jit(solution)/shard_map/ppermute | solution.py:26
  282.7 14.0 %collective-permute-done.49 = bf16[1,8,32,1024]{3,2,1,0:T(8,128)(2,1)S(1)} collective-permute-done((bf16[1,8,32,1024]{3,2,1,0:T(8,128)(2,1)S(1)}, bf16[1,8,32,1024]{3,2,1,0:T(8,128)(2,1)S(1)}, u32[]{:S(2)}, u32[]{:S(2)}) %collective-permute-start.49) | collective-permute-done | bytes 524320 | tf_op jit(solution)/shard_map/ppermute | solution.py:26
  297.0 17.6 %all_to_all.5 = bf16[8,32,1024]{2,1,0:T(8,128)(2,1)S(1)} all-to-all(bf16[8,32,1024]{2,1,0:T(8,128)(2,1)S(1)} %constant_dynamic-update-slice_fusion.48), channel_id=1, replica_groups=mesh['dp'=8,'tensor'=4] {'dp'}, dimensions={0} | all-to-all | bytes 1048576 | tf_op jit(solution)/shard_map/all_to_all | solution.py:110
  (190 shorter events, 127.2 us)
Async XLA Ops:
  1.1 9.3 %collective-permute-start = (bf16[64,2048]{1,0:T(8,128)(2,1)S(1)}, bf16[64,2048]{1,0:T(8,128)(2,1)S(1)}, u32[]{:S(2)}, u32[]{:S(2)}) collective-permute-start(bf16[64,2048]{1,0:T(8,128)(2,1)S(1)} %bitcast.126), channel_id=1, source_target_pairs={{0,8},{8,16},{16,24},{24,28},{28,20},{20,12},{12,4},{4,0},{1,9},{9... | collective-permute-start | bytes 786440 | tf_op jit(solution)/shard_map/ppermute | solution.py:20
  74.5 30.3 %collective-permute-start.28 = (f32[8,64,1024]{2,1,0:T(8,128)}, f32[8,64,1024]{2,1,0:T(8,128)S(1)}, u32[]{:S(2)}, u32[]{:S(2)}) collective-permute-start(f32[8,64,1024]{2,1,0:T(8,128)} %dynamic-slice_bitcast_fusion.1), channel_id=1, source_target_pairs={{0,1},{1,0},{2,3},{3,2},{4,5},{5,4},{6,7},{7,6},{8,9},{9,8},{10,11... | collective-permute-start | bytes 6291464 | tf_op jit(solution)/shard_map/ppermute | solution.py:26
  74.5 14.4 %collective-permute-start.14 = (bf16[2,64,2048]{2,1,0:T(8,128)(2,1)S(1)}, bf16[2,64,2048]{2,1,0:T(8,128)(2,1)}, u32[]{:S(2)}, u32[]{:S(2)}) collective-permute-start(bf16[2,64,2048]{2,1,0:T(8,128)(2,1)S(1)} %get-tuple-element.9), channel_id=1, source_target_pairs={{0,8},{8,16},{16,24},{24,28},{28,20},{20,12},{12,4},{4,0},{1,9},{9... | collective-permute-start | bytes 1572872 | tf_op jit(solution)/shard_map/ppermute | solution.py:20
  76.1 14.4 %collective-permute-start.21 = (bf16[2,64,2048]{2,1,0:T(8,128)(2,1)S(1)}, bf16[2,64,2048]{2,1,0:T(8,128)(2,1)}, u32[]{:S(2)}, u32[]{:S(2)}) collective-permute-start(bf16[2,64,2048]{2,1,0:T(8,128)(2,1)S(1)} %get-tuple-element.10), channel_id=1, source_target_pairs={{8,0},{16,8},{24,16},{28,24},{20,28},{12,20},{4,12},{0,4},{9,1},{1... | collective-permute-start | bytes 1572872 | tf_op jit(solution)/shard_map/ppermute | solution.py:21
  89.0 13.9 %collective-permute-start.15 = (bf16[2,64,2048]{2,1,0:T(8,128)(2,1)}, bf16[2,64,2048]{2,1,0:T(8,128)(2,1)}, u32[]{:S(2)}, u32[]{:S(2)}) collective-permute-start(bf16[2,64,2048]{2,1,0:T(8,128)(2,1)} %collective-permute-done.14), channel_id=1, source_target_pairs={{0,8},{8,16},{16,24},{24,28},{28,20},{20,12},{12,4},{4,0},{1,9},{9... | collective-permute-start | bytes 1572872 | tf_op jit(solution)/shard_map/ppermute | solution.py:20
  90.5 13.9 %collective-permute-start.22 = (bf16[2,64,2048]{2,1,0:T(8,128)(2,1)}, bf16[2,64,2048]{2,1,0:T(8,128)(2,1)}, u32[]{:S(2)}, u32[]{:S(2)}) collective-permute-start(bf16[2,64,2048]{2,1,0:T(8,128)(2,1)} %collective-permute-done.21), channel_id=1, source_target_pairs={{8,0},{16,8},{24,16},{28,24},{20,28},{12,20},{4,12},{0,4},{9,1},{1... | collective-permute-start | bytes 1572872 | tf_op jit(solution)/shard_map/ppermute | solution.py:21
  102.8 13.0 %collective-permute-start.16 = (bf16[2,64,2048]{2,1,0:T(8,128)(2,1)}, bf16[2,64,2048]{2,1,0:T(8,128)(2,1)}, u32[]{:S(2)}, u32[]{:S(2)}) collective-permute-start(bf16[2,64,2048]{2,1,0:T(8,128)(2,1)} %collective-permute-done.15), channel_id=1, source_target_pairs={{0,8},{8,16},{16,24},{24,28},{28,20},{20,12},{12,4},{4,0},{1,9},{9... | collective-permute-start | bytes 1572872 | tf_op jit(solution)/shard_map/ppermute | solution.py:20
  104.4 14.1 %collective-permute-start.23 = (bf16[2,64,2048]{2,1,0:T(8,128)(2,1)}, bf16[2,64,2048]{2,1,0:T(8,128)(2,1)}, u32[]{:S(2)}, u32[]{:S(2)}) collective-permute-start(bf16[2,64,2048]{2,1,0:T(8,128)(2,1)} %collective-permute-done.22), channel_id=1, source_target_pairs={{8,0},{16,8},{24,16},{28,24},{20,28},{12,20},{4,12},{0,4},{9,1},{1... | collective-permute-start | bytes 1572872 | tf_op jit(solution)/shard_map/ppermute | solution.py:21
  108.0 12.4 %collective-permute-start.29 = (bf16[1,4,64,1024]{3,2,1,0:T(8,128)(2,1)}, bf16[1,4,64,1024]{3,2,1,0:T(8,128)(2,1)}, u32[]{:S(2)}, u32[]{:S(2)}) collective-permute-start(bf16[1,4,64,1024]{3,2,1,0:T(8,128)(2,1)} %fusion.11), channel_id=1, source_target_pairs={{0,2},{1,3},{2,0},{3,1},{4,6},{5,7},{6,4},{7,5},{8,10},{9,11},{10,... | collective-permute-start | bytes 1572872 | tf_op jit(solution)/shard_map/ppermute | solution.py:26
  115.8 15.1 %collective-permute-start.17 = (bf16[2,64,2048]{2,1,0:T(8,128)(2,1)}, bf16[2,64,2048]{2,1,0:T(8,128)(2,1)S(1)}, u32[]{:S(2)}, u32[]{:S(2)}) collective-permute-start(bf16[2,64,2048]{2,1,0:T(8,128)(2,1)} %collective-permute-done.16), channel_id=1, source_target_pairs={{0,8},{8,16},{16,24},{24,28},{28,20},{20,12},{12,4},{4,0},{1,9},{9... | collective-permute-start | bytes 1572872 | tf_op jit(solution)/shard_map/ppermute | solution.py:20
  118.5 14.2 %collective-permute-start.24 = (bf16[2,64,2048]{2,1,0:T(8,128)(2,1)}, bf16[2,64,2048]{2,1,0:T(8,128)(2,1)S(1)}, u32[]{:S(2)}, u32[]{:S(2)}) collective-permute-start(bf16[2,64,2048]{2,1,0:T(8,128)(2,1)} %collective-permute-done.23), channel_id=1, source_target_pairs={{8,0},{16,8},{24,16},{28,24},{20,28},{12,20},{4,12},{0,4},{9,1},{1... | collective-permute-start | bytes 1572872 | tf_op jit(solution)/shard_map/ppermute | solution.py:21
  121.7 14.4 %collective-permute-start.33 = (bf16[64,1024]{1,0:T(8,128)(2,1)S(1)}, bf16[64,1024]{1,0:T(8,128)(2,1)S(1)}, u32[]{:S(2)}, u32[]{:S(2)}) collective-permute-start(bf16[64,1024]{1,0:T(8,128)(2,1)S(1)} %get-tuple-element.20), channel_id=1, source_target_pairs={{0,24},{1,16},{2,4},{3,12},{4,8},{5,0},{6,20},{7,28},{8,25},{9,17}... | collective-permute-start | bytes 393224 | tf_op jit(solution)/shard_map/ppermute | solution.py:91
  127.4 11.7 %collective-permute-start.32 = (bf16[64,1024]{1,0:T(8,128)(2,1)S(1)}, bf16[64,1024]{1,0:T(8,128)(2,1)S(1)}, u32[]{:S(2)}, u32[]{:S(2)}) collective-permute-start(bf16[64,1024]{1,0:T(8,128)(2,1)S(1)} %get-tuple-element.21), channel_id=1, source_target_pairs={{0,16},{1,8},{2,12},{3,20},{4,0},{5,24},{6,28},{7,4},{8,17},{9,9},... | collective-permute-start | bytes 393224 | tf_op jit(solution)/shard_map/ppermute | solution.py:91
  132.7 19.2 %collective-permute-start.18 = (bf16[2,64,2048]{2,1,0:T(8,128)(2,1)S(1)}, bf16[2,64,2048]{2,1,0:T(8,128)(2,1)S(1)}, u32[]{:S(2)}, u32[]{:S(2)}) collective-permute-start(bf16[2,64,2048]{2,1,0:T(8,128)(2,1)S(1)} %collective-permute-done.17), channel_id=1, source_target_pairs={{0,8},{8,16},{16,24},{24,28},{28,20},{20,12},{12,4},{4,0},{1,9},{9... | collective-permute-start | bytes 1572872 | tf_op jit(solution)/shard_map/ppermute | solution.py:20
  136.1 17.6 %collective-permute-start.25 = (bf16[2,64,2048]{2,1,0:T(8,128)(2,1)S(1)}, bf16[2,64,2048]{2,1,0:T(8,128)(2,1)S(1)}, u32[]{:S(2)}, u32[]{:S(2)}) collective-permute-start(bf16[2,64,2048]{2,1,0:T(8,128)(2,1)S(1)} %collective-permute-done.24), channel_id=1, source_target_pairs={{8,0},{16,8},{24,16},{28,24},{20,28},{12,20},{4,12},{0,4},{9,1},{1... | collective-permute-start | bytes 1572872 | tf_op jit(solution)/shard_map/ppermute | solution.py:21
  139.4 18.1 %collective-permute-start.34 = (bf16[64,2048]{1,0:T(8,128)(2,1)S(1)}, bf16[64,2048]{1,0:T(8,128)(2,1)S(1)}, u32[]{:S(2)}, u32[]{:S(2)}) collective-permute-start(bf16[64,2048]{1,0:T(8,128)(2,1)S(1)} %get-tuple-element.30), channel_id=1, source_target_pairs={{0,8},{8,16},{16,24},{24,28},{28,20},{20,12},{12,4},{4,0},{1,9},{9... | collective-permute-start | bytes 786440 | tf_op jit(solution)/shard_map/ppermute | solution.py:20
  151.9 16.9 %collective-permute-start.19 = (bf16[2,64,2048]{2,1,0:T(8,128)(2,1)S(1)}, bf16[2,64,2048]{2,1,0:T(8,128)(2,1)S(1)}, u32[]{:S(2)}, u32[]{:S(2)}) collective-permute-start(bf16[2,64,2048]{2,1,0:T(8,128)(2,1)S(1)} %collective-permute-done.18), channel_id=1, source_target_pairs={{0,8},{8,16},{16,24},{24,28},{28,20},{20,12},{12,4},{4,0},{1,9},{9... | collective-permute-start | bytes 1572872 | tf_op jit(solution)/shard_map/ppermute | solution.py:20
  153.7 20.7 %collective-permute-start.26 = (bf16[2,64,2048]{2,1,0:T(8,128)(2,1)S(1)}, bf16[2,64,2048]{2,1,0:T(8,128)(2,1)S(1)}, u32[]{:S(2)}, u32[]{:S(2)}) collective-permute-start(bf16[2,64,2048]{2,1,0:T(8,128)(2,1)S(1)} %collective-permute-done.25), channel_id=1, source_target_pairs={{8,0},{16,8},{24,16},{28,24},{20,28},{12,20},{4,12},{0,4},{9,1},{1... | collective-permute-start | bytes 1572872 | tf_op jit(solution)/shard_map/ppermute | solution.py:21
  157.5 16.9 %collective-permute-start.35 = (bf16[64,2048]{1,0:T(8,128)(2,1)S(1)}, bf16[64,2048]{1,0:T(8,128)(2,1)S(1)}, u32[]{:S(2)}, u32[]{:S(2)}) collective-permute-start(bf16[64,2048]{1,0:T(8,128)(2,1)S(1)} %collective-permute-done.34), channel_id=1, source_target_pairs={{0,8},{8,16},{16,24},{24,28},{28,20},{20,12},{12,4},{4,0},{1,9},{9... | collective-permute-start | bytes 786440 | tf_op jit(solution)/shard_map/ppermute | solution.py:20
  168.7 21.5 %collective-permute-start.20 = (bf16[2,64,2048]{2,1,0:T(8,128)(2,1)S(1)}, bf16[2,64,2048]{2,1,0:T(8,128)(2,1)S(1)}, u32[]{:S(2)}, u32[]{:S(2)}) collective-permute-start(bf16[2,64,2048]{2,1,0:T(8,128)(2,1)S(1)} %collective-permute-done.19), channel_id=1, source_target_pairs={{0,8},{8,16},{16,24},{24,28},{28,20},{20,12},{12,4},{4,0},{1,9},{9... | collective-permute-start | bytes 1572872 | tf_op jit(solution)/shard_map/ppermute | solution.py:20
  174.3 15.9 %collective-permute-start.36 = (bf16[64,2048]{1,0:T(8,128)(2,1)S(1)}, bf16[64,2048]{1,0:T(8,128)(2,1)S(1)}, u32[]{:S(2)}, u32[]{:S(2)}) collective-permute-start(bf16[64,2048]{1,0:T(8,128)(2,1)S(1)} %collective-permute-done.35), channel_id=1, source_target_pairs={{0,8},{8,16},{16,24},{24,28},{28,20},{20,12},{12,4},{4,0},{1,9},{9... | collective-permute-start | bytes 786440 | tf_op jit(solution)/shard_map/ppermute | solution.py:20
  174.4 54.4 %collective-permute-start.27 = (bf16[2,64,2048]{2,1,0:T(8,128)(2,1)S(1)}, bf16[2,64,2048]{2,1,0:T(8,128)(2,1)S(1)}, u32[]{:S(2)}, u32[]{:S(2)}) collective-permute-start(bf16[2,64,2048]{2,1,0:T(8,128)(2,1)S(1)} %collective-permute-done.26), channel_id=1, source_target_pairs={{8,0},{16,8},{24,16},{28,24},{20,28},{12,20},{4,12},{0,4},{9,1},{1... | collective-permute-start | bytes 1572872 | tf_op jit(solution)/shard_map/ppermute | solution.py:21
  235.6 9.3 %collective-permute-start.43 = (bf16[64,2048]{1,0:T(8,128)(2,1)S(1)}, bf16[64,2048]{1,0:T(8,128)(2,1)S(1)}, u32[]{:S(2)}, u32[]{:S(2)}) collective-permute-start(bf16[64,2048]{1,0:T(8,128)(2,1)S(1)} %collective-permute-done.42), channel_id=1, source_target_pairs={{8,0},{16,8},{24,16},{28,24},{20,28},{12,20},{4,12},{0,4},{9,1},{1... | collective-permute-start | bytes 786440 | tf_op jit(solution)/shard_map/ppermute | solution.py:21
  282.6 14.0 %collective-permute-start.49 = (bf16[1,8,32,1024]{3,2,1,0:T(8,128)(2,1)S(1)}, bf16[1,8,32,1024]{3,2,1,0:T(8,128)(2,1)S(1)}, u32[]{:S(2)}, u32[]{:S(2)}) collective-permute-start(bf16[1,8,32,1024]{3,2,1,0:T(8,128)(2,1)S(1)} %fusion.12), channel_id=1, source_target_pairs={{0,2},{1,3},{2,0},{3,1},{4,6},{5,7},{6,4},{7,5},{8,10},{9,11},{10,... | collective-permute-start | bytes 1572872 | tf_op jit(solution)/shard_map/ppermute | solution.py:26
  (37 other events, 570.8 us)

commit v2 on v1

--- a/solution.py
+++ b/solution.py
@@ -63,19 +63,23 @@
     def slot_of(q):
         return jnp.where(core == 0, lax.rem(place - q + groups, groups), lax.rem(q - place + groups, groups))
 
+    depth_pair = jnp.concatenate(sides(jnp.concatenate([low_hidden, mid_hidden], axis=1)), axis=0)
+    depth_all = lax.all_gather(depth_pair, "dp", axis=0, tiled=True)
+
+    def both_sides(up, down, weight):
+        product = jnp.dot(jnp.concatenate(up + down, axis=0), weight, preferred_element_type=jnp.float32)
+        return product.reshape(2, len(up), side_rows, width)
+
+    def sum_cores(products):
+        return pick(products, core) + swap(pick(products, 1 - core), 1)
+
     attn_up, attn_down = ring_gather(*sides(attn_heads))
-    low_sides, mid_sides = sides(low_hidden), sides(mid_hidden)
-    depth_sides = [jnp.stack([low_sides[s], mid_sides[s]]) for s in range(2)]
-    depth_sides[0], depth_sides[1], last_up, last_down = lax.optimization_barrier(
-        (depth_sides[0], depth_sides[1], attn_up[-1], attn_down[-1])
+    head_core = jnp.concatenate(
+        [
+            sum_cores(both_sides(attn_up[low:high], attn_down[low:high], out_weight))
+            for low, high in ((0, groups - 2), (groups - 2, groups))
+        ]
     )
-    attn_up[-1], attn_down[-1] = last_up, last_down
-    depth_up, depth_down = ring_gather(*depth_sides)
-
-    attn_all = jnp.concatenate(attn_up + attn_down, axis=0)
-    head_partial = jnp.dot(attn_all, out_weight, preferred_element_type=jnp.float32)
-    head_partial = head_partial.reshape(2, groups, side_rows, width)
-    head_core = pick(head_partial, core) + swap(pick(head_partial, 1 - core), 1)
     by_place = jnp.stack([pick(head_core, slot_of(q)) for q in range(groups)])
     held = reduce_over_x(by_place.reshape(xs, rounds, side_rows, width), x).astype(jnp.bfloat16)
 
@@ -97,18 +101,33 @@
         top_sides.append((rest.astype(jnp.float32) + head_sum).astype(jnp.bfloat16))
     top_up, top_down = ring_gather(*top_sides)
 
-    depth_all = jnp.concatenate(depth_up + depth_down, axis=1)
-    top_all = jnp.concatenate(top_up + top_down, axis=0)
-    joined = jnp.dot(depth_all[0], join_weight[0], preferred_element_type=jnp.float32)
-    joined = joined + jnp.dot(depth_all[1], join_weight[1], preferred_element_type=jnp.float32)
-    joined = joined + jnp.dot(top_all, join_weight[2], preferred_element_type=jnp.float32)
-    joined = joined.reshape(2, groups, side_rows, width)
-    joined_core = pick(joined, core) + swap(pick(joined, 1 - core), 1)
-    by_owner = jnp.moveaxis(joined_core.reshape(groups, xs, rows, width), 1, 0)
-    owned = reduce_over_x(by_owner, x)
-    by_group = jnp.stack([pick(owned, slot_of(int(place_of[g]))) for g in range(groups)]).astype(jnp.bfloat16)
-    moved = lax.all_to_all(by_group, "dp", split_axis=0, concat_axis=0, tiled=True)
-    joined_sum = jnp.moveaxis(moved, 0, 1).reshape(rows, groups * width).astype(jnp.float32)
+    joined_depths = jnp.dot(depth_all, join_weight[:2].reshape(2 * features, width), preferred_element_type=jnp.float32)
+    joined_depths = joined_depths.reshape(groups, 2, side_rows, width)
+    ring_index = jnp.asarray(ring, jnp.int32)
+    owned = []
+    starts = sorted({0, groups // 2 - 1, groups - 3, groups - 1, groups})
+    for low, high in zip(starts, starts[1:]):
+        product = both_sides(top_up[low:high], top_down[low:high], join_weight[2])
+        rest = [
+            [pick(joined_depths, ring_index[lax.rem(place + sign * s + groups, groups)])[side] for s in range(low, high)]
+            for side, sign in ((0, -1), (1, 1))
+        ]
+        joined_core = sum_cores(product + jnp.stack([jnp.stack(part) for part in rest]))
+        by_owner = jnp.moveaxis(joined_core.reshape(high - low, xs, rows, width), 1, 0)
+        chunk = reduce_over_x(by_owner, x).astype(jnp.bfloat16)
+        for s in range(low, high):
+            moves = [
+                (int(ring[q]) * owners + t, int(ring[(q + (s if t % 2 else -s)) % groups]) * owners + t)
+                for q in range(groups)
+                for t in range(owners)
+            ]
+            owned.append(lax.ppermute(chunk[s - low], ("dp", "tensor"), moves) if s else chunk[0])
+    owned = jnp.stack(owned)
+    by_columns = []
+    for g in range(groups):
+        ahead = lax.rem(int(place_of[g]) - place + groups, groups)
+        by_columns.append(pick(owned, jnp.where(core == 0, ahead, lax.rem(groups - ahead, groups))))
+    joined_sum = jnp.concatenate(by_columns, axis=1).astype(jnp.float32)
     inverse_rms = lax.rsqrt(jnp.mean(joined_sum * joined_sum, axis=1, keepdims=True) + 1e-05)
     return (joined_sum * inverse_rms * join_gain).astype(jnp.bfloat16)
 

time: 317 us -> 355 us (1.12)
  between operations: 11.6 us -> 60.6 us
  starting transfers between devices: 58.4 us -> 85.7 us
  blocking collectives: 17.6 us -> 0 us
  local copies, waits for them, and re-layouts: 32.2 us -> 17.2 us
  waiting for transfers between devices: 171 us -> 159 us
    ppermute x21 -> x14, waiting for transfers between devices: 110 us -> 58.5 us  [ring_gather(): above.append(lax.ppermute(above[-1], 'dp', up))]
    ppermute x21 -> x14, waiting for transfers between devices: 41.2 us -> 64.9 us  [ring_gather(): below.append(lax.ppermute(below[-1], 'dp', down))]
    unnamed x79 -> x52, local copies, waits for them, and re-layouts: 24 us -> 3.44 us
    all_to_all x1 -> x0, blocking collectives: 17.6 us -> none  [local(): lax.all_to_all(by_group, 'dp', split_axis=0, concat_axis=0, tiled=True)]
    ppermute x0 -> x7, waiting for transfers between devices: none -> 13 us  [local(): lax.ppermute(chunk[s - low], ('dp', 'tensor'), moves)]
    ppermute x0 -> x7, starting transfers between devices: none -> 9.53 us  [local(): lax.ppermute(chunk[s - low], ('dp', 'tensor'), moves)]
    ppermute x4 -> x11, starting transfers between devices: 1.63 us -> 9.97 us  [swap(): lax.ppermute(values, 'tensor', [(t, t ^ bit) for t in range(lax.axis_size...]
    slice x0 -> x1, local copies, waits for them, and re-layouts: none -> 7.66 us  [local(): join_weight[:2].reshape(2 * features, width)]
  transfers between devices with their start and end apart: 50 -> 51, of which waited for: 32 -> 30; matrix products, arithmetic and copies ran while one was open for 10% -> 8% of each run, Pallas kernels for 0% -> 0%
where the time goes in v2:
time: 355 us; the launch traced here: 354 us
  waiting for transfers between devices  159 us (45%)
  starting transfers between devices  85.7 us (24%)
  between operations  60.6 us (17%)
  matrix products  22.6 us (6%)
  local copies, waits for them, and re-layouts  17.2 us (5%)
  other arithmetic  8.5 us (2%)
    ppermute x14, waiting for transfers between devices, ring_gather(): below.append(lax.ppermute(below[-1], 'dp', down))  64.9 us
    ppermute x14, waiting for transfers between devices, ring_gather(): above.append(lax.ppermute(above[-1], 'dp', up))  58.5 us
    ppermute x14, starting transfers between devices, ring_gather(): above.append(lax.ppermute(above[-1], 'dp', up))  36 us
    ppermute x11, waiting for transfers between devices, swap(): lax.ppermute(values, 'tensor', [(t, t ^ bit) for t in range(lax.axis_size...  22.4 us
    ppermute x14, starting transfers between devices, ring_gather(): below.append(lax.ppermute(below[-1], 'dp', down))  16.8 us
    ppermute x4, starting transfers between devices, local(): arrived.append(lax.ppermute(piece, ('dp', 'tensor'), moves))  13.3 us
    ppermute x7, waiting for transfers between devices, local(): lax.ppermute(chunk[s - low], ('dp', 'tensor'), moves)  13 us
    dot_general x1, matrix products, local(): jnp.dot(depth_all, join_weight[:2].reshape(2 * features, width), preferre...  12.7 us
  transfers between devices with their start and end apart: 51, of which 30 were waited for; matrix products, arithmetic and copies ran while one was open for 8% of the time, Pallas kernels for 0%

profile of v2, /device:TPU:0, one launch (start us, length us, event | category | flops | bytes accessed | tf_op | source)
XLA Modules:
  0.0 353.8 jit_solution(3568453718303320720)
XLA Ops:
  12.2 6.2 %collective-permute-done = bf16[64,2048]{1,0:T(8,128)(2,1)S(1)} collective-permute-done((bf16[64,2048]{1,0:T(8,128)(2,1)S(1)}, bf16[64,2048]{1,0:T(8,128)(2,1)S(1)}, u32[]{:S(2)}, u32[]{:S(2)}) %collective-permute-start) | collective-permute-done | bytes 262176 | tf_op jit(solution)/shard_map/ppermute | solution.py:20
  20.5 11.0 %collective-permute-done.1 = bf16[64,2048]{1,0:T(8,128)(2,1)S(1)} collective-permute-done((bf16[64,2048]{1,0:T(8,128)(2,1)S(1)}, bf16[64,2048]{1,0:T(8,128)(2,1)S(1)}, u32[]{:S(2)}, u32[]{:S(2)}) %collective-permute-start.1) | collective-permute-done | bytes 262176 | tf_op jit(solution)/shard_map/ppermute | solution.py:20
  31.4 5.9 %collective-permute-start.2 = (bf16[64,2048]{1,0:T(8,128)(2,1)S(1)}, bf16[64,2048]{1,0:T(8,128)(2,1)S(1)}, u32[]{:S(2)}, u32[]{:S(2)}) collective-permute-start(bf16[64,2048]{1,0:T(8,128)(2,1)S(1)} %collective-permute-done.1), channel_id=1, source_target_pairs={{0,8},{8,16},{16,24},{24,28},{28,20},{20,12},{12,4},{4,0},{1,9},{9... | collective-permute-start | bytes 786440 | tf_op jit(solution)/shard_map/ppermute | solution.py:20
  40.3 7.1 %collective-permute-done.2 = bf16[64,2048]{1,0:T(8,128)(2,1)S(1)} collective-permute-done((bf16[64,2048]{1,0:T(8,128)(2,1)S(1)}, bf16[64,2048]{1,0:T(8,128)(2,1)S(1)}, u32[]{:S(2)}, u32[]{:S(2)}) %collective-permute-start.2) | collective-permute-done | bytes 262176 | tf_op jit(solution)/shard_map/ppermute | solution.py:20
  47.4 9.8 %collective-permute-start.3 = (bf16[64,2048]{1,0:T(8,128)(2,1)S(1)}, bf16[64,2048]{1,0:T(8,128)(2,1)S(1)}, u32[]{:S(2)}, u32[]{:S(2)}) collective-permute-start(bf16[64,2048]{1,0:T(8,128)(2,1)S(1)} %collective-permute-done.2), channel_id=1, source_target_pairs={{0,8},{8,16},{16,24},{24,28},{28,20},{20,12},{12,4},{4,0},{1,9},{9... | collective-permute-start | bytes 786440 | tf_op jit(solution)/shard_map/ppermute | solution.py:20
  60.5 7.1 %collective-permute-done.3 = bf16[64,2048]{1,0:T(8,128)(2,1)S(1)} collective-permute-done((bf16[64,2048]{1,0:T(8,128)(2,1)S(1)}, bf16[64,2048]{1,0:T(8,128)(2,1)S(1)}, u32[]{:S(2)}, u32[]{:S(2)}) %collective-permute-start.3) | collective-permute-done | bytes 262176 | tf_op jit(solution)/shard_map/ppermute | solution.py:20
  67.5 5.7 %collective-permute-start.4 = (bf16[64,2048]{1,0:T(8,128)(2,1)S(1)}, bf16[64,2048]{1,0:T(8,128)(2,1)S(1)}, u32[]{:S(2)}, u32[]{:S(2)}) collective-permute-start(bf16[64,2048]{1,0:T(8,128)(2,1)S(1)} %collective-permute-done.3), channel_id=1, source_target_pairs={{0,8},{8,16},{16,24},{24,28},{28,20},{20,12},{12,4},{4,0},{1,9},{9... | collective-permute-start | bytes 786440 | tf_op jit(solution)/shard_map/ppermute | solution.py:20
  74.1 9.6 %collective-permute-done.9 = bf16[64,2048]{1,0:T(8,128)(2,1)S(1)} collective-permute-done((bf16[64,2048]{1,0:T(8,128)(2,1)S(1)}, bf16[64,2048]{1,0:T(8,128)(2,1)S(1)}, u32[]{:S(2)}, u32[]{:S(2)}) %collective-permute-start.9) | collective-permute-done | bytes 262176 | tf_op jit(solution)/shard_map/ppermute | solution.py:21
  89.3 14.4 %collective-permute-done.13 = bf16[64,2048]{1,0:T(8,128)(2,1)S(1)} collective-permute-done((bf16[64,2048]{1,0:T(8,128)(2,1)S(1)}, bf16[64,2048]{1,0:T(8,128)(2,1)S(1)}, u32[]{:S(2)}, u32[]{:S(2)}) %collective-permute-start.13) | collective-permute-done | bytes 262176 | tf_op jit(solution)/shard_map/ppermute | solution.py:21
  107.0 15.1 %collective-permute-done.14 = bf16[64,2048]{1,0:T(8,128)(2,1)S(1)} collective-permute-done((bf16[64,2048]{1,0:T(8,128)(2,1)S(1)}, bf16[64,2048]{1,0:T(8,128)(2,1)S(1)}, u32[]{:S(2)}, u32[]{:S(2)}) %collective-permute-start.14) | collective-permute-done | bytes 262176 | tf_op jit(solution)/shard_map/ppermute | solution.py:21
  143.0 13.2 %collective-permute-done.16 = bf16[1,4,64,1024]{3,2,1,0:T(8,128)(2,1)S(1)} collective-permute-done((bf16[1,4,64,1024]{3,2,1,0:T(8,128)(2,1)}, bf16[1,4,64,1024]{3,2,1,0:T(8,128)(2,1)S(1)}, u32[]{:S(2)}, u32[]{:S(2)}) %collective-permute-start.16) | collective-permute-done | bytes 524320 | tf_op jit(solution)/shard_map/ppermute | solution.py:26
  156.4 6.9 %collective-permute-start.20 = (bf16[64,1024]{1,0:T(8,128)(2,1)S(1)}, bf16[64,1024]{1,0:T(8,128)(2,1)S(1)}, u32[]{:S(2)}, u32[]{:S(2)}) collective-permute-start(bf16[64,1024]{1,0:T(8,128)(2,1)S(1)} %get-tuple-element.30), channel_id=1, source_target_pairs={{0,24},{1,16},{2,4},{3,12},{4,8},{5,0},{6,20},{7,28},{8,25},{9,17}... | collective-permute-start | bytes 393224 | tf_op jit(solution)/shard_map/ppermute | solution.py:95
  163.3 4.3 %collective-permute-start.19 = (bf16[64,1024]{1,0:T(8,128)(2,1)S(1)}, bf16[64,1024]{1,0:T(8,128)(2,1)S(1)}, u32[]{:S(2)}, u32[]{:S(2)}) collective-permute-start(bf16[64,1024]{1,0:T(8,128)(2,1)S(1)} %get-tuple-element.31), channel_id=1, source_target_pairs={{0,16},{1,8},{2,12},{3,20},{4,0},{5,24},{6,28},{7,4},{8,17},{9,9},... | collective-permute-start | bytes 393224 | tf_op jit(solution)/shard_map/ppermute | solution.py:95
  172.5 5.2 %collective-permute-start.21 = (bf16[64,2048]{1,0:T(8,128)(2,1)S(1)}, bf16[64,2048]{1,0:T(8,128)(2,1)S(1)}, u32[]{:S(2)}, u32[]{:S(2)}) collective-permute-start(bf16[64,2048]{1,0:T(8,128)(2,1)S(1)} %get-tuple-element.57), channel_id=1, source_target_pairs={{0,8},{8,16},{16,24},{24,28},{28,20},{20,12},{12,4},{4,0},{1,9},{9... | collective-permute-start | bytes 786440 | tf_op jit(solution)/shard_map/ppermute | solution.py:20
  177.7 11.2 %collective-permute-done.21 = bf16[64,2048]{1,0:T(8,128)(2,1)S(1)} collective-permute-done((bf16[64,2048]{1,0:T(8,128)(2,1)S(1)}, bf16[64,2048]{1,0:T(8,128)(2,1)S(1)}, u32[]{:S(2)}, u32[]{:S(2)}) %collective-permute-start.21) | collective-permute-done | bytes 262176 | tf_op jit(solution)/shard_map/ppermute | solution.py:20
  188.9 7.4 %collective-permute-done.22 = bf16[64,2048]{1,0:T(8,128)(2,1)S(1)} collective-permute-done((bf16[64,2048]{1,0:T(8,128)(2,1)S(1)}, bf16[64,2048]{1,0:T(8,128)(2,1)S(1)}, u32[]{:S(2)}, u32[]{:S(2)}) %collective-permute-start.22) | collective-permute-done | bytes 262176 | tf_op jit(solution)/shard_map/ppermute | solution.py:20
  197.9 5.1 %collective-permute-done.23 = bf16[64,2048]{1,0:T(8,128)(2,1)S(1)} collective-permute-done((bf16[64,2048]{1,0:T(8,128)(2,1)S(1)}, bf16[64,2048]{1,0:T(8,128)(2,1)S(1)}, u32[]{:S(2)}, u32[]{:S(2)}) %collective-permute-start.23) | collective-permute-done | bytes 262176 | tf_op jit(solution)/shard_map/ppermute | solution.py:21
  205.9 4.4 %collective-permute-done.24 = bf16[64,2048]{1,0:T(8,128)(2,1)S(1)} collective-permute-done((bf16[64,2048]{1,0:T(8,128)(2,1)S(1)}, bf16[64,2048]{1,0:T(8,128)(2,1)S(1)}, u32[]{:S(2)}, u32[]{:S(2)}) %collective-permute-start.24) | collective-permute-done | bytes 262176 | tf_op jit(solution)/shard_map/ppermute | solution.py:21
  220.1 5.3 %collective-permute-done.32 = bf16[64,2048]{1,0:T(8,128)(2,1)S(1)} collective-permute-done((bf16[64,2048]{1,0:T(8,128)(2,1)S(1)}, bf16[64,2048]{1,0:T(8,128)(2,1)S(1)}, u32[]{:S(2)}, u32[]{:S(2)}) %collective-permute-start.32) | collective-permute-done | bytes 262176 | tf_op jit(solution)/shard_map/ppermute | solution.py:21
  252.3 7.7 %slice.156 = bf16[2,2048,1024]{2,1,0:T(8,128)(2,1)} slice(bf16[3,2048,1024]{2,1,0:T(8,128)(2,1)} %param.14), slice={[0:2], [0:2048], [0:1024]} | slice | bytes 16777216 | tf_op jit(solution)/shard_map/slice | solution.py:104
  279.6 4.1 %collective-permute-done.45 = bf16[64,2048]{1,0:T(8,128)(2,1)S(1)} collective-permute-done((bf16[64,2048]{1,0:T(8,128)(2,1)S(1)}, bf16[64,2048]{1,0:T(8,128)(2,1)S(1)}, u32[]{:S(2)}, u32[]{:S(2)}) %collective-permute-start.45) | collective-permute-done | bytes 262176 | tf_op jit(solution)/shard_map/ppermute | solution.py:20
  284.1 12.7 %fusion.69 = f32[8,2,64,1024]{3,2,1,0:T(8,128)S(1)} fusion(bf16[8,2,64,4096]{3,2,1,0:T(8,128)(2,1)} %bitcast.285, bf16[4096,1024,1,1]{1,0,3,2:T(8,128)(2,1)} %bitcast.251), kind=kOutput, calls=%fused_computation.182 | convolution fusion | flops 8589934592 | bytes 20971520 | tf_op jit(solution)/shard_map/dot_general | solution.py:104
  334.4 5.2 %collective-permute-done.28 = bf16[32,1024]{1,0:T(8,128)(2,1)S(1)} collective-permute-done((bf16[32,1024]{1,0:T(8,128)(2,1)S(1)}, bf16[32,1024]{1,0:T(8,128)(2,1)S(1)}, u32[]{:S(2)}, u32[]{:S(2)}) %collective-permute-start.28) | collective-permute-done | bytes 65568 | tf_op jit(solution)/shard_map/ppermute | solution.py:124
  340.6 4.9 %collective-permute-done.44 = bf16[32,1024]{1,0:T(8,128)(2,1)S(1)} collective-permute-done((bf16[32,1024]{1,0:T(8,128)(2,1)S(1)}, bf16[32,1024]{1,0:T(8,128)(2,1)S(1)}, u32[]{:S(2)}, u32[]{:S(2)}) %collective-permute-start.44) | collective-permute-done | bytes 65568 | tf_op jit(solution)/shard_map/ppermute | solution.py:124
  (199 shorter events, 103.8 us)
Async XLA Ops:
  6.5 277.5 %all-gather.2.cloned.1.call-start = ((), (), s32[]{:S(2)}) async-start(), calls=%async_computation | async-start | bytes 9437184 | tf_op jit(solution)/shard_map/all_gather | solution.py:67
  18.4 13.0 %collective-permute-start.1 = (bf16[64,2048]{1,0:T(8,128)(2,1)S(1)}, bf16[64,2048]{1,0:T(8,128)(2,1)S(1)}, u32[]{:S(2)}, u32[]{:S(2)}) collective-permute-start(bf16[64,2048]{1,0:T(8,128)(2,1)S(1)} %collective-permute-done), channel_id=1, source_target_pairs={{0,8},{8,16},{16,24},{24,28},{28,20},{20,12},{12,4},{4,0},{1,9},{9... | collective-permute-start | bytes 786440 | tf_op jit(solution)/shard_map/ppermute | solution.py:20
  20.2 20.1 %collective-permute-start.6 = (bf16[64,2048]{1,0:T(8,128)(2,1)S(1)}, bf16[64,2048]{1,0:T(8,128)(2,1)S(1)}, u32[]{:S(2)}, u32[]{:S(2)}) collective-permute-start(bf16[64,2048]{1,0:T(8,128)(2,1)S(1)} %collective-permute-done.5), channel_id=1, source_target_pairs={{8,0},{16,8},{24,16},{28,24},{20,28},{12,20},{4,12},{0,4},{9,1},{1... | collective-permute-start | bytes 786440 | tf_op jit(solution)/shard_map/ppermute | solution.py:21
  31.4 16.0 %collective-permute-start.2 = (bf16[64,2048]{1,0:T(8,128)(2,1)S(1)}, bf16[64,2048]{1,0:T(8,128)(2,1)S(1)}, u32[]{:S(2)}, u32[]{:S(2)}) collective-permute-start(bf16[64,2048]{1,0:T(8,128)(2,1)S(1)} %collective-permute-done.1), channel_id=1, source_target_pairs={{0,8},{8,16},{16,24},{24,28},{28,20},{20,12},{12,4},{4,0},{1,9},{9... | collective-permute-start | bytes 786440 | tf_op jit(solution)/shard_map/ppermute | solution.py:20
  40.3 20.1 %collective-permute-start.7 = (bf16[64,2048]{1,0:T(8,128)(2,1)S(1)}, bf16[64,2048]{1,0:T(8,128)(2,1)S(1)}, u32[]{:S(2)}, u32[]{:S(2)}) collective-permute-start(bf16[64,2048]{1,0:T(8,128)(2,1)S(1)} %collective-permute-done.6), channel_id=1, source_target_pairs={{8,0},{16,8},{24,16},{28,24},{20,28},{12,20},{4,12},{0,4},{9,1},{1... | collective-permute-start | bytes 786440 | tf_op jit(solution)/shard_map/ppermute | solution.py:21
  47.4 20.1 %collective-permute-start.3 = (bf16[64,2048]{1,0:T(8,128)(2,1)S(1)}, bf16[64,2048]{1,0:T(8,128)(2,1)S(1)}, u32[]{:S(2)}, u32[]{:S(2)}) collective-permute-start(bf16[64,2048]{1,0:T(8,128)(2,1)S(1)} %collective-permute-done.2), channel_id=1, source_target_pairs={{0,8},{8,16},{16,24},{24,28},{28,20},{20,12},{12,4},{4,0},{1,9},{9... | collective-permute-start | bytes 786440 | tf_op jit(solution)/shard_map/ppermute | solution.py:20
  60.4 13.6 %collective-permute-start.8 = (bf16[64,2048]{1,0:T(8,128)(2,1)S(1)}, bf16[64,2048]{1,0:T(8,128)(2,1)S(1)}, u32[]{:S(2)}, u32[]{:S(2)}) collective-permute-start(bf16[64,2048]{1,0:T(8,128)(2,1)S(1)} %collective-permute-done.7), channel_id=1, source_target_pairs={{8,0},{16,8},{24,16},{28,24},{20,28},{12,20},{4,12},{0,4},{9,1},{1... | collective-permute-start | bytes 786440 | tf_op jit(solution)/shard_map/ppermute | solution.py:21
  67.5 16.1 %collective-permute-start.4 = (bf16[64,2048]{1,0:T(8,128)(2,1)S(1)}, bf16[64,2048]{1,0:T(8,128)(2,1)S(1)}, u32[]{:S(2)}, u32[]{:S(2)}) collective-permute-start(bf16[64,2048]{1,0:T(8,128)(2,1)S(1)} %collective-permute-done.3), channel_id=1, source_target_pairs={{0,8},{8,16},{16,24},{24,28},{28,20},{20,12},{12,4},{4,0},{1,9},{9... | collective-permute-start | bytes 786440 | tf_op jit(solution)/shard_map/ppermute | solution.py:20
  83.6 20.1 %collective-permute-start.13 = (bf16[64,2048]{1,0:T(8,128)(2,1)S(1)}, bf16[64,2048]{1,0:T(8,128)(2,1)S(1)}, u32[]{:S(2)}, u32[]{:S(2)}) collective-permute-start(bf16[64,2048]{1,0:T(8,128)(2,1)S(1)} %collective-permute-done.9), channel_id=1, source_target_pairs={{8,0},{16,8},{24,16},{28,24},{20,28},{12,20},{4,12},{0,4},{9,1},{1... | collective-permute-start | bytes 786440 | tf_op jit(solution)/shard_map/ppermute | solution.py:21
  83.6 20.1 %collective-permute-start.11 = (bf16[64,2048]{1,0:T(8,128)(2,1)S(1)}, bf16[64,2048]{1,0:T(8,128)(2,1)S(1)}, u32[]{:S(2)}, u32[]{:S(2)}) collective-permute-start(bf16[64,2048]{1,0:T(8,128)(2,1)S(1)} %collective-permute-done.4), channel_id=1, source_target_pairs={{0,8},{8,16},{16,24},{24,28},{28,20},{20,12},{12,4},{4,0},{1,9},{9... | collective-permute-start | bytes 786440 | tf_op jit(solution)/shard_map/ppermute | solution.py:20
  103.7 18.4 %collective-permute-start.14 = (bf16[64,2048]{1,0:T(8,128)(2,1)S(1)}, bf16[64,2048]{1,0:T(8,128)(2,1)S(1)}, u32[]{:S(2)}, u32[]{:S(2)}) collective-permute-start(bf16[64,2048]{1,0:T(8,128)(2,1)S(1)} %collective-permute-done.13), channel_id=1, source_target_pairs={{8,0},{16,8},{24,16},{28,24},{20,28},{12,20},{4,12},{0,4},{9,1},{1... | collective-permute-start | bytes 786440 | tf_op jit(solution)/shard_map/ppermute | solution.py:21
  103.7 18.4 %collective-permute-start.12 = (bf16[64,2048]{1,0:T(8,128)(2,1)S(1)}, bf16[64,2048]{1,0:T(8,128)(2,1)S(1)}, u32[]{:S(2)}, u32[]{:S(2)}) collective-permute-start(bf16[64,2048]{1,0:T(8,128)(2,1)S(1)} %collective-permute-done.11), channel_id=1, source_target_pairs={{0,8},{8,16},{16,24},{24,28},{28,20},{20,12},{12,4},{4,0},{1,9},{9... | collective-permute-start | bytes 786440 | tf_op jit(solution)/shard_map/ppermute | solution.py:20
  107.0 31.5 %collective-permute-start.10 = (f32[6,64,1024]{2,1,0:T(8,128)}, f32[6,64,1024]{2,1,0:T(8,128)}, u32[]{:S(2)}, u32[]{:S(2)}) collective-permute-start(f32[6,64,1024]{2,1,0:T(8,128)} %dynamic-slice_bitcast_fusion), channel_id=1, source_target_pairs={{0,1},{1,0},{2,3},{3,2},{4,5},{5,4},{6,7},{7,6},{8,9},{9,8},{10,11... | collective-permute-start | bytes 4718600 | tf_op jit(solution)/shard_map/ppermute | solution.py:26
  125.3 11.9 %collective-permute-start.15 = (f32[2,64,1024]{2,1,0:T(8,128)}, f32[2,64,1024]{2,1,0:T(8,128)}, u32[]{:S(2)}, u32[]{:S(2)}) collective-permute-start(f32[2,64,1024]{2,1,0:T(8,128)} %dynamic-slice_bitcast_fusion.4), channel_id=1, source_target_pairs={{0,1},{1,0},{2,3},{3,2},{4,5},{5,4},{6,7},{7,6},{8,9},{9,8},{10,11... | collective-permute-start | bytes 1572872 | tf_op jit(solution)/shard_map/ppermute | solution.py:26
  141.7 14.5 %collective-permute-start.16 = (bf16[1,4,64,1024]{3,2,1,0:T(8,128)(2,1)}, bf16[1,4,64,1024]{3,2,1,0:T(8,128)(2,1)S(1)}, u32[]{:S(2)}, u32[]{:S(2)}) collective-permute-start(bf16[1,4,64,1024]{3,2,1,0:T(8,128)(2,1)} %fusion.35), channel_id=1, source_target_pairs={{0,2},{1,3},{2,0},{3,1},{4,6},{5,7},{6,4},{7,5},{8,10},{9,11},{10,... | collective-permute-start | bytes 1572872 | tf_op jit(solution)/shard_map/ppermute | solution.py:26
  156.4 15.5 %collective-permute-start.20 = (bf16[64,1024]{1,0:T(8,128)(2,1)S(1)}, bf16[64,1024]{1,0:T(8,128)(2,1)S(1)}, u32[]{:S(2)}, u32[]{:S(2)}) collective-permute-start(bf16[64,1024]{1,0:T(8,128)(2,1)S(1)} %get-tuple-element.30), channel_id=1, source_target_pairs={{0,24},{1,16},{2,4},{3,12},{4,8},{5,0},{6,20},{7,28},{8,25},{9,17}... | collective-permute-start | bytes 393224 | tf_op jit(solution)/shard_map/ppermute | solution.py:95
  172.5 16.4 %collective-permute-start.21 = (bf16[64,2048]{1,0:T(8,128)(2,1)S(1)}, bf16[64,2048]{1,0:T(8,128)(2,1)S(1)}, u32[]{:S(2)}, u32[]{:S(2)}) collective-permute-start(bf16[64,2048]{1,0:T(8,128)(2,1)S(1)} %get-tuple-element.57), channel_id=1, source_target_pairs={{0,8},{8,16},{16,24},{24,28},{28,20},{20,12},{12,4},{4,0},{1,9},{9... | collective-permute-start | bytes 786440 | tf_op jit(solution)/shard_map/ppermute | solution.py:20
  220.1 49.3 %collective-permute-start.37 = (bf16[64,2048]{1,0:T(8,128)(2,1)S(1)}, bf16[64,2048]{1,0:T(8,128)(2,1)S(1)}, u32[]{:S(2)}, u32[]{:S(2)}) collective-permute-start(bf16[64,2048]{1,0:T(8,128)(2,1)S(1)} %collective-permute-done.30), channel_id=1, source_target_pairs={{0,8},{8,16},{16,24},{24,28},{28,20},{20,12},{12,4},{4,0},{1,9},{9... | collective-permute-start | bytes 786440 | tf_op jit(solution)/shard_map/ppermute | solution.py:20
  225.3 44.1 %collective-permute-start.39 = (bf16[64,2048]{1,0:T(8,128)(2,1)S(1)}, bf16[64,2048]{1,0:T(8,128)(2,1)S(1)}, u32[]{:S(2)}, u32[]{:S(2)}) collective-permute-start(bf16[64,2048]{1,0:T(8,128)(2,1)S(1)} %collective-permute-done.32), channel_id=1, source_target_pairs={{8,0},{16,8},{24,16},{28,24},{20,28},{12,20},{4,12},{0,4},{9,1},{1... | collective-permute-start | bytes 786440 | tf_op jit(solution)/shard_map/ppermute | solution.py:21
  300.6 22.2 %collective-permute-start.25 = (f32[3,64,1024]{2,1,0:T(8,128)S(1)}, f32[3,64,1024]{2,1,0:T(8,128)S(1)}, u32[]{:S(2)}, u32[]{:S(2)}) collective-permute-start(f32[3,64,1024]{2,1,0:T(8,128)S(1)} %dynamic-slice_bitcast_fusion.1), channel_id=1, source_target_pairs={{0,1},{1,0},{2,3},{3,2},{4,5},{5,4},{6,7},{7,6},{8,9},{9,8},{10,11... | collective-permute-start | bytes 2359304 | tf_op jit(solution)/shard_map/ppermute | solution.py:26
  311.9 33.6 %collective-permute-start.49 = (bf16[32,1024]{1,0:T(8,128)(2,1)S(1)}, bf16[32,1024]{1,0:T(8,128)(2,1)S(1)}, u32[]{:S(2)}, u32[]{:S(2)}) collective-permute-start(bf16[32,1024]{1,0:T(8,128)(2,1)S(1)} %fusion.62), channel_id=1, source_target_pairs={{0,8},{1,5},{2,10},{3,7},{8,16},{9,1},{10,18},{11,3},{16,24},{17,9... | collective-permute-start | bytes 196616 | tf_op jit(solution)/shard_map/ppermute | solution.py:124
  318.7 21.8 %collective-permute-start.35 = (bf16[32,1024]{1,0:T(8,128)(2,1)S(1)}, bf16[32,1024]{1,0:T(8,128)(2,1)S(1)}, u32[]{:S(2)}, u32[]{:S(2)}) collective-permute-start(bf16[32,1024]{1,0:T(8,128)(2,1)S(1)} %get-tuple-element.40), channel_id=1, source_target_pairs={{0,20},{1,25},{2,22},{3,27},{8,12},{9,29},{10,14},{11,31},{16,4},{... | collective-permute-start | bytes 196616 | tf_op jit(solution)/shard_map/ppermute | solution.py:124
  320.9 19.7 %collective-permute-start.36 = (bf16[32,1024]{1,0:T(8,128)(2,1)S(1)}, bf16[32,1024]{1,0:T(8,128)(2,1)S(1)}, u32[]{:S(2)}, u32[]{:S(2)}) collective-permute-start(bf16[32,1024]{1,0:T(8,128)(2,1)S(1)} %get-tuple-element.39), channel_id=1, source_target_pairs={{0,28},{1,29},{2,30},{3,31},{8,20},{9,21},{10,22},{11,23},{16,12},... | collective-permute-start | bytes 196616 | tf_op jit(solution)/shard_map/ppermute | solution.py:124
  324.5 16.1 %collective-permute-start.43 = (bf16[32,1024]{1,0:T(8,128)(2,1)S(1)}, bf16[32,1024]{1,0:T(8,128)(2,1)S(1)}, u32[]{:S(2)}, u32[]{:S(2)}) collective-permute-start(bf16[32,1024]{1,0:T(8,128)(2,1)S(1)} %get-tuple-element.38), channel_id=1, source_target_pairs={{0,24},{1,21},{2,26},{3,23},{8,28},{9,13},{10,30},{11,15},{16,20},... | collective-permute-start | bytes 196616 | tf_op jit(solution)/shard_map/ppermute | solution.py:124
  (39 other events, 398.7 us)
Sparse Core Ops, SparseCore 0:
  9.5 149.7 all-gather.1

commit v3 on v0

v3 whole, which is shorter than its diff:
```python
import functools

import jax
import jax.numpy as jnp
import numpy as np
from jax import lax
from jax.experimental import pallas as pl
from jax.experimental.pallas import tpu as pltpu
from jax.sharding import PartitionSpec as P


def ring_of(groups):
    half = groups // 2
    return [2 * q for q in range(half)] + [2 * q + 1 for q in reversed(range(half))]


def home_rounds(groups, owners):
    ring = ring_of(groups)
    xs, per_owner = owners // 2, groups // owners
    moves = {}
    for p, d in enumerate(ring):
        for t in range(owners):
            x, core = t // 2, t % 2
            for k in range(groups // xs):
                s = k * xs + x
                q = (p + (s if core else -s)) % groups
                moves.setdefault(d * owners + t, []).append((ring[q] * owners + d // per_owner, k, 2 * (d % per_owner) + core))
    pairs, items, pieces = [], [], []
    for _ in range(groups // xs):
        taken = {}

        def place(source, seen):
            for move in moves[source]:
                if move[0] not in seen:
                    seen.add(move[0])
                    if move[0] not in taken or place(taken[move[0]][0], seen):
                        taken[move[0]] = (source, move)
                        return True
            return False

        for source in sorted(moves):
            place(source, set())
        pairs.append(sorted((source, target) for target, (source, _) in taken.items()))
        items.append([0] * len(moves))
        pieces.append([0] * len(moves))
        for target, (source, move) in taken.items():
            items[-1][source] = move[1]
            pieces[-1][target] = move[2]
            moves[source].remove(move)
    return pairs, np.array(items, np.uint32).T, np.array(pieces, np.int32).T


def tie(values, after):
    flat, tree = jax.tree.flatten(values)
    held = lax.optimization_barrier(tuple(flat) + tuple(jax.tree.leaves(after)))
    return jax.tree.unflatten(tree, held[: len(flat)])


def pick(values, index):
    return lax.dynamic_index_in_dim(values, index, 0, keepdims=False)


def top_body(rounds, width, pieces_ref, *refs):
    arrived, rests, tops = refs[:rounds], refs[rounds : rounds + 2], refs[rounds + 2 :]
    for k in range(rounds):
        piece = pieces_ref[0, k]
        columns = pl.ds(pl.multiple_of(lax.div(piece, 2) * width, width), width)
        for side in range(2):

            @pl.when(lax.rem(piece, 2) == side)
            def _(side=side, k=k, columns=columns):
                total = rests[side][:, columns].astype(jnp.float32) + arrived[k][...].astype(jnp.float32)
                tops[side][:, columns] = total.astype(jnp.bfloat16)


def norm_body(groups, width, *refs):
    slots, gain_ref, out_ref = refs[:groups], refs[groups], refs[groups + 1]
    dp, core = lax.axis_index("dp"), lax.rem(lax.axis_index("tensor"), 2)
    place = jnp.where(lax.rem(dp, 2) == 0, lax.div(dp, 2), groups - 1 - lax.div(dp, 2))
    total = 0.0
    for slot in slots:
        block = slot[...].astype(jnp.float32)
        total = total + jnp.sum(block * block, axis=1, keepdims=True)
    inverse_rms = lax.rsqrt(total / (groups * width) + 1e-05)
    for s, slot in enumerate(slots):
        q = lax.rem(place + jnp.where(core == 0, s, groups - s), groups)
        d = jnp.where(q < groups // 2, 2 * q, 2 * (groups - 1 - q) + 1)
        columns = pl.ds(pl.multiple_of(d * width, width), width)
        out_ref[:, columns] = (slot[...].astype(jnp.float32) * inverse_rms * gain_ref[:, columns]).astype(jnp.bfloat16)


VMEM = pl.BlockSpec(memory_space=pltpu.VMEM)
SMEM = pl.BlockSpec(memory_space=pltpu.SMEM)


def local(attn_heads, residual, low_hidden, mid_hidden, out_weight, join_weight, join_gain):
    groups, owners = lax.axis_size("dp"), lax.axis_size("tensor")
    tokens, features = attn_heads.shape
    width = out_weight.shape[1]
    xs = owners // 2
    side_rows = tokens // 2
    rows = tokens // owners
    ring = ring_of(groups)
    up = [(ring[q], ring[(q + 1) % groups]) for q in range(groups)]
    down = [(target, source) for source, target in up]
    tensor = lax.axis_index("tensor").astype(jnp.uint32)
    core, x = tensor & 1, tensor >> 1
    device = lax.axis_index("dp").astype(jnp.uint32) * owners + tensor

    def sides(values):
        split = values.reshape((xs, 2, rows) + values.shape[1:])
        return [split[:, s].reshape((side_rows,) + values.shape[1:]) for s in range(2)]

    def hop(pair):
        return [lax.ppermute(pair[0], "dp", up), lax.ppermute(pair[1], "dp", down)]

    def swap(values, bit):
        return lax.ppermute(values, "tensor", [(t, t ^ bit) for t in range(owners)])

    def product(pairs, weight):
        rows_in = jnp.concatenate([pair[s] for s in range(2) for pair in pairs], axis=0)
        return jnp.dot(rows_in, weight, preferred_element_type=jnp.float32).reshape(2, len(pairs), side_rows, width)

    def sum_cores(products):
        return pick(products, core) + swap(pick(products, 1 - core), 1)

    def sum_xs(pieces):
        half = pieces.shape[0] // 2
        while half:
            pieces = pieces.reshape((2, half) + pieces.shape[1:])
            side = (x >> (half.bit_length() - 1)) & 1
            pieces = pick(pieces, side) + swap(pick(pieces, 1 - side), 2 * half)
            half //= 2
        return pieces[0]

    attn = [sides(attn_heads)]
    deep = [[jnp.stack(pair) for pair in zip(sides(low_hidden), sides(mid_hidden))]]
    heads = []
    cuts = sorted({0, groups // 2, groups - xs, groups})
    for step in range(1, groups):
        if step % 2:
            deep.append(hop(tie(deep[-1], attn[-1]) if step > 1 else deep[-1]))
        attn.append(hop(attn[-1]))
    deep.append(hop(tie(deep[-1], attn[-1])))
    for low, high in zip(cuts, cuts[1:]):
        summed = sum_cores(product(attn[low:high], out_weight))
        by_x = jnp.moveaxis(summed.reshape((high - low) // xs, xs, side_rows, width), 1, 0)
        heads.append((summed, sum_xs(by_x)))
    for after in heads[-1]:
        if len(deep) < groups:
            deep.append(hop(tie(deep[-1], after)))
    while len(deep) < groups:
        deep.append(hop(deep[-1]))
    held = jnp.concatenate([part for _, part in heads], axis=0).astype(jnp.bfloat16)

    pairs, items, pieces = home_rounds(groups, owners)
    item = lax.dynamic_slice(jnp.asarray(items), (device, jnp.uint32(0)), (1, len(pairs)))
    piece = lax.dynamic_slice(jnp.asarray(pieces), (device, jnp.uint32(0)), (1, len(pairs)))
    arrived = [lax.ppermute(pick(held, item[0, k]), ("dp", "tensor"), moves) for k, moves in enumerate(pairs)]
    side_shape = jax.ShapeDtypeStruct((side_rows, features), jnp.bfloat16)
    top = [
        pl.pallas_call(
            functools.partial(top_body, len(pairs), width),
            out_shape=[side_shape] * 2,
            in_specs=[SMEM] + [VMEM] * (len(pairs) + 2),
            out_specs=[VMEM] * 2,
            name="add_residual",
        )(piece, *arrived, *sides(residual))
    ]

    low_sum = product([[side[0] for side in pair] for pair in deep], join_weight[0])
    deep_sum = low_sum + product([[side[1] for side in pair] for pair in deep], join_weight[1])
    cuts = sorted({0, groups // 2 - 1, groups - 3, groups - 1, groups})
    chunks = []

    def start_chunk():
        low, high = cuts[len(chunks)], cuts[len(chunks) + 1]
        chunks.append([product(top[low:high], join_weight[2]) + deep_sum[:, low:high]])

    def step_chunk(chunk):
        if len(chunk) == 1:
            chunk.append(sum_cores(chunk[0]))
        elif len(chunk) == 2:
            by_owner = chunk[1].reshape(chunk[1].shape[0], xs, rows, width)
            chunk.append(sum_xs(jnp.moveaxis(by_owner, 1, 0)))

    for step in range(1, groups):
        pair = top[-1]
        if step == 2:
            pair = tie(pair, low_sum)
        elif step == 3:
            pair = tie(pair, deep_sum)
        elif chunks:
            pair = tie(pair, [chunk[-1] for chunk in chunks])
        top.append(hop(pair))
        for chunk in chunks:
            step_chunk(chunk)
        if step == cuts[len(chunks) + 1]:
            start_chunk()
    while len(chunks) < len(cuts) - 1:
        start_chunk()
    for chunk in chunks:
        while len(chunk) < 3:
            step_chunk(chunk)

    owned = [part for chunk in chunks for part in chunk[-1]]
    for s in range(1, groups):
        moves = [
            (ring[q] * owners + t, ring[(q + (s if t % 2 else -s)) % groups] * owners + t)
            for q in range(groups)
            for t in range(owners)
        ]
        owned[s] = lax.ppermute(owned[s].astype(jnp.bfloat16), ("dp", "tensor"), moves)
    return pl.pallas_call(
        functools.partial(norm_body, groups, width),
        out_shape=jax.ShapeDtypeStruct((rows, groups * width), jnp.bfloat16),
        in_specs=[VMEM] * (groups + 1),
        out_specs=VMEM,
        name="norm_rows",
    )(*owned, join_gain.reshape(1, groups * width))


def solution(mesh):
    return jax.shard_map(
        local,
        mesh=mesh,
        in_specs=(
            P("dp", "tensor"),
            P("dp", "tensor"),
            P("dp", "tensor"),
            P("dp", "tensor"),
            P("tensor", "dp"),
            P(None, "tensor", "dp"),
            P(),
        ),
        out_specs=P(("dp", "tensor"), None),
        check_vma=False,
    )
```

time: 1060 us -> 282 us (0.27)
  waiting for transfers between devices: 908 us -> 131 us
  blocking collectives: 95.9 us -> 0 us
  starting transfers between devices: 0.13 us -> 82.4 us
  local copies, waits for them, and re-layouts: 2.28 us -> 36.1 us
  between operations: 13.2 us -> 0.73 us
    all_gather x2 -> x0, waiting for transfers between devices: 819 us -> none  [the longest x1 642 us: local(): lax.all_gather(out_weight, 'dp', axis=1, tiled=True)]
    ppermute x0 -> x67, waiting for transfers between devices: none -> 131 us  [the longest x42 94.8 us: hop(): return [lax.ppermute(pair[0], 'dp', up), lax.ppermute(pair[1], 'dp', down)]]
    all_to_all x1 -> x0, blocking collectives: 95.9 us -> none  [local(): lax.all_to_all(blocked, 'dp', split_axis=0, concat_axis=3, tiled=True)]
    reduce_scatter x2 -> x0, waiting for transfers between devices: 88.2 us -> none  [the longest x1 44.6 us: local(): lax.psum_scatter(head_partial, 'tensor', scatter_dimension=1, tiled=True)]
    ppermute x0 -> x67, starting transfers between devices: none -> 82.4 us  [the longest x42 49.6 us: hop(): return [lax.ppermute(pair[0], 'dp', up), lax.ppermute(pair[1], 'dp', down)]]
    unnamed x12 -> x66, local copies, waits for them, and re-layouts: 0.02 us -> 25.1 us
    dot_general x2 -> x9, matrix products: 34.3 us -> 23.8 us  [product(): jnp.dot(rows_in, weight, preferred_element_type=jnp.float32)]
  transfers between devices with their start and end apart: 4 -> 67, of which waited for: 4 -> 34; matrix products, arithmetic and copies ran while one was open for 0% -> 21% of each run, Pallas kernels for 0% -> 1%
where the time goes in v3:
time: 282 us
  waiting for transfers between devices  131 us (46%)
  starting transfers between devices  82.4 us (29%)
  local copies, waits for them, and re-layouts  36.1 us (13%)
  matrix products  23.8 us (8%)
  Pallas kernels  4.54 us (2%)
    ppermute x42, waiting for transfers between devices, hop(): return [lax.ppermute(pair[0], 'dp', up), lax.ppermute(pair[1], 'dp', down)]  94.8 us
    ppermute x42, starting transfers between devices, hop(): return [lax.ppermute(pair[0], 'dp', up), lax.ppermute(pair[1], 'dp', down)]  49.6 us
    ppermute x14, waiting for transfers between devices, swap(): return lax.ppermute(values, 'tensor', [(t, t ^ bit) for t in range(owners)])  31 us
    unnamed x66, local copies, waits for them, and re-layouts  25.1 us
    dot_general x9, matrix products, product(): jnp.dot(rows_in, weight, preferred_element_type=jnp.float32)  23.8 us
    ppermute x4, starting transfers between devices, local(): lax.ppermute(pick(held, item[0, k]), ('dp', 'tensor'), moves)  14.4 us
    ppermute x7, starting transfers between devices, local(): lax.ppermute(owned[s].astype(jnp.bfloat16), ('dp', 'tensor'), moves)  11.2 us
    ppermute x14, starting transfers between devices, swap(): return lax.ppermute(values, 'tensor', [(t, t ^ bit) for t in range(owners)])  7.27 us
  transfers between devices with their start and end apart: 67, of which 34 were waited for; matrix products, arithmetic and copies ran while one was open for 21% of the time, Pallas kernels for 1%

profile of v3, /device:TPU:0, one launch (start us, length us, event | category | flops | bytes accessed | tf_op | source)
XLA Modules:
  0.0 281.5 jit_solution(4055630197618907299)
XLA Ops:
  3.1 3.0 %collective-permute-start.26 = (bf16[2,64,2048]{2,1,0:T(8,128)(2,1)}, bf16[2,64,2048]{2,1,0:T(8,128)(2,1)S(1)}, u32[]{:S(2)}, u32[]{:S(2)}) collective-permute-start(bf16[2,64,2048]{2,1,0:T(8,128)(2,1)} %pad_maximum_fusion.3), channel_id=1, source_target_pairs={{0,8},{8,16},{16,24},{24,28},{28,20},{20,12},{12,4},{4,0},{1,9},{9... | collective-permute-start | bytes 1572872 | tf_op jit(solution)/shard_map/ppermute | solution.py:115
  12.9 11.0 %collective-permute-done = bf16[64,2048]{1,0:T(8,128)(2,1)} collective-permute-done((bf16[64,2048]{1,0:T(8,128)(2,1)S(1)}, bf16[64,2048]{1,0:T(8,128)(2,1)}, u32[]{:S(2)}, u32[]{:S(2)}) %collective-permute-start) | collective-permute-done | bytes 262176 | tf_op jit(solution)/shard_map/ppermute | solution.py:115
  38.7 12.1 %collective-permute-done.2 = bf16[64,2048]{1,0:T(8,128)(2,1)S(1)} collective-permute-done((bf16[64,2048]{1,0:T(8,128)(2,1)S(1)}, bf16[64,2048]{1,0:T(8,128)(2,1)S(1)}, u32[]{:S(2)}, u32[]{:S(2)}) %collective-permute-start.2) | collective-permute-done | bytes 262176 | tf_op jit(solution)/shard_map/ppermute | solution.py:115
  56.4 4.0 %fusion.96 = f32[512,1024]{1,0:T(8,128)S(1)} fusion(bf16[512,2048]{1,0:T(8,128)(2,1)} %constant_dynamic-update-slice_fusion, bf16[2048,1024]{1,0:T(8,128)(2,1)S(1)} %copy-done.15), kind=kOutput, calls=%fused_computation.178 | convolution fusion | flops 2147483648 | bytes 8388608 | tf_op jit(solution)/shard_map/dot_general | solution.py:122
  65.5 15.1 %collective-permute-done.9 = bf16[64,2048]{1,0:T(8,128)(2,1)S(1)} collective-permute-done((bf16[64,2048]{1,0:T(8,128)(2,1)S(1)}, bf16[64,2048]{1,0:T(8,128)(2,1)S(1)}, u32[]{:S(2)}, u32[]{:S(2)}) %collective-permute-start.9) | collective-permute-done | bytes 262176 | tf_op jit(solution)/shard_map/ppermute | solution.py:115
  84.0 4.5 %collective-permute-done.14 = bf16[64,2048]{1,0:T(8,128)(2,1)S(1)} collective-permute-done((bf16[64,2048]{1,0:T(8,128)(2,1)S(1)}, bf16[64,2048]{1,0:T(8,128)(2,1)S(1)}, u32[]{:S(2)}, u32[]{:S(2)}) %collective-permute-start.14) | collective-permute-done | bytes 262176 | tf_op jit(solution)/shard_map/ppermute | solution.py:115
  92.9 4.8 %collective-permute-done.15 = bf16[64,2048]{1,0:T(8,128)(2,1)S(1)} collective-permute-done((bf16[64,2048]{1,0:T(8,128)(2,1)S(1)}, bf16[64,2048]{1,0:T(8,128)(2,1)S(1)}, u32[]{:S(2)}, u32[]{:S(2)}) %collective-permute-start.15) | collective-permute-done | bytes 262176 | tf_op jit(solution)/shard_map/ppermute | solution.py:115
  102.3 4.4 %collective-permute-done.32 = bf16[2,64,2048]{2,1,0:T(8,128)(2,1)S(1)} collective-permute-done((bf16[2,64,2048]{2,1,0:T(8,128)(2,1)S(1)}, bf16[2,64,2048]{2,1,0:T(8,128)(2,1)S(1)}, u32[]{:S(2)}, u32[]{:S(2)}) %collective-permute-start.32) | collective-permute-done | bytes 524320 | tf_op jit(solution)/shard_map/ppermute | solution.py:115
  111.7 8.6 %collective-permute-done.7 = f32[1,2,64,1024]{3,2,1,0:T(8,128)S(1)} collective-permute-done((f32[1,2,64,1024]{3,2,1,0:T(8,128)S(1)}, f32[1,2,64,1024]{3,2,1,0:T(8,128)S(1)}, u32[]{:S(2)}, u32[]{:S(2)}) %collective-permute-start.7) | collective-permute-done | bytes 524320 | tf_op jit(solution)/shard_map/ppermute | solution.py:118
  120.4 5.1 %collective-permute-done.19 = f32[1,1,64,1024]{3,2,1,0:T(8,128)S(1)} collective-permute-done((f32[1,1,64,1024]{3,2,1,0:T(8,128)S(1)}, f32[1,1,64,1024]{3,2,1,0:T(8,128)S(1)}, u32[]{:S(2)}, u32[]{:S(2)}) %collective-permute-start.19) | collective-permute-done | bytes 262176 | tf_op jit(solution)/shard_map/ppermute | solution.py:118
  128.1 4.3 %collective-permute-start.20 = (bf16[64,1024]{1,0:T(8,128)(2,1)S(1)}, bf16[64,1024]{1,0:T(8,128)(2,1)S(1)}, u32[]{:S(2)}, u32[]{:S(2)}) collective-permute-start(bf16[64,1024]{1,0:T(8,128)(2,1)S(1)} %get-tuple-element.64), channel_id=1, source_target_pairs={{0,12},{1,16},{2,24},{3,8},{4,20},{5,4},{6,28},{7,0},{8,9},{9,25},... | collective-permute-start | bytes 393224 | tf_op jit(solution)/shard_map/ppermute | solution.py:159
  132.4 4.5 %collective-permute-start.21 = (bf16[64,1024]{1,0:T(8,128)(2,1)S(1)}, bf16[64,1024]{1,0:T(8,128)(2,1)S(1)}, u32[]{:S(2)}, u32[]{:S(2)}) collective-permute-start(bf16[64,1024]{1,0:T(8,128)(2,1)S(1)} %get-tuple-element.63), channel_id=1, source_target_pairs={{0,28},{1,0},{2,20},{3,24},{4,4},{5,8},{6,12},{7,16},{8,5},{9,21},... | collective-permute-start | bytes 393224 | tf_op jit(solution)/shard_map/ppermute | solution.py:159
  137.5 4.9 %collective-permute-start.23 = (bf16[64,1024]{1,0:T(8,128)(2,1)S(1)}, bf16[64,1024]{1,0:T(8,128)(2,1)S(1)}, u32[]{:S(2)}, u32[]{:S(2)}) collective-permute-start(bf16[64,1024]{1,0:T(8,128)(2,1)S(1)} %get-tuple-element.61), channel_id=1, source_target_pairs={{0,16},{1,28},{2,8},{3,4},{4,24},{5,20},{6,0},{7,12},{8,25},{9,9},... | collective-permute-start | bytes 393224 | tf_op jit(solution)/shard_map/ppermute | solution.py:159
  150.1 4.2 %collective-permute-start.24 = (bf16[64,2048]{1,0:T(8,128)(2,1)}, bf16[64,2048]{1,0:T(8,128)(2,1)S(1)}, u32[]{:S(2)}, u32[]{:S(2)}) collective-permute-start(bf16[64,2048]{1,0:T(8,128)(2,1)} %get-tuple-element.31), channel_id=1, source_target_pairs={{0,8},{8,16},{16,24},{24,28},{28,20},{20,12},{12,4},{4,0},{1,9},{9... | collective-permute-start | bytes 786440 | tf_op jit(solution)/shard_map/ppermute | solution.py:115
  162.0 3.1 %collective-permute-done.24 = bf16[64,2048]{1,0:T(8,128)(2,1)S(1)} collective-permute-done((bf16[64,2048]{1,0:T(8,128)(2,1)}, bf16[64,2048]{1,0:T(8,128)(2,1)S(1)}, u32[]{:S(2)}, u32[]{:S(2)}) %collective-permute-start.24) | collective-permute-done | bytes 262176 | tf_op jit(solution)/shard_map/ppermute | solution.py:115
  165.1 2.9 %collective-permute-start.39 = (bf16[2,64,2048]{2,1,0:T(8,128)(2,1)}, bf16[2,64,2048]{2,1,0:T(8,128)(2,1)S(1)}, u32[]{:S(2)}, u32[]{:S(2)}) collective-permute-start(bf16[2,64,2048]{2,1,0:T(8,128)(2,1)} %collective-permute-done.37), channel_id=1, source_target_pairs={{8,0},{16,8},{24,16},{28,24},{20,28},{12,20},{4,12},{0,4},{9,1},{1... | collective-permute-start | bytes 1572872 | tf_op jit(solution)/shard_map/ppermute | solution.py:115
  169.9 6.4 %collective-permute-done.38 = bf16[2,64,2048]{2,1,0:T(8,128)(2,1)S(1)} collective-permute-done((bf16[2,64,2048]{2,1,0:T(8,128)(2,1)}, bf16[2,64,2048]{2,1,0:T(8,128)(2,1)S(1)}, u32[]{:S(2)}, u32[]{:S(2)}) %collective-permute-start.38) | collective-permute-done | bytes 524320 | tf_op jit(solution)/shard_map/ppermute | solution.py:115
  186.0 7.6 %fusion.2 = f32[2,8,64,1024]{3,2,1,0:T(8,128)S(1)} fusion(bf16[2,8,64,2048]{3,2,1,0:T(8,128)(2,1)} %bitcast.350, bf16[3,2048,1024]{2,1,0:T(8,128)(2,1)} %param.14), kind=kOutput, calls=%fused_computation.2 | convolution fusion | flops 4294967296 | bytes 12582912 | tf_op jit(solution)/shard_map/dot_general | solution.py:122
  195.0 4.5 %fusion.18 = f32[2,8,64,1024]{3,2,1,0:T(8,128)S(1)} fusion(f32[2,8,64,1024]{3,2,1,0:T(8,128)S(1)} %fusion.2, bf16[2,8,64,2048]{3,2,1,0:T(8,128)(2,1)S(1)} %bitcast.351, bf16[3,2048,1024]{2,1,0:T(8,128)(2,1)S(1)} %bitcast.353), kind=kOutput, calls=%fused_computation.18 | convolution fusion | flops 4296015872 | bytes 16777216 | tf_op jit(solution)/shard_map/dot_general | solution.py:122
  202.6 4.3 %collective-permute-done.41 = bf16[64,2048]{1,0:T(8,128)(2,1)S(1)} collective-permute-done((bf16[64,2048]{1,0:T(8,128)(2,1)S(1)}, bf16[64,2048]{1,0:T(8,128)(2,1)S(1)}, u32[]{:S(2)}, u32[]{:S(2)}) %collective-permute-start.41) | collective-permute-done | bytes 262176 | tf_op jit(solution)/shard_map/ppermute | solution.py:115
  210.8 3.4 %collective-permute-done.46 = bf16[64,2048]{1,0:T(8,128)(2,1)S(1)} collective-permute-done((bf16[64,2048]{1,0:T(8,128)(2,1)S(1)}, bf16[64,2048]{1,0:T(8,128)(2,1)S(1)}, u32[]{:S(2)}, u32[]{:S(2)}) %collective-permute-start.46) | collective-permute-done | bytes 262176 | tf_op jit(solution)/shard_map/ppermute | solution.py:115
  217.2 4.2 %collective-permute-done.49 = bf16[64,2048]{1,0:T(8,128)(2,1)S(1)} collective-permute-done((bf16[64,2048]{1,0:T(8,128)(2,1)S(1)}, bf16[64,2048]{1,0:T(8,128)(2,1)S(1)}, u32[]{:S(2)}, u32[]{:S(2)}) %collective-permute-start.49) | collective-permute-done | bytes 262176 | tf_op jit(solution)/shard_map/ppermute | solution.py:115
  228.4 7.7 %collective-permute-done.43 = f32[1,3,32,1024]{3,2,1,0:T(8,128)S(1)} collective-permute-done((f32[1,3,32,1024]{3,2,1,0:T(8,128)S(1)}, f32[1,3,32,1024]{3,2,1,0:T(8,128)S(1)}, u32[]{:S(2)}, u32[]{:S(2)}) %collective-permute-start.43) | collective-permute-done | bytes 393248 | tf_op jit(solution)/shard_map/ppermute | solution.py:118
  259.4 8.3 %collective-permute-done.65 = f32[1,1,32,1024]{3,2,1,0:T(8,128)S(1)} collective-permute-done((f32[1,1,32,1024]{3,2,1,0:T(8,128)S(1)}, f32[1,1,32,1024]{3,2,1,0:T(8,128)S(1)}, u32[]{:S(2)}, u32[]{:S(2)}) %collective-permute-start.65) | collective-permute-done | bytes 131104 | tf_op jit(solution)/shard_map/ppermute | solution.py:118
  (237 shorter events, 137.8 us)
Async XLA Ops:
  3.1 26.4 %collective-permute-start.26 = (bf16[2,64,2048]{2,1,0:T(8,128)(2,1)}, bf16[2,64,2048]{2,1,0:T(8,128)(2,1)S(1)}, u32[]{:S(2)}, u32[]{:S(2)}) collective-permute-start(bf16[2,64,2048]{2,1,0:T(8,128)(2,1)} %pad_maximum_fusion.3), channel_id=1, source_target_pairs={{0,8},{8,16},{16,24},{24,28},{28,20},{20,12},{12,4},{4,0},{1,9},{9... | collective-permute-start | bytes 1572872 | tf_op jit(solution)/shard_map/ppermute | solution.py:115
  7.0 22.6 %collective-permute-start.27 = (bf16[2,64,2048]{2,1,0:T(8,128)(2,1)}, bf16[2,64,2048]{2,1,0:T(8,128)(2,1)S(1)}, u32[]{:S(2)}, u32[]{:S(2)}) collective-permute-start(bf16[2,64,2048]{2,1,0:T(8,128)(2,1)} %pad_maximum_fusion.4), channel_id=1, source_target_pairs={{8,0},{16,8},{24,16},{28,24},{20,28},{12,20},{4,12},{0,4},{9,1},{1... | collective-permute-start | bytes 1572872 | tf_op jit(solution)/shard_map/ppermute | solution.py:115
  7.0 16.9 %collective-permute-start = (bf16[64,2048]{1,0:T(8,128)(2,1)S(1)}, bf16[64,2048]{1,0:T(8,128)(2,1)}, u32[]{:S(2)}, u32[]{:S(2)}) collective-permute-start(bf16[64,2048]{1,0:T(8,128)(2,1)S(1)} %bitcast.339), channel_id=1, source_target_pairs={{0,8},{8,16},{16,24},{24,28},{28,20},{20,12},{12,4},{4,0},{1,9},{9... | collective-permute-start | bytes 786440 | tf_op jit(solution)/shard_map/ppermute | solution.py:115
  9.1 17.1 %collective-permute-start.3 = (bf16[64,2048]{1,0:T(8,128)(2,1)S(1)}, bf16[64,2048]{1,0:T(8,128)(2,1)S(1)}, u32[]{:S(2)}, u32[]{:S(2)}) collective-permute-start(bf16[64,2048]{1,0:T(8,128)(2,1)S(1)} %bitcast.337), channel_id=1, source_target_pairs={{8,0},{16,8},{24,16},{28,24},{20,28},{12,20},{4,12},{0,4},{9,1},{1... | collective-permute-start | bytes 786440 | tf_op jit(solution)/shard_map/ppermute | solution.py:115
  33.0 27.5 %collective-permute-start.28 = (bf16[2,64,2048]{2,1,0:T(8,128)(2,1)S(1)}, bf16[2,64,2048]{2,1,0:T(8,128)(2,1)S(1)}, u32[]{:S(2)}, u32[]{:S(2)}) collective-permute-start(bf16[2,64,2048]{2,1,0:T(8,128)(2,1)S(1)} %collective-permute-done.26), channel_id=1, source_target_pairs={{0,8},{8,16},{16,24},{24,28},{28,20},{20,12},{12,4},{4,0},{1,9},{9... | collective-permute-start | bytes 1572872 | tf_op jit(solution)/shard_map/ppermute | solution.py:115
  34.6 25.9 %collective-permute-start.29 = (bf16[2,64,2048]{2,1,0:T(8,128)(2,1)S(1)}, bf16[2,64,2048]{2,1,0:T(8,128)(2,1)S(1)}, u32[]{:S(2)}, u32[]{:S(2)}) collective-permute-start(bf16[2,64,2048]{2,1,0:T(8,128)(2,1)S(1)} %collective-permute-done.27), channel_id=1, source_target_pairs={{8,0},{16,8},{24,16},{28,24},{20,28},{12,20},{4,12},{0,4},{9,1},{1... | collective-permute-start | bytes 1572872 | tf_op jit(solution)/shard_map/ppermute | solution.py:115
  35.1 15.7 %collective-permute-start.2 = (bf16[64,2048]{1,0:T(8,128)(2,1)S(1)}, bf16[64,2048]{1,0:T(8,128)(2,1)S(1)}, u32[]{:S(2)}, u32[]{:S(2)}) collective-permute-start(bf16[64,2048]{1,0:T(8,128)(2,1)S(1)} %collective-permute-done.1), channel_id=1, source_target_pairs={{0,8},{8,16},{16,24},{24,28},{28,20},{20,12},{12,4},{4,0},{1,9},{9... | collective-permute-start | bytes 786440 | tf_op jit(solution)/shard_map/ppermute | solution.py:115
  36.6 17.1 %collective-permute-start.5 = (bf16[64,2048]{1,0:T(8,128)(2,1)S(1)}, bf16[64,2048]{1,0:T(8,128)(2,1)S(1)}, u32[]{:S(2)}, u32[]{:S(2)}) collective-permute-start(bf16[64,2048]{1,0:T(8,128)(2,1)S(1)} %collective-permute-done.4), channel_id=1, source_target_pairs={{8,0},{16,8},{24,16},{28,24},{20,28},{12,20},{4,12},{0,4},{9,1},{1... | collective-permute-start | bytes 786440 | tf_op jit(solution)/shard_map/ppermute | solution.py:115
  60.5 40.9 %collective-permute-start.6 = (f32[4,64,1024]{2,1,0:T(8,128)S(1)}, f32[4,64,1024]{2,1,0:T(8,128)S(1)}, u32[]{:S(2)}, u32[]{:S(2)}) collective-permute-start(f32[4,64,1024]{2,1,0:T(8,128)S(1)} %dynamic-slice_bitcast_fusion), channel_id=1, source_target_pairs={{0,1},{1,0},{2,3},{3,2},{4,5},{5,4},{6,7},{7,6},{8,9},{9,8},{10,11... | collective-permute-start | bytes 3145736 | tf_op jit(solution)/shard_map/ppermute | solution.py:118
  60.6 23.3 %collective-permute-start.30 = (bf16[2,64,2048]{2,1,0:T(8,128)(2,1)S(1)}, bf16[2,64,2048]{2,1,0:T(8,128)(2,1)S(1)}, u32[]{:S(2)}, u32[]{:S(2)}) collective-permute-start(bf16[2,64,2048]{2,1,0:T(8,128)(2,1)S(1)} %collective-permute-done.28), channel_id=1, source_target_pairs={{0,8},{8,16},{16,24},{24,28},{28,20},{20,12},{12,4},{4,0},{1,9},{9... | collective-permute-start | bytes 1572872 | tf_op jit(solution)/shard_map/ppermute | solution.py:115
  62.2 29.1 %collective-permute-start.31 = (bf16[2,64,2048]{2,1,0:T(8,128)(2,1)S(1)}, bf16[2,64,2048]{2,1,0:T(8,128)(2,1)S(1)}, u32[]{:S(2)}, u32[]{:S(2)}) collective-permute-start(bf16[2,64,2048]{2,1,0:T(8,128)(2,1)S(1)} %collective-permute-done.29), channel_id=1, source_target_pairs={{8,0},{16,8},{24,16},{28,24},{20,28},{12,20},{4,12},{0,4},{9,1},{1... | collective-permute-start | bytes 1572872 | tf_op jit(solution)/shard_map/ppermute | solution.py:115
  62.7 17.9 %collective-permute-start.9 = (bf16[64,2048]{1,0:T(8,128)(2,1)S(1)}, bf16[64,2048]{1,0:T(8,128)(2,1)S(1)}, u32[]{:S(2)}, u32[]{:S(2)}) collective-permute-start(bf16[64,2048]{1,0:T(8,128)(2,1)S(1)} %collective-permute-done.8), channel_id=1, source_target_pairs={{0,8},{8,16},{16,24},{24,28},{28,20},{20,12},{12,4},{4,0},{1,9},{9... | collective-permute-start | bytes 786440 | tf_op jit(solution)/shard_map/ppermute | solution.py:115
  64.2 17.9 %collective-permute-start.11 = (bf16[64,2048]{1,0:T(8,128)(2,1)S(1)}, bf16[64,2048]{1,0:T(8,128)(2,1)S(1)}, u32[]{:S(2)}, u32[]{:S(2)}) collective-permute-start(bf16[64,2048]{1,0:T(8,128)(2,1)S(1)} %collective-permute-done.10), channel_id=1, source_target_pairs={{8,0},{16,8},{24,16},{28,24},{20,28},{12,20},{4,12},{0,4},{9,1},{1... | collective-permute-start | bytes 786440 | tf_op jit(solution)/shard_map/ppermute | solution.py:115
  83.9 15.9 %collective-permute-start.12 = (f32[2,64,1024]{2,1,0:T(8,128)S(1)}, f32[2,64,1024]{2,1,0:T(8,128)S(1)}, u32[]{:S(2)}, u32[]{:S(2)}) collective-permute-start(f32[2,64,1024]{2,1,0:T(8,128)S(1)} %dynamic-slice_bitcast_fusion.5), channel_id=1, source_target_pairs={{0,1},{1,0},{2,3},{3,2},{4,5},{5,4},{6,7},{7,6},{8,9},{9,8},{10,11... | collective-permute-start | bytes 1572872 | tf_op jit(solution)/shard_map/ppermute | solution.py:118
  101.6 18.7 %collective-permute-start.7 = (f32[1,2,64,1024]{3,2,1,0:T(8,128)S(1)}, f32[1,2,64,1024]{3,2,1,0:T(8,128)S(1)}, u32[]{:S(2)}, u32[]{:S(2)}) collective-permute-start(f32[1,2,64,1024]{3,2,1,0:T(8,128)S(1)} %dynamic-slice_bitcast_fusion.6), channel_id=1, source_target_pairs={{0,2},{1,3},{2,0},{3,1},{4,6},{5,7},{6,4},{7,5},{8,10},{9,11},{10,... | collective-permute-start | bytes 1572872 | tf_op jit(solution)/shard_map/ppermute | solution.py:118
  108.0 29.5 %collective-permute-start.34 = (bf16[2,64,2048]{2,1,0:T(8,128)(2,1)S(1)}, bf16[2,64,2048]{2,1,0:T(8,128)(2,1)}, u32[]{:S(2)}, u32[]{:S(2)}) collective-permute-start(bf16[2,64,2048]{2,1,0:T(8,128)(2,1)S(1)} %collective-permute-done.32), channel_id=1, source_target_pairs={{0,8},{8,16},{16,24},{24,28},{28,20},{20,12},{12,4},{4,0},{1,9},{9... | collective-permute-start | bytes 1572872 | tf_op jit(solution)/shard_map/ppermute | solution.py:115
  109.6 33.8 %collective-permute-start.35 = (bf16[2,64,2048]{2,1,0:T(8,128)(2,1)S(1)}, bf16[2,64,2048]{2,1,0:T(8,128)(2,1)S(1)}, u32[]{:S(2)}, u32[]{:S(2)}) collective-permute-start(bf16[2,64,2048]{2,1,0:T(8,128)(2,1)S(1)} %collective-permute-done.33), channel_id=1, source_target_pairs={{8,0},{16,8},{24,16},{28,24},{20,28},{12,20},{4,12},{0,4},{9,1},{1... | collective-permute-start | bytes 1572872 | tf_op jit(solution)/shard_map/ppermute | solution.py:115
  128.1 17.8 %collective-permute-start.20 = (bf16[64,1024]{1,0:T(8,128)(2,1)S(1)}, bf16[64,1024]{1,0:T(8,128)(2,1)S(1)}, u32[]{:S(2)}, u32[]{:S(2)}) collective-permute-start(bf16[64,1024]{1,0:T(8,128)(2,1)S(1)} %get-tuple-element.64), channel_id=1, source_target_pairs={{0,12},{1,16},{2,24},{3,8},{4,20},{5,4},{6,28},{7,0},{8,9},{9,25},... | collective-permute-start | bytes 393224 | tf_op jit(solution)/shard_map/ppermute | solution.py:159
  143.3 16.3 %collective-permute-start.36 = (bf16[2,64,2048]{2,1,0:T(8,128)(2,1)}, bf16[2,64,2048]{2,1,0:T(8,128)(2,1)}, u32[]{:S(2)}, u32[]{:S(2)}) collective-permute-start(bf16[2,64,2048]{2,1,0:T(8,128)(2,1)} %collective-permute-done.34), channel_id=1, source_target_pairs={{0,8},{8,16},{16,24},{24,28},{28,20},{20,12},{12,4},{4,0},{1,9},{9... | collective-permute-start | bytes 1572872 | tf_op jit(solution)/shard_map/ppermute | solution.py:115
  156.2 37.4 %collective-permute-start.25 = (bf16[64,2048]{1,0:T(8,128)(2,1)}, bf16[64,2048]{1,0:T(8,128)(2,1)S(1)}, u32[]{:S(2)}, u32[]{:S(2)}) collective-permute-start(bf16[64,2048]{1,0:T(8,128)(2,1)} %get-tuple-element.32), channel_id=1, source_target_pairs={{8,0},{16,8},{24,16},{28,24},{20,28},{12,20},{4,12},{0,4},{9,1},{1... | collective-permute-start | bytes 786440 | tf_op jit(solution)/shard_map/ppermute | solution.py:115
  165.1 19.9 %collective-permute-start.39 = (bf16[2,64,2048]{2,1,0:T(8,128)(2,1)}, bf16[2,64,2048]{2,1,0:T(8,128)(2,1)S(1)}, u32[]{:S(2)}, u32[]{:S(2)}) collective-permute-start(bf16[2,64,2048]{2,1,0:T(8,128)(2,1)} %collective-permute-done.37), channel_id=1, source_target_pairs={{8,0},{16,8},{24,16},{28,24},{20,28},{12,20},{4,12},{0,4},{9,1},{1... | collective-permute-start | bytes 1572872 | tf_op jit(solution)/shard_map/ppermute | solution.py:115
  238.2 32.1 %collective-permute-start.44 = (bf16[32,1024]{1,0:T(8,128)(2,1)S(1)}, bf16[32,1024]{1,0:T(8,128)(2,1)S(1)}, u32[]{:S(2)}, u32[]{:S(2)}) collective-permute-start(bf16[32,1024]{1,0:T(8,128)(2,1)S(1)} %get-tuple-element.100), channel_id=1, source_target_pairs={{0,4},{1,9},{2,6},{3,11},{8,0},{9,17},{10,2},{11,19},{16,8},{17,25... | collective-permute-start | bytes 196616 | tf_op jit(solution)/shard_map/ppermute | solution.py:213
  240.0 33.2 %collective-permute-start.45 = (bf16[32,1024]{1,0:T(8,128)(2,1)S(1)}, bf16[32,1024]{1,0:T(8,128)(2,1)S(1)}, u32[]{:S(2)}, u32[]{:S(2)}) collective-permute-start(bf16[32,1024]{1,0:T(8,128)(2,1)S(1)} %get-tuple-element.99), channel_id=1, source_target_pairs={{0,12},{1,17},{2,14},{3,19},{8,4},{9,25},{10,6},{11,27},{16,0},{17... | collective-permute-start | bytes 196616 | tf_op jit(solution)/shard_map/ppermute | solution.py:213
  258.4 16.1 %collective-permute-start.52 = (bf16[32,1024]{1,0:T(8,128)(2,1)S(1)}, bf16[32,1024]{1,0:T(8,128)(2,1)S(1)}, u32[]{:S(2)}, u32[]{:S(2)}) collective-permute-start(bf16[32,1024]{1,0:T(8,128)(2,1)S(1)} %get-tuple-element.104), channel_id=1, source_target_pairs={{0,20},{1,25},{2,22},{3,27},{8,12},{9,29},{10,14},{11,31},{16,4},{... | collective-permute-start | bytes 196616 | tf_op jit(solution)/shard_map/ppermute | solution.py:213
  (62 other events, 517.6 us)

commit v4 on v0

v4 whole, which is shorter than its diff:
```python
import functools

import jax
import jax.numpy as jnp
from jax import lax
from jax.experimental import pallas as pl
from jax.experimental.pallas import tpu as pltpu
from jax.sharding import PartitionSpec as P


def ring_of(groups):
    half = groups // 2
    return [2 * q for q in range(half)] + [2 * q + 1 for q in reversed(range(half))]


def tie(values, after):
    flat, tree = jax.tree.flatten(values)
    held = lax.optimization_barrier(tuple(flat) + tuple(jax.tree.leaves(after)))
    return jax.tree.unflatten(tree, held[: len(flat)])


def pick(values, index):
    return lax.dynamic_index_in_dim(values, index, 0, keepdims=False)


def place_on_ring(groups):
    dp = lax.axis_index("dp")
    return jnp.where(lax.rem(dp, 2) == 0, lax.div(dp, 2), groups - 1 - lax.div(dp, 2))


def top_body(groups, classes, width, *refs):
    arrived, rest_ref, top_ref = refs[: len(classes)], refs[-2], refs[-1]
    home = lax.axis_index("tensor") + place_on_ring(groups)
    for kind, piece_ref in zip(classes, arrived):
        j = lax.rem(home + kind, len(classes))
        columns = pl.ds(pl.multiple_of(j * width, width), width)
        total = rest_ref[:, columns].astype(jnp.float32) + piece_ref[...].astype(jnp.float32)
        top_ref[:, columns] = total.astype(jnp.bfloat16)


def norm_body(offsets, width, *refs):
    groups = len(offsets)
    slots, gain_ref, out_ref = refs[:groups], refs[groups], refs[groups + 1]
    place = place_on_ring(groups)
    total = 0.0
    for slot in slots:
        block = slot[...].astype(jnp.float32)
        total = total + jnp.sum(block * block, axis=1, keepdims=True)
    inverse_rms = lax.rsqrt(total / (groups * width) + 1e-05)
    for offset, slot in zip(offsets, slots):
        q = lax.rem(place + offset + groups, groups)
        d = jnp.where(q < groups // 2, 2 * q, 2 * (groups - 1 - q) + 1)
        columns = pl.ds(pl.multiple_of(d * width, width), width)
        out_ref[:, columns] = (slot[...].astype(jnp.float32) * inverse_rms * gain_ref[:, columns]).astype(jnp.bfloat16)


VMEM = pl.BlockSpec(memory_space=pltpu.VMEM)


class Gather:
    def __init__(self, own, axis):
        self.ring = ring_of(lax.axis_size("dp"))
        self.axis, self.last, self.hops = axis, len(self.ring) // 2, 0
        self.ends = [own, own]
        self.slots = {0: [own]}

    def hop(self, after=()):
        count = len(self.ring)
        ends = tie(self.ends, after) if jax.tree.leaves(after) else self.ends
        self.hops += 1
        if self.hops == self.last:
            middle = ends[0].shape[self.axis] // 2
            ends = [
                lax.slice_in_dim(ends[0], 0, middle, axis=self.axis),
                lax.slice_in_dim(ends[1], middle, 2 * middle, axis=self.axis),
            ]
        up = [(self.ring[q], self.ring[(q + 1) % count]) for q in range(count)]
        down = [(target, source) for source, target in up]
        self.ends = [lax.ppermute(ends[0], "dp", up), lax.ppermute(ends[1], "dp", down)]
        if self.hops == self.last:
            self.slots[self.hops] = self.ends
        else:
            self.slots[self.hops], self.slots[-self.hops] = [self.ends[0]], [self.ends[1]]


def local(attn_heads, residual, low_hidden, mid_hidden, out_weight, join_weight, join_gain):
    groups, owners = lax.axis_size("dp"), lax.axis_size("tensor")
    tokens, features = attn_heads.shape
    width = out_weight.shape[1]
    xs = owners // 2
    rows = tokens // owners
    ring = ring_of(groups)
    last = groups // 2
    offsets = [0] + [sign * s for s in range(1, last) for sign in (1, -1)] + [last]
    tensor = lax.axis_index("tensor").astype(jnp.uint32)
    core, x = tensor & 1, tensor >> 1

    def swap(values, bit):
        return lax.ppermute(values, "tensor", [(t, t ^ bit) for t in range(owners)])

    def product(slots, weight):
        rows_in = jnp.concatenate([piece for slot in slots for piece in slot], axis=0)
        return jnp.dot(rows_in, weight, preferred_element_type=jnp.float32).reshape(len(slots), tokens, width)

    def bit_of_x(half):
        return (x >> (half.bit_length() - 1)) & 1

    attn = Gather(attn_heads, 0)
    per_owner = groups // owners
    classes = list(reversed(range(per_owner)))
    kept = {kind: [k for k in offsets if k % per_owner == kind] for kind in classes}
    pair_sums = {kind: [] for kind in classes}

    def sum_pairs():
        for kind in classes:
            while len(pair_sums[kind]) < xs:
                i = 2 * len(pair_sums[kind])
                pair = kept[kind][i : i + 2]
                if not all(k in attn.slots for k in pair):
                    break
                products = product([attn.slots[k] for k in pair], out_weight)
                pair_sums[kind].append(pick(products, core) + swap(pick(products, 1 - core), 1))

    while attn.hops < last:
        ready = [pair_sums[kind] for kind in classes]
        ready = [list(part) for part in ready]
        if attn.hops:
            sum_pairs()
        attn.hop(ready)
    arrived_heads = attn.ends
    sum_pairs()

    def sum_xs(parts):
        while len(parts) > 1:
            half = len(parts) // 2
            high = bit_of_x(half) == 1
            sent = jnp.stack([jnp.where(high, a, b) for a, b in zip(parts[:half], parts[half:])]).astype(jnp.bfloat16)
            came = swap(sent, 2 * half)
            parts = [
                jnp.where(high, b, a) + came[i].astype(jnp.float32)
                for i, (a, b) in enumerate(zip(parts[:half], parts[half:]))
            ]
        return parts[0]

    arrived = []
    for kind in classes:
        held = sum_xs(pair_sums[kind]).astype(jnp.bfloat16)
        moves = [
            (d * owners + t, ring[(p - kept[kind][t]) % groups] * owners + d // per_owner)
            for p, d in enumerate(ring)
            for t in range(owners)
        ]
        arrived.append(lax.ppermute(held, ("dp", "tensor"), moves))
    own_top = pl.pallas_call(
        functools.partial(top_body, groups, classes, width),
        out_shape=jax.ShapeDtypeStruct((tokens, features), jnp.bfloat16),
        in_specs=[VMEM] * (len(classes) + 1),
        out_specs=VMEM,
        name="add_residual",
    )(*arrived, residual)

    deep = Gather(jnp.stack([low_hidden, mid_hidden]), 1)
    deep.hop(arrived_heads)
    deep.hop(held)
    top = Gather(own_top, 0)
    cuts = [0] + list(range(3, groups, 2)) + [groups]
    chunks = []

    def start_chunk():
        part = offsets[cuts[len(chunks)] : cuts[len(chunks) + 1]]
        total = product([top.slots[k] for k in part], join_weight[2])
        for depth in range(2):
            total = total + product([[piece[depth] for piece in deep.slots[k]] for k in part], join_weight[depth])
        chunks.append([total])

    def step_chunk(chunk):
        if len(chunk) == 1:
            by_owner = chunk[0].reshape(chunk[0].shape[0], xs, 2, rows, width)
            kept_part = lax.dynamic_index_in_dim(by_owner, core, 2, keepdims=False)
            sent_part = lax.dynamic_index_in_dim(by_owner, 1 - core, 2, keepdims=False)
            chunk.append(kept_part + swap(sent_part, 1))
        elif len(chunk) == 2:
            part, half = chunk[1], xs // 2
            while half:
                part = part.reshape((part.shape[0], 2, half) + part.shape[-2:])
                side = bit_of_x(half)
                part = lax.dynamic_index_in_dim(part, side, 1, keepdims=False) + swap(
                    lax.dynamic_index_in_dim(part, 1 - side, 1, keepdims=False), 2 * half
                )
                half //= 2
            chunk.append(part.reshape(part.shape[0], rows, width))

    while top.hops < last:
        top.hop([chunk[-1] for chunk in chunks])
        if deep.hops < last:
            deep.hop(top.ends)
        for chunk in chunks:
            step_chunk(chunk)
        if top.hops > 1:
            start_chunk()
            step_chunk(chunks[-1])
    while len(chunks) < len(cuts) - 1:
        start_chunk()
    for chunk in chunks:
        while len(chunk) < 3:
            step_chunk(chunk)

    owned = [part for chunk in chunks for part in chunk[-1]]
    for i, k in enumerate(offsets):
        if k:
            moves = [(ring[q], ring[(q - k) % groups]) for q in range(groups)]
            owned[i] = lax.ppermute(owned[i].astype(jnp.bfloat16), "dp", moves)
    return pl.pallas_call(
        functools.partial(norm_body, offsets, width),
        out_shape=jax.ShapeDtypeStruct((rows, groups * width), jnp.bfloat16),
        in_specs=[VMEM] * (groups + 1),
        out_specs=VMEM,
        name="norm_rows",
    )(*owned, join_gain.reshape(1, groups * width))


def solution(mesh):
    return jax.shard_map(
        local,
        mesh=mesh,
        in_specs=(
            P("dp", "tensor"),
            P("dp", "tensor"),
            P("dp", "tensor"),
            P("dp", "tensor"),
            P("tensor", "dp"),
            P(None, "tensor", "dp"),
            P(),
        ),
        out_specs=P(("dp", "tensor"), None),
        check_vma=False,
    )
```

time: 1060 us -> 265 us (0.25)
  waiting for transfers between devices: 908 us -> 140 us
  blocking collectives: 95.9 us -> 0 us
  starting transfers between devices: 0.13 us -> 69.8 us
  between operations: 13.2 us -> 0.8 us
    all_gather x2 -> x0, waiting for transfers between devices: 819 us -> none  [the longest x1 642 us: local(): lax.all_gather(out_weight, 'dp', axis=1, tiled=True)]
    ppermute x0 -> x47, waiting for transfers between devices: none -> 140 us  [the longest x12 74.3 us: hop(): lax.ppermute(ends[1], 'dp', down)]
    all_to_all x1 -> x0, blocking collectives: 95.9 us -> none  [local(): lax.all_to_all(blocked, 'dp', split_axis=0, concat_axis=3, tiled=True)]
    reduce_scatter x2 -> x0, waiting for transfers between devices: 88.2 us -> none  [the longest x1 44.6 us: local(): lax.psum_scatter(head_partial, 'tensor', scatter_dimension=1, tiled=True)]
    ppermute x0 -> x47, starting transfers between devices: none -> 69.8 us  [the longest x14 22.8 us: swap(): return lax.ppermute(values, 'tensor', [(t, t ^ bit) for t in range(owners)])]
    dot_general x2 -> x16, matrix products: 34.3 us -> 27.3 us  [product(): jnp.dot(rows_in, weight, preferred_element_type=jnp.float32)]
  transfers between devices with their start and end apart: 4 -> 47, of which waited for: 4 -> 24; matrix products, arithmetic and copies ran while one was open for 0% -> 17% of each run, Pallas kernels for 0% -> 1%
where the time goes in v4:
time: 265 us; the launch traced here: 264 us
  waiting for transfers between devices  140 us (53%)
  starting transfers between devices  69.8 us (26%)
  matrix products  27.3 us (10%)
  local copies, waits for them, and re-layouts  12.4 us (5%)
  other arithmetic  9.57 us (4%)
  Pallas kernels  4.4 us (2%)
    ppermute x12, waiting for transfers between devices, hop(): lax.ppermute(ends[1], 'dp', down)  74.3 us
    dot_general x16, matrix products, product(): jnp.dot(rows_in, weight, preferred_element_type=jnp.float32)  27.3 us
    ppermute x12, waiting for transfers between devices, hop(): lax.ppermute(ends[0], 'dp', up)  23.4 us
    ppermute x14, starting transfers between devices, swap(): return lax.ppermute(values, 'tensor', [(t, t ^ bit) for t in range(owners)])  22.8 us
    ppermute x14, waiting for transfers between devices, swap(): return lax.ppermute(values, 'tensor', [(t, t ^ bit) for t in range(owners)])  20.1 us
    ppermute x12, starting transfers between devices, hop(): lax.ppermute(ends[0], 'dp', up)  19.9 us
    ppermute x2, waiting for transfers between devices, local(): arrived.append(lax.ppermute(held, ('dp', 'tensor'), moves))  17.3 us
    ppermute x12, starting transfers between devices, hop(): lax.ppermute(ends[1], 'dp', down)  14.1 us
  transfers between devices with their start and end apart: 47, of which 24 were waited for; matrix products, arithmetic and copies ran while one was open for 17% of the time, Pallas kernels for 1%

profile of v4, /device:TPU:0, one launch (start us, length us, event | category | flops | bytes accessed | tf_op | source)
XLA Modules:
  0.0 264.5 jit_solution(11044826399564825921)
XLA Ops:
  0.0 3.0 %collective-permute-start = (bf16[128,2048]{1,0:T(8,128)(2,1)}, bf16[128,2048]{1,0:T(8,128)(2,1)S(1)}, u32[]{:S(2)}, u32[]{:S(2)}) collective-permute-start(bf16[128,2048]{1,0:T(8,128)(2,1)} %param.7), channel_id=1, source_target_pairs={{0,8},{8,16},{16,24},{24,28},{28,20},{20,12},{12,4},{4,0},{1,9},{9... | collective-permute-start | bytes 1572872 | tf_op jit(solution)/shard_map/ppermute | solution.py:79
  3.0 12.1 %collective-permute-done = bf16[128,2048]{1,0:T(8,128)(2,1)S(1)} collective-permute-done((bf16[128,2048]{1,0:T(8,128)(2,1)}, bf16[128,2048]{1,0:T(8,128)(2,1)S(1)}, u32[]{:S(2)}, u32[]{:S(2)}) %collective-permute-start) | collective-permute-done | bytes 524320 | tf_op jit(solution)/shard_map/ppermute | solution.py:79
  16.9 3.4 %fusion.54 = f32[256,1024]{1,0:T(8,128)S(1)} fusion(bf16[2048,1024]{1,0:T(8,128)(2,1)} %param.11, bf16[128,2048]{1,0:T(8,128)(2,1)S(1)} %collective-permute-done.2, bf16[128,2048]{1,0:T(8,128)(2,1)S(1)} %collective-permute-done), kind=kOutput, calls=%fused_computation.46 | convolution fusion | flops 1075838976 | bytes 6291456 | tf_op jit(solution)/shard_map/dot_general | solution.py:103
  20.8 7.5 %collective-permute-done.1 = bf16[128,2048]{1,0:T(8,128)(2,1)S(1)} collective-permute-done((bf16[128,2048]{1,0:T(8,128)(2,1)S(1)}, bf16[128,2048]{1,0:T(8,128)(2,1)S(1)}, u32[]{:S(2)}, u32[]{:S(2)}) %collective-permute-start.1) | collective-permute-done | bytes 524320 | tf_op jit(solution)/shard_map/ppermute | solution.py:79
  29.7 5.1 %collective-permute-done.3 = bf16[128,2048]{1,0:T(8,128)(2,1)S(1)} collective-permute-done((bf16[128,2048]{1,0:T(8,128)(2,1)S(1)}, bf16[128,2048]{1,0:T(8,128)(2,1)S(1)}, u32[]{:S(2)}, u32[]{:S(2)}) %collective-permute-start.3) | collective-permute-done | bytes 524320 | tf_op jit(solution)/shard_map/ppermute | solution.py:79
  36.9 11.4 %collective-permute-done.6 = bf16[128,2048]{1,0:T(8,128)(2,1)S(1)} collective-permute-done((bf16[128,2048]{1,0:T(8,128)(2,1)S(1)}, bf16[128,2048]{1,0:T(8,128)(2,1)S(1)}, u32[]{:S(2)}, u32[]{:S(2)}) %collective-permute-start.6) | collective-permute-done | bytes 524320 | tf_op jit(solution)/shard_map/ppermute | solution.py:79
  52.6 2.7 %collective-permute-done.12 = bf16[64,2048]{1,0:T(8,128)(2,1)S(1)} collective-permute-done((bf16[64,2048]{1,0:T(8,128)(2,1)S(1)}, bf16[64,2048]{1,0:T(8,128)(2,1)S(1)}, u32[]{:S(2)}, u32[]{:S(2)}) %collective-permute-start.12) | collective-permute-done | bytes 262176 | tf_op jit(solution)/shard_map/ppermute | solution.py:79
  71.4 3.3 %collective-permute-done.14 = bf16[1,128,1024]{2,1,0:T(8,128)(2,1)S(1)} collective-permute-done((bf16[1,128,1024]{2,1,0:T(8,128)(2,1)S(1)}, bf16[1,128,1024]{2,1,0:T(8,128)(2,1)S(1)}, u32[]{:S(2)}, u32[]{:S(2)}) %collective-permute-start.14) | collective-permute-done | bytes 262176 | tf_op jit(solution)/shard_map/ppermute | solution.py:99
  76.7 17.3 %collective-permute-done.9.refs_0_ = bf16[128,1024]{1,0:T(8,128)(2,1)S(1)} collective-permute-done((bf16[128,1024]{1,0:T(8,128)(2,1)S(1)}, bf16[128,1024]{1,0:T(8,128)(2,1)S(1)}, u32[]{:S(2)}, u32[]{:S(2)}) %collective-permute-start.9) | collective-permute-done | bytes 262176 | tf_op jit(solution)/shard_map/ppermute | solution.py:153
  99.0 6.8 %collective-permute-start.16 = (bf16[128,2048]{1,0:T(8,128)(2,1)}, bf16[128,2048]{1,0:T(8,128)(2,1)S(1)}, u32[]{:S(2)}, u32[]{:S(2)}) collective-permute-start(bf16[128,2048]{1,0:T(8,128)(2,1)} %add_residual.1), channel_id=1, source_target_pairs={{0,8},{8,16},{16,24},{24,28},{28,20},{20,12},{12,4},{4,0},{1,9},{9... | collective-permute-start | bytes 1572872 | tf_op jit(solution)/shard_map/ppermute | solution.py:79
  111.0 4.2 %fusion.12 = f32[3,128,1024]{2,1,0:T(8,128)S(1)} fusion(bf16[3,128,2048]{2,1,0:T(8,128)(2,1)S(1)} %bitcast.202, bf16[3,2048,1024]{2,1,0:T(8,128)(2,1)} %param.12), kind=kOutput, calls=%fused_computation.12 | convolution fusion | flops 1610612736 | bytes 7340032 | tf_op jit(solution)/shard_map/dot_general | solution.py:103
  115.2 3.6 %collective-permute-done.17 = bf16[128,2048]{1,0:T(8,128)(2,1)S(1)} collective-permute-done((bf16[128,2048]{1,0:T(8,128)(2,1)}, bf16[128,2048]{1,0:T(8,128)(2,1)S(1)}, u32[]{:S(2)}, u32[]{:S(2)}) %collective-permute-start.17) | collective-permute-done | bytes 524320 | tf_op jit(solution)/shard_map/ppermute | solution.py:79
  126.0 6.1 %collective-permute-start.20 = (f32[3,2,32,1024]{3,2,1,0:T(8,128)}, f32[3,2,32,1024]{3,2,1,0:T(8,128)S(1)}, u32[]{:S(2)}, u32[]{:S(2)}) collective-permute-start(f32[3,2,32,1024]{3,2,1,0:T(8,128)} %dynamic-slice_bitcast_fusion), channel_id=1, source_target_pairs={{0,1},{1,0},{2,3},{3,2},{4,5},{5,4},{6,7},{7,6},{8,9},{9,8},{10,11... | collective-permute-start | bytes 2359304 | tf_op jit(solution)/shard_map/ppermute | solution.py:99
  132.1 16.6 %collective-permute-done.25 = bf16[128,2048]{1,0:T(8,128)(2,1)S(1)} collective-permute-done((bf16[128,2048]{1,0:T(8,128)(2,1)S(1)}, bf16[128,2048]{1,0:T(8,128)(2,1)S(1)}, u32[]{:S(2)}, u32[]{:S(2)}) %collective-permute-start.25) | collective-permute-done | bytes 524320 | tf_op jit(solution)/shard_map/ppermute | solution.py:79
  155.8 9.6 %collective-permute-start.21 = (f32[3,1,32,1024]{3,2,1,0:T(8,128)S(1)}, f32[3,1,32,1024]{3,2,1,0:T(8,128)S(1)}, u32[]{:S(2)}, u32[]{:S(2)}) collective-permute-start(f32[3,1,32,1024]{3,2,1,0:T(8,128)S(1)} %constant_dynamic-slice_fusion.3), channel_id=1, source_target_pairs={{0,2},{1,3},{2,0},{3,1},{4,6},{5,7},{6,4},{7,5},{8,10},{9,11},{10,... | collective-permute-start | bytes 1179656 | tf_op jit(solution)/shard_map/ppermute | solution.py:99
  165.4 3.7 %collective-permute-start.35 = (bf16[2,128,2048]{2,1,0:T(8,128)(2,1)S(1)}, bf16[2,128,2048]{2,1,0:T(8,128)(2,1)S(1)}, u32[]{:S(2)}, u32[]{:S(2)}) collective-permute-start(bf16[2,128,2048]{2,1,0:T(8,128)(2,1)S(1)} %copy-done.4), channel_id=1, source_target_pairs={{8,0},{16,8},{24,16},{28,24},{20,28},{12,20},{4,12},{0,4},{9,1},{1... | collective-permute-start | bytes 3145736 | tf_op jit(solution)/shard_map/ppermute | solution.py:79
  172.3 2.9 %collective-permute-done.21 = f32[3,1,32,1024]{3,2,1,0:T(8,128)S(1)} collective-permute-done((f32[3,1,32,1024]{3,2,1,0:T(8,128)S(1)}, f32[3,1,32,1024]{3,2,1,0:T(8,128)S(1)}, u32[]{:S(2)}, u32[]{:S(2)}) %collective-permute-start.21) | collective-permute-done | bytes 393248 | tf_op jit(solution)/shard_map/ppermute | solution.py:99
  177.0 26.1 %collective-permute-done.33 = bf16[128,2048]{1,0:T(8,128)(2,1)S(1)} collective-permute-done((bf16[128,2048]{1,0:T(8,128)(2,1)S(1)}, bf16[128,2048]{1,0:T(8,128)(2,1)S(1)}, u32[]{:S(2)}, u32[]{:S(2)}) %collective-permute-start.33) | collective-permute-done | bytes 524320 | tf_op jit(solution)/shard_map/ppermute | solution.py:79
  208.3 3.6 %fusion = f32[2,128,1024]{2,1,0:T(8,128)S(1)} fusion(bf16[2,128,2048]{2,1,0:T(8,128)(2,1)S(1)} %bitcast.217, bf16[3,2048,1024]{2,1,0:T(8,128)(2,1)} %param.12), kind=kOutput, calls=%fused_computation | convolution fusion | flops 1073741824 | bytes 6291456 | tf_op jit(solution)/shard_map/dot_general | solution.py:103
  217.6 8.8 %collective-permute-done.43 = bf16[2,64,2048]{2,1,0:T(8,128)(2,1)S(1)} collective-permute-done((bf16[2,64,2048]{2,1,0:T(8,128)(2,1)S(1)}, bf16[2,64,2048]{2,1,0:T(8,128)(2,1)S(1)}, u32[]{:S(2)}, u32[]{:S(2)}) %collective-permute-start.43) | collective-permute-done | bytes 524320 | tf_op jit(solution)/shard_map/ppermute | solution.py:79
  238.9 6.8 %collective-permute-done.37 = f32[2,1,32,1024]{3,2,1,0:T(8,128)S(1)} collective-permute-done((f32[2,1,32,1024]{3,2,1,0:T(8,128)S(1)}, f32[2,1,32,1024]{3,2,1,0:T(8,128)S(1)}, u32[]{:S(2)}, u32[]{:S(2)}) %collective-permute-start.37) | collective-permute-done | bytes 262176 | tf_op jit(solution)/shard_map/ppermute | solution.py:99
  247.2 3.4 %collective-permute-done.45 = f32[1,1,32,1024]{3,2,1,0:T(8,128)S(1)} collective-permute-done((f32[1,1,32,1024]{3,2,1,0:T(8,128)S(1)}, f32[1,1,32,1024]{3,2,1,0:T(8,128)S(1)}, u32[]{:S(2)}, u32[]{:S(2)}) %collective-permute-start.45) | collective-permute-done | bytes 131104 | tf_op jit(solution)/shard_map/ppermute | solution.py:99
  251.5 3.0 %collective-permute-start.39 = (bf16[32,1024]{1,0:T(8,128)(2,1)S(1)}, bf16[32,1024]{1,0:T(8,128)(2,1)S(1)}, u32[]{:S(2)}, u32[]{:S(2)}) collective-permute-start(bf16[32,1024]{1,0:T(8,128)(2,1)S(1)} %get-tuple-element.57), channel_id=1, source_target_pairs={{0,24},{8,28},{16,20},{24,12},{28,4},{20,0},{12,8},{4,16},{1,25},{... | collective-permute-start | bytes 196616 | tf_op jit(solution)/shard_map/ppermute | solution.py:212
  256.8 3.3 %collective-permute-done.39.refs_6_ = bf16[32,1024]{1,0:T(8,128)(2,1)S(1)} collective-permute-done((bf16[32,1024]{1,0:T(8,128)(2,1)S(1)}, bf16[32,1024]{1,0:T(8,128)(2,1)S(1)}, u32[]{:S(2)}, u32[]{:S(2)}) %collective-permute-start.39) | collective-permute-done | bytes 65568 | tf_op jit(solution)/shard_map/ppermute | solution.py:212
  (198 shorter events, 89.4 us)
Async XLA Ops:
  0.0 15.1 %collective-permute-start = (bf16[128,2048]{1,0:T(8,128)(2,1)}, bf16[128,2048]{1,0:T(8,128)(2,1)S(1)}, u32[]{:S(2)}, u32[]{:S(2)}) collective-permute-start(bf16[128,2048]{1,0:T(8,128)(2,1)} %param.7), channel_id=1, source_target_pairs={{0,8},{8,16},{16,24},{24,28},{28,20},{20,12},{12,4},{4,0},{1,9},{9... | collective-permute-start | bytes 1572872 | tf_op jit(solution)/shard_map/ppermute | solution.py:79
  63.6 42.2 %collective-permute-start.19 = (bf16[2,128,2048]{2,1,0:T(8,128)(2,1)}, bf16[2,128,2048]{2,1,0:T(8,128)(2,1)}, u32[]{:S(2)}, u32[]{:S(2)}) collective-permute-start(bf16[2,128,2048]{2,1,0:T(8,128)(2,1)} %pad_maximum_fusion.3), channel_id=1, source_target_pairs={{8,0},{16,8},{24,16},{28,24},{20,28},{12,20},{4,12},{0,4},{9,1},{1... | collective-permute-start | bytes 3145736 | tf_op jit(solution)/shard_map/ppermute | solution.py:79
  65.2 40.6 %collective-permute-start.18 = (bf16[2,128,2048]{2,1,0:T(8,128)(2,1)}, bf16[2,128,2048]{2,1,0:T(8,128)(2,1)}, u32[]{:S(2)}, u32[]{:S(2)}) collective-permute-start(bf16[2,128,2048]{2,1,0:T(8,128)(2,1)} %pad_maximum_fusion.3), channel_id=1, source_target_pairs={{0,8},{8,16},{16,24},{24,28},{28,20},{20,12},{12,4},{4,0},{1,9},{9... | collective-permute-start | bytes 3145736 | tf_op jit(solution)/shard_map/ppermute | solution.py:79
  69.8 24.2 %collective-permute-start.9 = (bf16[128,1024]{1,0:T(8,128)(2,1)S(1)}, bf16[128,1024]{1,0:T(8,128)(2,1)S(1)}, u32[]{:S(2)}, u32[]{:S(2)}) collective-permute-start(bf16[128,1024]{1,0:T(8,128)(2,1)S(1)} %fusion.82), channel_id=1, source_target_pairs={{0,4},{1,8},{2,20},{3,24},{8,1},{9,17},{10,13},{11,29},{16,10},{17... | collective-permute-start | bytes 786440 | tf_op jit(solution)/shard_map/ppermute | solution.py:153
  75.9 18.1 %collective-permute-start.15 = (bf16[128,1024]{1,0:T(8,128)(2,1)S(1)}, bf16[128,1024]{1,0:T(8,128)(2,1)S(1)}, u32[]{:S(2)}, u32[]{:S(2)}) collective-permute-start(bf16[128,1024]{1,0:T(8,128)(2,1)S(1)} %fusion.81), channel_id=1, source_target_pairs={{0,0},{1,12},{2,16},{3,28},{8,9},{9,5},{10,25},{11,21},{16,18},{17... | collective-permute-start | bytes 786440 | tf_op jit(solution)/shard_map/ppermute | solution.py:153
  97.6 21.3 %collective-permute-start.17 = (bf16[128,2048]{1,0:T(8,128)(2,1)}, bf16[128,2048]{1,0:T(8,128)(2,1)S(1)}, u32[]{:S(2)}, u32[]{:S(2)}) collective-permute-start(bf16[128,2048]{1,0:T(8,128)(2,1)} %add_residual.1), channel_id=1, source_target_pairs={{8,0},{16,8},{24,16},{28,24},{20,28},{12,20},{4,12},{0,4},{9,1},{1... | collective-permute-start | bytes 1572872 | tf_op jit(solution)/shard_map/ppermute | solution.py:79
  99.0 19.8 %collective-permute-start.16 = (bf16[128,2048]{1,0:T(8,128)(2,1)}, bf16[128,2048]{1,0:T(8,128)(2,1)S(1)}, u32[]{:S(2)}, u32[]{:S(2)}) collective-permute-start(bf16[128,2048]{1,0:T(8,128)(2,1)} %add_residual.1), channel_id=1, source_target_pairs={{0,8},{8,16},{16,24},{24,28},{28,20},{20,12},{12,4},{4,0},{1,9},{9... | collective-permute-start | bytes 1572872 | tf_op jit(solution)/shard_map/ppermute | solution.py:79
  105.8 42.9 %collective-permute-start.27 = (bf16[2,128,2048]{2,1,0:T(8,128)(2,1)}, bf16[2,128,2048]{2,1,0:T(8,128)(2,1)S(1)}, u32[]{:S(2)}, u32[]{:S(2)}) collective-permute-start(bf16[2,128,2048]{2,1,0:T(8,128)(2,1)} %collective-permute-done.19), channel_id=1, source_target_pairs={{8,0},{16,8},{24,16},{28,24},{20,28},{12,20},{4,12},{0,4},{9,1},{1... | collective-permute-start | bytes 3145736 | tf_op jit(solution)/shard_map/ppermute | solution.py:79
  105.8 43.0 %collective-permute-start.26 = (bf16[2,128,2048]{2,1,0:T(8,128)(2,1)}, bf16[2,128,2048]{2,1,0:T(8,128)(2,1)S(1)}, u32[]{:S(2)}, u32[]{:S(2)}) collective-permute-start(bf16[2,128,2048]{2,1,0:T(8,128)(2,1)} %collective-permute-done.18), channel_id=1, source_target_pairs={{0,8},{8,16},{16,24},{24,28},{28,20},{20,12},{12,4},{4,0},{1,9},{9... | collective-permute-start | bytes 3145736 | tf_op jit(solution)/shard_map/ppermute | solution.py:79
  120.9 27.7 %collective-permute-start.25 = (bf16[128,2048]{1,0:T(8,128)(2,1)S(1)}, bf16[128,2048]{1,0:T(8,128)(2,1)S(1)}, u32[]{:S(2)}, u32[]{:S(2)}) collective-permute-start(bf16[128,2048]{1,0:T(8,128)(2,1)S(1)} %collective-permute-done.17), channel_id=1, source_target_pairs={{8,0},{16,8},{24,16},{28,24},{20,28},{12,20},{4,12},{0,4},{9,1},{1... | collective-permute-start | bytes 1572872 | tf_op jit(solution)/shard_map/ppermute | solution.py:79
  121.0 27.7 %collective-permute-start.24 = (bf16[128,2048]{1,0:T(8,128)(2,1)S(1)}, bf16[128,2048]{1,0:T(8,128)(2,1)S(1)}, u32[]{:S(2)}, u32[]{:S(2)}) collective-permute-start(bf16[128,2048]{1,0:T(8,128)(2,1)S(1)} %collective-permute-done.16), channel_id=1, source_target_pairs={{0,8},{8,16},{16,24},{24,28},{28,20},{20,12},{12,4},{4,0},{1,9},{9... | collective-permute-start | bytes 1572872 | tf_op jit(solution)/shard_map/ppermute | solution.py:79
  126.0 29.7 %collective-permute-start.20 = (f32[3,2,32,1024]{3,2,1,0:T(8,128)}, f32[3,2,32,1024]{3,2,1,0:T(8,128)S(1)}, u32[]{:S(2)}, u32[]{:S(2)}) collective-permute-start(f32[3,2,32,1024]{3,2,1,0:T(8,128)} %dynamic-slice_bitcast_fusion), channel_id=1, source_target_pairs={{0,1},{1,0},{2,3},{3,2},{4,5},{5,4},{6,7},{7,6},{8,9},{9,8},{10,11... | collective-permute-start | bytes 2359304 | tf_op jit(solution)/shard_map/ppermute | solution.py:99
  155.7 15.5 %collective-permute-start.28 = (f32[2,2,32,1024]{3,2,1,0:T(8,128)}, f32[2,2,32,1024]{3,2,1,0:T(8,128)}, u32[]{:S(2)}, u32[]{:S(2)}) collective-permute-start(f32[2,2,32,1024]{3,2,1,0:T(8,128)} %dynamic-slice_bitcast_fusion.2), channel_id=1, source_target_pairs={{0,1},{1,0},{2,3},{3,2},{4,5},{5,4},{6,7},{7,6},{8,9},{9,8},{10,11... | collective-permute-start | bytes 1572872 | tf_op jit(solution)/shard_map/ppermute | solution.py:99
  155.8 19.4 %collective-permute-start.21 = (f32[3,1,32,1024]{3,2,1,0:T(8,128)S(1)}, f32[3,1,32,1024]{3,2,1,0:T(8,128)S(1)}, u32[]{:S(2)}, u32[]{:S(2)}) collective-permute-start(f32[3,1,32,1024]{3,2,1,0:T(8,128)S(1)} %constant_dynamic-slice_fusion.3), channel_id=1, source_target_pairs={{0,2},{1,3},{2,0},{3,1},{4,6},{5,7},{6,4},{7,5},{8,10},{9,11},{10,... | collective-permute-start | bytes 1179656 | tf_op jit(solution)/shard_map/ppermute | solution.py:99
  165.4 42.4 %collective-permute-start.35 = (bf16[2,128,2048]{2,1,0:T(8,128)(2,1)S(1)}, bf16[2,128,2048]{2,1,0:T(8,128)(2,1)S(1)}, u32[]{:S(2)}, u32[]{:S(2)}) collective-permute-start(bf16[2,128,2048]{2,1,0:T(8,128)(2,1)S(1)} %copy-done.4), channel_id=1, source_target_pairs={{8,0},{16,8},{24,16},{28,24},{20,28},{12,20},{4,12},{0,4},{9,1},{1... | collective-permute-start | bytes 3145736 | tf_op jit(solution)/shard_map/ppermute | solution.py:79
  169.1 38.9 %collective-permute-start.34 = (bf16[2,128,2048]{2,1,0:T(8,128)(2,1)S(1)}, bf16[2,128,2048]{2,1,0:T(8,128)(2,1)S(1)}, u32[]{:S(2)}, u32[]{:S(2)}) collective-permute-start(bf16[2,128,2048]{2,1,0:T(8,128)(2,1)S(1)} %collective-permute-done.26), channel_id=1, source_target_pairs={{0,8},{8,16},{16,24},{24,28},{28,20},{20,12},{12,4},{4,0},{1,9},{9... | collective-permute-start | bytes 3145736 | tf_op jit(solution)/shard_map/ppermute | solution.py:79
  169.1 34.0 %collective-permute-start.33 = (bf16[128,2048]{1,0:T(8,128)(2,1)S(1)}, bf16[128,2048]{1,0:T(8,128)(2,1)S(1)}, u32[]{:S(2)}, u32[]{:S(2)}) collective-permute-start(bf16[128,2048]{1,0:T(8,128)(2,1)S(1)} %copy-done.10), channel_id=1, source_target_pairs={{8,0},{16,8},{24,16},{28,24},{20,28},{12,20},{4,12},{0,4},{9,1},{1... | collective-permute-start | bytes 1572872 | tf_op jit(solution)/shard_map/ppermute | solution.py:79
  171.1 34.5 %collective-permute-start.32 = (bf16[128,2048]{1,0:T(8,128)(2,1)S(1)}, bf16[128,2048]{1,0:T(8,128)(2,1)S(1)}, u32[]{:S(2)}, u32[]{:S(2)}) collective-permute-start(bf16[128,2048]{1,0:T(8,128)(2,1)S(1)} %copy-done.8), channel_id=1, source_target_pairs={{0,8},{8,16},{16,24},{24,28},{28,20},{20,12},{12,4},{4,0},{1,9},{9... | collective-permute-start | bytes 1572872 | tf_op jit(solution)/shard_map/ppermute | solution.py:79
  175.2 30.5 %collective-permute-start.29 = (f32[2,1,32,1024]{3,2,1,0:T(8,128)S(1)}, f32[2,1,32,1024]{3,2,1,0:T(8,128)S(1)}, u32[]{:S(2)}, u32[]{:S(2)}) collective-permute-start(f32[2,1,32,1024]{3,2,1,0:T(8,128)S(1)} %constant_dynamic-slice_fusion.2), channel_id=1, source_target_pairs={{0,2},{1,3},{2,0},{3,1},{4,6},{5,7},{6,4},{7,5},{8,10},{9,11},{10,... | collective-permute-start | bytes 786440 | tf_op jit(solution)/shard_map/ppermute | solution.py:99
  203.1 48.4 %collective-permute-start.22 = (bf16[32,1024]{1,0:T(8,128)(2,1)S(1)}, bf16[32,1024]{1,0:T(8,128)(2,1)S(1)}, u32[]{:S(2)}, u32[]{:S(2)}) collective-permute-start(bf16[32,1024]{1,0:T(8,128)(2,1)S(1)} %get-tuple-element.56), channel_id=1, source_target_pairs={{0,4},{8,0},{16,8},{24,16},{28,24},{20,28},{12,20},{4,12},{1,5},{9... | collective-permute-start | bytes 196616 | tf_op jit(solution)/shard_map/ppermute | solution.py:212
  205.6 49.0 %collective-permute-start.23 = (bf16[32,1024]{1,0:T(8,128)(2,1)S(1)}, bf16[32,1024]{1,0:T(8,128)(2,1)S(1)}, u32[]{:S(2)}, u32[]{:S(2)}) collective-permute-start(bf16[32,1024]{1,0:T(8,128)(2,1)S(1)} %get-tuple-element.55), channel_id=1, source_target_pairs={{0,8},{8,16},{16,24},{24,28},{28,20},{20,12},{12,4},{4,0},{1,9},{9... | collective-permute-start | bytes 196616 | tf_op jit(solution)/shard_map/ppermute | solution.py:212
  205.8 25.1 %collective-permute-start.41 = (bf16[64,2048]{1,0:T(8,128)(2,1)S(1)}, bf16[64,2048]{1,0:T(8,128)(2,1)S(1)}, u32[]{:S(2)}, u32[]{:S(2)}) collective-permute-start(bf16[64,2048]{1,0:T(8,128)(2,1)S(1)} %slice.115), channel_id=1, source_target_pairs={{8,0},{16,8},{24,16},{28,24},{20,28},{12,20},{4,12},{0,4},{9,1},{1... | collective-permute-start | bytes 786440 | tf_op jit(solution)/shard_map/ppermute | solution.py:79
  228.5 27.8 %collective-permute-start.30 = (bf16[32,1024]{1,0:T(8,128)(2,1)S(1)}, bf16[32,1024]{1,0:T(8,128)(2,1)S(1)}, u32[]{:S(2)}, u32[]{:S(2)}) collective-permute-start(bf16[32,1024]{1,0:T(8,128)(2,1)S(1)} %get-tuple-element.60), channel_id=1, source_target_pairs={{0,12},{8,4},{16,0},{24,8},{28,16},{20,24},{12,28},{4,20},{1,13},{... | collective-permute-start | bytes 196616 | tf_op jit(solution)/shard_map/ppermute | solution.py:212
  230.9 25.5 %collective-permute-start.31 = (bf16[32,1024]{1,0:T(8,128)(2,1)S(1)}, bf16[32,1024]{1,0:T(8,128)(2,1)S(1)}, u32[]{:S(2)}, u32[]{:S(2)}) collective-permute-start(bf16[32,1024]{1,0:T(8,128)(2,1)S(1)} %get-tuple-element.59), channel_id=1, source_target_pairs={{0,16},{8,24},{16,28},{24,20},{28,12},{20,4},{12,0},{4,8},{1,17},{... | collective-permute-start | bytes 196616 | tf_op jit(solution)/shard_map/ppermute | solution.py:212
  (51 other events, 428.6 us)

commit v5 on v4

--- a/solution.py
+++ b/solution.py
@@ -2,6 +2,7 @@
 
 import jax
 import jax.numpy as jnp
+import numpy as np
 from jax import lax
 from jax.experimental import pallas as pl
 from jax.experimental.pallas import tpu as pltpu
@@ -105,6 +106,12 @@
     def bit_of_x(half):
         return (x >> (half.bit_length() - 1)) & 1
 
+    low_all = lax.all_gather(low_hidden, "dp", axis=0, tiled=True)
+    group_table = np.array([[ring[(p - k) % groups] for k in offsets] for p in np.argsort(ring)], np.uint32)
+    group_at = lax.dynamic_slice(
+        jnp.asarray(group_table), (lax.axis_index("dp").astype(jnp.uint32), jnp.uint32(0)), (1, groups)
+    )
+
     attn = Gather(attn_heads, 0)
     per_owner = groups // owners
     classes = list(reversed(range(per_owner)))
@@ -127,7 +134,7 @@
         if attn.hops:
             sum_pairs()
         attn.hop(ready)
-    arrived_heads = attn.ends
+    mid_all = lax.all_gather(tie(mid_hidden, attn.ends), "dp", axis=0, tiled=True)
     sum_pairs()
 
     def sum_xs(parts):
@@ -159,9 +166,9 @@
         name="add_residual",
     )(*arrived, residual)
 
-    deep = Gather(jnp.stack([low_hidden, mid_hidden]), 1)
-    deep.hop(arrived_heads)
-    deep.hop(held)
+    deep_sum = jnp.dot(low_all, join_weight[0], preferred_element_type=jnp.float32)
+    deep_sum = deep_sum + jnp.dot(mid_all, join_weight[1], preferred_element_type=jnp.float32)
+    deep_sum = deep_sum.reshape(groups, tokens, width)
     top = Gather(own_top, 0)
     cuts = [0] + list(range(3, groups, 2)) + [groups]
     chunks = []
@@ -169,8 +176,7 @@
     def start_chunk():
         part = offsets[cuts[len(chunks)] : cuts[len(chunks) + 1]]
         total = product([top.slots[k] for k in part], join_weight[2])
-        for depth in range(2):
-            total = total + product([[piece[depth] for piece in deep.slots[k]] for k in part], join_weight[depth])
+        total = total + jnp.stack([pick(deep_sum, group_at[0, offsets.index(k)]) for k in part])
         chunks.append([total])
 
     def step_chunk(chunk):
@@ -192,11 +198,9 @@
 
     while top.hops < last:
         top.hop([chunk[-1] for chunk in chunks])
-        if deep.hops < last:
-            deep.hop(top.ends)
         for chunk in chunks:
             step_chunk(chunk)
-        if top.hops > 1:
+        while last - 2 < top.hops and len(chunks) < top.hops - 1:
             start_chunk()
             step_chunk(chunks[-1])
     while len(chunks) < len(cuts) - 1:

time: 265 us -> 319 us (1.20)
  starting transfers between devices: 69.8 us -> 84.9 us
  between operations: 0.8 us -> 13.9 us
  matrix products: 27.3 us -> 39.2 us
  waiting for transfers between devices: 140 us -> 147 us
  local copies, waits for them, and re-layouts: 12.4 us -> 17 us
    ppermute x12 -> x8, waiting for transfers between devices: 23.4 us -> 60.3 us  [hop(): lax.ppermute(ends[0], 'dp', up)]
    ppermute x12 -> x8, starting transfers between devices: 19.9 us -> 45.4 us  [hop(): lax.ppermute(ends[0], 'dp', up)]
    dot_general x0 -> x2, matrix products: none -> 19.3 us  [the longest x1 10.1 us: local(): jnp.dot(low_all, join_weight[0], preferred_element_type=jnp.float32)]
    ppermute x2, waiting for transfers between devices: 17.3 us -> 0.45 us  [local(): arrived.append(lax.ppermute(held, ('dp', 'tensor'), moves))]
    dot_general x16 -> x8, matrix products: 27.3 us -> 19.9 us  [product(): jnp.dot(rows_in, weight, preferred_element_type=jnp.float32)]
    dynamic_slice x0 -> x2, local copies, waits for them, and re-layouts: none -> 7.27 us  [the longest x1 6.57 us: pick(): return lax.dynamic_index_in_dim(values, index, 0, keepdims=False)]
    ppermute x14, starting transfers between devices: 22.8 us -> 15.7 us  [swap(): return lax.ppermute(values, 'tensor', [(t, t ^ bit) for t in range(owners)])]
    ppermute x12 -> x8, waiting for transfers between devices: 74.3 us -> 67.4 us  [hop(): lax.ppermute(ends[1], 'dp', down)]
  transfers between devices with their start and end apart: 47 -> 41, of which waited for: 24 -> 19; matrix products, arithmetic and copies ran while one was open for 17% -> 14% of each run, Pallas kernels for 1% -> 1%
where the time goes in v5:
time: 319 us; the launch traced here: 318 us
  waiting for transfers between devices  147 us (46%)
  starting transfers between devices  84.9 us (27%)
  matrix products  39.2 us (12%)
  local copies, waits for them, and re-layouts  17 us (5%)
  between operations  13.9 us (4%)
  other arithmetic  12.1 us (4%)
  Pallas kernels  4.4 us (1%)
    ppermute x8, waiting for transfers between devices, hop(): lax.ppermute(ends[1], 'dp', down)  67.4 us
    ppermute x8, waiting for transfers between devices, hop(): lax.ppermute(ends[0], 'dp', up)  60.3 us
    ppermute x8, starting transfers between devices, hop(): lax.ppermute(ends[0], 'dp', up)  45.4 us
    dot_general x8, matrix products, product(): jnp.dot(rows_in, weight, preferred_element_type=jnp.float32)  19.9 us
    ppermute x14, starting transfers between devices, swap(): return lax.ppermute(values, 'tensor', [(t, t ^ bit) for t in range(owners)])  15.7 us
    ppermute x14, waiting for transfers between devices, swap(): return lax.ppermute(values, 'tensor', [(t, t ^ bit) for t in range(owners)])  15.1 us
    ppermute x7, starting transfers between devices, local(): owned[i] = lax.ppermute(owned[i].astype(jnp.bfloat16), 'dp', moves)  14.9 us
    dot_general x1, matrix products, local(): jnp.dot(low_all, join_weight[0], preferred_element_type=jnp.float32)  10.1 us
  transfers between devices with their start and end apart: 41, of which 19 were waited for; matrix products, arithmetic and copies ran while one was open for 14% of the time, Pallas kernels for 1%

profile of v5, /device:TPU:0, one launch (start us, length us, event | category | flops | bytes accessed | tf_op | source)
XLA Modules:
  0.0 318.4 jit_solution(11157084574403787198)
XLA Ops:
  10.4 12.7 %collective-permute-done = bf16[128,2048]{1,0:T(8,128)(2,1)S(1)} collective-permute-done((bf16[128,2048]{1,0:T(8,128)(2,1)}, bf16[128,2048]{1,0:T(8,128)(2,1)S(1)}, u32[]{:S(2)}, u32[]{:S(2)}) %collective-permute-start) | collective-permute-done | bytes 524320 | tf_op jit(solution)/shard_map/ppermute | solution.py:80
  29.7 18.2 %collective-permute-done.1 = bf16[128,2048]{1,0:T(8,128)(2,1)S(1)} collective-permute-done((bf16[128,2048]{1,0:T(8,128)(2,1)S(1)}, bf16[128,2048]{1,0:T(8,128)(2,1)S(1)}, u32[]{:S(2)}, u32[]{:S(2)}) %collective-permute-start.1) | collective-permute-done | bytes 524320 | tf_op jit(solution)/shard_map/ppermute | solution.py:80
  54.6 20.3 %collective-permute-done.5 = bf16[128,2048]{1,0:T(8,128)(2,1)S(1)} collective-permute-done((bf16[128,2048]{1,0:T(8,128)(2,1)S(1)}, bf16[128,2048]{1,0:T(8,128)(2,1)S(1)}, u32[]{:S(2)}, u32[]{:S(2)}) %collective-permute-start.5) | collective-permute-done | bytes 524320 | tf_op jit(solution)/shard_map/ppermute | solution.py:80
  74.9 10.6 %collective-permute-done.6 = bf16[128,2048]{1,0:T(8,128)(2,1)S(1)} collective-permute-done((bf16[128,2048]{1,0:T(8,128)(2,1)S(1)}, bf16[128,2048]{1,0:T(8,128)(2,1)S(1)}, u32[]{:S(2)}, u32[]{:S(2)}) %collective-permute-start.6) | collective-permute-done | bytes 524320 | tf_op jit(solution)/shard_map/ppermute | solution.py:80
  87.6 7.5 %collective-permute-done.11 = bf16[64,2048]{1,0:T(8,128)(2,1)S(1)} collective-permute-done((bf16[64,2048]{1,0:T(8,128)(2,1)S(1)}, bf16[64,2048]{1,0:T(8,128)(2,1)S(1)}, u32[]{:S(2)}, u32[]{:S(2)}) %collective-permute-start.11) | collective-permute-done | bytes 262176 | tf_op jit(solution)/shard_map/ppermute | solution.py:80
  95.1 12.0 %collective-permute-done.12 = bf16[64,2048]{1,0:T(8,128)(2,1)S(1)} collective-permute-done((bf16[64,2048]{1,0:T(8,128)(2,1)S(1)}, bf16[64,2048]{1,0:T(8,128)(2,1)S(1)}, u32[]{:S(2)}, u32[]{:S(2)}) %collective-permute-start.12) | collective-permute-done | bytes 262176 | tf_op jit(solution)/shard_map/ppermute | solution.py:80
  107.9 3.6 %fusion.39 = f32[256,1024]{1,0:T(8,128)S(1)} fusion(bf16[2048,1024]{1,0:T(8,128)(2,1)} %param.12, bf16[128,2048]{1,0:T(8,128)(2,1)S(1)} %collective-permute-done.6, bf16[128,2048]{1,0:T(8,128)(2,1)S(1)} %collective-permute-done.5), kind=kOutput, calls=%fused_computation.29 | convolution fusion | flops 1075838976 | bytes 6291456 | tf_op jit(solution)/shard_map/dot_general | solution.py:104
  119.6 5.7 %collective-permute-done.8 = bf16[1,128,1024]{2,1,0:T(8,128)(2,1)S(1)} collective-permute-done((bf16[1,128,1024]{2,1,0:T(8,128)(2,1)S(1)}, bf16[1,128,1024]{2,1,0:T(8,128)(2,1)S(1)}, u32[]{:S(2)}, u32[]{:S(2)}) %collective-permute-start.8) | collective-permute-done | bytes 262176 | tf_op jit(solution)/shard_map/ppermute | solution.py:100
  126.6 3.4 %collective-permute-done.14 = bf16[1,128,1024]{2,1,0:T(8,128)(2,1)S(1)} collective-permute-done((bf16[1,128,1024]{2,1,0:T(8,128)(2,1)S(1)}, bf16[1,128,1024]{2,1,0:T(8,128)(2,1)S(1)}, u32[]{:S(2)}, u32[]{:S(2)}) %collective-permute-start.14) | collective-permute-done | bytes 262176 | tf_op jit(solution)/shard_map/ppermute | solution.py:100
  135.9 4.9 %collective-permute-start.17 = (bf16[128,2048]{1,0:T(8,128)(2,1)}, bf16[128,2048]{1,0:T(8,128)(2,1)S(1)}, u32[]{:S(2)}, u32[]{:S(2)}) collective-permute-start(bf16[128,2048]{1,0:T(8,128)(2,1)} %add_residual.1), channel_id=1, source_target_pairs={{8,0},{16,8},{24,16},{28,24},{20,28},{12,20},{4,12},{0,4},{9,1},{1... | collective-permute-start | bytes 1572872 | tf_op jit(solution)/shard_map/ppermute | solution.py:80
  140.8 13.4 %collective-permute-start.16 = (bf16[128,2048]{1,0:T(8,128)(2,1)}, bf16[128,2048]{1,0:T(8,128)(2,1)S(1)}, u32[]{:S(2)}, u32[]{:S(2)}) collective-permute-start(bf16[128,2048]{1,0:T(8,128)(2,1)} %add_residual.1), channel_id=1, source_target_pairs={{0,8},{8,16},{16,24},{24,28},{28,20},{20,12},{12,4},{4,0},{1,9},{9... | collective-permute-start | bytes 1572872 | tf_op jit(solution)/shard_map/ppermute | solution.py:80
  154.3 18.3 %collective-permute-done.17 = bf16[128,2048]{1,0:T(8,128)(2,1)S(1)} collective-permute-done((bf16[128,2048]{1,0:T(8,128)(2,1)}, bf16[128,2048]{1,0:T(8,128)(2,1)S(1)}, u32[]{:S(2)}, u32[]{:S(2)}) %collective-permute-start.17) | collective-permute-done | bytes 524320 | tf_op jit(solution)/shard_map/ppermute | solution.py:80
  172.6 14.3 %collective-permute-start.22 = (bf16[128,2048]{1,0:T(8,128)(2,1)S(1)}, bf16[128,2048]{1,0:T(8,128)(2,1)}, u32[]{:S(2)}, u32[]{:S(2)}) collective-permute-start(bf16[128,2048]{1,0:T(8,128)(2,1)S(1)} %collective-permute-done.16), channel_id=1, source_target_pairs={{0,8},{8,16},{16,24},{24,28},{28,20},{20,12},{12,4},{4,0},{1,9},{9... | collective-permute-start | bytes 1572872 | tf_op jit(solution)/shard_map/ppermute | solution.py:80
  187.5 17.2 %collective-permute-done.23 = bf16[128,2048]{1,0:T(8,128)(2,1)S(1)} collective-permute-done((bf16[128,2048]{1,0:T(8,128)(2,1)S(1)}, bf16[128,2048]{1,0:T(8,128)(2,1)S(1)}, u32[]{:S(2)}, u32[]{:S(2)}) %collective-permute-start.23) | collective-permute-done | bytes 524320 | tf_op jit(solution)/shard_map/ppermute | solution.py:80
  204.7 8.4 %collective-permute-start.28 = (bf16[128,2048]{1,0:T(8,128)(2,1)}, bf16[128,2048]{1,0:T(8,128)(2,1)S(1)}, u32[]{:S(2)}, u32[]{:S(2)}) collective-permute-start(bf16[128,2048]{1,0:T(8,128)(2,1)} %collective-permute-done.22), channel_id=1, source_target_pairs={{0,8},{8,16},{16,24},{24,28},{28,20},{20,12},{12,4},{4,0},{1,9},{9... | collective-permute-start | bytes 1572872 | tf_op jit(solution)/shard_map/ppermute | solution.py:80
  216.1 6.3 %collective-permute-done.29 = bf16[128,2048]{1,0:T(8,128)(2,1)S(1)} collective-permute-done((bf16[128,2048]{1,0:T(8,128)(2,1)S(1)}, bf16[128,2048]{1,0:T(8,128)(2,1)S(1)}, u32[]{:S(2)}, u32[]{:S(2)}) %collective-permute-start.29) | collective-permute-done | bytes 524320 | tf_op jit(solution)/shard_map/ppermute | solution.py:80
  226.0 10.1 %fusion.2 = f32[1024,1024]{1,0:T(8,128)} fusion(bf16[1024,2048]{1,0:T(8,128)(2,1)} %all-gather.3.cloned.1.call-done, bf16[3,2048,1024]{2,1,0:T(8,128)(2,1)} %param.13), kind=kOutput, calls=%fused_computation.2 | convolution fusion | flops 4294967296 | bytes 12582912 | tf_op jit(solution)/shard_map/dot_general | solution.py:169
  236.0 9.3 %fusion.18 = f32[1024,1024]{1,0:T(8,128)S(1)} fusion(f32[1024,1024]{1,0:T(8,128)} %fusion.2, bf16[1024,2048]{1,0:T(8,128)(2,1)} %all-gather.5.cloned.1.call-done, bf16[3,2048,1024]{2,1,0:T(8,128)(2,1)} %param.13), kind=kOutput, calls=%fused_computation.18 | convolution fusion | flops 4296015872 | bytes 16777216 | tf_op jit(solution)/shard_map/dot_general | solution.py:170
  245.3 6.6 %constant_dynamic-slice_fusion.3 = (f32[1,128,1024]{2,1,0:T(8,128)S(1)}, f32[1,128,1024]{2,1,0:T(8,128)S(1)}, f32[1,128,1024]{2,1,0:T(8,128)S(1)}, f32[1,128,102...) fusion(f32[8,128,1024]{2,1,0:T(8,128)S(1)} %bitcast.144, ...), kind=kLoop, calls=%fused_computation.87 | loop fusion | bytes 7340060 | tf_op jit(solution)/shard_map/jit(dynamic_index_in_dim)/dynamic_slice | solution.py:24
  251.9 3.5 %fusion.23 = f32[2,128,1024]{2,1,0:T(8,128)S(1)} fusion(bf16[2,128,2048]{2,1,0:T(8,128)(2,1)S(1)} %bitcast.155, bf16[3,2048,1024]{2,1,0:T(8,128)(2,1)} %param.13, f32[1,128,1024]{2,1,0:T(8,128)S(1)} %get-tuple-element.23, f32[1,128,1024]{2,1,0:T(8,128)S(1)} %get-tuple-element.24), kind=kOutput, calls=%fused_computation.21 | convolution fusion | flops 1074266112 | bytes 7340032 | tf_op jit(solution)/shard_map/dot_general | solution.py:104
  265.0 6.5 %collective-permute-start.25 = (f32[2,1,32,1024]{3,2,1,0:T(8,128)S(1)}, f32[2,1,32,1024]{3,2,1,0:T(8,128)S(1)}, u32[]{:S(2)}, u32[]{:S(2)}) collective-permute-start(f32[2,1,32,1024]{3,2,1,0:T(8,128)S(1)} %constant_dynamic-slice_fusion.4), channel_id=1, source_target_pairs={{0,2},{1,3},{2,0},{3,1},{4,6},{5,7},{6,4},{7,5},{8,10},{9,11},{10,... | collective-permute-start | bytes 786440 | tf_op jit(solution)/shard_map/ppermute | solution.py:100
  285.8 3.6 %fusion.32 = f32[1,128,1024]{2,1,0:T(8,128)S(1)} fusion(bf16[3,2048,1024]{2,1,0:T(8,128)(2,1)} %param.13, bf16[64,2048]{1,0:T(8,128)(2,1)S(1)} %collective-permute-done.35, bf16[64,2048]{1,0:T(8,128)(2,1)S(1)} %collective-permute-done.34, f32[8,128,1024]{2,1,0:T(8,128)} %bitcast.145, u32[]{:T(128)} %bitcast.48), kind=kOutput, calls=%fused_computation.24 | convolution fusion | flops 538050560 | bytes 5767680 | tf_op jit(solution)/shard_map/dot_general | solution.py:104
  289.6 3.8 %collective-permute-start.32 = (bf16[32,1024]{1,0:T(8,128)(2,1)S(1)}, bf16[32,1024]{1,0:T(8,128)(2,1)S(1)}, u32[]{:S(2)}, u32[]{:S(2)}) collective-permute-start(bf16[32,1024]{1,0:T(8,128)(2,1)S(1)} %get-tuple-element.31), channel_id=1, source_target_pairs={{0,20},{8,12},{16,4},{24,0},{28,8},{20,16},{12,24},{4,28},{1,21},{... | collective-permute-start | bytes 196616 | tf_op jit(solution)/shard_map/ppermute | solution.py:216
  301.6 3.6 %collective-permute-start.38 = (bf16[32,1024]{1,0:T(8,128)(2,1)S(1)}, bf16[32,1024]{1,0:T(8,128)(2,1)S(1)}, u32[]{:S(2)}, u32[]{:S(2)}) collective-permute-start(bf16[32,1024]{1,0:T(8,128)(2,1)S(1)} %fusion.60), channel_id=1, source_target_pairs={{0,28},{8,20},{16,12},{24,4},{28,0},{20,8},{12,16},{4,24},{1,29},{... | collective-permute-start | bytes 196616 | tf_op jit(solution)/shard_map/ppermute | solution.py:216
  (167 shorter events, 80.8 us)
Async XLA Ops:
  6.5 219.4 %all-gather.3.cloned.1.call-start = ((), (), s32[]{:S(2)}) async-start(), calls=%async_computation | async-start | bytes 4718592 | tf_op jit(solution)/shard_map/all_gather | solution.py:109
  7.3 228.8 %all-gather.5.cloned.1.call-start = ((), (), s32[]{:S(2)}) async-start(), calls=%async_computation.1 | async-start | bytes 4718592 | tf_op jit(solution)/shard_map/all_gather | solution.py:137
  7.3 15.8 %collective-permute-start = (bf16[128,2048]{1,0:T(8,128)(2,1)}, bf16[128,2048]{1,0:T(8,128)(2,1)S(1)}, u32[]{:S(2)}, u32[]{:S(2)}) collective-permute-start(bf16[128,2048]{1,0:T(8,128)(2,1)} %param.8), channel_id=1, source_target_pairs={{0,8},{8,16},{16,24},{24,28},{28,20},{20,12},{12,4},{4,0},{1,9},{9... | collective-permute-start | bytes 1572872 | tf_op jit(solution)/shard_map/ppermute | solution.py:80
  10.4 15.5 %collective-permute-start.2 = (bf16[128,2048]{1,0:T(8,128)(2,1)}, bf16[128,2048]{1,0:T(8,128)(2,1)S(1)}, u32[]{:S(2)}, u32[]{:S(2)}) collective-permute-start(bf16[128,2048]{1,0:T(8,128)(2,1)} %param.8), channel_id=1, source_target_pairs={{8,0},{16,8},{24,16},{28,24},{20,28},{12,20},{4,12},{0,4},{9,1},{1... | collective-permute-start | bytes 1572872 | tf_op jit(solution)/shard_map/ppermute | solution.py:80
  23.1 24.8 %collective-permute-start.1 = (bf16[128,2048]{1,0:T(8,128)(2,1)S(1)}, bf16[128,2048]{1,0:T(8,128)(2,1)S(1)}, u32[]{:S(2)}, u32[]{:S(2)}) collective-permute-start(bf16[128,2048]{1,0:T(8,128)(2,1)S(1)} %collective-permute-done), channel_id=1, source_target_pairs={{0,8},{8,16},{16,24},{24,28},{28,20},{20,12},{12,4},{4,0},{1,9},{9... | collective-permute-start | bytes 1572872 | tf_op jit(solution)/shard_map/ppermute | solution.py:80
  29.4 19.9 %collective-permute-start.4 = (f32[128,1024]{1,0:T(8,128)S(1)}, f32[128,1024]{1,0:T(8,128)S(1)}, u32[]{:S(2)}, u32[]{:S(2)}) collective-permute-start(f32[128,1024]{1,0:T(8,128)S(1)} %dynamic-slice_bitcast_fusion.6), channel_id=1, source_target_pairs={{0,1},{1,0},{2,3},{3,2},{4,5},{5,4},{6,7},{7,6},{8,9},{9,8},{10,11... | collective-permute-start | bytes 1572872 | tf_op jit(solution)/shard_map/ppermute | solution.py:100
  29.5 22.6 %collective-permute-start.3 = (bf16[128,2048]{1,0:T(8,128)(2,1)S(1)}, bf16[128,2048]{1,0:T(8,128)(2,1)S(1)}, u32[]{:S(2)}, u32[]{:S(2)}) collective-permute-start(bf16[128,2048]{1,0:T(8,128)(2,1)S(1)} %collective-permute-done.2), channel_id=1, source_target_pairs={{8,0},{16,8},{24,16},{28,24},{20,28},{12,20},{4,12},{0,4},{9,1},{1... | collective-permute-start | bytes 1572872 | tf_op jit(solution)/shard_map/ppermute | solution.py:80
  52.1 22.8 %collective-permute-start.5 = (bf16[128,2048]{1,0:T(8,128)(2,1)S(1)}, bf16[128,2048]{1,0:T(8,128)(2,1)S(1)}, u32[]{:S(2)}, u32[]{:S(2)}) collective-permute-start(bf16[128,2048]{1,0:T(8,128)(2,1)S(1)} %collective-permute-done.1), channel_id=1, source_target_pairs={{0,8},{8,16},{16,24},{24,28},{28,20},{20,12},{12,4},{4,0},{1,9},{9... | collective-permute-start | bytes 1572872 | tf_op jit(solution)/shard_map/ppermute | solution.py:80
  53.6 31.8 %collective-permute-start.6 = (bf16[128,2048]{1,0:T(8,128)(2,1)S(1)}, bf16[128,2048]{1,0:T(8,128)(2,1)S(1)}, u32[]{:S(2)}, u32[]{:S(2)}) collective-permute-start(bf16[128,2048]{1,0:T(8,128)(2,1)S(1)} %collective-permute-done.3), channel_id=1, source_target_pairs={{8,0},{16,8},{24,16},{28,24},{20,28},{12,20},{4,12},{0,4},{9,1},{1... | collective-permute-start | bytes 1572872 | tf_op jit(solution)/shard_map/ppermute | solution.py:80
  87.5 19.6 %collective-permute-start.12 = (bf16[64,2048]{1,0:T(8,128)(2,1)S(1)}, bf16[64,2048]{1,0:T(8,128)(2,1)S(1)}, u32[]{:S(2)}, u32[]{:S(2)}) collective-permute-start(bf16[64,2048]{1,0:T(8,128)(2,1)S(1)} %slice.62), channel_id=1, source_target_pairs={{8,0},{16,8},{24,16},{28,24},{20,28},{12,20},{4,12},{0,4},{9,1},{1... | collective-permute-start | bytes 786440 | tf_op jit(solution)/shard_map/ppermute | solution.py:80
  118.8 11.2 %collective-permute-start.14 = (bf16[1,128,1024]{2,1,0:T(8,128)(2,1)S(1)}, bf16[1,128,1024]{2,1,0:T(8,128)(2,1)S(1)}, u32[]{:S(2)}, u32[]{:S(2)}) collective-permute-start(bf16[1,128,1024]{2,1,0:T(8,128)(2,1)S(1)} %fusion.59), channel_id=1, source_target_pairs={{0,2},{1,3},{2,0},{3,1},{4,6},{5,7},{6,4},{7,5},{8,10},{9,11},{10,... | collective-permute-start | bytes 786440 | tf_op jit(solution)/shard_map/ppermute | solution.py:100
  135.9 36.7 %collective-permute-start.17 = (bf16[128,2048]{1,0:T(8,128)(2,1)}, bf16[128,2048]{1,0:T(8,128)(2,1)S(1)}, u32[]{:S(2)}, u32[]{:S(2)}) collective-permute-start(bf16[128,2048]{1,0:T(8,128)(2,1)} %add_residual.1), channel_id=1, source_target_pairs={{8,0},{16,8},{24,16},{28,24},{20,28},{12,20},{4,12},{0,4},{9,1},{1... | collective-permute-start | bytes 1572872 | tf_op jit(solution)/shard_map/ppermute | solution.py:80
  140.8 31.7 %collective-permute-start.16 = (bf16[128,2048]{1,0:T(8,128)(2,1)}, bf16[128,2048]{1,0:T(8,128)(2,1)S(1)}, u32[]{:S(2)}, u32[]{:S(2)}) collective-permute-start(bf16[128,2048]{1,0:T(8,128)(2,1)} %add_residual.1), channel_id=1, source_target_pairs={{0,8},{8,16},{16,24},{24,28},{28,20},{20,12},{12,4},{4,0},{1,9},{9... | collective-permute-start | bytes 1572872 | tf_op jit(solution)/shard_map/ppermute | solution.py:80
  172.6 32.1 %collective-permute-start.23 = (bf16[128,2048]{1,0:T(8,128)(2,1)S(1)}, bf16[128,2048]{1,0:T(8,128)(2,1)S(1)}, u32[]{:S(2)}, u32[]{:S(2)}) collective-permute-start(bf16[128,2048]{1,0:T(8,128)(2,1)S(1)} %collective-permute-done.17), channel_id=1, source_target_pairs={{8,0},{16,8},{24,16},{28,24},{20,28},{12,20},{4,12},{0,4},{9,1},{1... | collective-permute-start | bytes 1572872 | tf_op jit(solution)/shard_map/ppermute | solution.py:80
  172.6 32.1 %collective-permute-start.22 = (bf16[128,2048]{1,0:T(8,128)(2,1)S(1)}, bf16[128,2048]{1,0:T(8,128)(2,1)}, u32[]{:S(2)}, u32[]{:S(2)}) collective-permute-start(bf16[128,2048]{1,0:T(8,128)(2,1)S(1)} %collective-permute-done.16), channel_id=1, source_target_pairs={{0,8},{8,16},{16,24},{24,28},{28,20},{20,12},{12,4},{4,0},{1,9},{9... | collective-permute-start | bytes 1572872 | tf_op jit(solution)/shard_map/ppermute | solution.py:80
  204.7 17.7 %collective-permute-start.29 = (bf16[128,2048]{1,0:T(8,128)(2,1)S(1)}, bf16[128,2048]{1,0:T(8,128)(2,1)S(1)}, u32[]{:S(2)}, u32[]{:S(2)}) collective-permute-start(bf16[128,2048]{1,0:T(8,128)(2,1)S(1)} %collective-permute-done.23), channel_id=1, source_target_pairs={{8,0},{16,8},{24,16},{28,24},{20,28},{12,20},{4,12},{0,4},{9,1},{1... | collective-permute-start | bytes 1572872 | tf_op jit(solution)/shard_map/ppermute | solution.py:80
  204.7 19.4 %collective-permute-start.28 = (bf16[128,2048]{1,0:T(8,128)(2,1)}, bf16[128,2048]{1,0:T(8,128)(2,1)S(1)}, u32[]{:S(2)}, u32[]{:S(2)}) collective-permute-start(bf16[128,2048]{1,0:T(8,128)(2,1)} %collective-permute-done.22), channel_id=1, source_target_pairs={{0,8},{8,16},{16,24},{24,28},{28,20},{20,12},{12,4},{4,0},{1,9},{9... | collective-permute-start | bytes 1572872 | tf_op jit(solution)/shard_map/ppermute | solution.py:80
  265.0 13.6 %collective-permute-start.25 = (f32[2,1,32,1024]{3,2,1,0:T(8,128)S(1)}, f32[2,1,32,1024]{3,2,1,0:T(8,128)S(1)}, u32[]{:S(2)}, u32[]{:S(2)}) collective-permute-start(f32[2,1,32,1024]{3,2,1,0:T(8,128)S(1)} %constant_dynamic-slice_fusion.4), channel_id=1, source_target_pairs={{0,2},{1,3},{2,0},{3,1},{4,6},{5,7},{6,4},{7,5},{8,10},{9,11},{10,... | collective-permute-start | bytes 786440 | tf_op jit(solution)/shard_map/ppermute | solution.py:100
  272.8 11.4 %collective-permute-start.31 = (f32[2,1,32,1024]{3,2,1,0:T(8,128)S(1)}, f32[2,1,32,1024]{3,2,1,0:T(8,128)S(1)}, u32[]{:S(2)}, u32[]{:S(2)}) collective-permute-start(f32[2,1,32,1024]{3,2,1,0:T(8,128)S(1)} %constant_dynamic-slice_fusion.1), channel_id=1, source_target_pairs={{0,2},{1,3},{2,0},{3,1},{4,6},{5,7},{6,4},{7,5},{8,10},{9,11},{10,... | collective-permute-start | bytes 786440 | tf_op jit(solution)/shard_map/ppermute | solution.py:100
  274.2 19.2 %collective-permute-start.19 = (f32[3,1,32,1024]{3,2,1,0:T(8,128)S(1)}, f32[3,1,32,1024]{3,2,1,0:T(8,128)S(1)}, u32[]{:S(2)}, u32[]{:S(2)}) collective-permute-start(f32[3,1,32,1024]{3,2,1,0:T(8,128)S(1)} %constant_dynamic-slice_fusion.7), channel_id=1, source_target_pairs={{0,2},{1,3},{2,0},{3,1},{4,6},{5,7},{6,4},{7,5},{8,10},{9,11},{10,... | collective-permute-start | bytes 1179656 | tf_op jit(solution)/shard_map/ppermute | solution.py:100
  278.7 21.9 %collective-permute-start.26 = (bf16[32,1024]{1,0:T(8,128)(2,1)S(1)}, bf16[32,1024]{1,0:T(8,128)(2,1)S(1)}, u32[]{:S(2)}, u32[]{:S(2)}) collective-permute-start(bf16[32,1024]{1,0:T(8,128)(2,1)S(1)} %get-tuple-element.33), channel_id=1, source_target_pairs={{0,12},{8,4},{16,0},{24,8},{28,16},{20,24},{12,28},{4,20},{1,13},{... | collective-permute-start | bytes 196616 | tf_op jit(solution)/shard_map/ppermute | solution.py:216
  284.2 17.4 %collective-permute-start.27 = (bf16[32,1024]{1,0:T(8,128)(2,1)S(1)}, bf16[32,1024]{1,0:T(8,128)(2,1)S(1)}, u32[]{:S(2)}, u32[]{:S(2)}) collective-permute-start(bf16[32,1024]{1,0:T(8,128)(2,1)S(1)} %get-tuple-element.32), channel_id=1, source_target_pairs={{0,16},{8,24},{16,28},{24,20},{28,12},{20,4},{12,0},{4,8},{1,17},{... | collective-permute-start | bytes 196616 | tf_op jit(solution)/shard_map/ppermute | solution.py:216
  289.6 16.3 %collective-permute-start.32 = (bf16[32,1024]{1,0:T(8,128)(2,1)S(1)}, bf16[32,1024]{1,0:T(8,128)(2,1)S(1)}, u32[]{:S(2)}, u32[]{:S(2)}) collective-permute-start(bf16[32,1024]{1,0:T(8,128)(2,1)S(1)} %get-tuple-element.31), channel_id=1, source_target_pairs={{0,20},{8,12},{16,4},{24,0},{28,8},{20,16},{12,24},{4,28},{1,21},{... | collective-permute-start | bytes 196616 | tf_op jit(solution)/shard_map/ppermute | solution.py:216
  293.4 12.5 %collective-permute-start.33 = (bf16[32,1024]{1,0:T(8,128)(2,1)S(1)}, bf16[32,1024]{1,0:T(8,128)(2,1)S(1)}, u32[]{:S(2)}, u32[]{:S(2)}) collective-permute-start(bf16[32,1024]{1,0:T(8,128)(2,1)S(1)} %get-tuple-element.30), channel_id=1, source_target_pairs={{0,24},{8,28},{16,20},{24,12},{28,4},{20,0},{12,8},{4,16},{1,25},{... | collective-permute-start | bytes 196616 | tf_op jit(solution)/shard_map/ppermute | solution.py:216
  (44 other events, 379.6 us)
Sparse Core Ops, SparseCore 0:
  9.5 99.2 all-gather.2
  110.9 99.6 all-gather.4

commit v6 on v4

--- a/solution.py
+++ b/solution.py
@@ -38,20 +38,22 @@
         top_ref[:, columns] = total.astype(jnp.bfloat16)
 
 
-def norm_body(offsets, width, *refs):
+def norm_body(offsets, counts, width, *refs):
     groups = len(offsets)
-    slots, gain_ref, out_ref = refs[:groups], refs[groups], refs[groups + 1]
+    gain_ref, out_ref = refs[-2:]
     place = place_on_ring(groups)
-    total = 0.0
-    for slot in slots:
-        block = slot[...].astype(jnp.float32)
+    blocks, total, first = [], 0.0, 0
+    for count in counts:
+        block = sum(ref[...].astype(jnp.float32) for ref in refs[first : first + count])
         total = total + jnp.sum(block * block, axis=1, keepdims=True)
+        blocks.append(block)
+        first += count
     inverse_rms = lax.rsqrt(total / (groups * width) + 1e-05)
-    for offset, slot in zip(offsets, slots):
+    for offset, block in zip(offsets, blocks):
         q = lax.rem(place + offset + groups, groups)
         d = jnp.where(q < groups // 2, 2 * q, 2 * (groups - 1 - q) + 1)
         columns = pl.ds(pl.multiple_of(d * width, width), width)
-        out_ref[:, columns] = (slot[...].astype(jnp.float32) * inverse_rms * gain_ref[:, columns]).astype(jnp.bfloat16)
+        out_ref[:, columns] = (block * inverse_rms * gain_ref[:, columns]).astype(jnp.bfloat16)
 
 
 VMEM = pl.BlockSpec(memory_space=pltpu.VMEM)
@@ -64,9 +66,9 @@
         self.ends = [own, own]
         self.slots = {0: [own]}
 
-    def hop(self, after=()):
+    def hop(self):
         count = len(self.ring)
-        ends = tie(self.ends, after) if jax.tree.leaves(after) else self.ends
+        ends = self.ends
         self.hops += 1
         if self.hops == self.last:
             middle = ends[0].shape[self.axis] // 2
@@ -122,12 +124,15 @@
                 pair_sums[kind].append(pick(products, core) + swap(pick(products, 1 - core), 1))
 
     while attn.hops < last:
-        ready = [pair_sums[kind] for kind in classes]
-        ready = [list(part) for part in ready]
+        ready = [list(pair_sums[kind]) for kind in classes]
         if attn.hops:
             sum_pairs()
-        attn.hop(ready)
-    arrived_heads = attn.ends
+        attn.ends = tie(attn.ends, ready)
+        attn.hop()
+    deep = Gather(jnp.stack([low_hidden, mid_hidden]), 1)
+    deep.ends = tie(deep.ends, attn.ends)
+    deep.hop()
+    attn.slots[last] = tie(attn.ends, [list(pair_sums[kind]) for kind in classes])
     sum_pairs()
 
     def sum_xs(parts):
@@ -159,64 +164,74 @@
         name="add_residual",
     )(*arrived, residual)
 
-    deep = Gather(jnp.stack([low_hidden, mid_hidden]), 1)
-    deep.hop(arrived_heads)
-    deep.hop(held)
     top = Gather(own_top, 0)
     cuts = [0] + list(range(3, groups, 2)) + [groups]
-    chunks = []
-
-    def start_chunk():
-        part = offsets[cuts[len(chunks)] : cuts[len(chunks) + 1]]
-        total = product([top.slots[k] for k in part], join_weight[2])
-        for depth in range(2):
-            total = total + product([[piece[depth] for piece in deep.slots[k]] for k in part], join_weight[depth])
-        chunks.append([total])
-
-    def step_chunk(chunk):
-        if len(chunk) == 1:
-            by_owner = chunk[0].reshape(chunk[0].shape[0], xs, 2, rows, width)
-            kept_part = lax.dynamic_index_in_dim(by_owner, core, 2, keepdims=False)
-            sent_part = lax.dynamic_index_in_dim(by_owner, 1 - core, 2, keepdims=False)
-            chunk.append(kept_part + swap(sent_part, 1))
-        elif len(chunk) == 2:
-            part, half = chunk[1], xs // 2
-            while half:
-                part = part.reshape((part.shape[0], 2, half) + part.shape[-2:])
-                side = bit_of_x(half)
-                part = lax.dynamic_index_in_dim(part, side, 1, keepdims=False) + swap(
-                    lax.dynamic_index_in_dim(part, 1 - side, 1, keepdims=False), 2 * half
-                )
-                half //= 2
-            chunk.append(part.reshape(part.shape[0], rows, width))
+    chunks = [offsets[low:high] for low, high in zip(cuts, cuts[1:])]
+    deep_sums, totals, sums, owned = [], [], [], {}
+
+    def add_deep():
+        part = chunks[len(deep_sums)]
+        total = product([[piece[0] for piece in deep.slots[k]] for k in part], join_weight[0])
+        deep_sums.append(total + product([[piece[1] for piece in deep.slots[k]] for k in part], join_weight[1]))
+
+    def add_top():
+        n = len(totals)
+        total = product([top.slots[k] for k in chunks[n]], join_weight[2]) + deep_sums[n]
+        by_owner = total.reshape(len(chunks[n]), xs, 2, rows, width)
+        kept_part = lax.dynamic_index_in_dim(by_owner, core, 2, keepdims=False)
+        sent_part = lax.dynamic_index_in_dim(by_owner, 1 - core, 2, keepdims=False)
+        totals.append(kept_part + swap(sent_part, 1))
+
+    def send(part, k, flip=0):
+        if not k and not flip:
+            return part
+        moves = [
+            (ring[q] * owners + t, ring[(q - k) % groups] * owners + (t ^ (2 * flip)))
+            for q in range(groups)
+            for t in range(owners)
+        ]
+        return lax.ppermute(part.astype(jnp.bfloat16), ("dp", "tensor"), moves)
+
+    def add_x():
+        n = len(sums)
+        part, half = totals[n], xs // 2
+        while half:
+            part = part.reshape((part.shape[0], 2, half) + part.shape[-2:])
+            side = bit_of_x(half)
+            part = lax.dynamic_index_in_dim(part, side, 1, keepdims=False) + swap(
+                lax.dynamic_index_in_dim(part, 1 - side, 1, keepdims=False), 2 * half
+            )
+            half //= 2
+        part = part.reshape(part.shape[0], rows, width)
+        sums.append(part)
+        for i, k in enumerate(chunks[n]):
+            owned[k] = [send(part[i], k)]
 
     while top.hops < last:
-        top.hop([chunk[-1] for chunk in chunks])
+        top.ends, deep.ends = tie((top.ends, deep.ends), [deep_sums, totals, sums])
+        top.hop()
         if deep.hops < last:
-            deep.hop(top.ends)
-        for chunk in chunks:
-            step_chunk(chunk)
+            deep.hop()
         if top.hops > 1:
-            start_chunk()
-            step_chunk(chunks[-1])
-    while len(chunks) < len(cuts) - 1:
-        start_chunk()
-    for chunk in chunks:
-        while len(chunk) < 3:
-            step_chunk(chunk)
-
-    owned = [part for chunk in chunks for part in chunk[-1]]
-    for i, k in enumerate(offsets):
-        if k:
-            moves = [(ring[q], ring[(q - k) % groups]) for q in range(groups)]
-            owned[i] = lax.ppermute(owned[i].astype(jnp.bfloat16), "dp", moves)
+            add_top()
+            if top.hops < last:
+                add_x()
+        add_deep()
+    top.slots[last] = tie(top.ends, [deep_sums, totals])
+    add_top()
+    add_x()
+    for flip in range(xs):
+        part = pick(totals[-1][0], x ^ flip)
+        owned.setdefault(last, []).append(send(part, last, flip))
+    parts = [part for k in offsets for part in owned[k]]
+    counts = [len(owned[k]) for k in offsets]
     return pl.pallas_call(
-        functools.partial(norm_body, offsets, width),
+        functools.partial(norm_body, offsets, counts, width),
         out_shape=jax.ShapeDtypeStruct((rows, groups * width), jnp.bfloat16),
-        in_specs=[VMEM] * (groups + 1),
+        in_specs=[VMEM] * (len(parts) + 1),
         out_specs=VMEM,
         name="norm_rows",
-    )(*owned, join_gain.reshape(1, groups * width))
+    )(*parts, join_gain.reshape(1, groups * width))
 
 
 def solution(mesh):

time: 265 us -> 268 us (1.011)
  starting transfers between devices: 69.8 us -> 54.2 us
  waiting for transfers between devices: 140 us -> 148 us
  matrix products: 27.3 us -> 34.5 us
    ppermute x12, waiting for transfers between devices: 23.4 us -> 114 us  [hop(): lax.ppermute(ends[0], 'dp', up)]
    ppermute x12, waiting for transfers between devices: 74.3 us -> 19.6 us  [hop(): lax.ppermute(ends[1], 'dp', down)]
    ppermute x2, waiting for transfers between devices: 17.3 us -> 0.01 us  [local(): arrived.append(lax.ppermute(held, ('dp', 'tensor'), moves))]
    ppermute x14 -> x13, starting transfers between devices: 22.8 us -> 7 us  [swap(): return lax.ppermute(values, 'tensor', [(t, t ^ bit) for t in range(owners)])]
    ppermute x12, starting transfers between devices: 14.1 us -> 3.3 us  [hop(): lax.ppermute(ends[1], 'dp', down)]
    ppermute x14 -> x13, waiting for transfers between devices: 20.1 us -> 10.3 us  [swap(): return lax.ppermute(values, 'tensor', [(t, t ^ bit) for t in range(owners)])]
    dot_general x16, matrix products: 27.3 us -> 34.5 us  [product(): jnp.dot(rows_in, weight, preferred_element_type=jnp.float32)]
    ppermute x12, starting transfers between devices: 19.9 us -> 26.7 us  [hop(): lax.ppermute(ends[0], 'dp', up)]
  transfers between devices with their start and end apart: 47 -> 47, of which waited for: 24 -> 27; matrix products, arithmetic and copies ran while one was open for 17% -> 20% of each run, Pallas kernels for 1% -> 0%
where the time goes in v6:
time: 268 us
  waiting for transfers between devices  148 us (55%)
  starting transfers between devices  54.2 us (20%)
  matrix products  34.5 us (13%)
  local copies, waits for them, and re-layouts  14.4 us (5%)
  other arithmetic  11.3 us (4%)
  Pallas kernels  4.41 us (2%)
    ppermute x12, waiting for transfers between devices, hop(): lax.ppermute(ends[0], 'dp', up)  114 us
    dot_general x16, matrix products, product(): jnp.dot(rows_in, weight, preferred_element_type=jnp.float32)  34.5 us
    ppermute x12, starting transfers between devices, hop(): lax.ppermute(ends[0], 'dp', up)  26.7 us
    ppermute x12, waiting for transfers between devices, hop(): lax.ppermute(ends[1], 'dp', down)  19.6 us
    ppermute x8, starting transfers between devices, send(): return lax.ppermute(part.astype(jnp.bfloat16), ('dp', 'tensor'), moves)  15 us
    ppermute x13, waiting for transfers between devices, swap(): return lax.ppermute(values, 'tensor', [(t, t ^ bit) for t in range(owners)])  10.3 us
    ppermute x13, starting transfers between devices, swap(): return lax.ppermute(values, 'tensor', [(t, t ^ bit) for t in range(owners)])  7 us
  transfers between devices with their start and end apart: 47, of which 27 were waited for; matrix products, arithmetic and copies ran while one was open for 20% of the time, Pallas kernels for 0%

profile of v6, /device:TPU:0, one launch (start us, length us, event | category | flops | bytes accessed | tf_op | source)
XLA Modules:
  0.0 267.8 jit_solution(10096079015709986035)
XLA Ops:
  0.0 3.0 %collective-permute-start = (bf16[128,2048]{1,0:T(8,128)(2,1)}, bf16[128,2048]{1,0:T(8,128)(2,1)S(1)}, u32[]{:S(2)}, u32[]{:S(2)}) collective-permute-start(bf16[128,2048]{1,0:T(8,128)(2,1)} %param.7), channel_id=1, source_target_pairs={{0,8},{8,16},{16,24},{24,28},{28,20},{20,12},{12,4},{4,0},{1,9},{9... | collective-permute-start | bytes 1572872 | tf_op jit(solution)/shard_map/ppermute | solution.py:81
  3.0 12.1 %collective-permute-done = bf16[128,2048]{1,0:T(8,128)(2,1)S(1)} collective-permute-done((bf16[128,2048]{1,0:T(8,128)(2,1)}, bf16[128,2048]{1,0:T(8,128)(2,1)S(1)}, u32[]{:S(2)}, u32[]{:S(2)}) %collective-permute-start) | collective-permute-done | bytes 524320 | tf_op jit(solution)/shard_map/ppermute | solution.py:81
  16.6 3.4 %fusion.60 = f32[256,1024]{1,0:T(8,128)S(1)} fusion(bf16[2048,1024]{1,0:T(8,128)(2,1)} %param.11, bf16[128,2048]{1,0:T(8,128)(2,1)S(1)} %collective-permute-done.1, bf16[128,2048]{1,0:T(8,128)(2,1)S(1)} %collective-permute-done), kind=kOutput, calls=%fused_computation.47 | convolution fusion | flops 1075838976 | bytes 6291456 | tf_op jit(solution)/shard_map/dot_general | solution.py:105
  22.3 12.2 %collective-permute-done.2 = bf16[128,2048]{1,0:T(8,128)(2,1)S(1)} collective-permute-done((bf16[128,2048]{1,0:T(8,128)(2,1)S(1)}, bf16[128,2048]{1,0:T(8,128)(2,1)S(1)}, u32[]{:S(2)}, u32[]{:S(2)}) %collective-permute-start.2) | collective-permute-done | bytes 524320 | tf_op jit(solution)/shard_map/ppermute | solution.py:81
  39.3 9.7 %collective-permute-done.5 = bf16[128,2048]{1,0:T(8,128)(2,1)S(1)} collective-permute-done((bf16[128,2048]{1,0:T(8,128)(2,1)S(1)}, bf16[128,2048]{1,0:T(8,128)(2,1)S(1)}, u32[]{:S(2)}, u32[]{:S(2)}) %collective-permute-start.5) | collective-permute-done | bytes 524320 | tf_op jit(solution)/shard_map/ppermute | solution.py:81
  56.4 5.0 %collective-permute-done.11 = bf16[64,2048]{1,0:T(8,128)(2,1)} collective-permute-done((bf16[64,2048]{1,0:T(8,128)(2,1)S(1)}, bf16[64,2048]{1,0:T(8,128)(2,1)}, u32[]{:S(2)}, u32[]{:S(2)}) %collective-permute-start.11) | collective-permute-done | bytes 262176 | tf_op jit(solution)/shard_map/ppermute | solution.py:81
  67.6 2.5 fusion.72
  78.6 11.4 %collective-permute-done.16 = bf16[2,128,2048]{2,1,0:T(8,128)(2,1)} collective-permute-done((bf16[2,128,2048]{2,1,0:T(8,128)(2,1)}, bf16[2,128,2048]{2,1,0:T(8,128)(2,1)}, u32[]{:S(2)}, u32[]{:S(2)}) %collective-permute-start.16) | collective-permute-done | bytes 1048608 | tf_op jit(solution)/shard_map/ppermute | solution.py:81
  91.2 5.6 %collective-permute-done.17 = bf16[2,128,2048]{2,1,0:T(8,128)(2,1)} collective-permute-done((bf16[2,128,2048]{2,1,0:T(8,128)(2,1)}, bf16[2,128,2048]{2,1,0:T(8,128)(2,1)}, u32[]{:S(2)}, u32[]{:S(2)}) %collective-permute-start.17) | collective-permute-done | bytes 1048608 | tf_op jit(solution)/shard_map/ppermute | solution.py:81
  101.4 5.3 %fusion.4 = f32[3,128,1024]{2,1,0:T(8,128)} fusion(bf16[3,128,2048]{2,1,0:T(8,128)(2,1)S(1)} %bitcast.202, bf16[3,2048,1024]{2,1,0:T(8,128)(2,1)} %param.12), kind=kOutput, calls=%fused_computation.4 | convolution fusion | flops 1610612736 | bytes 7340032 | tf_op jit(solution)/shard_map/dot_general | solution.py:105
  110.2 5.8 %collective-permute-start.24 = (bf16[2,128,2048]{2,1,0:T(8,128)(2,1)}, bf16[2,128,2048]{2,1,0:T(8,128)(2,1)}, u32[]{:S(2)}, u32[]{:S(2)}) collective-permute-start(bf16[2,128,2048]{2,1,0:T(8,128)(2,1)} %collective-permute-done.16), channel_id=1, source_target_pairs={{0,8},{8,16},{16,24},{24,28},{28,20},{20,12},{12,4},{4,0},{1,9},{9... | collective-permute-start | bytes 3145736 | tf_op jit(solution)/shard_map/ppermute | solution.py:81
  118.1 4.5 %fusion.39 = f32[3,128,1024]{2,1,0:T(8,128)S(1)} fusion(f32[3,128,1024]{2,1,0:T(8,128)} %fusion.4, bf16[3,128,2048]{2,1,0:T(8,128)(2,1)S(1)} %bitcast.201, bf16[3,2048,1024]{2,1,0:T(8,128)(2,1)} %param.12), kind=kOutput, calls=%fused_computation.40 | convolution fusion | flops 1611005952 | bytes 8912896 | tf_op jit(solution)/shard_map/dot_general | solution.py:105
  122.6 27.6 %collective-permute-done.18 = bf16[128,2048]{1,0:T(8,128)(2,1)S(1)} collective-permute-done((bf16[128,2048]{1,0:T(8,128)(2,1)}, bf16[128,2048]{1,0:T(8,128)(2,1)S(1)}, u32[]{:S(2)}, u32[]{:S(2)}) %collective-permute-start.18) | collective-permute-done | bytes 524320 | tf_op jit(solution)/shard_map/ppermute | solution.py:81
  152.5 4.2 %fusion.36 = f32[3,128,1024]{2,1,0:T(8,128)S(1)} fusion(f32[3,128,1024]{2,1,0:T(8,128)S(1)} %fusion.39, bf16[3,128,2048]{2,1,0:T(8,128)(2,1)S(1)} %bitcast.200, bf16[3,2048,1024]{2,1,0:T(8,128)(2,1)} %param.12), kind=kOutput, calls=%fused_computation.39 | convolution fusion | flops 1611005952 | bytes 8912896 | tf_op jit(solution)/shard_map/dot_general | solution.py:105
  169.7 24.2 %collective-permute-done.26 = bf16[128,2048]{1,0:T(8,128)(2,1)S(1)} collective-permute-done((bf16[128,2048]{1,0:T(8,128)(2,1)S(1)}, bf16[128,2048]{1,0:T(8,128)(2,1)S(1)}, u32[]{:S(2)}, u32[]{:S(2)}) %collective-permute-start.26) | collective-permute-done | bytes 524320 | tf_op jit(solution)/shard_map/ppermute | solution.py:81
  203.1 2.4 collective-permute-start.40
  208.0 3.6 %fusion = f32[2,128,1024]{2,1,0:T(8,128)S(1)} fusion(bf16[2,128,2048]{2,1,0:T(8,128)(2,1)S(1)} %bitcast.205, bf16[3,2048,1024]{2,1,0:T(8,128)(2,1)} %param.12), kind=kOutput, calls=%fused_computation | convolution fusion | flops 1073741824 | bytes 6291456 | tf_op jit(solution)/shard_map/dot_general | solution.py:105
  215.2 2.7 %collective-permute-done.40 = bf16[2,64,2048]{2,1,0:T(8,128)(2,1)S(1)} collective-permute-done((bf16[2,64,2048]{2,1,0:T(8,128)(2,1)S(1)}, bf16[2,64,2048]{2,1,0:T(8,128)(2,1)S(1)}, u32[]{:S(2)}, u32[]{:S(2)}) %collective-permute-start.40) | collective-permute-done | bytes 524320 | tf_op jit(solution)/shard_map/ppermute | solution.py:81
  220.5 8.3 %collective-permute-done.34 = bf16[128,2048]{1,0:T(8,128)(2,1)S(1)} collective-permute-done((bf16[128,2048]{1,0:T(8,128)(2,1)S(1)}, bf16[128,2048]{1,0:T(8,128)(2,1)S(1)}, u32[]{:S(2)}, u32[]{:S(2)}) %collective-permute-start.34) | collective-permute-done | bytes 524320 | tf_op jit(solution)/shard_map/ppermute | solution.py:81
  240.2 2.9 %collective-permute-start.31 = (bf16[32,1024]{1,0:T(8,128)(2,1)S(1)}, bf16[32,1024]{1,0:T(8,128)(2,1)S(1)}, u32[]{:S(2)}, u32[]{:S(2)}) collective-permute-start(bf16[32,1024]{1,0:T(8,128)(2,1)S(1)} %get-tuple-element.87), channel_id=1, source_target_pairs={{0,16},{1,17},{2,18},{3,19},{8,24},{9,25},{10,26},{11,27},{16,28},... | collective-permute-start | bytes 196616 | tf_op jit(solution)/shard_map/ppermute | solution.py:193
  243.5 7.8 %collective-permute-done.37 = f32[2,1,32,1024]{3,2,1,0:T(8,128)S(1)} collective-permute-done((f32[2,1,32,1024]{3,2,1,0:T(8,128)S(1)}, f32[2,1,32,1024]{3,2,1,0:T(8,128)S(1)}, u32[]{:S(2)}, u32[]{:S(2)}) %collective-permute-start.37) | collective-permute-done | bytes 262176 | tf_op jit(solution)/shard_map/ppermute | solution.py:101
  252.6 3.3 %collective-permute-start.46 = (bf16[32,1024]{1,0:T(8,128)(2,1)S(1)}, bf16[32,1024]{1,0:T(8,128)(2,1)S(1)}, u32[]{:S(2)}, u32[]{:S(2)}) collective-permute-start(bf16[32,1024]{1,0:T(8,128)(2,1)S(1)} %get-tuple-element.83), channel_id=1, source_target_pairs={{0,30},{1,31},{2,28},{3,29},{8,22},{9,23},{10,20},{11,21},{16,14},... | collective-permute-start | bytes 196616 | tf_op jit(solution)/shard_map/ppermute | solution.py:193
  255.9 3.8 %collective-permute-start.39 = (bf16[32,1024]{1,0:T(8,128)(2,1)S(1)}, bf16[32,1024]{1,0:T(8,128)(2,1)S(1)}, u32[]{:S(2)}, u32[]{:S(2)}) collective-permute-start(bf16[32,1024]{1,0:T(8,128)(2,1)S(1)} %get-tuple-element.85), channel_id=1, source_target_pairs={{0,24},{1,25},{2,26},{3,27},{8,28},{9,29},{10,30},{11,31},{16,20},... | collective-permute-start | bytes 196616 | tf_op jit(solution)/shard_map/ppermute | solution.py:193
  262.0 2.9 %collective-permute-done.39.refs_6_ = bf16[32,1024]{1,0:T(8,128)(2,1)S(1)} collective-permute-done((bf16[32,1024]{1,0:T(8,128)(2,1)S(1)}, bf16[32,1024]{1,0:T(8,128)(2,1)S(1)}, u32[]{:S(2)}, u32[]{:S(2)}) %collective-permute-start.39) | collective-permute-done | bytes 65568 | tf_op jit(solution)/shard_map/ppermute | solution.py:193
  (199 shorter events, 92.8 us)
Async XLA Ops:
  0.0 15.1 %collective-permute-start = (bf16[128,2048]{1,0:T(8,128)(2,1)}, bf16[128,2048]{1,0:T(8,128)(2,1)S(1)}, u32[]{:S(2)}, u32[]{:S(2)}) collective-permute-start(bf16[128,2048]{1,0:T(8,128)(2,1)} %param.7), channel_id=1, source_target_pairs={{0,8},{8,16},{16,24},{24,28},{28,20},{20,12},{12,4},{4,0},{1,9},{9... | collective-permute-start | bytes 1572872 | tf_op jit(solution)/shard_map/ppermute | solution.py:81
  20.2 14.3 %collective-permute-start.2 = (bf16[128,2048]{1,0:T(8,128)(2,1)S(1)}, bf16[128,2048]{1,0:T(8,128)(2,1)S(1)}, u32[]{:S(2)}, u32[]{:S(2)}) collective-permute-start(bf16[128,2048]{1,0:T(8,128)(2,1)S(1)} %collective-permute-done), channel_id=1, source_target_pairs={{0,8},{8,16},{16,24},{24,28},{28,20},{20,12},{12,4},{4,0},{1,9},{9... | collective-permute-start | bytes 1572872 | tf_op jit(solution)/shard_map/ppermute | solution.py:81
  21.8 14.0 %collective-permute-start.3 = (bf16[128,2048]{1,0:T(8,128)(2,1)S(1)}, bf16[128,2048]{1,0:T(8,128)(2,1)S(1)}, u32[]{:S(2)}, u32[]{:S(2)}) collective-permute-start(bf16[128,2048]{1,0:T(8,128)(2,1)S(1)} %collective-permute-done.1), channel_id=1, source_target_pairs={{8,0},{16,8},{24,16},{28,24},{20,28},{12,20},{4,12},{0,4},{9,1},{1... | collective-permute-start | bytes 1572872 | tf_op jit(solution)/shard_map/ppermute | solution.py:81
  63.6 26.4 %collective-permute-start.16 = (bf16[2,128,2048]{2,1,0:T(8,128)(2,1)}, bf16[2,128,2048]{2,1,0:T(8,128)(2,1)}, u32[]{:S(2)}, u32[]{:S(2)}) collective-permute-start(bf16[2,128,2048]{2,1,0:T(8,128)(2,1)} %pad_maximum_fusion.3), channel_id=1, source_target_pairs={{0,8},{8,16},{16,24},{24,28},{28,20},{20,12},{12,4},{4,0},{1,9},{9... | collective-permute-start | bytes 3145736 | tf_op jit(solution)/shard_map/ppermute | solution.py:81
  70.9 25.9 %collective-permute-start.17 = (bf16[2,128,2048]{2,1,0:T(8,128)(2,1)}, bf16[2,128,2048]{2,1,0:T(8,128)(2,1)}, u32[]{:S(2)}, u32[]{:S(2)}) collective-permute-start(bf16[2,128,2048]{2,1,0:T(8,128)(2,1)} %pad_maximum_fusion.3), channel_id=1, source_target_pairs={{8,0},{16,8},{24,16},{28,24},{20,28},{12,20},{4,12},{0,4},{9,1},{1... | collective-permute-start | bytes 3145736 | tf_op jit(solution)/shard_map/ppermute | solution.py:81
  74.6 32.0 %collective-permute-start.9 = (bf16[128,1024]{1,0:T(8,128)(2,1)S(1)}, bf16[128,1024]{1,0:T(8,128)(2,1)S(1)}, u32[]{:S(2)}, u32[]{:S(2)}) collective-permute-start(bf16[128,1024]{1,0:T(8,128)(2,1)S(1)} %fusion.88), channel_id=1, source_target_pairs={{0,4},{1,8},{2,20},{3,24},{8,1},{9,17},{10,13},{11,29},{16,10},{17... | collective-permute-start | bytes 786440 | tf_op jit(solution)/shard_map/ppermute | solution.py:158
  77.2 22.2 %collective-permute-start.14 = (bf16[1,128,1024]{2,1,0:T(8,128)(2,1)S(1)}, bf16[1,128,1024]{2,1,0:T(8,128)(2,1)S(1)}, u32[]{:S(2)}, u32[]{:S(2)}) collective-permute-start(bf16[1,128,1024]{2,1,0:T(8,128)(2,1)S(1)} %fusion.90), channel_id=1, source_target_pairs={{0,2},{1,3},{2,0},{3,1},{4,6},{5,7},{6,4},{7,5},{8,10},{9,11},{10,... | collective-permute-start | bytes 786440 | tf_op jit(solution)/shard_map/ppermute | solution.py:101
  110.2 46.6 %collective-permute-start.24 = (bf16[2,128,2048]{2,1,0:T(8,128)(2,1)}, bf16[2,128,2048]{2,1,0:T(8,128)(2,1)}, u32[]{:S(2)}, u32[]{:S(2)}) collective-permute-start(bf16[2,128,2048]{2,1,0:T(8,128)(2,1)} %collective-permute-done.16), channel_id=1, source_target_pairs={{0,8},{8,16},{16,24},{24,28},{28,20},{20,12},{12,4},{4,0},{1,9},{9... | collective-permute-start | bytes 3145736 | tf_op jit(solution)/shard_map/ppermute | solution.py:81
  116.0 40.8 %collective-permute-start.25 = (bf16[2,128,2048]{2,1,0:T(8,128)(2,1)}, bf16[2,128,2048]{2,1,0:T(8,128)(2,1)}, u32[]{:S(2)}, u32[]{:S(2)}) collective-permute-start(bf16[2,128,2048]{2,1,0:T(8,128)(2,1)} %collective-permute-done.17), channel_id=1, source_target_pairs={{8,0},{16,8},{24,16},{28,24},{20,28},{12,20},{4,12},{0,4},{9,1},{1... | collective-permute-start | bytes 3145736 | tf_op jit(solution)/shard_map/ppermute | solution.py:81
  116.1 34.1 %collective-permute-start.18 = (bf16[128,2048]{1,0:T(8,128)(2,1)}, bf16[128,2048]{1,0:T(8,128)(2,1)S(1)}, u32[]{:S(2)}, u32[]{:S(2)}) collective-permute-start(bf16[128,2048]{1,0:T(8,128)(2,1)} %add_residual.1), channel_id=1, source_target_pairs={{0,8},{8,16},{16,24},{24,28},{28,20},{20,12},{12,4},{4,0},{1,9},{9... | collective-permute-start | bytes 1572872 | tf_op jit(solution)/shard_map/ppermute | solution.py:81
  118.1 34.2 %collective-permute-start.19 = (bf16[128,2048]{1,0:T(8,128)(2,1)}, bf16[128,2048]{1,0:T(8,128)(2,1)S(1)}, u32[]{:S(2)}, u32[]{:S(2)}) collective-permute-start(bf16[128,2048]{1,0:T(8,128)(2,1)} %add_residual.1), channel_id=1, source_target_pairs={{8,0},{16,8},{24,16},{28,24},{20,28},{12,20},{4,12},{0,4},{9,1},{1... | collective-permute-start | bytes 1572872 | tf_op jit(solution)/shard_map/ppermute | solution.py:81
  156.8 46.2 %collective-permute-start.32 = (bf16[2,128,2048]{2,1,0:T(8,128)(2,1)}, bf16[2,128,2048]{2,1,0:T(8,128)(2,1)S(1)}, u32[]{:S(2)}, u32[]{:S(2)}) collective-permute-start(bf16[2,128,2048]{2,1,0:T(8,128)(2,1)} %collective-permute-done.24), channel_id=1, source_target_pairs={{0,8},{8,16},{16,24},{24,28},{28,20},{20,12},{12,4},{4,0},{1,9},{9... | collective-permute-start | bytes 3145736 | tf_op jit(solution)/shard_map/ppermute | solution.py:81
  159.0 44.0 %collective-permute-start.33 = (bf16[2,128,2048]{2,1,0:T(8,128)(2,1)}, bf16[2,128,2048]{2,1,0:T(8,128)(2,1)S(1)}, u32[]{:S(2)}, u32[]{:S(2)}) collective-permute-start(bf16[2,128,2048]{2,1,0:T(8,128)(2,1)} %collective-permute-done.25), channel_id=1, source_target_pairs={{8,0},{16,8},{24,16},{28,24},{20,28},{12,20},{4,12},{0,4},{9,1},{1... | collective-permute-start | bytes 3145736 | tf_op jit(solution)/shard_map/ppermute | solution.py:81
  159.0 34.8 %collective-permute-start.26 = (bf16[128,2048]{1,0:T(8,128)(2,1)S(1)}, bf16[128,2048]{1,0:T(8,128)(2,1)S(1)}, u32[]{:S(2)}, u32[]{:S(2)}) collective-permute-start(bf16[128,2048]{1,0:T(8,128)(2,1)S(1)} %collective-permute-done.18), channel_id=1, source_target_pairs={{0,8},{8,16},{16,24},{24,28},{28,20},{20,12},{12,4},{4,0},{1,9},{9... | collective-permute-start | bytes 1572872 | tf_op jit(solution)/shard_map/ppermute | solution.py:81
  161.0 34.3 %collective-permute-start.27 = (bf16[128,2048]{1,0:T(8,128)(2,1)S(1)}, bf16[128,2048]{1,0:T(8,128)(2,1)S(1)}, u32[]{:S(2)}, u32[]{:S(2)}) collective-permute-start(bf16[128,2048]{1,0:T(8,128)(2,1)S(1)} %collective-permute-done.19), channel_id=1, source_target_pairs={{8,0},{16,8},{24,16},{28,24},{20,28},{12,20},{4,12},{0,4},{9,1},{1... | collective-permute-start | bytes 1572872 | tf_op jit(solution)/shard_map/ppermute | solution.py:81
  167.3 31.3 %collective-permute-start.21 = (f32[3,1,32,1024]{3,2,1,0:T(8,128)}, f32[3,1,32,1024]{3,2,1,0:T(8,128)}, u32[]{:S(2)}, u32[]{:S(2)}) collective-permute-start(f32[3,1,32,1024]{3,2,1,0:T(8,128)} %constant_dynamic-slice_fusion.2), channel_id=1, source_target_pairs={{0,2},{1,3},{2,0},{3,1},{4,6},{5,7},{6,4},{7,5},{8,10},{9,11},{10,... | collective-permute-start | bytes 1179656 | tf_op jit(solution)/shard_map/ppermute | solution.py:101
  203.1 14.9 %collective-permute-start.40 = (bf16[2,64,2048]{2,1,0:T(8,128)(2,1)S(1)}, bf16[2,64,2048]{2,1,0:T(8,128)(2,1)S(1)}, u32[]{:S(2)}, u32[]{:S(2)}) collective-permute-start(bf16[2,64,2048]{2,1,0:T(8,128)(2,1)S(1)} %slice.142), channel_id=1, source_target_pairs={{0,8},{8,16},{16,24},{24,28},{28,20},{20,12},{12,4},{4,0},{1,9},{9... | collective-permute-start | bytes 1572872 | tf_op jit(solution)/shard_map/ppermute | solution.py:81
  205.6 14.9 %collective-permute-start.41 = (bf16[2,64,2048]{2,1,0:T(8,128)(2,1)S(1)}, bf16[2,64,2048]{2,1,0:T(8,128)(2,1)S(1)}, u32[]{:S(2)}, u32[]{:S(2)}) collective-permute-start(bf16[2,64,2048]{2,1,0:T(8,128)(2,1)S(1)} %slice.143), channel_id=1, source_target_pairs={{8,0},{16,8},{24,16},{28,24},{20,28},{12,20},{4,12},{0,4},{9,1},{1... | collective-permute-start | bytes 1572872 | tf_op jit(solution)/shard_map/ppermute | solution.py:81
  205.6 23.1 %collective-permute-start.34 = (bf16[128,2048]{1,0:T(8,128)(2,1)S(1)}, bf16[128,2048]{1,0:T(8,128)(2,1)S(1)}, u32[]{:S(2)}, u32[]{:S(2)}) collective-permute-start(bf16[128,2048]{1,0:T(8,128)(2,1)S(1)} %copy-done.6), channel_id=1, source_target_pairs={{0,8},{8,16},{16,24},{24,28},{28,20},{20,12},{12,4},{4,0},{1,9},{9... | collective-permute-start | bytes 1572872 | tf_op jit(solution)/shard_map/ppermute | solution.py:81
  207.6 23.3 %collective-permute-start.35 = (bf16[128,2048]{1,0:T(8,128)(2,1)S(1)}, bf16[128,2048]{1,0:T(8,128)(2,1)S(1)}, u32[]{:S(2)}, u32[]{:S(2)}) collective-permute-start(bf16[128,2048]{1,0:T(8,128)(2,1)S(1)} %copy-done.8), channel_id=1, source_target_pairs={{8,0},{16,8},{24,16},{28,24},{20,28},{12,20},{4,12},{0,4},{9,1},{1... | collective-permute-start | bytes 1572872 | tf_op jit(solution)/shard_map/ppermute | solution.py:81
  213.8 38.7 %collective-permute-start.22 = (bf16[32,1024]{1,0:T(8,128)(2,1)S(1)}, bf16[32,1024]{1,0:T(8,128)(2,1)S(1)}, u32[]{:S(2)}, u32[]{:S(2)}) collective-permute-start(bf16[32,1024]{1,0:T(8,128)(2,1)S(1)} %get-tuple-element.82), channel_id=1, source_target_pairs={{0,4},{1,5},{2,6},{3,7},{8,0},{9,1},{10,2},{11,3},{16,8},{17,9},{1... | collective-permute-start | bytes 196616 | tf_op jit(solution)/shard_map/ppermute | solution.py:193
  217.9 38.0 %collective-permute-start.23 = (bf16[32,1024]{1,0:T(8,128)(2,1)S(1)}, bf16[32,1024]{1,0:T(8,128)(2,1)S(1)}, u32[]{:S(2)}, u32[]{:S(2)}) collective-permute-start(bf16[32,1024]{1,0:T(8,128)(2,1)S(1)} %get-tuple-element.81), channel_id=1, source_target_pairs={{0,8},{1,9},{2,10},{3,11},{8,16},{9,17},{10,18},{11,19},{16,24},{1... | collective-permute-start | bytes 196616 | tf_op jit(solution)/shard_map/ppermute | solution.py:193
  240.1 15.8 %collective-permute-start.30 = (bf16[32,1024]{1,0:T(8,128)(2,1)S(1)}, bf16[32,1024]{1,0:T(8,128)(2,1)S(1)}, u32[]{:S(2)}, u32[]{:S(2)}) collective-permute-start(bf16[32,1024]{1,0:T(8,128)(2,1)S(1)} %get-tuple-element.88), channel_id=1, source_target_pairs={{0,12},{1,13},{2,14},{3,15},{8,4},{9,5},{10,6},{11,7},{16,0},{17,1... | collective-permute-start | bytes 196616 | tf_op jit(solution)/shard_map/ppermute | solution.py:193
  240.2 20.3 %collective-permute-start.31 = (bf16[32,1024]{1,0:T(8,128)(2,1)S(1)}, bf16[32,1024]{1,0:T(8,128)(2,1)S(1)}, u32[]{:S(2)}, u32[]{:S(2)}) collective-permute-start(bf16[32,1024]{1,0:T(8,128)(2,1)S(1)} %get-tuple-element.87), channel_id=1, source_target_pairs={{0,16},{1,17},{2,18},{3,19},{8,24},{9,25},{10,26},{11,27},{16,28},... | collective-permute-start | bytes 196616 | tf_op jit(solution)/shard_map/ppermute | solution.py:193
  (52 other events, 448.0 us)

commit v7 on v6

--- a/solution.py
+++ b/solution.py
@@ -113,27 +113,38 @@
     kept = {kind: [k for k in offsets if k % per_owner == kind] for kind in classes}
     pair_sums = {kind: [] for kind in classes}
 
-    def sum_pairs():
+    done_pairs = {kind: 0 for kind in classes}
+
+    def multiply_pairs(reach):
+        made = {kind: [] for kind in classes}
         for kind in classes:
-            while len(pair_sums[kind]) < xs:
-                i = 2 * len(pair_sums[kind])
+            while done_pairs[kind] < xs:
+                i = 2 * done_pairs[kind]
                 pair = kept[kind][i : i + 2]
-                if not all(k in attn.slots for k in pair):
+                if any(abs(k) > reach for k in pair):
                     break
-                products = product([attn.slots[k] for k in pair], out_weight)
-                pair_sums[kind].append(pick(products, core) + swap(pick(products, 1 - core), 1))
-
-    while attn.hops < last:
-        ready = [list(pair_sums[kind]) for kind in classes]
-        if attn.hops:
-            sum_pairs()
-        attn.ends = tie(attn.ends, ready)
+                made[kind].append(product([attn.slots[k] for k in pair], out_weight))
+                done_pairs[kind] += 1
+        return made
+
+    def sum_cores(products):
+        return pick(products, core) + swap(pick(products, 1 - core), 1)
+
+    low = Gather(low_hidden, 0)
+    waiting = {kind: [] for kind in classes}
+    for hop in range(1, last + 1):
+        attn.ends, low.ends, waiting = tie((attn.ends, low.ends, waiting), ())
         attn.hop()
-    deep = Gather(jnp.stack([low_hidden, mid_hidden]), 1)
-    deep.ends = tie(deep.ends, attn.ends)
-    deep.hop()
-    attn.slots[last] = tie(attn.ends, [list(pair_sums[kind]) for kind in classes])
-    sum_pairs()
+        low.hop()
+        for kind in classes:
+            pair_sums[kind] += [sum_cores(products) for products in waiting[kind]]
+        waiting = multiply_pairs(hop - 1)
+    mid = Gather(mid_hidden, 0)
+    mid.ends = tie(mid.ends, attn.ends)
+    mid.hop()
+    for part in (waiting, multiply_pairs(last)):
+        for kind in classes:
+            pair_sums[kind] += [sum_cores(products) for products in part[kind]]
 
     def sum_xs(parts):
         while len(parts) > 1:
@@ -166,21 +177,19 @@
 
     top = Gather(own_top, 0)
     cuts = [0] + list(range(3, groups, 2)) + [groups]
-    chunks = [offsets[low:high] for low, high in zip(cuts, cuts[1:])]
-    deep_sums, totals, sums, owned = [], [], [], {}
-
-    def add_deep():
-        part = chunks[len(deep_sums)]
-        total = product([[piece[0] for piece in deep.slots[k]] for k in part], join_weight[0])
-        deep_sums.append(total + product([[piece[1] for piece in deep.slots[k]] for k in part], join_weight[1]))
-
-    def add_top():
-        n = len(totals)
-        total = product([top.slots[k] for k in chunks[n]], join_weight[2]) + deep_sums[n]
-        by_owner = total.reshape(len(chunks[n]), xs, 2, rows, width)
+    chunks = [offsets[low_cut:high_cut] for low_cut, high_cut in zip(cuts, cuts[1:])]
+    owned = {}
+
+    def multiply(part):
+        total = product([low.slots[k] for k in part], join_weight[0])
+        total = total + product([mid.slots[k] for k in part], join_weight[1])
+        return total + product([top.slots[k] for k in part], join_weight[2])
+
+    def add_cores(total):
+        by_owner = total.reshape(total.shape[0], xs, 2, rows, width)
         kept_part = lax.dynamic_index_in_dim(by_owner, core, 2, keepdims=False)
         sent_part = lax.dynamic_index_in_dim(by_owner, 1 - core, 2, keepdims=False)
-        totals.append(kept_part + swap(sent_part, 1))
+        return kept_part + swap(sent_part, 1)
 
     def send(part, k, flip=0):
         if not k and not flip:
@@ -192,37 +201,36 @@
         ]
         return lax.ppermute(part.astype(jnp.bfloat16), ("dp", "tensor"), moves)
 
-    def add_x():
-        n = len(sums)
-        part, half = totals[n], xs // 2
+    def add_x(part, total):
+        half = xs // 2
         while half:
-            part = part.reshape((part.shape[0], 2, half) + part.shape[-2:])
+            total = total.reshape((total.shape[0], 2, half) + total.shape[-2:])
             side = bit_of_x(half)
-            part = lax.dynamic_index_in_dim(part, side, 1, keepdims=False) + swap(
-                lax.dynamic_index_in_dim(part, 1 - side, 1, keepdims=False), 2 * half
+            total = lax.dynamic_index_in_dim(total, side, 1, keepdims=False) + swap(
+                lax.dynamic_index_in_dim(total, 1 - side, 1, keepdims=False), 2 * half
             )
             half //= 2
-        part = part.reshape(part.shape[0], rows, width)
-        sums.append(part)
-        for i, k in enumerate(chunks[n]):
-            owned[k] = [send(part[i], k)]
-
-    while top.hops < last:
-        top.ends, deep.ends = tie((top.ends, deep.ends), [deep_sums, totals, sums])
+        total = total.reshape(total.shape[0], rows, width)
+        for i, k in enumerate(part):
+            owned[k] = [send(total[i], k)]
+
+    def add_halves(part, total):
+        for flip in range(xs):
+            for i, k in enumerate(part):
+                owned.setdefault(k, []).append(send(pick(total[i], x ^ flip), k, flip))
+
+    cored = {}
+    for hop in range(1, last + 1):
+        top.ends, mid.ends, cored = tie((top.ends, mid.ends, cored), low.ends)
         top.hop()
-        if deep.hops < last:
-            deep.hop()
-        if top.hops > 1:
-            add_top()
-            if top.hops < last:
-                add_x()
-        add_deep()
-    top.slots[last] = tie(top.ends, [deep_sums, totals])
-    add_top()
-    add_x()
-    for flip in range(xs):
-        part = pick(totals[-1][0], x ^ flip)
-        owned.setdefault(last, []).append(send(part, last, flip))
+        if mid.hops < last:
+            mid.hop()
+        for n, total in cored.items():
+            add_x(chunks[n], total)
+        cored = {hop - 2: add_cores(multiply(chunks[hop - 2]))} if hop > 1 else {}
+    for n, total in cored.items():
+        add_halves(chunks[n], total)
+    add_halves(chunks[-1], add_cores(multiply(chunks[-1])))
     parts = [part for k in offsets for part in owned[k]]
     counts = [len(owned[k]) for k in offsets]
     return pl.pallas_call(

time: 268 us -> 240 us (0.90)
  waiting for transfers between devices: 148 us -> 119 us
  starting transfers between devices: 54.2 us -> 75.4 us
  local copies, waits for them, and re-layouts: 14.4 us -> 3.97 us
  other arithmetic: 11.3 us -> 4.07 us
  matrix products: 34.5 us -> 31.8 us
    ppermute x12 -> x16, waiting for transfers between devices: 114 us -> 74.4 us  [hop(): lax.ppermute(ends[0], 'dp', up)]
    ppermute x12 -> x16, starting transfers between devices: 3.3 us -> 12.1 us  [hop(): lax.ppermute(ends[1], 'dp', down)]
    ppermute x8 -> x10, starting transfers between devices: 15 us -> 23 us  [send(): return lax.ppermute(part.astype(jnp.bfloat16), ('dp', 'tensor'), moves)]
    squeeze x16 -> x7, local copies, waits for them, and re-layouts: 7.74 us -> 0.9 us  [the longest x1 0.66 us: add_x(): owned[k] = [send(total[i], k)]]
    ppermute x13 -> x12, waiting for transfers between devices: 10.3 us -> 16.8 us  [swap(): return lax.ppermute(values, 'tensor', [(t, t ^ bit) for t in range(owners)])]
    ppermute x12 -> x16, waiting for transfers between devices: 19.6 us -> 23.9 us  [hop(): lax.ppermute(ends[1], 'dp', down)]
    ppermute x8 -> x10, waiting for transfers between devices: 4.45 us -> 1.54 us  [send(): return lax.ppermute(part.astype(jnp.bfloat16), ('dp', 'tensor'), moves)]
    dot_general x16, matrix products: 34.5 us -> 31.8 us  [product(): jnp.dot(rows_in, weight, preferred_element_type=jnp.float32)]
  transfers between devices with their start and end apart: 47 -> 56, of which waited for: 27 -> 33; matrix products, arithmetic and copies ran while one was open for 20% -> 16% of each run, Pallas kernels for 0% -> 1%
where the time goes in v7:
time: 240 us; the launch traced here: 239 us
  waiting for transfers between devices  119 us (50%)
  starting transfers between devices  75.4 us (31%)
  matrix products  31.8 us (13%)
  Pallas kernels  4.46 us (2%)
  other arithmetic  4.07 us (2%)
  local copies, waits for them, and re-layouts  3.97 us (2%)
    ppermute x16, waiting for transfers between devices, hop(): lax.ppermute(ends[0], 'dp', up)  74.4 us
    dot_general x16, matrix products, product(): jnp.dot(rows_in, weight, preferred_element_type=jnp.float32)  31.8 us
    ppermute x16, starting transfers between devices, hop(): lax.ppermute(ends[0], 'dp', up)  29 us
    ppermute x16, waiting for transfers between devices, hop(): lax.ppermute(ends[1], 'dp', down)  23.9 us
    ppermute x10, starting transfers between devices, send(): return lax.ppermute(part.astype(jnp.bfloat16), ('dp', 'tensor'), moves)  23 us
    ppermute x12, waiting for transfers between devices, swap(): return lax.ppermute(values, 'tensor', [(t, t ^ bit) for t in range(owners)])  16.8 us
    ppermute x16, starting transfers between devices, hop(): lax.ppermute(ends[1], 'dp', down)  12.1 us
    ppermute x12, starting transfers between devices, swap(): return lax.ppermute(values, 'tensor', [(t, t ^ bit) for t in range(owners)])  9.58 us
  transfers between devices with their start and end apart: 56, of which 33 were waited for; matrix products, arithmetic and copies ran while one was open for 16% of the time, Pallas kernels for 1%

profile of v7, /device:TPU:0, one launch (start us, length us, event | category | flops | bytes accessed | tf_op | source)
XLA Modules:
  0.0 239.3 jit_solution(13856125594339686098)
XLA Ops:
  0.0 3.0 %collective-permute-start = (bf16[128,2048]{1,0:T(8,128)(2,1)}, bf16[128,2048]{1,0:T(8,128)(2,1)S(1)}, u32[]{:S(2)}, u32[]{:S(2)}) collective-permute-start(bf16[128,2048]{1,0:T(8,128)(2,1)} %param.7), channel_id=1, source_target_pairs={{0,8},{8,16},{16,24},{24,28},{28,20},{20,12},{12,4},{4,0},{1,9},{9... | collective-permute-start | bytes 1572872 | tf_op jit(solution)/shard_map/ppermute | solution.py:81
  5.1 10.9 %collective-permute-done = bf16[128,2048]{1,0:T(8,128)(2,1)S(1)} collective-permute-done((bf16[128,2048]{1,0:T(8,128)(2,1)}, bf16[128,2048]{1,0:T(8,128)(2,1)S(1)}, u32[]{:S(2)}, u32[]{:S(2)}) %collective-permute-start) | collective-permute-done | bytes 524320 | tf_op jit(solution)/shard_map/ppermute | solution.py:81
  18.1 8.2 %collective-permute-done.2 = bf16[128,2048]{1,0:T(8,128)(2,1)S(1)} collective-permute-done((bf16[128,2048]{1,0:T(8,128)(2,1)}, bf16[128,2048]{1,0:T(8,128)(2,1)S(1)}, u32[]{:S(2)}, u32[]{:S(2)}) %collective-permute-start.2) | collective-permute-done | bytes 524320 | tf_op jit(solution)/shard_map/ppermute | solution.py:81
  33.1 3.4 %fusion.54 = f32[256,1024]{1,0:T(8,128)S(1)} fusion(bf16[2048,1024]{1,0:T(8,128)(2,1)} %param.11, bf16[128,2048]{1,0:T(8,128)(2,1)S(1)} %collective-permute-done.1, bf16[128,2048]{1,0:T(8,128)(2,1)S(1)} %collective-permute-done), kind=kOutput, calls=%fused_computation.46 | convolution fusion | flops 1075838976 | bytes 6291456 | tf_op jit(solution)/shard_map/dot_general | solution.py:105
  36.5 5.3 %fusion.20 = f32[3,128,1024]{2,1,0:T(8,128)} fusion(bf16[3,128,2048]{2,1,0:T(8,128)(2,1)S(1)} %bitcast.187, bf16[3,2048,1024]{2,1,0:T(8,128)(2,1)} %param.12), kind=kOutput, calls=%fused_computation.20 | convolution fusion | flops 1610612736 | bytes 7340032 | tf_op jit(solution)/shard_map/dot_general | solution.py:105
  44.3 7.3 %collective-permute-done.6 = bf16[128,2048]{1,0:T(8,128)(2,1)S(1)} collective-permute-done((bf16[128,2048]{1,0:T(8,128)(2,1)S(1)}, bf16[128,2048]{1,0:T(8,128)(2,1)S(1)}, u32[]{:S(2)}, u32[]{:S(2)}) %collective-permute-start.6) | collective-permute-done | bytes 524320 | tf_op jit(solution)/shard_map/ppermute | solution.py:81
  58.3 9.4 %collective-permute-done.14 = bf16[128,2048]{1,0:T(8,128)(2,1)S(1)} collective-permute-done((bf16[128,2048]{1,0:T(8,128)(2,1)S(1)}, bf16[128,2048]{1,0:T(8,128)(2,1)S(1)}, u32[]{:S(2)}, u32[]{:S(2)}) %collective-permute-start.14) | collective-permute-done | bytes 524320 | tf_op jit(solution)/shard_map/ppermute | solution.py:81
  69.3 6.1 %collective-permute-done.8 = bf16[128,2048]{1,0:T(8,128)(2,1)S(1)} collective-permute-done((bf16[128,2048]{1,0:T(8,128)(2,1)S(1)}, bf16[128,2048]{1,0:T(8,128)(2,1)S(1)}, u32[]{:S(2)}, u32[]{:S(2)}) %collective-permute-start.8) | collective-permute-done | bytes 524320 | tf_op jit(solution)/shard_map/ppermute | solution.py:81
  94.4 4.3 %collective-permute-done.12 = bf16[1,128,1024]{2,1,0:T(8,128)(2,1)S(1)} collective-permute-done((bf16[1,128,1024]{2,1,0:T(8,128)(2,1)S(1)}, bf16[1,128,1024]{2,1,0:T(8,128)(2,1)S(1)}, u32[]{:S(2)}, u32[]{:S(2)}) %collective-permute-start.12) | collective-permute-done | bytes 262176 | tf_op jit(solution)/shard_map/ppermute | solution.py:101
  100.4 5.7 %collective-permute-done.20 = bf16[1,128,1024]{2,1,0:T(8,128)(2,1)S(1)} collective-permute-done((bf16[1,128,1024]{2,1,0:T(8,128)(2,1)S(1)}, bf16[1,128,1024]{2,1,0:T(8,128)(2,1)S(1)}, u32[]{:S(2)}, u32[]{:S(2)}) %collective-permute-start.20) | collective-permute-done | bytes 262176 | tf_op jit(solution)/shard_map/ppermute | solution.py:101
  114.7 9.2 %collective-permute-start.26 = (bf16[128,2048]{1,0:T(8,128)(2,1)}, bf16[128,2048]{1,0:T(8,128)(2,1)S(1)}, u32[]{:S(2)}, u32[]{:S(2)}) collective-permute-start(bf16[128,2048]{1,0:T(8,128)(2,1)} %add_residual.1), channel_id=1, source_target_pairs={{0,8},{8,16},{16,24},{24,28},{28,20},{20,12},{12,4},{4,0},{1,9},{9... | collective-permute-start | bytes 1572872 | tf_op jit(solution)/shard_map/ppermute | solution.py:81
  124.0 4.1 %fusion.12 = f32[3,128,1024]{2,1,0:T(8,128)S(1)} fusion(bf16[3,128,2048]{2,1,0:T(8,128)(2,1)S(1)} %bitcast.185, bf16[3,2048,1024]{2,1,0:T(8,128)(2,1)} %param.12), kind=kOutput, calls=%fused_computation.12 | convolution fusion | flops 1610612736 | bytes 7340032 | tf_op jit(solution)/shard_map/dot_general | solution.py:105
  130.2 4.0 %collective-permute-done.26 = bf16[128,2048]{1,0:T(8,128)(2,1)S(1)} collective-permute-done((bf16[128,2048]{1,0:T(8,128)(2,1)}, bf16[128,2048]{1,0:T(8,128)(2,1)S(1)}, u32[]{:S(2)}, u32[]{:S(2)}) %collective-permute-start.26) | collective-permute-done | bytes 524320 | tf_op jit(solution)/shard_map/ppermute | solution.py:81
  134.2 4.5 %collective-permute-done.27 = bf16[128,2048]{1,0:T(8,128)(2,1)S(1)} collective-permute-done((bf16[128,2048]{1,0:T(8,128)(2,1)}, bf16[128,2048]{1,0:T(8,128)(2,1)S(1)}, u32[]{:S(2)}, u32[]{:S(2)}) %collective-permute-start.27) | collective-permute-done | bytes 524320 | tf_op jit(solution)/shard_map/ppermute | solution.py:81
  138.8 4.2 %add_add_fusion = f32[3,128,1024]{2,1,0:T(8,128)S(1)} fusion(f32[3,128,1024]{2,1,0:T(8,128)S(1)} %copy-done.18, f32[3,128,1024]{2,1,0:T(8,128)S(1)} %fusion.12, bf16[3,128,2048]{2,1,0:T(8,128)(2,1)S(1)} %bitcast.186, bf16[3,2048,1024]{2,1,0:T(8,128)(2,1)} %param.12), kind=kOutput, calls=%fused_computation.39 | convolution fusion | flops 1611399168 | bytes 10485760 | tf_op jit(solution)/shard_map/dot_general | solution.py:105
  144.0 5.9 %collective-permute-done.29 = bf16[128,2048]{1,0:T(8,128)(2,1)S(1)} collective-permute-done((bf16[128,2048]{1,0:T(8,128)(2,1)S(1)}, bf16[128,2048]{1,0:T(8,128)(2,1)S(1)}, u32[]{:S(2)}, u32[]{:S(2)}) %collective-permute-start.29) | collective-permute-done | bytes 524320 | tf_op jit(solution)/shard_map/ppermute | solution.py:81
  155.3 9.3 %collective-permute-done.30 = bf16[128,2048]{1,0:T(8,128)(2,1)S(1)} collective-permute-done((bf16[128,2048]{1,0:T(8,128)(2,1)S(1)}, bf16[128,2048]{1,0:T(8,128)(2,1)S(1)}, u32[]{:S(2)}, u32[]{:S(2)}) %collective-permute-start.30) | collective-permute-done | bytes 524320 | tf_op jit(solution)/shard_map/ppermute | solution.py:81
  168.2 6.9 %collective-permute-done.32 = bf16[128,2048]{1,0:T(8,128)(2,1)S(1)} collective-permute-done((bf16[128,2048]{1,0:T(8,128)(2,1)S(1)}, bf16[128,2048]{1,0:T(8,128)(2,1)S(1)}, u32[]{:S(2)}, u32[]{:S(2)}) %collective-permute-start.32) | collective-permute-done | bytes 524320 | tf_op jit(solution)/shard_map/ppermute | solution.py:81
  187.7 3.8 %collective-permute-done.35 = f32[3,1,32,1024]{3,2,1,0:T(8,128)S(1)} collective-permute-done((f32[3,1,32,1024]{3,2,1,0:T(8,128)S(1)}, f32[3,1,32,1024]{3,2,1,0:T(8,128)S(1)}, u32[]{:S(2)}, u32[]{:S(2)}) %collective-permute-start.35) | collective-permute-done | bytes 393248 | tf_op jit(solution)/shard_map/ppermute | solution.py:101
  193.6 3.6 %collective-permute-done.38 = bf16[128,2048]{1,0:T(8,128)(2,1)S(1)} collective-permute-done((bf16[128,2048]{1,0:T(8,128)(2,1)S(1)}, bf16[128,2048]{1,0:T(8,128)(2,1)S(1)}, u32[]{:S(2)}, u32[]{:S(2)}) %collective-permute-start.38) | collective-permute-done | bytes 524320 | tf_op jit(solution)/shard_map/ppermute | solution.py:81
  209.8 3.0 %collective-permute-done.43 = f32[2,1,32,1024]{3,2,1,0:T(8,128)S(1)} collective-permute-done((f32[2,1,32,1024]{3,2,1,0:T(8,128)S(1)}, f32[2,1,32,1024]{3,2,1,0:T(8,128)S(1)}, u32[]{:S(2)}, u32[]{:S(2)}) %collective-permute-start.43) | collective-permute-done | bytes 262176 | tf_op jit(solution)/shard_map/ppermute | solution.py:101
  216.1 3.4 %collective-permute-start.49 = (bf16[32,1024]{1,0:T(8,128)(2,1)S(1)}, bf16[32,1024]{1,0:T(8,128)(2,1)S(1)}, u32[]{:S(2)}, u32[]{:S(2)}) collective-permute-start(bf16[32,1024]{1,0:T(8,128)(2,1)S(1)} %get-tuple-element.86), channel_id=1, source_target_pairs={{0,24},{1,25},{2,26},{3,27},{8,28},{9,29},{10,30},{11,31},{16,20},... | collective-permute-start | bytes 196616 | tf_op jit(solution)/shard_map/ppermute | solution.py:202
  221.2 3.4 %collective-permute-start.47 = (bf16[32,1024]{1,0:T(8,128)(2,1)S(1)}, bf16[32,1024]{1,0:T(8,128)(2,1)S(1)}, u32[]{:S(2)}, u32[]{:S(2)}) collective-permute-start(bf16[32,1024]{1,0:T(8,128)(2,1)S(1)} %get-tuple-element.88), channel_id=1, source_target_pairs={{0,20},{1,21},{2,22},{3,23},{8,12},{9,13},{10,14},{11,15},{16,4},{... | collective-permute-start | bytes 196616 | tf_op jit(solution)/shard_map/ppermute | solution.py:202
  227.0 7.1 %collective-permute-start.55 = (bf16[32,1024]{1,0:T(8,128)(2,1)S(1)}, bf16[32,1024]{1,0:T(8,128)(2,1)S(1)}, u32[]{:S(2)}, u32[]{:S(2)}) collective-permute-start(bf16[32,1024]{1,0:T(8,128)(2,1)S(1)} %get-tuple-element.83), channel_id=1, source_target_pairs={{0,30},{1,31},{2,28},{3,29},{8,22},{9,23},{10,20},{11,21},{16,14},... | collective-permute-start | bytes 196616 | tf_op jit(solution)/shard_map/ppermute | solution.py:202
  (195 shorter events, 102.6 us)
Async XLA Ops:
  0.0 15.9 %collective-permute-start = (bf16[128,2048]{1,0:T(8,128)(2,1)}, bf16[128,2048]{1,0:T(8,128)(2,1)S(1)}, u32[]{:S(2)}, u32[]{:S(2)}) collective-permute-start(bf16[128,2048]{1,0:T(8,128)(2,1)} %param.7), channel_id=1, source_target_pairs={{0,8},{8,16},{16,24},{24,28},{28,20},{20,12},{12,4},{4,0},{1,9},{9... | collective-permute-start | bytes 1572872 | tf_op jit(solution)/shard_map/ppermute | solution.py:81
  3.0 15.1 %collective-permute-start.1 = (bf16[128,2048]{1,0:T(8,128)(2,1)}, bf16[128,2048]{1,0:T(8,128)(2,1)S(1)}, u32[]{:S(2)}, u32[]{:S(2)}) collective-permute-start(bf16[128,2048]{1,0:T(8,128)(2,1)} %param.7), channel_id=1, source_target_pairs={{8,0},{16,8},{24,16},{28,24},{20,28},{12,20},{4,12},{0,4},{9,1},{1... | collective-permute-start | bytes 1572872 | tf_op jit(solution)/shard_map/ppermute | solution.py:81
  3.0 23.3 %collective-permute-start.2 = (bf16[128,2048]{1,0:T(8,128)(2,1)}, bf16[128,2048]{1,0:T(8,128)(2,1)S(1)}, u32[]{:S(2)}, u32[]{:S(2)}) collective-permute-start(bf16[128,2048]{1,0:T(8,128)(2,1)} %param.9), channel_id=1, source_target_pairs={{0,8},{8,16},{16,24},{24,28},{28,20},{20,12},{12,4},{4,0},{1,9},{9... | collective-permute-start | bytes 1572872 | tf_op jit(solution)/shard_map/ppermute | solution.py:81
  5.1 22.8 %collective-permute-start.3 = (bf16[128,2048]{1,0:T(8,128)(2,1)}, bf16[128,2048]{1,0:T(8,128)(2,1)S(1)}, u32[]{:S(2)}, u32[]{:S(2)}) collective-permute-start(bf16[128,2048]{1,0:T(8,128)(2,1)} %param.9), channel_id=1, source_target_pairs={{8,0},{16,8},{24,16},{28,24},{20,28},{12,20},{4,12},{0,4},{9,1},{1... | collective-permute-start | bytes 1572872 | tf_op jit(solution)/shard_map/ppermute | solution.py:81
  29.9 21.7 %collective-permute-start.6 = (bf16[128,2048]{1,0:T(8,128)(2,1)S(1)}, bf16[128,2048]{1,0:T(8,128)(2,1)S(1)}, u32[]{:S(2)}, u32[]{:S(2)}) collective-permute-start(bf16[128,2048]{1,0:T(8,128)(2,1)S(1)} %collective-permute-done.2), channel_id=1, source_target_pairs={{0,8},{8,16},{16,24},{24,28},{28,20},{20,12},{12,4},{4,0},{1,9},{9... | collective-permute-start | bytes 1572872 | tf_op jit(solution)/shard_map/ppermute | solution.py:81
  31.5 21.4 %collective-permute-start.7 = (bf16[128,2048]{1,0:T(8,128)(2,1)S(1)}, bf16[128,2048]{1,0:T(8,128)(2,1)S(1)}, u32[]{:S(2)}, u32[]{:S(2)}) collective-permute-start(bf16[128,2048]{1,0:T(8,128)(2,1)S(1)} %collective-permute-done.3), channel_id=1, source_target_pairs={{8,0},{16,8},{24,16},{28,24},{20,28},{12,20},{4,12},{0,4},{9,1},{1... | collective-permute-start | bytes 1572872 | tf_op jit(solution)/shard_map/ppermute | solution.py:81
  54.9 20.5 %collective-permute-start.8 = (bf16[128,2048]{1,0:T(8,128)(2,1)S(1)}, bf16[128,2048]{1,0:T(8,128)(2,1)S(1)}, u32[]{:S(2)}, u32[]{:S(2)}) collective-permute-start(bf16[128,2048]{1,0:T(8,128)(2,1)S(1)} %collective-permute-done.4), channel_id=1, source_target_pairs={{0,8},{8,16},{16,24},{24,28},{28,20},{20,12},{12,4},{4,0},{1,9},{9... | collective-permute-start | bytes 1572872 | tf_op jit(solution)/shard_map/ppermute | solution.py:81
  56.5 20.2 %collective-permute-start.9 = (bf16[128,2048]{1,0:T(8,128)(2,1)S(1)}, bf16[128,2048]{1,0:T(8,128)(2,1)S(1)}, u32[]{:S(2)}, u32[]{:S(2)}) collective-permute-start(bf16[128,2048]{1,0:T(8,128)(2,1)S(1)} %collective-permute-done.5), channel_id=1, source_target_pairs={{8,0},{16,8},{24,16},{28,24},{20,28},{12,20},{4,12},{0,4},{9,1},{1... | collective-permute-start | bytes 1572872 | tf_op jit(solution)/shard_map/ppermute | solution.py:81
  57.0 32.1 %collective-permute-start.11 = (f32[128,1024]{1,0:T(8,128)S(1)}, f32[128,1024]{1,0:T(8,128)S(1)}, u32[]{:S(2)}, u32[]{:S(2)}) collective-permute-start(f32[128,1024]{1,0:T(8,128)S(1)} %dynamic-slice_bitcast_fusion.5), channel_id=1, source_target_pairs={{0,1},{1,0},{2,3},{3,2},{4,5},{5,4},{6,7},{7,6},{8,9},{9,8},{10,11... | collective-permute-start | bytes 1572872 | tf_op jit(solution)/shard_map/ppermute | solution.py:101
  87.5 27.2 %collective-permute-start.24 = (bf16[64,2048]{1,0:T(8,128)(2,1)S(1)}, bf16[64,2048]{1,0:T(8,128)(2,1)}, u32[]{:S(2)}, u32[]{:S(2)}) collective-permute-start(bf16[64,2048]{1,0:T(8,128)(2,1)S(1)} %slice.76), channel_id=1, source_target_pairs={{0,8},{8,16},{16,24},{24,28},{28,20},{20,12},{12,4},{4,0},{1,9},{9... | collective-permute-start | bytes 786440 | tf_op jit(solution)/shard_map/ppermute | solution.py:81
  89.1 25.6 %collective-permute-start.25 = (bf16[64,2048]{1,0:T(8,128)(2,1)}, bf16[64,2048]{1,0:T(8,128)(2,1)}, u32[]{:S(2)}, u32[]{:S(2)}) collective-permute-start(bf16[64,2048]{1,0:T(8,128)(2,1)} %slice.77), channel_id=1, source_target_pairs={{8,0},{16,8},{24,16},{28,24},{20,28},{12,20},{4,12},{0,4},{9,1},{1... | collective-permute-start | bytes 786440 | tf_op jit(solution)/shard_map/ppermute | solution.py:81
  92.1 15.4 %collective-permute-start.22 = (bf16[128,2048]{1,0:T(8,128)(2,1)S(1)}, bf16[128,2048]{1,0:T(8,128)(2,1)S(1)}, u32[]{:S(2)}, u32[]{:S(2)}) collective-permute-start(bf16[128,2048]{1,0:T(8,128)(2,1)S(1)} %copy-done.2), channel_id=1, source_target_pairs={{0,8},{8,16},{16,24},{24,28},{28,20},{20,12},{12,4},{4,0},{1,9},{9... | collective-permute-start | bytes 1572872 | tf_op jit(solution)/shard_map/ppermute | solution.py:81
  93.0 16.0 %collective-permute-start.23 = (bf16[128,2048]{1,0:T(8,128)(2,1)S(1)}, bf16[128,2048]{1,0:T(8,128)(2,1)S(1)}, u32[]{:S(2)}, u32[]{:S(2)}) collective-permute-start(bf16[128,2048]{1,0:T(8,128)(2,1)S(1)} %copy-done.2), channel_id=1, source_target_pairs={{8,0},{16,8},{24,16},{28,24},{20,28},{12,20},{4,12},{0,4},{9,1},{1... | collective-permute-start | bytes 1572872 | tf_op jit(solution)/shard_map/ppermute | solution.py:81
  114.7 19.5 %collective-permute-start.26 = (bf16[128,2048]{1,0:T(8,128)(2,1)}, bf16[128,2048]{1,0:T(8,128)(2,1)S(1)}, u32[]{:S(2)}, u32[]{:S(2)}) collective-permute-start(bf16[128,2048]{1,0:T(8,128)(2,1)} %add_residual.1), channel_id=1, source_target_pairs={{0,8},{8,16},{16,24},{24,28},{28,20},{20,12},{12,4},{4,0},{1,9},{9... | collective-permute-start | bytes 1572872 | tf_op jit(solution)/shard_map/ppermute | solution.py:81
  128.1 15.8 %collective-permute-start.28 = (bf16[128,2048]{1,0:T(8,128)(2,1)S(1)}, bf16[128,2048]{1,0:T(8,128)(2,1)S(1)}, u32[]{:S(2)}, u32[]{:S(2)}) collective-permute-start(bf16[128,2048]{1,0:T(8,128)(2,1)S(1)} %collective-permute-done.22), channel_id=1, source_target_pairs={{0,8},{8,16},{16,24},{24,28},{28,20},{20,12},{12,4},{4,0},{1,9},{9... | collective-permute-start | bytes 1572872 | tf_op jit(solution)/shard_map/ppermute | solution.py:81
  130.2 19.7 %collective-permute-start.29 = (bf16[128,2048]{1,0:T(8,128)(2,1)S(1)}, bf16[128,2048]{1,0:T(8,128)(2,1)S(1)}, u32[]{:S(2)}, u32[]{:S(2)}) collective-permute-start(bf16[128,2048]{1,0:T(8,128)(2,1)S(1)} %copy-done.4), channel_id=1, source_target_pairs={{8,0},{16,8},{24,16},{28,24},{20,28},{12,20},{4,12},{0,4},{9,1},{1... | collective-permute-start | bytes 1572872 | tf_op jit(solution)/shard_map/ppermute | solution.py:81
  143.1 33.5 %collective-permute-start.34 = (f32[3,2,32,1024]{3,2,1,0:T(8,128)S(1)}, f32[3,2,32,1024]{3,2,1,0:T(8,128)S(1)}, u32[]{:S(2)}, u32[]{:S(2)}) collective-permute-start(f32[3,2,32,1024]{3,2,1,0:T(8,128)S(1)} %dynamic-slice_bitcast_fusion), channel_id=1, source_target_pairs={{0,1},{1,0},{2,3},{3,2},{4,5},{5,4},{6,7},{7,6},{8,9},{9,8},{10,11... | collective-permute-start | bytes 2359304 | tf_op jit(solution)/shard_map/ppermute | solution.py:101
  151.9 23.2 %collective-permute-start.32 = (bf16[128,2048]{1,0:T(8,128)(2,1)S(1)}, bf16[128,2048]{1,0:T(8,128)(2,1)S(1)}, u32[]{:S(2)}, u32[]{:S(2)}) collective-permute-start(bf16[128,2048]{1,0:T(8,128)(2,1)S(1)} %collective-permute-done.28), channel_id=1, source_target_pairs={{0,8},{8,16},{16,24},{24,28},{28,20},{20,12},{12,4},{4,0},{1,9},{9... | collective-permute-start | bytes 1572872 | tf_op jit(solution)/shard_map/ppermute | solution.py:81
  151.9 23.3 %collective-permute-start.33 = (bf16[128,2048]{1,0:T(8,128)(2,1)S(1)}, bf16[128,2048]{1,0:T(8,128)(2,1)S(1)}, u32[]{:S(2)}, u32[]{:S(2)}) collective-permute-start(bf16[128,2048]{1,0:T(8,128)(2,1)S(1)} %collective-permute-done.29), channel_id=1, source_target_pairs={{8,0},{16,8},{24,16},{28,24},{20,28},{12,20},{4,12},{0,4},{9,1},{1... | collective-permute-start | bytes 1572872 | tf_op jit(solution)/shard_map/ppermute | solution.py:81
  179.0 18.2 %collective-permute-start.38 = (bf16[128,2048]{1,0:T(8,128)(2,1)S(1)}, bf16[128,2048]{1,0:T(8,128)(2,1)S(1)}, u32[]{:S(2)}, u32[]{:S(2)}) collective-permute-start(bf16[128,2048]{1,0:T(8,128)(2,1)S(1)} %collective-permute-done.30), channel_id=1, source_target_pairs={{0,8},{8,16},{16,24},{24,28},{28,20},{20,12},{12,4},{4,0},{1,9},{9... | collective-permute-start | bytes 1572872 | tf_op jit(solution)/shard_map/ppermute | solution.py:81
  179.8 18.4 %collective-permute-start.39 = (bf16[128,2048]{1,0:T(8,128)(2,1)S(1)}, bf16[128,2048]{1,0:T(8,128)(2,1)S(1)}, u32[]{:S(2)}, u32[]{:S(2)}) collective-permute-start(bf16[128,2048]{1,0:T(8,128)(2,1)S(1)} %collective-permute-done.31), channel_id=1, source_target_pairs={{8,0},{16,8},{24,16},{28,24},{20,28},{12,20},{4,12},{0,4},{9,1},{1... | collective-permute-start | bytes 1572872 | tf_op jit(solution)/shard_map/ppermute | solution.py:81
  191.6 28.0 %collective-permute-start.36 = (bf16[32,1024]{1,0:T(8,128)(2,1)S(1)}, bf16[32,1024]{1,0:T(8,128)(2,1)S(1)}, u32[]{:S(2)}, u32[]{:S(2)}) collective-permute-start(bf16[32,1024]{1,0:T(8,128)(2,1)S(1)} %get-tuple-element.82), channel_id=1, source_target_pairs={{0,4},{1,5},{2,6},{3,7},{8,0},{9,1},{10,2},{11,3},{16,8},{17,9},{1... | collective-permute-start | bytes 196616 | tf_op jit(solution)/shard_map/ppermute | solution.py:202
  193.3 27.9 %collective-permute-start.37 = (bf16[32,1024]{1,0:T(8,128)(2,1)S(1)}, bf16[32,1024]{1,0:T(8,128)(2,1)S(1)}, u32[]{:S(2)}, u32[]{:S(2)}) collective-permute-start(bf16[32,1024]{1,0:T(8,128)(2,1)S(1)} %get-tuple-element.81), channel_id=1, source_target_pairs={{0,8},{1,9},{2,10},{3,11},{8,16},{9,17},{10,18},{11,19},{16,24},{1... | collective-permute-start | bytes 196616 | tf_op jit(solution)/shard_map/ppermute | solution.py:202
  219.5 15.2 %collective-permute-start.50 = (bf16[32,1024]{1,0:T(8,128)(2,1)S(1)}, bf16[32,1024]{1,0:T(8,128)(2,1)S(1)}, u32[]{:S(2)}, u32[]{:S(2)}) collective-permute-start(bf16[32,1024]{1,0:T(8,128)(2,1)S(1)} %get-tuple-element.85), channel_id=1, source_target_pairs={{0,26},{1,27},{2,24},{3,25},{8,30},{9,31},{10,28},{11,29},{16,22},... | collective-permute-start | bytes 196616 | tf_op jit(solution)/shard_map/ppermute | solution.py:202
  (54 other events, 558.9 us)

commit v8 on v7

--- a/solution.py
+++ b/solution.py
@@ -13,10 +13,9 @@
     return [2 * q for q in range(half)] + [2 * q + 1 for q in reversed(range(half))]
 
 
-def tie(values, after):
+def tie(*values):
     flat, tree = jax.tree.flatten(values)
-    held = lax.optimization_barrier(tuple(flat) + tuple(jax.tree.leaves(after)))
-    return jax.tree.unflatten(tree, held[: len(flat)])
+    return jax.tree.unflatten(tree, lax.optimization_barrier(tuple(flat)))
 
 
 def pick(values, index):
@@ -111,40 +110,37 @@
     per_owner = groups // owners
     classes = list(reversed(range(per_owner)))
     kept = {kind: [k for k in offsets if k % per_owner == kind] for kind in classes}
-    pair_sums = {kind: [] for kind in classes}
-
-    done_pairs = {kind: 0 for kind in classes}
+    kept = {kind: slots[-1:] + slots[:-1] for kind, slots in kept.items()}
+    pair_sums = {kind: [None] * xs for kind in classes}
 
     def multiply_pairs(reach):
-        made = {kind: [] for kind in classes}
+        made = {}
         for kind in classes:
-            while done_pairs[kind] < xs:
-                i = 2 * done_pairs[kind]
-                pair = kept[kind][i : i + 2]
-                if any(abs(k) > reach for k in pair):
-                    break
-                made[kind].append(product([attn.slots[k] for k in pair], out_weight))
-                done_pairs[kind] += 1
+            for i in range(xs):
+                pair = kept[kind][2 * i : 2 * i + 2]
+                if max(abs(k) for k in pair) == reach:
+                    made[kind, i] = product([attn.slots[k] for k in pair], out_weight)
         return made
 
-    def sum_cores(products):
-        return pick(products, core) + swap(pick(products, 1 - core), 1)
+    def sum_cores(made):
+        for (kind, i), products in made.items():
+            pair_sums[kind][i] = pick(products, core) + swap(pick(products, 1 - core), 1)
 
     low = Gather(low_hidden, 0)
-    waiting = {kind: [] for kind in classes}
+    mid = Gather(mid_hidden, 0)
+    made = {}
     for hop in range(1, last + 1):
-        attn.ends, low.ends, waiting = tie((attn.ends, low.ends, waiting), ())
+        attn.ends, low.ends, mid.ends, values = tie(attn.ends, low.ends, mid.ends, list(made.values()))
+        made = dict(zip(made, values))
         attn.hop()
-        low.hop()
-        for kind in classes:
-            pair_sums[kind] += [sum_cores(products) for products in waiting[kind]]
-        waiting = multiply_pairs(hop - 1)
-    mid = Gather(mid_hidden, 0)
-    mid.ends = tie(mid.ends, attn.ends)
-    mid.hop()
-    for part in (waiting, multiply_pairs(last)):
-        for kind in classes:
-            pair_sums[kind] += [sum_cores(products) for products in part[kind]]
+        (mid if hop == last else low).hop()
+        sum_cores(made)
+        made = multiply_pairs(hop - 1)
+    low.ends, attn.ends = tie(low.ends, attn.ends)
+    low.hop()
+    sum_cores(made)
+    attn.slots[last], pair_sums = tie(attn.ends, pair_sums)
+    sum_cores(multiply_pairs(last))
 
     def sum_xs(parts):
         while len(parts) > 1:
@@ -160,7 +156,7 @@
 
     arrived = []
     for kind in classes:
-        held = sum_xs(pair_sums[kind]).astype(jnp.bfloat16)
+        held, mid.ends = tie(sum_xs(pair_sums[kind]).astype(jnp.bfloat16), mid.ends)
         moves = [
             (d * owners + t, ring[(p - kept[kind][t]) % groups] * owners + d // per_owner)
             for p, d in enumerate(ring)
@@ -175,15 +171,18 @@
         name="add_residual",
     )(*arrived, residual)
 
+    own_top, low.slots[last] = tie(own_top, low.slots[last])
     top = Gather(own_top, 0)
     cuts = [0] + list(range(3, groups, 2)) + [groups]
     chunks = [offsets[low_cut:high_cut] for low_cut, high_cut in zip(cuts, cuts[1:])]
     owned = {}
 
-    def multiply(part):
+    def multiply_deep(part):
         total = product([low.slots[k] for k in part], join_weight[0])
-        total = total + product([mid.slots[k] for k in part], join_weight[1])
-        return total + product([top.slots[k] for k in part], join_weight[2])
+        return total + product([mid.slots[k] for k in part], join_weight[1])
+
+    def multiply(part, deep_sum):
+        return product([top.slots[k] for k in part], join_weight[2]) + deep_sum
 
     def add_cores(total):
         by_owner = total.reshape(total.shape[0], xs, 2, rows, width)
@@ -201,14 +200,13 @@
         ]
         return lax.ppermute(part.astype(jnp.bfloat16), ("dp", "tensor"), moves)
 
-    def add_x(part, total):
+    def add_x(part, total, dtype):
         half = xs // 2
         while half:
             total = total.reshape((total.shape[0], 2, half) + total.shape[-2:])
             side = bit_of_x(half)
-            total = lax.dynamic_index_in_dim(total, side, 1, keepdims=False) + swap(
-                lax.dynamic_index_in_dim(total, 1 - side, 1, keepdims=False), 2 * half
-            )
+            sent = lax.dynamic_index_in_dim(total, 1 - side, 1, keepdims=False).astype(dtype)
+            total = lax.dynamic_index_in_dim(total, side, 1, keepdims=False) + swap(sent, 2 * half).astype(jnp.float32)
             half //= 2
         total = total.reshape(total.shape[0], rows, width)
         for i, k in enumerate(part):
@@ -219,18 +217,22 @@
             for i, k in enumerate(part):
                 owned.setdefault(k, []).append(send(pick(total[i], x ^ flip), k, flip))
 
-    cored = {}
+    cored, deep_sum = {}, None
     for hop in range(1, last + 1):
-        top.ends, mid.ends, cored = tie((top.ends, mid.ends, cored), low.ends)
+        top.ends, mid.ends, cored, deep_sum = tie(top.ends, mid.ends, cored, deep_sum)
         top.hop()
         if mid.hops < last:
             mid.hop()
         for n, total in cored.items():
-            add_x(chunks[n], total)
-        cored = {hop - 2: add_cores(multiply(chunks[hop - 2]))} if hop > 1 else {}
+            add_x(chunks[n], total, jnp.float32 if n == 0 else jnp.bfloat16)
+        cored = {hop - 2: add_cores(multiply(chunks[hop - 2], deep_sum))} if hop > 1 else {}
+        deep_sum = multiply_deep(chunks[hop - 1])
     for n, total in cored.items():
-        add_halves(chunks[n], total)
-    add_halves(chunks[-1], add_cores(multiply(chunks[-1])))
+        add_x(chunks[n], total, jnp.bfloat16)
+    early = {k: owned[k] for part in chunks[:-2] for k in part}
+    top.slots[last], early, deep_sum = tie(top.ends, early, deep_sum)
+    owned.update(early)
+    add_halves(chunks[-1], add_cores(multiply(chunks[-1], deep_sum)))
     parts = [part for k in offsets for part in owned[k]]
     counts = [len(owned[k]) for k in offsets]
     return pl.pallas_call(

time: 240 us -> 229 us (0.954)
  starting transfers between devices: 75.4 us -> 68.6 us
  waiting for transfers between devices: 119 us -> 115 us
    ppermute x16, waiting for transfers between devices: 23.9 us -> 13.3 us  [hop(): lax.ppermute(ends[1], 'dp', down)]
    ppermute x2, starting transfers between devices: 1.77 us -> 12.3 us  [local(): arrived.append(lax.ppermute(held, ('dp', 'tensor'), moves))]
    ppermute x16, waiting for transfers between devices: 74.4 us -> 84.9 us  [hop(): lax.ppermute(ends[0], 'dp', up)]
    ppermute x12 -> x13, waiting for transfers between devices: 16.8 us -> 7.52 us  [swap(): return lax.ppermute(values, 'tensor', [(t, t ^ bit) for t in range(owners)])]
    ppermute x10 -> x8, starting transfers between devices: 23 us -> 14.4 us  [send(): return lax.ppermute(part.astype(jnp.bfloat16), ('dp', 'tensor'), moves)]
    ppermute x16, starting transfers between devices: 29 us -> 20.9 us  [hop(): lax.ppermute(ends[0], 'dp', up)]
    ppermute x10 -> x8, waiting for transfers between devices: 1.54 us -> 7.54 us  [send(): return lax.ppermute(part.astype(jnp.bfloat16), ('dp', 'tensor'), moves)]
    ppermute x12 -> x13, starting transfers between devices: 9.58 us -> 6.69 us  [swap(): return lax.ppermute(values, 'tensor', [(t, t ^ bit) for t in range(owners)])]
  transfers between devices with their start and end apart: 56 -> 55, of which waited for: 33 -> 33; matrix products, arithmetic and copies ran while one was open for 16% -> 17% of each run, Pallas kernels for 1% -> 1%
where the time goes in v8:
time: 229 us
  waiting for transfers between devices  115 us (50%)
  starting transfers between devices  68.6 us (30%)
  matrix products  33.8 us (15%)
  Pallas kernels  4.41 us (2%)
  other arithmetic  4.1 us (2%)
  local copies, waits for them, and re-layouts  2.72 us (1%)
    ppermute x16, waiting for transfers between devices, hop(): lax.ppermute(ends[0], 'dp', up)  84.9 us
    dot_general x16, matrix products, product(): jnp.dot(rows_in, weight, preferred_element_type=jnp.float32)  33.8 us
    ppermute x16, starting transfers between devices, hop(): lax.ppermute(ends[0], 'dp', up)  20.9 us
    ppermute x8, starting transfers between devices, send(): return lax.ppermute(part.astype(jnp.bfloat16), ('dp', 'tensor'), moves)  14.4 us
    ppermute x16, starting transfers between devices, hop(): lax.ppermute(ends[1], 'dp', down)  14.3 us
    ppermute x16, waiting for transfers between devices, hop(): lax.ppermute(ends[1], 'dp', down)  13.3 us
    ppermute x2, starting transfers between devices, local(): arrived.append(lax.ppermute(held, ('dp', 'tensor'), moves))  12.3 us
    ppermute x8, waiting for transfers between devices, send(): return lax.ppermute(part.astype(jnp.bfloat16), ('dp', 'tensor'), moves)  7.54 us
  transfers between devices with their start and end apart: 55, of which 33 were waited for; matrix products, arithmetic and copies ran while one was open for 17% of the time, Pallas kernels for 1%

profile of v8, /device:TPU:0, one launch (start us, length us, event | category | flops | bytes accessed | tf_op | source)
XLA Modules:
  0.0 229.1 jit_solution(6520256651602502572)
XLA Ops:
  0.0 3.0 %collective-permute-start = (bf16[128,2048]{1,0:T(8,128)(2,1)}, bf16[128,2048]{1,0:T(8,128)(2,1)S(1)}, u32[]{:S(2)}, u32[]{:S(2)}) collective-permute-start(bf16[128,2048]{1,0:T(8,128)(2,1)} %param.7), channel_id=1, source_target_pairs={{0,8},{8,16},{16,24},{24,28},{28,20},{20,12},{12,4},{4,0},{1,9},{9... | collective-permute-start | bytes 1572872 | tf_op jit(solution)/shard_map/ppermute | solution.py:80
  5.1 10.9 %collective-permute-done = bf16[128,2048]{1,0:T(8,128)(2,1)S(1)} collective-permute-done((bf16[128,2048]{1,0:T(8,128)(2,1)}, bf16[128,2048]{1,0:T(8,128)(2,1)S(1)}, u32[]{:S(2)}, u32[]{:S(2)}) %collective-permute-start) | collective-permute-done | bytes 524320 | tf_op jit(solution)/shard_map/ppermute | solution.py:80
  18.1 8.2 %collective-permute-done.2 = bf16[128,2048]{1,0:T(8,128)(2,1)S(1)} collective-permute-done((bf16[128,2048]{1,0:T(8,128)(2,1)}, bf16[128,2048]{1,0:T(8,128)(2,1)S(1)}, u32[]{:S(2)}, u32[]{:S(2)}) %collective-permute-start.2) | collective-permute-done | bytes 524320 | tf_op jit(solution)/shard_map/ppermute | solution.py:80
  31.9 10.9 %collective-permute-done.4 = bf16[128,2048]{1,0:T(8,128)(2,1)} collective-permute-done((bf16[128,2048]{1,0:T(8,128)(2,1)S(1)}, bf16[128,2048]{1,0:T(8,128)(2,1)}, u32[]{:S(2)}, u32[]{:S(2)}) %collective-permute-start.4) | collective-permute-done | bytes 524320 | tf_op jit(solution)/shard_map/ppermute | solution.py:80
  44.4 7.2 %collective-permute-done.6 = bf16[128,2048]{1,0:T(8,128)(2,1)S(1)} collective-permute-done((bf16[128,2048]{1,0:T(8,128)(2,1)S(1)}, bf16[128,2048]{1,0:T(8,128)(2,1)S(1)}, u32[]{:S(2)}, u32[]{:S(2)}) %collective-permute-start.6) | collective-permute-done | bytes 524320 | tf_op jit(solution)/shard_map/ppermute | solution.py:80
  58.4 3.8 %fusion.63 = f32[256,1024]{1,0:T(8,128)S(1)} fusion(bf16[2048,1024]{1,0:T(8,128)(2,1)} %param.11, bf16[128,2048]{1,0:T(8,128)(2,1)} %collective-permute-done.5, bf16[128,2048]{1,0:T(8,128)(2,1)} %collective-permute-done.4), kind=kOutput, calls=%fused_computation.48 | convolution fusion | flops 1075838976 | bytes 6291456 | tf_op jit(solution)/shard_map/dot_general | solution.py:104
  62.2 5.8 %collective-permute-done.8 = bf16[128,2048]{1,0:T(8,128)(2,1)S(1)} collective-permute-done((bf16[128,2048]{1,0:T(8,128)(2,1)}, bf16[128,2048]{1,0:T(8,128)(2,1)S(1)}, u32[]{:S(2)}, u32[]{:S(2)}) %collective-permute-start.8) | collective-permute-done | bytes 524320 | tf_op jit(solution)/shard_map/ppermute | solution.py:80
  72.5 3.2 %collective-permute-done.10 = bf16[128,2048]{1,0:T(8,128)(2,1)S(1)} collective-permute-done((bf16[128,2048]{1,0:T(8,128)(2,1)S(1)}, bf16[128,2048]{1,0:T(8,128)(2,1)S(1)}, u32[]{:S(2)}, u32[]{:S(2)}) %collective-permute-start.10) | collective-permute-done | bytes 524320 | tf_op jit(solution)/shard_map/ppermute | solution.py:80
  75.7 2.7 %collective-permute-done.11 = bf16[128,2048]{1,0:T(8,128)(2,1)S(1)} collective-permute-done((bf16[128,2048]{1,0:T(8,128)(2,1)S(1)}, bf16[128,2048]{1,0:T(8,128)(2,1)S(1)}, u32[]{:S(2)}, u32[]{:S(2)}) %collective-permute-start.11) | collective-permute-done | bytes 524320 | tf_op jit(solution)/shard_map/ppermute | solution.py:80
  80.8 4.9 %collective-permute-done.12 = bf16[64,2048]{1,0:T(8,128)(2,1)S(1)} collective-permute-done((bf16[64,2048]{1,0:T(8,128)(2,1)S(1)}, bf16[64,2048]{1,0:T(8,128)(2,1)S(1)}, u32[]{:S(2)}, u32[]{:S(2)}) %collective-permute-start.12) | collective-permute-done | bytes 262176 | tf_op jit(solution)/shard_map/ppermute | solution.py:80
  93.6 4.6 %collective-permute-done.18 = bf16[128,2048]{1,0:T(8,128)(2,1)S(1)} collective-permute-done((bf16[128,2048]{1,0:T(8,128)(2,1)S(1)}, bf16[128,2048]{1,0:T(8,128)(2,1)S(1)}, u32[]{:S(2)}, u32[]{:S(2)}) %collective-permute-start.18) | collective-permute-done | bytes 524320 | tf_op jit(solution)/shard_map/ppermute | solution.py:80
  101.2 3.6 %collective-permute-done.17 = bf16[1,128,1024]{2,1,0:T(8,128)(2,1)S(1)} collective-permute-done((bf16[1,128,1024]{2,1,0:T(8,128)(2,1)S(1)}, bf16[1,128,1024]{2,1,0:T(8,128)(2,1)S(1)}, u32[]{:S(2)}, u32[]{:S(2)}) %collective-permute-start.17) | collective-permute-done | bytes 262176 | tf_op jit(solution)/shard_map/ppermute | solution.py:100
  107.8 10.1 %collective-permute-start.23 = (bf16[128,1024]{1,0:T(8,128)(2,1)S(1)}, bf16[128,1024]{1,0:T(8,128)(2,1)}, u32[]{:S(2)}, u32[]{:S(2)}) collective-permute-start(bf16[128,1024]{1,0:T(8,128)(2,1)S(1)} %fusion.95), channel_id=1, source_target_pairs={{0,28},{1,0},{2,12},{3,16},{8,21},{9,9},{10,5},{11,25},{16,14},{17... | collective-permute-start | bytes 786440 | tf_op jit(solution)/shard_map/ppermute | solution.py:165
  117.9 5.1 %fusion.12 = f32[3,128,1024]{2,1,0:T(8,128)} fusion(bf16[3,128,2048]{2,1,0:T(8,128)(2,1)S(1)} %bitcast.173, bf16[3,2048,1024]{2,1,0:T(8,128)(2,1)} %param.12), kind=kOutput, calls=%fused_computation.12 | convolution fusion | flops 1610612736 | bytes 7340032 | tf_op jit(solution)/shard_map/dot_general | solution.py:104
  128.8 4.5 %fusion.36 = f32[3,128,1024]{2,1,0:T(8,128)S(1)} fusion(f32[3,128,1024]{2,1,0:T(8,128)} %fusion.12, bf16[3,128,2048]{2,1,0:T(8,128)(2,1)S(1)} %bitcast.170, bf16[3,2048,1024]{2,1,0:T(8,128)(2,1)} %param.12), kind=kOutput, calls=%fused_computation.39 | convolution fusion | flops 1611005952 | bytes 8912896 | tf_op jit(solution)/shard_map/dot_general | solution.py:104
  135.4 3.2 %fusion.22 = f32[128,1024]{1,0:T(8,128)S(1)} fusion(bf16[3,2048,1024]{2,1,0:T(8,128)(2,1)} %param.12, bf16[64,2048]{1,0:T(8,128)(2,1)} %collective-permute-done.25, bf16[64,2048]{1,0:T(8,128)(2,1)} %collective-permute-done.24), kind=kOutput, calls=%fused_computation.22 | convolution fusion | flops 537919488 | bytes 5242880 | tf_op jit(solution)/shard_map/dot_general | solution.py:104
  138.6 3.0 %collective-permute-done.28 = bf16[128,2048]{1,0:T(8,128)(2,1)S(1)} collective-permute-done((bf16[128,2048]{1,0:T(8,128)(2,1)S(1)}, bf16[128,2048]{1,0:T(8,128)(2,1)S(1)}, u32[]{:S(2)}, u32[]{:S(2)}) %collective-permute-start.28) | collective-permute-done | bytes 524320 | tf_op jit(solution)/shard_map/ppermute | solution.py:80
  141.7 3.6 %fusion.10 = f32[2,128,1024]{2,1,0:T(8,128)S(1)} fusion(bf16[2,128,2048]{2,1,0:T(8,128)(2,1)S(1)} %bitcast.179, bf16[3,2048,1024]{2,1,0:T(8,128)(2,1)} %param.12), kind=kOutput, calls=%fused_computation.10 | convolution fusion | flops 1073741824 | bytes 6291456 | tf_op jit(solution)/shard_map/dot_general | solution.py:104
  145.4 4.9 %collective-permute-done.26 = bf16[128,2048]{1,0:T(8,128)(2,1)S(1)} collective-permute-done((bf16[128,2048]{1,0:T(8,128)(2,1)S(1)}, bf16[128,2048]{1,0:T(8,128)(2,1)S(1)}, u32[]{:S(2)}, u32[]{:S(2)}) %collective-permute-start.26) | collective-permute-done | bytes 524320 | tf_op jit(solution)/shard_map/ppermute | solution.py:80
  158.0 7.2 %collective-permute-done.32 = bf16[128,2048]{1,0:T(8,128)(2,1)S(1)} collective-permute-done((bf16[128,2048]{1,0:T(8,128)(2,1)S(1)}, bf16[128,2048]{1,0:T(8,128)(2,1)S(1)}, u32[]{:S(2)}, u32[]{:S(2)}) %collective-permute-start.32) | collective-permute-done | bytes 524320 | tf_op jit(solution)/shard_map/ppermute | solution.py:80
  166.8 7.1 %collective-permute-done.30 = bf16[128,2048]{1,0:T(8,128)(2,1)S(1)} collective-permute-done((bf16[128,2048]{1,0:T(8,128)(2,1)S(1)}, bf16[128,2048]{1,0:T(8,128)(2,1)S(1)}, u32[]{:S(2)}, u32[]{:S(2)}) %collective-permute-start.30) | collective-permute-done | bytes 524320 | tf_op jit(solution)/shard_map/ppermute | solution.py:80
  189.2 7.0 %collective-permute-done.35 = bf16[128,2048]{1,0:T(8,128)(2,1)S(1)} collective-permute-done((bf16[128,2048]{1,0:T(8,128)(2,1)S(1)}, bf16[128,2048]{1,0:T(8,128)(2,1)S(1)}, u32[]{:S(2)}, u32[]{:S(2)}) %collective-permute-start.35) | collective-permute-done | bytes 524320 | tf_op jit(solution)/shard_map/ppermute | solution.py:80
  215.5 3.0 %collective-permute-start.54 = (bf16[32,1024]{1,0:T(8,128)(2,1)S(1)}, bf16[32,1024]{1,0:T(8,128)(2,1)S(1)}, u32[]{:S(2)}, u32[]{:S(2)}) collective-permute-start(bf16[32,1024]{1,0:T(8,128)(2,1)S(1)} %get-tuple-element.149), channel_id=1, source_target_pairs={{0,30},{1,31},{2,28},{3,29},{8,22},{9,23},{10,20},{11,21},{16,14},... | collective-permute-start | bytes 196616 | tf_op jit(solution)/shard_map/ppermute | solution.py:201
  218.6 3.8 %collective-permute-start.51 = (bf16[32,1024]{1,0:T(8,128)(2,1)S(1)}, bf16[32,1024]{1,0:T(8,128)(2,1)S(1)}, u32[]{:S(2)}, u32[]{:S(2)}) collective-permute-start(bf16[32,1024]{1,0:T(8,128)(2,1)S(1)} %get-tuple-element.151), channel_id=1, source_target_pairs={{0,24},{1,25},{2,26},{3,27},{8,28},{9,29},{10,30},{11,31},{16,20},... | collective-permute-start | bytes 196616 | tf_op jit(solution)/shard_map/ppermute | solution.py:201
  (200 shorter events, 96.9 us)
Async XLA Ops:
  0.0 15.9 %collective-permute-start = (bf16[128,2048]{1,0:T(8,128)(2,1)}, bf16[128,2048]{1,0:T(8,128)(2,1)S(1)}, u32[]{:S(2)}, u32[]{:S(2)}) collective-permute-start(bf16[128,2048]{1,0:T(8,128)(2,1)} %param.7), channel_id=1, source_target_pairs={{0,8},{8,16},{16,24},{24,28},{28,20},{20,12},{12,4},{4,0},{1,9},{9... | collective-permute-start | bytes 1572872 | tf_op jit(solution)/shard_map/ppermute | solution.py:80
  3.0 15.1 %collective-permute-start.1 = (bf16[128,2048]{1,0:T(8,128)(2,1)}, bf16[128,2048]{1,0:T(8,128)(2,1)S(1)}, u32[]{:S(2)}, u32[]{:S(2)}) collective-permute-start(bf16[128,2048]{1,0:T(8,128)(2,1)} %param.7), channel_id=1, source_target_pairs={{8,0},{16,8},{24,16},{28,24},{20,28},{12,20},{4,12},{0,4},{9,1},{1... | collective-permute-start | bytes 1572872 | tf_op jit(solution)/shard_map/ppermute | solution.py:80
  3.0 23.3 %collective-permute-start.2 = (bf16[128,2048]{1,0:T(8,128)(2,1)}, bf16[128,2048]{1,0:T(8,128)(2,1)S(1)}, u32[]{:S(2)}, u32[]{:S(2)}) collective-permute-start(bf16[128,2048]{1,0:T(8,128)(2,1)} %param.9), channel_id=1, source_target_pairs={{0,8},{8,16},{16,24},{24,28},{28,20},{20,12},{12,4},{4,0},{1,9},{9... | collective-permute-start | bytes 1572872 | tf_op jit(solution)/shard_map/ppermute | solution.py:80
  5.1 22.8 %collective-permute-start.3 = (bf16[128,2048]{1,0:T(8,128)(2,1)}, bf16[128,2048]{1,0:T(8,128)(2,1)S(1)}, u32[]{:S(2)}, u32[]{:S(2)}) collective-permute-start(bf16[128,2048]{1,0:T(8,128)(2,1)} %param.9), channel_id=1, source_target_pairs={{8,0},{16,8},{24,16},{28,24},{20,28},{12,20},{4,12},{0,4},{9,1},{1... | collective-permute-start | bytes 1572872 | tf_op jit(solution)/shard_map/ppermute | solution.py:80
  27.9 15.0 %collective-permute-start.4 = (bf16[128,2048]{1,0:T(8,128)(2,1)S(1)}, bf16[128,2048]{1,0:T(8,128)(2,1)}, u32[]{:S(2)}, u32[]{:S(2)}) collective-permute-start(bf16[128,2048]{1,0:T(8,128)(2,1)S(1)} %collective-permute-done), channel_id=1, source_target_pairs={{0,8},{8,16},{16,24},{24,28},{28,20},{20,12},{12,4},{4,0},{1,9},{9... | collective-permute-start | bytes 1572872 | tf_op jit(solution)/shard_map/ppermute | solution.py:80
  29.9 21.7 %collective-permute-start.6 = (bf16[128,2048]{1,0:T(8,128)(2,1)S(1)}, bf16[128,2048]{1,0:T(8,128)(2,1)S(1)}, u32[]{:S(2)}, u32[]{:S(2)}) collective-permute-start(bf16[128,2048]{1,0:T(8,128)(2,1)S(1)} %collective-permute-done.2), channel_id=1, source_target_pairs={{0,8},{8,16},{16,24},{24,28},{28,20},{20,12},{12,4},{4,0},{1,9},{9... | collective-permute-start | bytes 1572872 | tf_op jit(solution)/shard_map/ppermute | solution.py:80
  31.5 21.4 %collective-permute-start.7 = (bf16[128,2048]{1,0:T(8,128)(2,1)S(1)}, bf16[128,2048]{1,0:T(8,128)(2,1)S(1)}, u32[]{:S(2)}, u32[]{:S(2)}) collective-permute-start(bf16[128,2048]{1,0:T(8,128)(2,1)S(1)} %collective-permute-done.3), channel_id=1, source_target_pairs={{8,0},{16,8},{24,16},{28,24},{20,28},{12,20},{4,12},{0,4},{9,1},{1... | collective-permute-start | bytes 1572872 | tf_op jit(solution)/shard_map/ppermute | solution.py:80
  52.9 15.1 %collective-permute-start.8 = (bf16[128,2048]{1,0:T(8,128)(2,1)}, bf16[128,2048]{1,0:T(8,128)(2,1)S(1)}, u32[]{:S(2)}, u32[]{:S(2)}) collective-permute-start(bf16[128,2048]{1,0:T(8,128)(2,1)} %collective-permute-done.4), channel_id=1, source_target_pairs={{0,8},{8,16},{16,24},{24,28},{28,20},{20,12},{12,4},{4,0},{1,9},{9... | collective-permute-start | bytes 1572872 | tf_op jit(solution)/shard_map/ppermute | solution.py:80
  55.9 15.1 %collective-permute-start.9 = (bf16[128,2048]{1,0:T(8,128)(2,1)}, bf16[128,2048]{1,0:T(8,128)(2,1)S(1)}, u32[]{:S(2)}, u32[]{:S(2)}) collective-permute-start(bf16[128,2048]{1,0:T(8,128)(2,1)} %collective-permute-done.5), channel_id=1, source_target_pairs={{8,0},{16,8},{24,16},{28,24},{20,28},{12,20},{4,12},{0,4},{9,1},{1... | collective-permute-start | bytes 1572872 | tf_op jit(solution)/shard_map/ppermute | solution.py:80
  56.4 19.3 %collective-permute-start.10 = (bf16[128,2048]{1,0:T(8,128)(2,1)S(1)}, bf16[128,2048]{1,0:T(8,128)(2,1)S(1)}, u32[]{:S(2)}, u32[]{:S(2)}) collective-permute-start(bf16[128,2048]{1,0:T(8,128)(2,1)S(1)} %collective-permute-done.6), channel_id=1, source_target_pairs={{0,8},{8,16},{16,24},{24,28},{28,20},{20,12},{12,4},{4,0},{1,9},{9... | collective-permute-start | bytes 1572872 | tf_op jit(solution)/shard_map/ppermute | solution.py:80
  58.0 20.4 %collective-permute-start.11 = (bf16[128,2048]{1,0:T(8,128)(2,1)S(1)}, bf16[128,2048]{1,0:T(8,128)(2,1)S(1)}, u32[]{:S(2)}, u32[]{:S(2)}) collective-permute-start(bf16[128,2048]{1,0:T(8,128)(2,1)S(1)} %collective-permute-done.7), channel_id=1, source_target_pairs={{8,0},{16,8},{24,16},{28,24},{20,28},{12,20},{4,12},{0,4},{9,1},{1... | collective-permute-start | bytes 1572872 | tf_op jit(solution)/shard_map/ppermute | solution.py:80
  69.3 18.7 %collective-permute-start.16 = (f32[128,1024]{1,0:T(8,128)S(1)}, f32[128,1024]{1,0:T(8,128)S(1)}, u32[]{:S(2)}, u32[]{:S(2)}) collective-permute-start(f32[128,1024]{1,0:T(8,128)S(1)} %dynamic-slice_bitcast_fusion.4), channel_id=1, source_target_pairs={{0,1},{1,0},{2,3},{3,2},{4,5},{5,4},{6,7},{7,6},{8,9},{9,8},{10,11... | collective-permute-start | bytes 1572872 | tf_op jit(solution)/shard_map/ppermute | solution.py:100
  72.4 15.7 %collective-permute-start.15 = (f32[128,1024]{1,0:T(8,128)S(1)}, f32[128,1024]{1,0:T(8,128)S(1)}, u32[]{:S(2)}, u32[]{:S(2)}) collective-permute-start(f32[128,1024]{1,0:T(8,128)S(1)} %dynamic-slice_bitcast_fusion.5), channel_id=1, source_target_pairs={{0,1},{1,0},{2,3},{3,2},{4,5},{5,4},{6,7},{7,6},{8,9},{9,8},{10,11... | collective-permute-start | bytes 1572872 | tf_op jit(solution)/shard_map/ppermute | solution.py:100
  90.7 36.0 %collective-permute-start.24 = (bf16[64,2048]{1,0:T(8,128)(2,1)S(1)}, bf16[64,2048]{1,0:T(8,128)(2,1)}, u32[]{:S(2)}, u32[]{:S(2)}) collective-permute-start(bf16[64,2048]{1,0:T(8,128)(2,1)S(1)} %slice.78), channel_id=1, source_target_pairs={{0,8},{8,16},{16,24},{24,28},{28,20},{20,12},{12,4},{4,0},{1,9},{9... | collective-permute-start | bytes 786440 | tf_op jit(solution)/shard_map/ppermute | solution.py:80
  93.5 33.3 %collective-permute-start.25 = (bf16[64,2048]{1,0:T(8,128)(2,1)}, bf16[64,2048]{1,0:T(8,128)(2,1)}, u32[]{:S(2)}, u32[]{:S(2)}) collective-permute-start(bf16[64,2048]{1,0:T(8,128)(2,1)} %slice.79), channel_id=1, source_target_pairs={{8,0},{16,8},{24,16},{28,24},{20,28},{12,20},{4,12},{0,4},{9,1},{1... | collective-permute-start | bytes 786440 | tf_op jit(solution)/shard_map/ppermute | solution.py:80
  105.0 18.1 %collective-permute-start.20 = (bf16[128,1024]{1,0:T(8,128)(2,1)S(1)}, bf16[128,1024]{1,0:T(8,128)(2,1)}, u32[]{:S(2)}, u32[]{:S(2)}) collective-permute-start(bf16[128,1024]{1,0:T(8,128)(2,1)S(1)} %fusion.96), channel_id=1, source_target_pairs={{0,24},{1,4},{2,8},{3,20},{8,29},{9,1},{10,17},{11,13},{16,22},{17... | collective-permute-start | bytes 786440 | tf_op jit(solution)/shard_map/ppermute | solution.py:165
  107.8 16.8 %collective-permute-start.23 = (bf16[128,1024]{1,0:T(8,128)(2,1)S(1)}, bf16[128,1024]{1,0:T(8,128)(2,1)}, u32[]{:S(2)}, u32[]{:S(2)}) collective-permute-start(bf16[128,1024]{1,0:T(8,128)(2,1)S(1)} %fusion.95), channel_id=1, source_target_pairs={{0,28},{1,0},{2,12},{3,16},{8,21},{9,9},{10,5},{11,25},{16,14},{17... | collective-permute-start | bytes 786440 | tf_op jit(solution)/shard_map/ppermute | solution.py:165
  133.3 17.0 %collective-permute-start.26 = (bf16[128,2048]{1,0:T(8,128)(2,1)S(1)}, bf16[128,2048]{1,0:T(8,128)(2,1)S(1)}, u32[]{:S(2)}, u32[]{:S(2)}) collective-permute-start(bf16[128,2048]{1,0:T(8,128)(2,1)S(1)} %copy-done), channel_id=1, source_target_pairs={{0,8},{8,16},{16,24},{24,28},{28,20},{20,12},{12,4},{4,0},{1,9},{9... | collective-permute-start | bytes 1572872 | tf_op jit(solution)/shard_map/ppermute | solution.py:80
  133.4 16.9 %collective-permute-start.27 = (bf16[128,2048]{1,0:T(8,128)(2,1)S(1)}, bf16[128,2048]{1,0:T(8,128)(2,1)S(1)}, u32[]{:S(2)}, u32[]{:S(2)}) collective-permute-start(bf16[128,2048]{1,0:T(8,128)(2,1)S(1)} %copy-done), channel_id=1, source_target_pairs={{8,0},{16,8},{24,16},{28,24},{20,28},{12,20},{4,12},{0,4},{9,1},{1... | collective-permute-start | bytes 1572872 | tf_op jit(solution)/shard_map/ppermute | solution.py:80
  154.5 20.8 %collective-permute-start.34 = (f32[3,2,32,1024]{3,2,1,0:T(8,128)S(1)}, f32[3,2,32,1024]{3,2,1,0:T(8,128)S(1)}, u32[]{:S(2)}, u32[]{:S(2)}) collective-permute-start(f32[3,2,32,1024]{3,2,1,0:T(8,128)S(1)} %dynamic-slice_bitcast_fusion), channel_id=1, source_target_pairs={{0,1},{1,0},{2,3},{3,2},{4,5},{5,4},{6,7},{7,6},{8,9},{9,8},{10,11... | collective-permute-start | bytes 2359304 | tf_op jit(solution)/shard_map/ppermute | solution.py:100
  154.5 19.4 %collective-permute-start.30 = (bf16[128,2048]{1,0:T(8,128)(2,1)S(1)}, bf16[128,2048]{1,0:T(8,128)(2,1)S(1)}, u32[]{:S(2)}, u32[]{:S(2)}) collective-permute-start(bf16[128,2048]{1,0:T(8,128)(2,1)S(1)} %collective-permute-done.26), channel_id=1, source_target_pairs={{0,8},{8,16},{16,24},{24,28},{28,20},{20,12},{12,4},{4,0},{1,9},{9... | collective-permute-start | bytes 1572872 | tf_op jit(solution)/shard_map/ppermute | solution.py:80
  154.8 19.1 %collective-permute-start.31 = (bf16[128,2048]{1,0:T(8,128)(2,1)S(1)}, bf16[128,2048]{1,0:T(8,128)(2,1)S(1)}, u32[]{:S(2)}, u32[]{:S(2)}) collective-permute-start(bf16[128,2048]{1,0:T(8,128)(2,1)S(1)} %collective-permute-done.27), channel_id=1, source_target_pairs={{8,0},{16,8},{24,16},{28,24},{20,28},{12,20},{4,12},{0,4},{9,1},{1... | collective-permute-start | bytes 1572872 | tf_op jit(solution)/shard_map/ppermute | solution.py:80
  187.1 16.0 %collective-permute-start.45 = (bf16[32,1024]{1,0:T(8,128)(2,1)S(1)}, bf16[32,1024]{1,0:T(8,128)(2,1)S(1)}, u32[]{:S(2)}, u32[]{:S(2)}) collective-permute-start(bf16[32,1024]{1,0:T(8,128)(2,1)S(1)} %get-tuple-element.148), channel_id=1, source_target_pairs={{0,8},{1,9},{2,10},{3,11},{8,16},{9,17},{10,18},{11,19},{16,24},{1... | collective-permute-start | bytes 196616 | tf_op jit(solution)/shard_map/ppermute | solution.py:201
  188.5 15.2 %collective-permute-start.46 = (bf16[32,1024]{1,0:T(8,128)(2,1)S(1)}, bf16[32,1024]{1,0:T(8,128)(2,1)S(1)}, u32[]{:S(2)}, u32[]{:S(2)}) collective-permute-start(bf16[32,1024]{1,0:T(8,128)(2,1)S(1)} %get-tuple-element.147), channel_id=1, source_target_pairs={{0,4},{1,5},{2,6},{3,7},{8,0},{9,1},{10,2},{11,3},{16,8},{17,9},{1... | collective-permute-start | bytes 196616 | tf_op jit(solution)/shard_map/ppermute | solution.py:201
  (55 other events, 554.1 us)

commit v9 on v8

--- a/solution.py
+++ b/solution.py
@@ -59,22 +59,22 @@
 
 
 class Gather:
-    def __init__(self, own, axis):
+    def __init__(self, own):
         self.ring = ring_of(lax.axis_size("dp"))
-        self.axis, self.last, self.hops = axis, len(self.ring) // 2, 0
+        self.last, self.hops = len(self.ring) // 2, 0
         self.ends = [own, own]
         self.slots = {0: [own]}
+
+    def halves(self):
+        middle = self.ends[0].shape[0] // 2
+        return [self.ends[0][:middle], self.ends[1][middle:]]
 
     def hop(self):
         count = len(self.ring)
         ends = self.ends
         self.hops += 1
         if self.hops == self.last:
-            middle = ends[0].shape[self.axis] // 2
-            ends = [
-                lax.slice_in_dim(ends[0], 0, middle, axis=self.axis),
-                lax.slice_in_dim(ends[1], middle, 2 * middle, axis=self.axis),
-            ]
+            ends = self.halves()
         up = [(self.ring[q], self.ring[(q + 1) % count]) for q in range(count)]
         down = [(target, source) for source, target in up]
         self.ends = [lax.ppermute(ends[0], "dp", up), lax.ppermute(ends[1], "dp", down)]
@@ -106,41 +106,43 @@
     def bit_of_x(half):
         return (x >> (half.bit_length() - 1)) & 1
 
-    attn = Gather(attn_heads, 0)
+    attn = Gather(attn_heads)
     per_owner = groups // owners
     classes = list(reversed(range(per_owner)))
     kept = {kind: [k for k in offsets if k % per_owner == kind] for kind in classes}
     kept = {kind: slots[-1:] + slots[:-1] for kind, slots in kept.items()}
     pair_sums = {kind: [None] * xs for kind in classes}
 
-    def multiply_pairs(reach):
-        made = {}
+    parts = {}
+
+    def multiply_slots(slots):
+        products = product([attn.slots[k] for k in slots], out_weight)
+        parts.update({k: products[n] for n, k in enumerate(slots)})
+
+    def sum_cores(reach):
+        ready = []
         for kind in classes:
-            for i in range(xs):
-                pair = kept[kind][2 * i : 2 * i + 2]
-                if max(abs(k) for k in pair) == reach:
-                    made[kind, i] = product([attn.slots[k] for k in pair], out_weight)
-        return made
-
-    def sum_cores(made):
-        for (kind, i), products in made.items():
-            pair_sums[kind][i] = pick(products, core) + swap(pick(products, 1 - core), 1)
-
-    low = Gather(low_hidden, 0)
-    mid = Gather(mid_hidden, 0)
-    made = {}
+            for i, pair in enumerate(zip(kept[kind][::2], kept[kind][1::2])):
+                if pair_sums[kind][i] is None and max(abs(k) for k in pair) <= reach:
+                    ready.append((kind, i, parts[pair[0]], parts[pair[1]]))
+        came = swap(jnp.stack([jnp.where(core == 0, second, first) for _, _, first, second in ready]), 1)
+        for n, (kind, i, first, second) in enumerate(ready):
+            pair_sums[kind][i] = jnp.where(core == 0, first, second) + came[n]
+
+    low = Gather(low_hidden)
+    mid = Gather(mid_hidden)
     for hop in range(1, last + 1):
-        attn.ends, low.ends, mid.ends, values = tie(attn.ends, low.ends, mid.ends, list(made.values()))
-        made = dict(zip(made, values))
+        attn.ends, low.ends, mid.ends, parts = tie(attn.ends, low.ends, mid.ends, parts)
         attn.hop()
         (mid if hop == last else low).hop()
-        sum_cores(made)
-        made = multiply_pairs(hop - 1)
-    low.ends, attn.ends = tie(low.ends, attn.ends)
-    low.hop()
-    sum_cores(made)
+        if hop == 2:
+            multiply_slots([0])
+        if hop > 1:
+            multiply_slots([hop - 1, 1 - hop])
+    sum_cores(last - 1)
     attn.slots[last], pair_sums = tie(attn.ends, pair_sums)
-    sum_cores(multiply_pairs(last))
+    multiply_slots([last])
+    sum_cores(last)
 
     def sum_xs(parts):
         while len(parts) > 1:
@@ -156,7 +158,9 @@
 
     arrived = []
     for kind in classes:
-        held, mid.ends = tie(sum_xs(pair_sums[kind]).astype(jnp.bfloat16), mid.ends)
+        held = sum_xs(pair_sums[kind]).astype(jnp.bfloat16)
+        if kind == classes[-1]:
+            held, mid.ends = tie(held, mid.ends)
         moves = [
             (d * owners + t, ring[(p - kept[kind][t]) % groups] * owners + d // per_owner)
             for p, d in enumerate(ring)
@@ -171,18 +175,14 @@
         name="add_residual",
     )(*arrived, residual)
 
-    own_top, low.slots[last] = tie(own_top, low.slots[last])
-    top = Gather(own_top, 0)
+    own_top, mid.ends, mid.slots = tie(own_top, mid.ends, mid.slots)
+    top = Gather(own_top)
     cuts = [0] + list(range(3, groups, 2)) + [groups]
     chunks = [offsets[low_cut:high_cut] for low_cut, high_cut in zip(cuts, cuts[1:])]
     owned = {}
 
-    def multiply_deep(part):
-        total = product([low.slots[k] for k in part], join_weight[0])
-        return total + product([mid.slots[k] for k in part], join_weight[1])
-
-    def multiply(part, deep_sum):
-        return product([top.slots[k] for k in part], join_weight[2]) + deep_sum
+    def multiply(part, depth, weight):
+        return product([depth.slots[k] for k in part], weight)
 
     def add_cores(total):
         by_owner = total.reshape(total.shape[0], xs, 2, rows, width)
@@ -200,15 +200,17 @@
         ]
         return lax.ppermute(part.astype(jnp.bfloat16), ("dp", "tensor"), moves)
 
-    def add_x(part, total, dtype):
+    def add_x(total):
         half = xs // 2
         while half:
             total = total.reshape((total.shape[0], 2, half) + total.shape[-2:])
             side = bit_of_x(half)
-            sent = lax.dynamic_index_in_dim(total, 1 - side, 1, keepdims=False).astype(dtype)
+            sent = lax.dynamic_index_in_dim(total, 1 - side, 1, keepdims=False).astype(jnp.bfloat16)
             total = lax.dynamic_index_in_dim(total, side, 1, keepdims=False) + swap(sent, 2 * half).astype(jnp.float32)
             half //= 2
-        total = total.reshape(total.shape[0], rows, width)
+        return total.reshape(total.shape[0], rows, width)
+
+    def send_all(part, total):
         for i, k in enumerate(part):
             owned[k] = [send(total[i], k)]
 
@@ -217,31 +219,42 @@
             for i, k in enumerate(part):
                 owned.setdefault(k, []).append(send(pick(total[i], x ^ flip), k, flip))
 
-    cored, deep_sum = {}, None
+    def last_hops(*gathers):
+        joint = Gather(None)
+        joint.hops = last - 1
+        joint.halves = lambda: [jnp.concatenate(ends) for ends in zip(*[gather.halves() for gather in gathers])]
+        joint.hop()
+        for gather, *pieces in zip(gathers, *[jnp.split(end, len(gathers)) for end in joint.ends]):
+            gather.slots[last] = pieces
+
+    deep_sum, cored = None, None
     for hop in range(1, last + 1):
-        top.ends, mid.ends, cored, deep_sum = tie(top.ends, mid.ends, cored, deep_sum)
+        top.ends, mid.ends, low.ends, deep_sum, cored, owned = tie(
+            top.ends, mid.ends, low.ends, deep_sum, cored, owned
+        )
         top.hop()
-        if mid.hops < last:
+        if hop < last - 1:
             mid.hop()
-        for n, total in cored.items():
-            add_x(chunks[n], total, jnp.float32 if n == 0 else jnp.bfloat16)
-        cored = {hop - 2: add_cores(multiply(chunks[hop - 2], deep_sum))} if hop > 1 else {}
-        deep_sum = multiply_deep(chunks[hop - 1])
-    for n, total in cored.items():
-        add_x(chunks[n], total, jnp.bfloat16)
-    early = {k: owned[k] for part in chunks[:-2] for k in part}
-    top.slots[last], early, deep_sum = tie(top.ends, early, deep_sum)
-    owned.update(early)
-    add_halves(chunks[-1], add_cores(multiply(chunks[-1], deep_sum)))
-    parts = [part for k in offsets for part in owned[k]]
+        elif hop == last:
+            last_hops(low, mid)
+        if hop > 2:
+            send_all(chunks[hop - 3], add_x(cored))
+        if hop > 1:
+            cored = add_cores(multiply(chunks[hop - 2], top, join_weight[2]) + deep_sum)
+        if hop < last:
+            deep_sum = multiply(chunks[hop - 1], low, join_weight[0]) + multiply(chunks[hop - 1], mid, join_weight[1])
+    add_halves(chunks[-2], cored)
+    deep_sum = multiply(chunks[-1], low, join_weight[0]) + multiply(chunks[-1], mid, join_weight[1])
+    add_halves(chunks[-1], add_cores(multiply(chunks[-1], top, join_weight[2]) + deep_sum))
+    blocks = [part for k in offsets for part in owned[k]]
     counts = [len(owned[k]) for k in offsets]
     return pl.pallas_call(
         functools.partial(norm_body, offsets, counts, width),
         out_shape=jax.ShapeDtypeStruct((rows, groups * width), jnp.bfloat16),
-        in_specs=[VMEM] * (len(parts) + 1),
+        in_specs=[VMEM] * (len(blocks) + 1),
         out_specs=VMEM,
         name="norm_rows",
-    )(*parts, join_gain.reshape(1, groups * width))
+    )(*blocks, join_gain.reshape(1, groups * width))
 
 
 def solution(mesh):

time: 229 us -> 243 us (1.061)
  waiting for transfers between devices: 115 us -> 127 us
  matrix products: 33.8 us -> 27.9 us
  other arithmetic: 4.1 us -> 9.19 us
    ppermute x16 -> x15, waiting for transfers between devices: 13.3 us -> 29.5 us  [hop(): lax.ppermute(ends[1], 'dp', down)]
    ppermute x16 -> x15, waiting for transfers between devices: 84.9 us -> 73.1 us  [hop(): lax.ppermute(ends[0], 'dp', up)]
    ppermute x13 -> x10, waiting for transfers between devices: 7.52 us -> 15 us  [swap(): return lax.ppermute(values, 'tensor', [(t, t ^ bit) for t in range(owners)])]
    ppermute x8 -> x10, starting transfers between devices: 14.4 us -> 20.9 us  [send(): return lax.ppermute(part.astype(jnp.bfloat16), ('dp', 'tensor'), moves)]
    ppermute x2, starting transfers between devices: 12.3 us -> 6.25 us  [local(): arrived.append(lax.ppermute(held, ('dp', 'tensor'), moves))]
    dot_general x16 -> x17, matrix products: 33.8 us -> 27.9 us  [product(): jnp.dot(rows_in, weight, preferred_element_type=jnp.float32)]
    ppermute x16 -> x15, starting transfers between devices: 20.9 us -> 25.8 us  [hop(): lax.ppermute(ends[0], 'dp', up)]
    ppermute x13 -> x10, starting transfers between devices: 6.69 us -> 3.28 us  [swap(): return lax.ppermute(values, 'tensor', [(t, t ^ bit) for t in range(owners)])]
  transfers between devices with their start and end apart: 55 -> 52, of which waited for: 33 -> 31; matrix products, arithmetic and copies ran while one was open for 17% -> 14% of each run, Pallas kernels for 1% -> 0%
where the time goes in v9:
time: 243 us
  waiting for transfers between devices  127 us (52%)
  starting transfers between devices  69.3 us (29%)
  matrix products  27.9 us (11%)
  other arithmetic  9.19 us (4%)
  Pallas kernels  4.48 us (2%)
  local copies, waits for them, and re-layouts  4.36 us (2%)
    ppermute x15, waiting for transfers between devices, hop(): lax.ppermute(ends[0], 'dp', up)  73.1 us
    ppermute x15, waiting for transfers between devices, hop(): lax.ppermute(ends[1], 'dp', down)  29.5 us
    dot_general x17, matrix products, product(): jnp.dot(rows_in, weight, preferred_element_type=jnp.float32)  27.9 us
    ppermute x15, starting transfers between devices, hop(): lax.ppermute(ends[0], 'dp', up)  25.8 us
    ppermute x10, starting transfers between devices, send(): return lax.ppermute(part.astype(jnp.bfloat16), ('dp', 'tensor'), moves)  20.9 us
    ppermute x10, waiting for transfers between devices, swap(): return lax.ppermute(values, 'tensor', [(t, t ^ bit) for t in range(owners)])  15 us
    ppermute x15, starting transfers between devices, hop(): lax.ppermute(ends[1], 'dp', down)  13 us
    ppermute x10, waiting for transfers between devices, send(): return lax.ppermute(part.astype(jnp.bfloat16), ('dp', 'tensor'), moves)  7.44 us
  transfers between devices with their start and end apart: 52, of which 31 were waited for; matrix products, arithmetic and copies ran while one was open for 14% of the time, Pallas kernels for 0%

profile of v9, /device:TPU:0, one launch (start us, length us, event | category | flops | bytes accessed | tf_op | source)
XLA Modules:
  0.0 242.9 jit_solution(5445407971495351474)
XLA Ops:
  0.0 3.0 %collective-permute-start = (bf16[128,2048]{1,0:T(8,128)(2,1)}, bf16[128,2048]{1,0:T(8,128)(2,1)S(1)}, u32[]{:S(2)}, u32[]{:S(2)}) collective-permute-start(bf16[128,2048]{1,0:T(8,128)(2,1)} %param.7), channel_id=1, source_target_pairs={{0,8},{8,16},{16,24},{24,28},{28,20},{20,12},{12,4},{4,0},{1,9},{9... | collective-permute-start | bytes 1572872 | tf_op jit(solution)/shard_map/ppermute | solution.py:80
  5.1 3.2 %fusion.111 = f32[128,1024]{1,0:T(8,128)S(1)} fusion(bf16[128,2048]{1,0:T(8,128)(2,1)} %param.7, bf16[2048,1024]{1,0:T(8,128)(2,1)} %param.11), kind=kOutput, calls=%fused_computation.142 | convolution fusion | flops 536870912 | bytes 5242880 | tf_op jit(solution)/shard_map/dot_general | solution.py:104
  8.3 7.7 %collective-permute-done = bf16[128,2048]{1,0:T(8,128)(2,1)S(1)} collective-permute-done((bf16[128,2048]{1,0:T(8,128)(2,1)}, bf16[128,2048]{1,0:T(8,128)(2,1)S(1)}, u32[]{:S(2)}, u32[]{:S(2)}) %collective-permute-start) | collective-permute-done | bytes 524320 | tf_op jit(solution)/shard_map/ppermute | solution.py:80
  18.1 8.2 %collective-permute-done.2 = bf16[128,2048]{1,0:T(8,128)(2,1)S(1)} collective-permute-done((bf16[128,2048]{1,0:T(8,128)(2,1)}, bf16[128,2048]{1,0:T(8,128)(2,1)S(1)}, u32[]{:S(2)}, u32[]{:S(2)}) %collective-permute-start.2) | collective-permute-done | bytes 524320 | tf_op jit(solution)/shard_map/ppermute | solution.py:80
  33.3 9.4 %collective-permute-done.4 = bf16[128,2048]{1,0:T(8,128)(2,1)S(1)} collective-permute-done((bf16[128,2048]{1,0:T(8,128)(2,1)S(1)}, bf16[128,2048]{1,0:T(8,128)(2,1)S(1)}, u32[]{:S(2)}, u32[]{:S(2)}) %collective-permute-start.4) | collective-permute-done | bytes 524320 | tf_op jit(solution)/shard_map/ppermute | solution.py:80
  44.3 7.3 %collective-permute-done.6 = bf16[128,2048]{1,0:T(8,128)(2,1)S(1)} collective-permute-done((bf16[128,2048]{1,0:T(8,128)(2,1)S(1)}, bf16[128,2048]{1,0:T(8,128)(2,1)S(1)}, u32[]{:S(2)}, u32[]{:S(2)}) %collective-permute-start.6) | collective-permute-done | bytes 524320 | tf_op jit(solution)/shard_map/ppermute | solution.py:80
  58.3 9.4 %collective-permute-done.8 = bf16[128,2048]{1,0:T(8,128)(2,1)S(1)} collective-permute-done((bf16[128,2048]{1,0:T(8,128)(2,1)S(1)}, bf16[128,2048]{1,0:T(8,128)(2,1)S(1)}, u32[]{:S(2)}, u32[]{:S(2)}) %collective-permute-start.8) | collective-permute-done | bytes 524320 | tf_op jit(solution)/shard_map/ppermute | solution.py:80
  69.3 6.1 %collective-permute-done.10 = bf16[128,2048]{1,0:T(8,128)(2,1)S(1)} collective-permute-done((bf16[128,2048]{1,0:T(8,128)(2,1)S(1)}, bf16[128,2048]{1,0:T(8,128)(2,1)S(1)}, u32[]{:S(2)}, u32[]{:S(2)}) %collective-permute-start.10) | collective-permute-done | bytes 524320 | tf_op jit(solution)/shard_map/ppermute | solution.py:80
  82.4 4.9 %collective-permute-done.12 = bf16[64,2048]{1,0:T(8,128)(2,1)S(1)} collective-permute-done((bf16[64,2048]{1,0:T(8,128)(2,1)S(1)}, bf16[64,2048]{1,0:T(8,128)(2,1)S(1)}, u32[]{:S(2)}, u32[]{:S(2)}) %collective-permute-start.12) | collective-permute-done | bytes 262176 | tf_op jit(solution)/shard_map/ppermute | solution.py:80
  98.5 5.9 %collective-permute-done.15 = bf16[1,128,1024]{2,1,0:T(8,128)(2,1)S(1)} collective-permute-done((bf16[1,128,1024]{2,1,0:T(8,128)(2,1)S(1)}, bf16[1,128,1024]{2,1,0:T(8,128)(2,1)S(1)}, u32[]{:S(2)}, u32[]{:S(2)}) %collective-permute-start.15) | collective-permute-done | bytes 262176 | tf_op jit(solution)/shard_map/ppermute | solution.py:100
  105.3 3.6 %collective-permute-done.18 = bf16[1,128,1024]{2,1,0:T(8,128)(2,1)S(1)} collective-permute-done((bf16[1,128,1024]{2,1,0:T(8,128)(2,1)S(1)}, bf16[1,128,1024]{2,1,0:T(8,128)(2,1)S(1)}, u32[]{:S(2)}, u32[]{:S(2)}) %collective-permute-start.18) | collective-permute-done | bytes 262176 | tf_op jit(solution)/shard_map/ppermute | solution.py:100
  110.6 5.4 %collective-permute-start.21 = (bf16[128,1024]{1,0:T(8,128)(2,1)S(1)}, bf16[128,1024]{1,0:T(8,128)(2,1)S(1)}, u32[]{:S(2)}, u32[]{:S(2)}) collective-permute-start(bf16[128,1024]{1,0:T(8,128)(2,1)S(1)} %fusion.88), channel_id=1, source_target_pairs={{0,28},{1,0},{2,12},{3,16},{8,21},{9,9},{10,5},{11,25},{16,14},{17... | collective-permute-start | bytes 786440 | tf_op jit(solution)/shard_map/ppermute | solution.py:169
  122.8 8.2 %collective-permute-start.22 = (bf16[128,2048]{1,0:T(8,128)(2,1)}, bf16[128,2048]{1,0:T(8,128)(2,1)S(1)}, u32[]{:S(2)}, u32[]{:S(2)}) collective-permute-start(bf16[128,2048]{1,0:T(8,128)(2,1)} %add_residual.1), channel_id=1, source_target_pairs={{0,8},{8,16},{16,24},{24,28},{28,20},{20,12},{12,4},{4,0},{1,9},{9... | collective-permute-start | bytes 1572872 | tf_op jit(solution)/shard_map/ppermute | solution.py:80
  133.3 4.1 %fusion.12 = f32[3,128,1024]{2,1,0:T(8,128)S(1)} fusion(bf16[3,128,2048]{2,1,0:T(8,128)(2,1)S(1)} %bitcast.166, bf16[3,2048,1024]{2,1,0:T(8,128)(2,1)} %param.12), kind=kOutput, calls=%fused_computation.12 | convolution fusion | flops 1610612736 | bytes 7340032 | tf_op jit(solution)/shard_map/dot_general | solution.py:104
  137.4 4.2 %fusion.36 = f32[3,128,1024]{2,1,0:T(8,128)S(1)} fusion(f32[3,128,1024]{2,1,0:T(8,128)S(1)} %fusion.12, bf16[3,128,2048]{2,1,0:T(8,128)(2,1)S(1)} %bitcast.162, bf16[3,2048,1024]{2,1,0:T(8,128)(2,1)} %param.12), kind=kOutput, calls=%fused_computation.40 | convolution fusion | flops 1611005952 | bytes 8912896 | tf_op jit(solution)/shard_map/dot_general | solution.py:104
  144.4 3.4 %collective-permute-done.24 = bf16[128,2048]{1,0:T(8,128)(2,1)S(1)} collective-permute-done((bf16[128,2048]{1,0:T(8,128)(2,1)S(1)}, bf16[128,2048]{1,0:T(8,128)(2,1)S(1)}, u32[]{:S(2)}, u32[]{:S(2)}) %collective-permute-start.24) | collective-permute-done | bytes 524320 | tf_op jit(solution)/shard_map/ppermute | solution.py:80
  147.8 5.8 %collective-permute-done.25 = bf16[128,2048]{1,0:T(8,128)(2,1)S(1)} collective-permute-done((bf16[128,2048]{1,0:T(8,128)(2,1)S(1)}, bf16[128,2048]{1,0:T(8,128)(2,1)S(1)}, u32[]{:S(2)}, u32[]{:S(2)}) %collective-permute-start.25) | collective-permute-done | bytes 524320 | tf_op jit(solution)/shard_map/ppermute | solution.py:80
  163.0 15.2 %collective-permute-done.28 = bf16[128,2048]{1,0:T(8,128)(2,1)S(1)} collective-permute-done((bf16[128,2048]{1,0:T(8,128)(2,1)S(1)}, bf16[128,2048]{1,0:T(8,128)(2,1)S(1)}, u32[]{:S(2)}, u32[]{:S(2)}) %collective-permute-start.28) | collective-permute-done | bytes 524320 | tf_op jit(solution)/shard_map/ppermute | solution.py:80
  184.8 4.3 %collective-permute-done.34 = bf16[3,1,32,1024]{3,2,1,0:T(8,128)(2,1)S(1)} collective-permute-done((bf16[3,1,32,1024]{3,2,1,0:T(8,128)(2,1)S(1)}, bf16[3,1,32,1024]{3,2,1,0:T(8,128)(2,1)S(1)}, u32[]{:S(2)}, u32[]{:S(2)}) %collective-permute-start.34) | collective-permute-done | bytes 196640 | tf_op jit(solution)/shard_map/ppermute | solution.py:100
  202.0 9.9 %collective-permute-done.48 = bf16[128,2048]{1,0:T(8,128)(2,1)S(1)} collective-permute-done((bf16[128,2048]{1,0:T(8,128)(2,1)S(1)}, bf16[128,2048]{1,0:T(8,128)(2,1)S(1)}, u32[]{:S(2)}, u32[]{:S(2)}) %collective-permute-start.48) | collective-permute-done | bytes 524320 | tf_op jit(solution)/shard_map/ppermute | solution.py:80
  219.4 3.5 %collective-permute-start.41 = (bf16[32,1024]{1,0:T(8,128)(2,1)S(1)}, bf16[32,1024]{1,0:T(8,128)(2,1)S(1)}, u32[]{:S(2)}, u32[]{:S(2)}) collective-permute-start(bf16[32,1024]{1,0:T(8,128)(2,1)S(1)} %get-tuple-element.187), channel_id=1, source_target_pairs={{0,20},{1,21},{2,22},{3,23},{8,12},{9,13},{10,14},{11,15},{16,4},{... | collective-permute-start | bytes 196616 | tf_op jit(solution)/shard_map/ppermute | solution.py:201
  225.0 3.3 %collective-permute-start.43 = (bf16[32,1024]{1,0:T(8,128)(2,1)S(1)}, bf16[32,1024]{1,0:T(8,128)(2,1)S(1)}, u32[]{:S(2)}, u32[]{:S(2)}) collective-permute-start(bf16[32,1024]{1,0:T(8,128)(2,1)S(1)} %get-tuple-element.185), channel_id=1, source_target_pairs={{0,24},{1,25},{2,26},{3,27},{8,28},{9,29},{10,30},{11,31},{16,20},... | collective-permute-start | bytes 196616 | tf_op jit(solution)/shard_map/ppermute | solution.py:201
  232.0 3.3 %collective-permute-start.51 = (bf16[32,1024]{1,0:T(8,128)(2,1)S(1)}, bf16[32,1024]{1,0:T(8,128)(2,1)S(1)}, u32[]{:S(2)}, u32[]{:S(2)}) collective-permute-start(bf16[32,1024]{1,0:T(8,128)(2,1)S(1)} %get-tuple-element.182), channel_id=1, source_target_pairs={{0,30},{1,31},{2,28},{3,29},{8,22},{9,23},{10,20},{11,21},{16,14},... | collective-permute-start | bytes 196616 | tf_op jit(solution)/shard_map/ppermute | solution.py:201
  235.3 3.6 %collective-permute-done.44.refs_8_ = bf16[32,1024]{1,0:T(8,128)(2,1)S(1)} collective-permute-done((bf16[32,1024]{1,0:T(8,128)(2,1)S(1)}, bf16[32,1024]{1,0:T(8,128)(2,1)S(1)}, u32[]{:S(2)}, u32[]{:S(2)}) %collective-permute-start.44) | collective-permute-done | bytes 65568 | tf_op jit(solution)/shard_map/ppermute | solution.py:201
  (219 shorter events, 99.2 us)
Async XLA Ops:
  0.0 15.9 %collective-permute-start = (bf16[128,2048]{1,0:T(8,128)(2,1)}, bf16[128,2048]{1,0:T(8,128)(2,1)S(1)}, u32[]{:S(2)}, u32[]{:S(2)}) collective-permute-start(bf16[128,2048]{1,0:T(8,128)(2,1)} %param.7), channel_id=1, source_target_pairs={{0,8},{8,16},{16,24},{24,28},{28,20},{20,12},{12,4},{4,0},{1,9},{9... | collective-permute-start | bytes 1572872 | tf_op jit(solution)/shard_map/ppermute | solution.py:80
  3.0 15.1 %collective-permute-start.1 = (bf16[128,2048]{1,0:T(8,128)(2,1)}, bf16[128,2048]{1,0:T(8,128)(2,1)S(1)}, u32[]{:S(2)}, u32[]{:S(2)}) collective-permute-start(bf16[128,2048]{1,0:T(8,128)(2,1)} %param.7), channel_id=1, source_target_pairs={{8,0},{16,8},{24,16},{28,24},{20,28},{12,20},{4,12},{0,4},{9,1},{1... | collective-permute-start | bytes 1572872 | tf_op jit(solution)/shard_map/ppermute | solution.py:80
  3.0 23.3 %collective-permute-start.2 = (bf16[128,2048]{1,0:T(8,128)(2,1)}, bf16[128,2048]{1,0:T(8,128)(2,1)S(1)}, u32[]{:S(2)}, u32[]{:S(2)}) collective-permute-start(bf16[128,2048]{1,0:T(8,128)(2,1)} %param.9), channel_id=1, source_target_pairs={{0,8},{8,16},{16,24},{24,28},{28,20},{20,12},{12,4},{4,0},{1,9},{9... | collective-permute-start | bytes 1572872 | tf_op jit(solution)/shard_map/ppermute | solution.py:80
  5.1 22.8 %collective-permute-start.3 = (bf16[128,2048]{1,0:T(8,128)(2,1)}, bf16[128,2048]{1,0:T(8,128)(2,1)S(1)}, u32[]{:S(2)}, u32[]{:S(2)}) collective-permute-start(bf16[128,2048]{1,0:T(8,128)(2,1)} %param.9), channel_id=1, source_target_pairs={{8,0},{16,8},{24,16},{28,24},{20,28},{12,20},{4,12},{0,4},{9,1},{1... | collective-permute-start | bytes 1572872 | tf_op jit(solution)/shard_map/ppermute | solution.py:80
  29.9 21.7 %collective-permute-start.6 = (bf16[128,2048]{1,0:T(8,128)(2,1)S(1)}, bf16[128,2048]{1,0:T(8,128)(2,1)S(1)}, u32[]{:S(2)}, u32[]{:S(2)}) collective-permute-start(bf16[128,2048]{1,0:T(8,128)(2,1)S(1)} %collective-permute-done.2), channel_id=1, source_target_pairs={{0,8},{8,16},{16,24},{24,28},{28,20},{20,12},{12,4},{4,0},{1,9},{9... | collective-permute-start | bytes 1572872 | tf_op jit(solution)/shard_map/ppermute | solution.py:80
  31.5 21.4 %collective-permute-start.7 = (bf16[128,2048]{1,0:T(8,128)(2,1)S(1)}, bf16[128,2048]{1,0:T(8,128)(2,1)S(1)}, u32[]{:S(2)}, u32[]{:S(2)}) collective-permute-start(bf16[128,2048]{1,0:T(8,128)(2,1)S(1)} %collective-permute-done.3), channel_id=1, source_target_pairs={{8,0},{16,8},{24,16},{28,24},{20,28},{12,20},{4,12},{0,4},{9,1},{1... | collective-permute-start | bytes 1572872 | tf_op jit(solution)/shard_map/ppermute | solution.py:80
  54.9 20.5 %collective-permute-start.10 = (bf16[128,2048]{1,0:T(8,128)(2,1)S(1)}, bf16[128,2048]{1,0:T(8,128)(2,1)S(1)}, u32[]{:S(2)}, u32[]{:S(2)}) collective-permute-start(bf16[128,2048]{1,0:T(8,128)(2,1)S(1)} %collective-permute-done.6), channel_id=1, source_target_pairs={{0,8},{8,16},{16,24},{24,28},{28,20},{20,12},{12,4},{4,0},{1,9},{9... | collective-permute-start | bytes 1572872 | tf_op jit(solution)/shard_map/ppermute | solution.py:80
  56.5 20.2 %collective-permute-start.11 = (bf16[128,2048]{1,0:T(8,128)(2,1)S(1)}, bf16[128,2048]{1,0:T(8,128)(2,1)S(1)}, u32[]{:S(2)}, u32[]{:S(2)}) collective-permute-start(bf16[128,2048]{1,0:T(8,128)(2,1)S(1)} %collective-permute-done.7), channel_id=1, source_target_pairs={{8,0},{16,8},{24,16},{28,24},{20,28},{12,20},{4,12},{0,4},{9,1},{1... | collective-permute-start | bytes 1572872 | tf_op jit(solution)/shard_map/ppermute | solution.py:80
  93.0 16.1 %collective-permute-start.19 = (bf16[128,2048]{1,0:T(8,128)(2,1)S(1)}, bf16[128,2048]{1,0:T(8,128)(2,1)S(1)}, u32[]{:S(2)}, u32[]{:S(2)}) collective-permute-start(bf16[128,2048]{1,0:T(8,128)(2,1)S(1)} %copy-done.7), channel_id=1, source_target_pairs={{0,8},{8,16},{16,24},{24,28},{28,20},{20,12},{12,4},{4,0},{1,9},{9... | collective-permute-start | bytes 1572872 | tf_op jit(solution)/shard_map/ppermute | solution.py:80
  93.8 15.2 %collective-permute-start.20 = (bf16[128,2048]{1,0:T(8,128)(2,1)S(1)}, bf16[128,2048]{1,0:T(8,128)(2,1)S(1)}, u32[]{:S(2)}, u32[]{:S(2)}) collective-permute-start(bf16[128,2048]{1,0:T(8,128)(2,1)S(1)} %copy-done.7), channel_id=1, source_target_pairs={{8,0},{16,8},{24,16},{28,24},{20,28},{12,20},{4,12},{0,4},{9,1},{1... | collective-permute-start | bytes 1572872 | tf_op jit(solution)/shard_map/ppermute | solution.py:80
  122.8 19.4 %collective-permute-start.22 = (bf16[128,2048]{1,0:T(8,128)(2,1)}, bf16[128,2048]{1,0:T(8,128)(2,1)S(1)}, u32[]{:S(2)}, u32[]{:S(2)}) collective-permute-start(bf16[128,2048]{1,0:T(8,128)(2,1)} %add_residual.1), channel_id=1, source_target_pairs={{0,8},{8,16},{16,24},{24,28},{28,20},{20,12},{12,4},{4,0},{1,9},{9... | collective-permute-start | bytes 1572872 | tf_op jit(solution)/shard_map/ppermute | solution.py:80
  131.1 16.7 %collective-permute-start.24 = (bf16[128,2048]{1,0:T(8,128)(2,1)S(1)}, bf16[128,2048]{1,0:T(8,128)(2,1)S(1)}, u32[]{:S(2)}, u32[]{:S(2)}) collective-permute-start(bf16[128,2048]{1,0:T(8,128)(2,1)S(1)} %copy-done.16), channel_id=1, source_target_pairs={{0,8},{8,16},{16,24},{24,28},{28,20},{20,12},{12,4},{4,0},{1,9},{9... | collective-permute-start | bytes 1572872 | tf_op jit(solution)/shard_map/ppermute | solution.py:80
  133.1 20.5 %collective-permute-start.25 = (bf16[128,2048]{1,0:T(8,128)(2,1)S(1)}, bf16[128,2048]{1,0:T(8,128)(2,1)S(1)}, u32[]{:S(2)}, u32[]{:S(2)}) collective-permute-start(bf16[128,2048]{1,0:T(8,128)(2,1)S(1)} %copy-done.18), channel_id=1, source_target_pairs={{8,0},{16,8},{24,16},{28,24},{20,28},{12,20},{4,12},{0,4},{9,1},{1... | collective-permute-start | bytes 1572872 | tf_op jit(solution)/shard_map/ppermute | solution.py:80
  153.6 26.0 %collective-permute-start.26 = (bf16[128,2048]{1,0:T(8,128)(2,1)S(1)}, bf16[128,2048]{1,0:T(8,128)(2,1)S(1)}, u32[]{:S(2)}, u32[]{:S(2)}) collective-permute-start(bf16[128,2048]{1,0:T(8,128)(2,1)S(1)} %collective-permute-done.22), channel_id=1, source_target_pairs={{0,8},{8,16},{16,24},{24,28},{28,20},{20,12},{12,4},{4,0},{1,9},{9... | collective-permute-start | bytes 1572872 | tf_op jit(solution)/shard_map/ppermute | solution.py:80
  153.6 26.0 %collective-permute-start.27 = (bf16[128,2048]{1,0:T(8,128)(2,1)S(1)}, bf16[128,2048]{1,0:T(8,128)(2,1)S(1)}, u32[]{:S(2)}, u32[]{:S(2)}) collective-permute-start(bf16[128,2048]{1,0:T(8,128)(2,1)S(1)} %collective-permute-done.23), channel_id=1, source_target_pairs={{8,0},{16,8},{24,16},{28,24},{20,28},{12,20},{4,12},{0,4},{9,1},{1... | collective-permute-start | bytes 1572872 | tf_op jit(solution)/shard_map/ppermute | solution.py:80
  156.1 22.1 %collective-permute-start.28 = (bf16[128,2048]{1,0:T(8,128)(2,1)S(1)}, bf16[128,2048]{1,0:T(8,128)(2,1)S(1)}, u32[]{:S(2)}, u32[]{:S(2)}) collective-permute-start(bf16[128,2048]{1,0:T(8,128)(2,1)S(1)} %collective-permute-done.24), channel_id=1, source_target_pairs={{0,8},{8,16},{16,24},{24,28},{28,20},{20,12},{12,4},{4,0},{1,9},{9... | collective-permute-start | bytes 1572872 | tf_op jit(solution)/shard_map/ppermute | solution.py:80
  156.1 22.1 %collective-permute-start.29 = (bf16[128,2048]{1,0:T(8,128)(2,1)S(1)}, bf16[128,2048]{1,0:T(8,128)(2,1)S(1)}, u32[]{:S(2)}, u32[]{:S(2)}) collective-permute-start(bf16[128,2048]{1,0:T(8,128)(2,1)S(1)} %collective-permute-done.25), channel_id=1, source_target_pairs={{8,0},{16,8},{24,16},{28,24},{20,28},{12,20},{4,12},{0,4},{9,1},{1... | collective-permute-start | bytes 1572872 | tf_op jit(solution)/shard_map/ppermute | solution.py:80
  161.7 19.4 %collective-permute-start.30 = (f32[3,2,32,1024]{3,2,1,0:T(8,128)S(1)}, f32[3,2,32,1024]{3,2,1,0:T(8,128)S(1)}, u32[]{:S(2)}, u32[]{:S(2)}) collective-permute-start(f32[3,2,32,1024]{3,2,1,0:T(8,128)S(1)} %dynamic-slice_bitcast_fusion), channel_id=1, source_target_pairs={{0,1},{1,0},{2,3},{3,2},{4,5},{5,4},{6,7},{7,6},{8,9},{9,8},{10,11... | collective-permute-start | bytes 2359304 | tf_op jit(solution)/shard_map/ppermute | solution.py:100
  196.9 22.3 %collective-permute-start.40 = (f32[2,2,32,1024]{3,2,1,0:T(8,128)S(1)}, f32[2,2,32,1024]{3,2,1,0:T(8,128)S(1)}, u32[]{:S(2)}, u32[]{:S(2)}) collective-permute-start(f32[2,2,32,1024]{3,2,1,0:T(8,128)S(1)} %dynamic-slice_bitcast_fusion.1), channel_id=1, source_target_pairs={{0,1},{1,0},{2,3},{3,2},{4,5},{5,4},{6,7},{7,6},{8,9},{9,8},{10,11... | collective-permute-start | bytes 1572872 | tf_op jit(solution)/shard_map/ppermute | solution.py:100
  198.7 15.5 %collective-permute-start.47 = (bf16[128,2048]{1,0:T(8,128)(2,1)S(1)}, bf16[128,2048]{1,0:T(8,128)(2,1)S(1)}, u32[]{:S(2)}, u32[]{:S(2)}) collective-permute-start(bf16[128,2048]{1,0:T(8,128)(2,1)S(1)} %pad_maximum_fusion.10), channel_id=1, source_target_pairs={{0,8},{8,16},{16,24},{24,28},{28,20},{20,12},{12,4},{4,0},{1,9},{9... | collective-permute-start | bytes 1572872 | tf_op jit(solution)/shard_map/ppermute | solution.py:80
  199.3 18.1 %collective-permute-start.46 = (bf16[64,2048]{1,0:T(8,128)(2,1)S(1)}, bf16[64,2048]{1,0:T(8,128)(2,1)S(1)}, u32[]{:S(2)}, u32[]{:S(2)}) collective-permute-start(bf16[64,2048]{1,0:T(8,128)(2,1)S(1)} %slice.129), channel_id=1, source_target_pairs={{8,0},{16,8},{24,16},{28,24},{20,28},{12,20},{4,12},{0,4},{9,1},{1... | collective-permute-start | bytes 786440 | tf_op jit(solution)/shard_map/ppermute | solution.py:80
  200.9 17.5 %collective-permute-start.45 = (bf16[64,2048]{1,0:T(8,128)(2,1)S(1)}, bf16[64,2048]{1,0:T(8,128)(2,1)S(1)}, u32[]{:S(2)}, u32[]{:S(2)}) collective-permute-start(bf16[64,2048]{1,0:T(8,128)(2,1)S(1)} %slice.128), channel_id=1, source_target_pairs={{0,8},{8,16},{16,24},{24,28},{28,20},{20,12},{12,4},{4,0},{1,9},{9... | collective-permute-start | bytes 786440 | tf_op jit(solution)/shard_map/ppermute | solution.py:80
  211.9 16.4 %collective-permute-start.38 = (bf16[32,1024]{1,0:T(8,128)(2,1)S(1)}, bf16[32,1024]{1,0:T(8,128)(2,1)S(1)}, u32[]{:S(2)}, u32[]{:S(2)}) collective-permute-start(bf16[32,1024]{1,0:T(8,128)(2,1)S(1)} %get-tuple-element.189), channel_id=1, source_target_pairs={{0,12},{1,13},{2,14},{3,15},{8,4},{9,5},{10,6},{11,7},{16,0},{17,1... | collective-permute-start | bytes 196616 | tf_op jit(solution)/shard_map/ppermute | solution.py:201
  214.2 15.4 %collective-permute-start.39 = (bf16[32,1024]{1,0:T(8,128)(2,1)S(1)}, bf16[32,1024]{1,0:T(8,128)(2,1)S(1)}, u32[]{:S(2)}, u32[]{:S(2)}) collective-permute-start(bf16[32,1024]{1,0:T(8,128)(2,1)S(1)} %get-tuple-element.188), channel_id=1, source_target_pairs={{0,16},{1,17},{2,18},{3,19},{8,24},{9,25},{10,26},{11,27},{16,28},... | collective-permute-start | bytes 196616 | tf_op jit(solution)/shard_map/ppermute | solution.py:201
  (63 other events, 588.5 us)

commit v10 on v9

--- a/solution.py
+++ b/solution.py
@@ -139,11 +139,6 @@
             multiply_slots([0])
         if hop > 1:
             multiply_slots([hop - 1, 1 - hop])
-    sum_cores(last - 1)
-    attn.slots[last], pair_sums = tie(attn.ends, pair_sums)
-    multiply_slots([last])
-    sum_cores(last)
-
     def sum_xs(parts):
         while len(parts) > 1:
             half = len(parts) // 2
@@ -156,17 +151,22 @@
             ]
         return parts[0]
 
+    sum_cores(last - 1)
+    held = {kind: sum_xs(pair_sums[kind]).astype(jnp.bfloat16) for kind in classes[:-1]}
+    attn.slots[last], pair_sums, held = tie(attn.ends, pair_sums, held)
+    multiply_slots([last])
+    sum_cores(last)
+    held[classes[-1]] = sum_xs(pair_sums[classes[-1]]).astype(jnp.bfloat16)
+    held[classes[-1]], mid.ends = tie(held[classes[-1]], mid.ends)
+
     arrived = []
     for kind in classes:
-        held = sum_xs(pair_sums[kind]).astype(jnp.bfloat16)
-        if kind == classes[-1]:
-            held, mid.ends = tie(held, mid.ends)
         moves = [
             (d * owners + t, ring[(p - kept[kind][t]) % groups] * owners + d // per_owner)
             for p, d in enumerate(ring)
             for t in range(owners)
         ]
-        arrived.append(lax.ppermute(held, ("dp", "tensor"), moves))
+        arrived.append(lax.ppermute(held[kind], ("dp", "tensor"), moves))
     own_top = pl.pallas_call(
         functools.partial(top_body, groups, classes, width),
         out_shape=jax.ShapeDtypeStruct((tokens, features), jnp.bfloat16),
@@ -177,8 +177,7 @@
 
     own_top, mid.ends, mid.slots = tie(own_top, mid.ends, mid.slots)
     top = Gather(own_top)
-    cuts = [0] + list(range(3, groups, 2)) + [groups]
-    chunks = [offsets[low_cut:high_cut] for low_cut, high_cut in zip(cuts, cuts[1:])]
+    chunks = [[s, -s] for s in range(1, last)] + [[last, 0]]
     owned = {}
 
     def multiply(part, depth, weight):
@@ -227,24 +226,27 @@
         for gather, *pieces in zip(gathers, *[jnp.split(end, len(gathers)) for end in joint.ends]):
             gather.slots[last] = pieces
 
-    deep_sum, cored = None, None
+    def multiply_deep(part):
+        return multiply(part, low, join_weight[0]) + multiply(part, mid, join_weight[1])
+
+    deep_sum, cored, summed = None, None, None
     for hop in range(1, last + 1):
-        top.ends, mid.ends, low.ends, deep_sum, cored, owned = tie(
-            top.ends, mid.ends, low.ends, deep_sum, cored, owned
-        )
+        top.ends, mid.ends, low.ends, deep_sum, cored = tie(top.ends, mid.ends, low.ends, deep_sum, cored)
         top.hop()
         if hop < last - 1:
             mid.hop()
-        elif hop == last:
+        elif hop == last - 1:
             last_hops(low, mid)
-        if hop > 2:
-            send_all(chunks[hop - 3], add_x(cored))
+        if cored is not None:
+            summed = add_x(cored)
+            if hop < last:
+                send_all(chunks[hop - 3], summed)
         if hop > 1:
             cored = add_cores(multiply(chunks[hop - 2], top, join_weight[2]) + deep_sum)
-        if hop < last:
-            deep_sum = multiply(chunks[hop - 1], low, join_weight[0]) + multiply(chunks[hop - 1], mid, join_weight[1])
-    add_halves(chunks[-2], cored)
-    deep_sum = multiply(chunks[-1], low, join_weight[0]) + multiply(chunks[-1], mid, join_weight[1])
+        deep_sum = multiply_deep(chunks[hop - 1])
+    top.slots[last], deep_sum, summed = tie(top.ends, deep_sum, summed)
+    send_all(chunks[-3], summed)
+    send_all(chunks[-2], add_x(cored))
     add_halves(chunks[-1], add_cores(multiply(chunks[-1], top, join_weight[2]) + deep_sum))
     blocks = [part for k in offsets for part in owned[k]]
     counts = [len(owned[k]) for k in offsets]

time: 243 us -> 244 us (level)
  starting transfers between devices: 69.3 us -> 60.8 us
  other arithmetic: 9.19 us -> 14.2 us
  local copies, waits for them, and re-layouts: 4.36 us -> 7.97 us
    ppermute x15, waiting for transfers between devices: 73.1 us -> 80.5 us  [hop(): lax.ppermute(ends[0], 'dp', up)]
    ppermute x15, waiting for transfers between devices: 29.5 us -> 23.5 us  [hop(): lax.ppermute(ends[1], 'dp', down)]
    ppermute x10 -> x9, starting transfers between devices: 20.9 us -> 15.5 us  [send(): return lax.ppermute(part.astype(jnp.bfloat16), ('dp', 'tensor'), moves)]
    slice x9 -> x11, local copies, waits for them, and re-layouts: 0.13 us -> 2.7 us  [halves(): return [self.ends[0][:middle], self.ends[1][middle:]]]
    ppermute x10 -> x9, waiting for transfers between devices: 7.44 us -> 5.12 us  [send(): return lax.ppermute(part.astype(jnp.bfloat16), ('dp', 'tensor'), moves)]
    ppermute x10 -> x11, waiting for transfers between devices: 15 us -> 16.9 us  [swap(): return lax.ppermute(values, 'tensor', [(t, t ^ bit) for t in range(owners)])]
    concatenate x9 -> x12, other arithmetic: 5.48 us -> 6.74 us  [product(): jnp.concatenate([piece for slot in slots for piece in slot], axis=0)]
  transfers between devices with their start and end apart: 52 -> 52, of which waited for: 31 -> 32; matrix products, arithmetic and copies ran while one was open for 14% -> 17% of each run, Pallas kernels for 0% -> 0%
where the time goes in v10:
time: 244 us
  waiting for transfers between devices  127 us (52%)
  starting transfers between devices  60.8 us (25%)
  matrix products  28.9 us (12%)
  other arithmetic  14.2 us (6%)
  local copies, waits for them, and re-layouts  7.97 us (3%)
  Pallas kernels  4.44 us (2%)
    ppermute x15, waiting for transfers between devices, hop(): lax.ppermute(ends[0], 'dp', up)  80.5 us
    dot_general x17, matrix products, product(): jnp.dot(rows_in, weight, preferred_element_type=jnp.float32)  28.9 us
    ppermute x15, starting transfers between devices, hop(): lax.ppermute(ends[0], 'dp', up)  25.1 us
    ppermute x15, waiting for transfers between devices, hop(): lax.ppermute(ends[1], 'dp', down)  23.5 us
    ppermute x11, waiting for transfers between devices, swap(): return lax.ppermute(values, 'tensor', [(t, t ^ bit) for t in range(owners)])  16.9 us
    ppermute x9, starting transfers between devices, send(): return lax.ppermute(part.astype(jnp.bfloat16), ('dp', 'tensor'), moves)  15.5 us
    ppermute x15, starting transfers between devices, hop(): lax.ppermute(ends[1], 'dp', down)  11.7 us
    concatenate x12, other arithmetic, product(): jnp.concatenate([piece for slot in slots for piece in slot], axis=0)  6.74 us
  transfers between devices with their start and end apart: 52, of which 32 were waited for; matrix products, arithmetic and copies ran while one was open for 17% of the time, Pallas kernels for 0%

profile of v10, /device:TPU:0, one launch (start us, length us, event | category | flops | bytes accessed | tf_op | source)
XLA Modules:
  0.0 244.0 jit_solution(15713434145576810497)
XLA Ops:
  0.0 3.0 %collective-permute-start = (bf16[128,2048]{1,0:T(8,128)(2,1)}, bf16[128,2048]{1,0:T(8,128)(2,1)S(1)}, u32[]{:S(2)}, u32[]{:S(2)}) collective-permute-start(bf16[128,2048]{1,0:T(8,128)(2,1)} %param.7), channel_id=1, source_target_pairs={{0,8},{8,16},{16,24},{24,28},{28,20},{20,12},{12,4},{4,0},{1,9},{9... | collective-permute-start | bytes 1572872 | tf_op jit(solution)/shard_map/ppermute | solution.py:80
  5.1 3.2 %fusion.94 = f32[128,1024]{1,0:T(8,128)S(1)} fusion(bf16[128,2048]{1,0:T(8,128)(2,1)} %param.7, bf16[2048,1024]{1,0:T(8,128)(2,1)} %param.11), kind=kOutput, calls=%fused_computation.131 | convolution fusion | flops 536870912 | bytes 5242880 | tf_op jit(solution)/shard_map/dot_general | solution.py:104
  8.3 7.7 %collective-permute-done = bf16[128,2048]{1,0:T(8,128)(2,1)S(1)} collective-permute-done((bf16[128,2048]{1,0:T(8,128)(2,1)}, bf16[128,2048]{1,0:T(8,128)(2,1)S(1)}, u32[]{:S(2)}, u32[]{:S(2)}) %collective-permute-start) | collective-permute-done | bytes 524320 | tf_op jit(solution)/shard_map/ppermute | solution.py:80
  18.2 8.1 %collective-permute-done.2 = bf16[128,2048]{1,0:T(8,128)(2,1)S(1)} collective-permute-done((bf16[128,2048]{1,0:T(8,128)(2,1)}, bf16[128,2048]{1,0:T(8,128)(2,1)S(1)}, u32[]{:S(2)}, u32[]{:S(2)}) %collective-permute-start.2) | collective-permute-done | bytes 524320 | tf_op jit(solution)/shard_map/ppermute | solution.py:80
  34.4 8.3 %collective-permute-done.4 = bf16[128,2048]{1,0:T(8,128)(2,1)S(1)} collective-permute-done((bf16[128,2048]{1,0:T(8,128)(2,1)S(1)}, bf16[128,2048]{1,0:T(8,128)(2,1)S(1)}, u32[]{:S(2)}, u32[]{:S(2)}) %collective-permute-start.4) | collective-permute-done | bytes 524320 | tf_op jit(solution)/shard_map/ppermute | solution.py:80
  44.5 7.1 %collective-permute-done.6 = bf16[128,2048]{1,0:T(8,128)(2,1)S(1)} collective-permute-done((bf16[128,2048]{1,0:T(8,128)(2,1)S(1)}, bf16[128,2048]{1,0:T(8,128)(2,1)S(1)}, u32[]{:S(2)}, u32[]{:S(2)}) %collective-permute-start.6) | collective-permute-done | bytes 524320 | tf_op jit(solution)/shard_map/ppermute | solution.py:80
  58.5 9.4 %collective-permute-done.8 = bf16[128,2048]{1,0:T(8,128)(2,1)S(1)} collective-permute-done((bf16[128,2048]{1,0:T(8,128)(2,1)S(1)}, bf16[128,2048]{1,0:T(8,128)(2,1)S(1)}, u32[]{:S(2)}, u32[]{:S(2)}) %collective-permute-start.8) | collective-permute-done | bytes 524320 | tf_op jit(solution)/shard_map/ppermute | solution.py:80
  69.5 6.1 %collective-permute-done.10 = bf16[128,2048]{1,0:T(8,128)(2,1)S(1)} collective-permute-done((bf16[128,2048]{1,0:T(8,128)(2,1)S(1)}, bf16[128,2048]{1,0:T(8,128)(2,1)S(1)}, u32[]{:S(2)}, u32[]{:S(2)}) %collective-permute-start.10) | collective-permute-done | bytes 524320 | tf_op jit(solution)/shard_map/ppermute | solution.py:80
  90.5 5.4 %collective-permute-done.15 = bf16[1,128,1024]{2,1,0:T(8,128)(2,1)S(1)} collective-permute-done((bf16[1,128,1024]{2,1,0:T(8,128)(2,1)S(1)}, bf16[1,128,1024]{2,1,0:T(8,128)(2,1)S(1)}, u32[]{:S(2)}, u32[]{:S(2)}) %collective-permute-start.15) | collective-permute-done | bytes 262176 | tf_op jit(solution)/shard_map/ppermute | solution.py:100
  109.4 8.3 %collective-permute-done.19 = bf16[128,2048]{1,0:T(8,128)(2,1)S(1)} collective-permute-done((bf16[128,2048]{1,0:T(8,128)(2,1)S(1)}, bf16[128,2048]{1,0:T(8,128)(2,1)S(1)}, u32[]{:S(2)}, u32[]{:S(2)}) %collective-permute-start.19) | collective-permute-done | bytes 524320 | tf_op jit(solution)/shard_map/ppermute | solution.py:80
  117.8 2.4 collective-permute-start.21
  127.0 5.8 %collective-permute-start.22 = (bf16[128,2048]{1,0:T(8,128)(2,1)}, bf16[128,2048]{1,0:T(8,128)(2,1)S(1)}, u32[]{:S(2)}, u32[]{:S(2)}) collective-permute-start(bf16[128,2048]{1,0:T(8,128)(2,1)} %add_residual.1), channel_id=1, source_target_pairs={{0,8},{8,16},{16,24},{24,28},{28,20},{20,12},{12,4},{4,0},{1,9},{9... | collective-permute-start | bytes 1572872 | tf_op jit(solution)/shard_map/ppermute | solution.py:80
  136.1 3.6 %fusion.14 = f32[2,128,1024]{2,1,0:T(8,128)S(1)} fusion(bf16[2,128,2048]{2,1,0:T(8,128)(2,1)S(1)} %bitcast.178, bf16[3,2048,1024]{2,1,0:T(8,128)(2,1)} %param.12), kind=kOutput, calls=%fused_computation.14 | convolution fusion | flops 1073741824 | bytes 6291456 | tf_op jit(solution)/shard_map/dot_general | solution.py:104
  139.7 3.8 %fusion.36 = f32[2,128,1024]{2,1,0:T(8,128)S(1)} fusion(f32[2,128,1024]{2,1,0:T(8,128)S(1)} %fusion.14, bf16[2,128,2048]{2,1,0:T(8,128)(2,1)S(1)} %bitcast.171, bf16[3,2048,1024]{2,1,0:T(8,128)(2,1)} %param.12), kind=kOutput, calls=%fused_computation.37 | convolution fusion | flops 1074003968 | bytes 7340032 | tf_op jit(solution)/shard_map/dot_general | solution.py:104
  147.8 6.6 %collective-permute-done.24 = bf16[128,2048]{1,0:T(8,128)(2,1)S(1)} collective-permute-done((bf16[128,2048]{1,0:T(8,128)(2,1)}, bf16[128,2048]{1,0:T(8,128)(2,1)S(1)}, u32[]{:S(2)}, u32[]{:S(2)}) %collective-permute-start.24) | collective-permute-done | bytes 524320 | tf_op jit(solution)/shard_map/ppermute | solution.py:80
  164.9 6.3 %collective-permute-done.26 = bf16[128,2048]{1,0:T(8,128)(2,1)S(1)} collective-permute-done((bf16[128,2048]{1,0:T(8,128)(2,1)S(1)}, bf16[128,2048]{1,0:T(8,128)(2,1)S(1)}, u32[]{:S(2)}, u32[]{:S(2)}) %collective-permute-start.26) | collective-permute-done | bytes 524320 | tf_op jit(solution)/shard_map/ppermute | solution.py:80
  171.6 10.6 %collective-permute-done.28 = bf16[128,2048]{1,0:T(8,128)(2,1)S(1)} collective-permute-done((bf16[128,2048]{1,0:T(8,128)(2,1)S(1)}, bf16[128,2048]{1,0:T(8,128)(2,1)S(1)}, u32[]{:S(2)}, u32[]{:S(2)}) %collective-permute-start.28) | collective-permute-done | bytes 524320 | tf_op jit(solution)/shard_map/ppermute | solution.py:80
  191.2 3.6 %collective-permute-done.41 = bf16[2,1,32,1024]{3,2,1,0:T(8,128)(2,1)S(1)} collective-permute-done((bf16[2,1,32,1024]{3,2,1,0:T(8,128)(2,1)S(1)}, bf16[2,1,32,1024]{3,2,1,0:T(8,128)(2,1)S(1)}, u32[]{:S(2)}, u32[]{:S(2)}) %collective-permute-start.41) | collective-permute-done | bytes 131104 | tf_op jit(solution)/shard_map/ppermute | solution.py:100
  199.2 8.6 %collective-permute-done.37 = bf16[128,2048]{1,0:T(8,128)(2,1)S(1)} collective-permute-done((bf16[128,2048]{1,0:T(8,128)(2,1)S(1)}, bf16[128,2048]{1,0:T(8,128)(2,1)S(1)}, u32[]{:S(2)}, u32[]{:S(2)}) %collective-permute-start.37) | collective-permute-done | bytes 524320 | tf_op jit(solution)/shard_map/ppermute | solution.py:80
  218.8 2.4 collective-permute-start.44
  221.2 2.8 %collective-permute-done.47 = bf16[2,1,32,1024]{3,2,1,0:T(8,128)(2,1)S(1)} collective-permute-done((bf16[2,1,32,1024]{3,2,1,0:T(8,128)(2,1)S(1)}, bf16[2,1,32,1024]{3,2,1,0:T(8,128)(2,1)S(1)}, u32[]{:S(2)}, u32[]{:S(2)}) %collective-permute-start.47) | collective-permute-done | bytes 131104 | tf_op jit(solution)/shard_map/ppermute | solution.py:100
  224.9 3.3 %collective-permute-start.48 = (bf16[32,1024]{1,0:T(8,128)(2,1)S(1)}, bf16[32,1024]{1,0:T(8,128)(2,1)S(1)}, u32[]{:S(2)}, u32[]{:S(2)}) collective-permute-start(bf16[32,1024]{1,0:T(8,128)(2,1)S(1)} %get-tuple-element.173), channel_id=1, source_target_pairs={{0,20},{1,21},{2,22},{3,23},{8,12},{9,13},{10,14},{11,15},{16,4},{... | collective-permute-start | bytes 196616 | tf_op jit(solution)/shard_map/ppermute | solution.py:200
  229.3 3.8 %collective-permute-start.50 = (bf16[32,1024]{1,0:T(8,128)(2,1)S(1)}, bf16[32,1024]{1,0:T(8,128)(2,1)S(1)}, u32[]{:S(2)}, u32[]{:S(2)}) collective-permute-start(bf16[32,1024]{1,0:T(8,128)(2,1)S(1)} %get-tuple-element.171), channel_id=1, source_target_pairs={{0,28},{1,29},{2,30},{3,31},{8,20},{9,21},{10,22},{11,23},{16,12},... | collective-permute-start | bytes 196616 | tf_op jit(solution)/shard_map/ppermute | solution.py:200
  236.9 4.2 %collective-permute-done.51.refs_9_ = bf16[32,1024]{1,0:T(8,128)(2,1)S(1)} collective-permute-done((bf16[32,1024]{1,0:T(8,128)(2,1)S(1)}, bf16[32,1024]{1,0:T(8,128)(2,1)S(1)}, u32[]{:S(2)}, u32[]{:S(2)}) %collective-permute-start.51) | collective-permute-done | bytes 65568 | tf_op jit(solution)/shard_map/ppermute | solution.py:200
  (229 shorter events, 108.7 us)
Async XLA Ops:
  0.0 15.9 %collective-permute-start = (bf16[128,2048]{1,0:T(8,128)(2,1)}, bf16[128,2048]{1,0:T(8,128)(2,1)S(1)}, u32[]{:S(2)}, u32[]{:S(2)}) collective-permute-start(bf16[128,2048]{1,0:T(8,128)(2,1)} %param.7), channel_id=1, source_target_pairs={{0,8},{8,16},{16,24},{24,28},{28,20},{20,12},{12,4},{4,0},{1,9},{9... | collective-permute-start | bytes 1572872 | tf_op jit(solution)/shard_map/ppermute | solution.py:80
  3.0 15.2 %collective-permute-start.1 = (bf16[128,2048]{1,0:T(8,128)(2,1)}, bf16[128,2048]{1,0:T(8,128)(2,1)}, u32[]{:S(2)}, u32[]{:S(2)}) collective-permute-start(bf16[128,2048]{1,0:T(8,128)(2,1)} %param.7), channel_id=1, source_target_pairs={{8,0},{16,8},{24,16},{28,24},{20,28},{12,20},{4,12},{0,4},{9,1},{1... | collective-permute-start | bytes 1572872 | tf_op jit(solution)/shard_map/ppermute | solution.py:80
  3.0 23.3 %collective-permute-start.2 = (bf16[128,2048]{1,0:T(8,128)(2,1)}, bf16[128,2048]{1,0:T(8,128)(2,1)S(1)}, u32[]{:S(2)}, u32[]{:S(2)}) collective-permute-start(bf16[128,2048]{1,0:T(8,128)(2,1)} %param.9), channel_id=1, source_target_pairs={{0,8},{8,16},{16,24},{24,28},{28,20},{20,12},{12,4},{4,0},{1,9},{9... | collective-permute-start | bytes 1572872 | tf_op jit(solution)/shard_map/ppermute | solution.py:80
  5.1 22.8 %collective-permute-start.3 = (bf16[128,2048]{1,0:T(8,128)(2,1)}, bf16[128,2048]{1,0:T(8,128)(2,1)S(1)}, u32[]{:S(2)}, u32[]{:S(2)}) collective-permute-start(bf16[128,2048]{1,0:T(8,128)(2,1)} %param.9), channel_id=1, source_target_pairs={{8,0},{16,8},{24,16},{28,24},{20,28},{12,20},{4,12},{0,4},{9,1},{1... | collective-permute-start | bytes 1572872 | tf_op jit(solution)/shard_map/ppermute | solution.py:80
  29.4 15.1 %collective-permute-start.5 = (bf16[128,2048]{1,0:T(8,128)(2,1)}, bf16[128,2048]{1,0:T(8,128)(2,1)S(1)}, u32[]{:S(2)}, u32[]{:S(2)}) collective-permute-start(bf16[128,2048]{1,0:T(8,128)(2,1)} %collective-permute-done.1), channel_id=1, source_target_pairs={{8,0},{16,8},{24,16},{28,24},{20,28},{12,20},{4,12},{0,4},{9,1},{1... | collective-permute-start | bytes 1572872 | tf_op jit(solution)/shard_map/ppermute | solution.py:80
  29.9 21.7 %collective-permute-start.6 = (bf16[128,2048]{1,0:T(8,128)(2,1)S(1)}, bf16[128,2048]{1,0:T(8,128)(2,1)S(1)}, u32[]{:S(2)}, u32[]{:S(2)}) collective-permute-start(bf16[128,2048]{1,0:T(8,128)(2,1)S(1)} %collective-permute-done.2), channel_id=1, source_target_pairs={{0,8},{8,16},{16,24},{24,28},{28,20},{20,12},{12,4},{4,0},{1,9},{9... | collective-permute-start | bytes 1572872 | tf_op jit(solution)/shard_map/ppermute | solution.py:80
  31.5 21.6 %collective-permute-start.7 = (bf16[128,2048]{1,0:T(8,128)(2,1)S(1)}, bf16[128,2048]{1,0:T(8,128)(2,1)S(1)}, u32[]{:S(2)}, u32[]{:S(2)}) collective-permute-start(bf16[128,2048]{1,0:T(8,128)(2,1)S(1)} %collective-permute-done.3), channel_id=1, source_target_pairs={{8,0},{16,8},{24,16},{28,24},{20,28},{12,20},{4,12},{0,4},{9,1},{1... | collective-permute-start | bytes 1572872 | tf_op jit(solution)/shard_map/ppermute | solution.py:80
  55.1 20.5 %collective-permute-start.10 = (bf16[128,2048]{1,0:T(8,128)(2,1)S(1)}, bf16[128,2048]{1,0:T(8,128)(2,1)S(1)}, u32[]{:S(2)}, u32[]{:S(2)}) collective-permute-start(bf16[128,2048]{1,0:T(8,128)(2,1)S(1)} %collective-permute-done.6), channel_id=1, source_target_pairs={{0,8},{8,16},{16,24},{24,28},{28,20},{20,12},{12,4},{4,0},{1,9},{9... | collective-permute-start | bytes 1572872 | tf_op jit(solution)/shard_map/ppermute | solution.py:80
  56.7 20.2 %collective-permute-start.11 = (bf16[128,2048]{1,0:T(8,128)(2,1)S(1)}, bf16[128,2048]{1,0:T(8,128)(2,1)S(1)}, u32[]{:S(2)}, u32[]{:S(2)}) collective-permute-start(bf16[128,2048]{1,0:T(8,128)(2,1)S(1)} %collective-permute-done.7), channel_id=1, source_target_pairs={{8,0},{16,8},{24,16},{28,24},{20,28},{12,20},{4,12},{0,4},{9,1},{1... | collective-permute-start | bytes 1572872 | tf_op jit(solution)/shard_map/ppermute | solution.py:80
  101.2 16.5 %collective-permute-start.19 = (bf16[128,2048]{1,0:T(8,128)(2,1)S(1)}, bf16[128,2048]{1,0:T(8,128)(2,1)S(1)}, u32[]{:S(2)}, u32[]{:S(2)}) collective-permute-start(bf16[128,2048]{1,0:T(8,128)(2,1)S(1)} %copy-done.10), channel_id=1, source_target_pairs={{0,8},{8,16},{16,24},{24,28},{28,20},{20,12},{12,4},{4,0},{1,9},{9... | collective-permute-start | bytes 1572872 | tf_op jit(solution)/shard_map/ppermute | solution.py:80
  102.8 15.0 %collective-permute-start.20 = (bf16[128,2048]{1,0:T(8,128)(2,1)S(1)}, bf16[128,2048]{1,0:T(8,128)(2,1)}, u32[]{:S(2)}, u32[]{:S(2)}) collective-permute-start(bf16[128,2048]{1,0:T(8,128)(2,1)S(1)} %copy-done.10), channel_id=1, source_target_pairs={{8,0},{16,8},{24,16},{28,24},{20,28},{12,20},{4,12},{0,4},{9,1},{1... | collective-permute-start | bytes 1572872 | tf_op jit(solution)/shard_map/ppermute | solution.py:80
  105.5 17.2 %collective-permute-start.16 = (bf16[128,1024]{1,0:T(8,128)(2,1)S(1)}, bf16[128,1024]{1,0:T(8,128)(2,1)S(1)}, u32[]{:S(2)}, u32[]{:S(2)}) collective-permute-start(bf16[128,1024]{1,0:T(8,128)(2,1)S(1)} %fusion.78), channel_id=1, source_target_pairs={{0,24},{1,4},{2,8},{3,20},{8,29},{9,1},{10,17},{11,13},{16,22},{17... | collective-permute-start | bytes 786440 | tf_op jit(solution)/shard_map/ppermute | solution.py:169
  127.0 18.5 %collective-permute-start.22 = (bf16[128,2048]{1,0:T(8,128)(2,1)}, bf16[128,2048]{1,0:T(8,128)(2,1)S(1)}, u32[]{:S(2)}, u32[]{:S(2)}) collective-permute-start(bf16[128,2048]{1,0:T(8,128)(2,1)} %add_residual.1), channel_id=1, source_target_pairs={{0,8},{8,16},{16,24},{24,28},{28,20},{20,12},{12,4},{4,0},{1,9},{9... | collective-permute-start | bytes 1572872 | tf_op jit(solution)/shard_map/ppermute | solution.py:80
  132.7 15.1 %collective-permute-start.23 = (bf16[128,2048]{1,0:T(8,128)(2,1)}, bf16[128,2048]{1,0:T(8,128)(2,1)S(1)}, u32[]{:S(2)}, u32[]{:S(2)}) collective-permute-start(bf16[128,2048]{1,0:T(8,128)(2,1)} %add_residual.1), channel_id=1, source_target_pairs={{8,0},{16,8},{24,16},{28,24},{20,28},{12,20},{4,12},{0,4},{9,1},{1... | collective-permute-start | bytes 1572872 | tf_op jit(solution)/shard_map/ppermute | solution.py:80
  132.7 21.7 %collective-permute-start.24 = (bf16[128,2048]{1,0:T(8,128)(2,1)}, bf16[128,2048]{1,0:T(8,128)(2,1)S(1)}, u32[]{:S(2)}, u32[]{:S(2)}) collective-permute-start(bf16[128,2048]{1,0:T(8,128)(2,1)} %copy-done.17), channel_id=1, source_target_pairs={{0,8},{8,16},{16,24},{24,28},{28,20},{20,12},{12,4},{4,0},{1,9},{9... | collective-permute-start | bytes 1572872 | tf_op jit(solution)/shard_map/ppermute | solution.py:80
  134.8 21.7 %collective-permute-start.25 = (bf16[128,2048]{1,0:T(8,128)(2,1)}, bf16[128,2048]{1,0:T(8,128)(2,1)S(1)}, u32[]{:S(2)}, u32[]{:S(2)}) collective-permute-start(bf16[128,2048]{1,0:T(8,128)(2,1)} %collective-permute-done.20), channel_id=1, source_target_pairs={{8,0},{16,8},{24,16},{28,24},{20,28},{12,20},{4,12},{0,4},{9,1},{1... | collective-permute-start | bytes 1572872 | tf_op jit(solution)/shard_map/ppermute | solution.py:80
  158.5 23.6 %collective-permute-start.28 = (bf16[128,2048]{1,0:T(8,128)(2,1)S(1)}, bf16[128,2048]{1,0:T(8,128)(2,1)S(1)}, u32[]{:S(2)}, u32[]{:S(2)}) collective-permute-start(bf16[128,2048]{1,0:T(8,128)(2,1)S(1)} %collective-permute-done.24), channel_id=1, source_target_pairs={{0,8},{8,16},{16,24},{24,28},{28,20},{20,12},{12,4},{4,0},{1,9},{9... | collective-permute-start | bytes 1572872 | tf_op jit(solution)/shard_map/ppermute | solution.py:80
  158.8 23.4 %collective-permute-start.29 = (bf16[128,2048]{1,0:T(8,128)(2,1)S(1)}, bf16[128,2048]{1,0:T(8,128)(2,1)S(1)}, u32[]{:S(2)}, u32[]{:S(2)}) collective-permute-start(bf16[128,2048]{1,0:T(8,128)(2,1)S(1)} %collective-permute-done.25), channel_id=1, source_target_pairs={{8,0},{16,8},{24,16},{28,24},{20,28},{12,20},{4,12},{0,4},{9,1},{1... | collective-permute-start | bytes 1572872 | tf_op jit(solution)/shard_map/ppermute | solution.py:80
  182.2 15.2 %collective-permute-start.32 = (bf16[128,2048]{1,0:T(8,128)(2,1)S(1)}, bf16[128,2048]{1,0:T(8,128)(2,1)S(1)}, u32[]{:S(2)}, u32[]{:S(2)}) collective-permute-start(bf16[128,2048]{1,0:T(8,128)(2,1)S(1)} %collective-permute-done.27), channel_id=1, source_target_pairs={{8,0},{16,8},{24,16},{28,24},{20,28},{12,20},{4,12},{0,4},{9,1},{1... | collective-permute-start | bytes 1572872 | tf_op jit(solution)/shard_map/ppermute | solution.py:80
  187.9 19.9 %collective-permute-start.37 = (bf16[128,2048]{1,0:T(8,128)(2,1)S(1)}, bf16[128,2048]{1,0:T(8,128)(2,1)S(1)}, u32[]{:S(2)}, u32[]{:S(2)}) collective-permute-start(bf16[128,2048]{1,0:T(8,128)(2,1)S(1)} %pad_maximum_fusion.14), channel_id=1, source_target_pairs={{8,0},{16,8},{24,16},{28,24},{20,28},{12,20},{4,12},{0,4},{9,1},{1... | collective-permute-start | bytes 1572872 | tf_op jit(solution)/shard_map/ppermute | solution.py:80
  194.8 14.9 %collective-permute-start.36 = (bf16[128,2048]{1,0:T(8,128)(2,1)S(1)}, bf16[128,2048]{1,0:T(8,128)(2,1)S(1)}, u32[]{:S(2)}, u32[]{:S(2)}) collective-permute-start(bf16[128,2048]{1,0:T(8,128)(2,1)S(1)} %pad_maximum_fusion.13), channel_id=1, source_target_pairs={{0,8},{8,16},{16,24},{24,28},{28,20},{20,12},{12,4},{4,0},{1,9},{9... | collective-permute-start | bytes 1572872 | tf_op jit(solution)/shard_map/ppermute | solution.py:80
  195.1 33.2 %collective-permute-start.42 = (bf16[32,1024]{1,0:T(8,128)(2,1)S(1)}, bf16[32,1024]{1,0:T(8,128)(2,1)S(1)}, u32[]{:S(2)}, u32[]{:S(2)}) collective-permute-start(bf16[32,1024]{1,0:T(8,128)(2,1)S(1)} %get-tuple-element.177), channel_id=1, source_target_pairs={{0,4},{1,5},{2,6},{3,7},{8,0},{9,1},{10,2},{11,3},{16,8},{17,9},{1... | collective-permute-start | bytes 196616 | tf_op jit(solution)/shard_map/ppermute | solution.py:200
  197.0 32.0 %collective-permute-start.43 = (bf16[32,1024]{1,0:T(8,128)(2,1)S(1)}, bf16[32,1024]{1,0:T(8,128)(2,1)S(1)}, u32[]{:S(2)}, u32[]{:S(2)}) collective-permute-start(bf16[32,1024]{1,0:T(8,128)(2,1)S(1)} %get-tuple-element.176), channel_id=1, source_target_pairs={{0,8},{1,9},{2,10},{3,11},{8,16},{9,17},{10,18},{11,19},{16,24},{1... | collective-permute-start | bytes 196616 | tf_op jit(solution)/shard_map/ppermute | solution.py:200
  197.4 18.8 %collective-permute-start.34 = (bf16[64,2048]{1,0:T(8,128)(2,1)S(1)}, bf16[64,2048]{1,0:T(8,128)(2,1)S(1)}, u32[]{:S(2)}, u32[]{:S(2)}) collective-permute-start(bf16[64,2048]{1,0:T(8,128)(2,1)S(1)} %slice.125), channel_id=1, source_target_pairs={{0,8},{8,16},{16,24},{24,28},{28,20},{20,12},{12,4},{4,0},{1,9},{9... | collective-permute-start | bytes 786440 | tf_op jit(solution)/shard_map/ppermute | solution.py:80
  (65 other events, 662.6 us)

commit v11 on v8

--- a/solution.py
+++ b/solution.py
@@ -128,17 +128,11 @@
 
     low = Gather(low_hidden, 0)
     mid = Gather(mid_hidden, 0)
-    made = {}
     for hop in range(1, last + 1):
-        attn.ends, low.ends, mid.ends, values = tie(attn.ends, low.ends, mid.ends, list(made.values()))
-        made = dict(zip(made, values))
+        attn.ends, low.ends, mid.ends, pair_sums = tie(attn.ends, low.ends, mid.ends, pair_sums)
         attn.hop()
         (mid if hop == last else low).hop()
-        sum_cores(made)
-        made = multiply_pairs(hop - 1)
-    low.ends, attn.ends = tie(low.ends, attn.ends)
-    low.hop()
-    sum_cores(made)
+        sum_cores(multiply_pairs(hop - 1))
     attn.slots[last], pair_sums = tie(attn.ends, pair_sums)
     sum_cores(multiply_pairs(last))
 
@@ -156,7 +150,9 @@
 
     arrived = []
     for kind in classes:
-        held, mid.ends = tie(sum_xs(pair_sums[kind]).astype(jnp.bfloat16), mid.ends)
+        held = sum_xs(pair_sums[kind]).astype(jnp.bfloat16)
+        if kind == classes[-1]:
+            held, mid.ends = tie(held, mid.ends)
         moves = [
             (d * owners + t, ring[(p - kept[kind][t]) % groups] * owners + d // per_owner)
             for p, d in enumerate(ring)
@@ -171,7 +167,7 @@
         name="add_residual",
     )(*arrived, residual)
 
-    own_top, low.slots[last] = tie(own_top, low.slots[last])
+    own_top, low.ends, mid.ends = tie(own_top, low.ends, mid.ends)
     top = Gather(own_top, 0)
     cuts = [0] + list(range(3, groups, 2)) + [groups]
     chunks = [offsets[low_cut:high_cut] for low_cut, high_cut in zip(cuts, cuts[1:])]
@@ -200,7 +196,7 @@
         ]
         return lax.ppermute(part.astype(jnp.bfloat16), ("dp", "tensor"), moves)
 
-    def add_x(part, total, dtype):
+    def add_x(total, dtype):
         half = xs // 2
         while half:
             total = total.reshape((total.shape[0], 2, half) + total.shape[-2:])
@@ -208,7 +204,9 @@
             sent = lax.dynamic_index_in_dim(total, 1 - side, 1, keepdims=False).astype(dtype)
             total = lax.dynamic_index_in_dim(total, side, 1, keepdims=False) + swap(sent, 2 * half).astype(jnp.float32)
             half //= 2
-        total = total.reshape(total.shape[0], rows, width)
+        return total.reshape(total.shape[0], rows, width)
+
+    def send_all(part, total):
         for i, k in enumerate(part):
             owned[k] = [send(total[i], k)]
 
@@ -217,21 +215,26 @@
             for i, k in enumerate(part):
                 owned.setdefault(k, []).append(send(pick(total[i], x ^ flip), k, flip))
 
-    cored, deep_sum = {}, None
+    cored, deep_sum, summed = None, None, None
     for hop in range(1, last + 1):
-        top.ends, mid.ends, cored, deep_sum = tie(top.ends, mid.ends, cored, deep_sum)
+        top.ends, mid.ends, low.ends, cored, deep_sum = tie(top.ends, mid.ends, low.ends, cored, deep_sum)
+        if hop == 2:
+            low.slots[last] = low.ends
         top.hop()
         if mid.hops < last:
             mid.hop()
-        for n, total in cored.items():
-            add_x(chunks[n], total, jnp.float32 if n == 0 else jnp.bfloat16)
-        cored = {hop - 2: add_cores(multiply(chunks[hop - 2], deep_sum))} if hop > 1 else {}
+        if hop == 1:
+            low.hop()
+        if hop > 2:
+            summed = add_x(cored, jnp.float32 if hop == 3 else jnp.bfloat16)
+            if hop < last:
+                send_all(chunks[hop - 3], summed)
+        if hop > 1:
+            cored = add_cores(multiply(chunks[hop - 2], deep_sum))
         deep_sum = multiply_deep(chunks[hop - 1])
-    for n, total in cored.items():
-        add_x(chunks[n], total, jnp.bfloat16)
-    early = {k: owned[k] for part in chunks[:-2] for k in part}
-    top.slots[last], early, deep_sum = tie(top.ends, early, deep_sum)
-    owned.update(early)
+    top.slots[last], deep_sum, owned, summed = tie(top.ends, deep_sum, owned, summed)
+    send_all(chunks[-3], summed)
+    send_all(chunks[-2], add_x(cored, jnp.bfloat16))
     add_halves(chunks[-1], add_cores(multiply(chunks[-1], deep_sum)))
     parts = [part for k in offsets for part in owned[k]]
     counts = [len(owned[k]) for k in offsets]

time: 229 us -> 247 us (1.079)
  waiting for transfers between devices: 115 us -> 137 us
  matrix products: 33.8 us -> 27.5 us
    ppermute x16, waiting for transfers between devices: 13.3 us -> 39.7 us  [hop(): lax.ppermute(ends[1], 'dp', down)]
    ppermute x16, waiting for transfers between devices: 84.9 us -> 68.4 us  [hop(): lax.ppermute(ends[0], 'dp', up)]
    ppermute x13, waiting for transfers between devices: 7.52 us -> 20 us  [swap(): return lax.ppermute(values, 'tensor', [(t, t ^ bit) for t in range(owners)])]
    ppermute x2, starting transfers between devices: 12.3 us -> 5.95 us  [local(): arrived.append(lax.ppermute(held, ('dp', 'tensor'), moves))]
    dot_general x16, matrix products: 33.8 us -> 27.5 us  [product(): jnp.dot(rows_in, weight, preferred_element_type=jnp.float32)]
    ppermute x16, starting transfers between devices: 20.9 us -> 25.5 us  [hop(): lax.ppermute(ends[0], 'dp', up)]
    ppermute x16, starting transfers between devices: 14.3 us -> 17.7 us  [hop(): lax.ppermute(ends[1], 'dp', down)]
    ppermute x13, starting transfers between devices: 6.69 us -> 3.99 us  [swap(): return lax.ppermute(values, 'tensor', [(t, t ^ bit) for t in range(owners)])]
  transfers between devices with their start and end apart: 55 -> 55, of which waited for: 33 -> 25; matrix products, arithmetic and copies ran while one was open for 17% -> 13% of each run, Pallas kernels for 1% -> 0%
where the time goes in v11:
time: 247 us
  waiting for transfers between devices  137 us (55%)
  starting transfers between devices  69.4 us (28%)
  matrix products  27.5 us (11%)
  Pallas kernels  4.41 us (2%)
  other arithmetic  3.88 us (2%)
  local copies, waits for them, and re-layouts  3.49 us (1%)
    ppermute x16, waiting for transfers between devices, hop(): lax.ppermute(ends[0], 'dp', up)  68.4 us
    ppermute x16, waiting for transfers between devices, hop(): lax.ppermute(ends[1], 'dp', down)  39.7 us
    dot_general x16, matrix products, product(): jnp.dot(rows_in, weight, preferred_element_type=jnp.float32)  27.5 us
    ppermute x16, starting transfers between devices, hop(): lax.ppermute(ends[0], 'dp', up)  25.5 us
    ppermute x13, waiting for transfers between devices, swap(): return lax.ppermute(values, 'tensor', [(t, t ^ bit) for t in range(owners)])  20 us
    ppermute x16, starting transfers between devices, hop(): lax.ppermute(ends[1], 'dp', down)  17.7 us
    ppermute x8, starting transfers between devices, send(): return lax.ppermute(part.astype(jnp.bfloat16), ('dp', 'tensor'), moves)  16.2 us
    ppermute x2, starting transfers between devices, local(): arrived.append(lax.ppermute(held, ('dp', 'tensor'), moves))  5.95 us
  transfers between devices with their start and end apart: 55, of which 25 were waited for; matrix products, arithmetic and copies ran while one was open for 13% of the time, Pallas kernels for 0%

profile of v11, /device:TPU:0, one launch (start us, length us, event | category | flops | bytes accessed | tf_op | source)
XLA Modules:
  0.0 246.9 jit_solution(7856239221092637488)
XLA Ops:
  5.1 10.9 %collective-permute-done = bf16[128,2048]{1,0:T(8,128)(2,1)S(1)} collective-permute-done((bf16[128,2048]{1,0:T(8,128)(2,1)}, bf16[128,2048]{1,0:T(8,128)(2,1)S(1)}, u32[]{:S(2)}, u32[]{:S(2)}) %collective-permute-start) | collective-permute-done | bytes 524320 | tf_op jit(solution)/shard_map/ppermute | solution.py:80
  18.1 8.2 %collective-permute-done.2 = bf16[128,2048]{1,0:T(8,128)(2,1)S(1)} collective-permute-done((bf16[128,2048]{1,0:T(8,128)(2,1)}, bf16[128,2048]{1,0:T(8,128)(2,1)S(1)}, u32[]{:S(2)}, u32[]{:S(2)}) %collective-permute-start.2) | collective-permute-done | bytes 524320 | tf_op jit(solution)/shard_map/ppermute | solution.py:80
  31.9 10.9 %collective-permute-done.4 = bf16[128,2048]{1,0:T(8,128)(2,1)} collective-permute-done((bf16[128,2048]{1,0:T(8,128)(2,1)S(1)}, bf16[128,2048]{1,0:T(8,128)(2,1)}, u32[]{:S(2)}, u32[]{:S(2)}) %collective-permute-start.4) | collective-permute-done | bytes 524320 | tf_op jit(solution)/shard_map/ppermute | solution.py:80
  44.4 7.2 %collective-permute-done.6 = bf16[128,2048]{1,0:T(8,128)(2,1)S(1)} collective-permute-done((bf16[128,2048]{1,0:T(8,128)(2,1)S(1)}, bf16[128,2048]{1,0:T(8,128)(2,1)S(1)}, u32[]{:S(2)}, u32[]{:S(2)}) %collective-permute-start.6) | collective-permute-done | bytes 524320 | tf_op jit(solution)/shard_map/ppermute | solution.py:80
  56.9 3.8 %fusion.63 = f32[256,1024]{1,0:T(8,128)S(1)} fusion(bf16[2048,1024]{1,0:T(8,128)(2,1)} %param.11, bf16[128,2048]{1,0:T(8,128)(2,1)} %collective-permute-done.5, bf16[128,2048]{1,0:T(8,128)(2,1)} %collective-permute-done.4), kind=kOutput, calls=%fused_computation.48 | convolution fusion | flops 1075838976 | bytes 6291456 | tf_op jit(solution)/shard_map/dot_general | solution.py:104
  60.8 8.7 %collective-permute-done.9 = bf16[128,2048]{1,0:T(8,128)(2,1)S(1)} collective-permute-done((bf16[128,2048]{1,0:T(8,128)(2,1)}, bf16[128,2048]{1,0:T(8,128)(2,1)S(1)}, u32[]{:S(2)}, u32[]{:S(2)}) %collective-permute-start.9) | collective-permute-done | bytes 524320 | tf_op jit(solution)/shard_map/ppermute | solution.py:80
  79.2 4.1 %collective-permute-done.13 = bf16[64,2048]{1,0:T(8,128)(2,1)S(1)} collective-permute-done((bf16[64,2048]{1,0:T(8,128)(2,1)S(1)}, bf16[64,2048]{1,0:T(8,128)(2,1)S(1)}, u32[]{:S(2)}, u32[]{:S(2)}) %collective-permute-start.13) | collective-permute-done | bytes 262176 | tf_op jit(solution)/shard_map/ppermute | solution.py:80
  93.1 5.9 %collective-permute-done.17 = bf16[1,128,1024]{2,1,0:T(8,128)(2,1)S(1)} collective-permute-done((bf16[1,128,1024]{2,1,0:T(8,128)(2,1)S(1)}, bf16[1,128,1024]{2,1,0:T(8,128)(2,1)S(1)}, u32[]{:S(2)}, u32[]{:S(2)}) %collective-permute-start.17) | collective-permute-done | bytes 262176 | tf_op jit(solution)/shard_map/ppermute | solution.py:100
  99.8 3.8 %collective-permute-done.20 = bf16[1,128,1024]{2,1,0:T(8,128)(2,1)S(1)} collective-permute-done((bf16[1,128,1024]{2,1,0:T(8,128)(2,1)S(1)}, bf16[1,128,1024]{2,1,0:T(8,128)(2,1)S(1)}, u32[]{:S(2)}, u32[]{:S(2)}) %collective-permute-start.20) | collective-permute-done | bytes 262176 | tf_op jit(solution)/shard_map/ppermute | solution.py:100
  103.8 5.3 %collective-permute-start.23 = (bf16[128,1024]{1,0:T(8,128)(2,1)S(1)}, bf16[128,1024]{1,0:T(8,128)(2,1)}, u32[]{:S(2)}, u32[]{:S(2)}) collective-permute-start(bf16[128,1024]{1,0:T(8,128)(2,1)S(1)} %fusion.96), channel_id=1, source_target_pairs={{0,28},{1,0},{2,12},{3,16},{8,21},{9,9},{10,5},{11,25},{16,14},{17... | collective-permute-start | bytes 786440 | tf_op jit(solution)/shard_map/ppermute | solution.py:161
  109.2 3.8 %collective-permute-done.23.refs_1_ = bf16[128,1024]{1,0:T(8,128)(2,1)} collective-permute-done((bf16[128,1024]{1,0:T(8,128)(2,1)S(1)}, bf16[128,1024]{1,0:T(8,128)(2,1)}, u32[]{:S(2)}, u32[]{:S(2)}) %collective-permute-start.23) | collective-permute-done | bytes 262176 | tf_op jit(solution)/shard_map/ppermute | solution.py:161
  116.1 8.3 %collective-permute-start.28 = (bf16[64,2048]{1,0:T(8,128)(2,1)S(1)}, bf16[64,2048]{1,0:T(8,128)(2,1)S(1)}, u32[]{:S(2)}, u32[]{:S(2)}) collective-permute-start(bf16[64,2048]{1,0:T(8,128)(2,1)S(1)} %slice.76), channel_id=1, source_target_pairs={{0,8},{8,16},{16,24},{24,28},{28,20},{20,12},{12,4},{4,0},{1,9},{9... | collective-permute-start | bytes 786440 | tf_op jit(solution)/shard_map/ppermute | solution.py:80
  124.5 4.1 %fusion.12 = f32[3,128,1024]{2,1,0:T(8,128)S(1)} fusion(bf16[3,128,2048]{2,1,0:T(8,128)(2,1)S(1)} %bitcast.174, bf16[3,2048,1024]{2,1,0:T(8,128)(2,1)} %param.12), kind=kOutput, calls=%fused_computation.12 | convolution fusion | flops 1610612736 | bytes 7340032 | tf_op jit(solution)/shard_map/dot_general | solution.py:104
  132.8 4.1 %fusion.36 = f32[3,128,1024]{2,1,0:T(8,128)S(1)} fusion(f32[3,128,1024]{2,1,0:T(8,128)S(1)} %fusion.12, bf16[3,128,2048]{2,1,0:T(8,128)(2,1)S(1)} %bitcast.171, bf16[3,2048,1024]{2,1,0:T(8,128)(2,1)} %param.12), kind=kOutput, calls=%fused_computation.39 | convolution fusion | flops 1611005952 | bytes 8912896 | tf_op jit(solution)/shard_map/dot_general | solution.py:104
  137.0 19.7 %collective-permute-done.29 = bf16[64,2048]{1,0:T(8,128)(2,1)S(1)} collective-permute-done((bf16[64,2048]{1,0:T(8,128)(2,1)S(1)}, bf16[64,2048]{1,0:T(8,128)(2,1)S(1)}, u32[]{:S(2)}, u32[]{:S(2)}) %collective-permute-start.29) | collective-permute-done | bytes 262176 | tf_op jit(solution)/shard_map/ppermute | solution.py:80
  167.4 13.0 %collective-permute-done.32 = bf16[128,2048]{1,0:T(8,128)(2,1)S(1)} collective-permute-done((bf16[128,2048]{1,0:T(8,128)(2,1)S(1)}, bf16[128,2048]{1,0:T(8,128)(2,1)S(1)}, u32[]{:S(2)}, u32[]{:S(2)}) %collective-permute-start.32) | collective-permute-done | bytes 524320 | tf_op jit(solution)/shard_map/ppermute | solution.py:80
  190.1 11.6 %collective-permute-done.37 = bf16[64,2048]{1,0:T(8,128)(2,1)S(1)} collective-permute-done((bf16[64,2048]{1,0:T(8,128)(2,1)S(1)}, bf16[64,2048]{1,0:T(8,128)(2,1)S(1)}, u32[]{:S(2)}, u32[]{:S(2)}) %collective-permute-start.37) | collective-permute-done | bytes 262176 | tf_op jit(solution)/shard_map/ppermute | solution.py:80
  203.9 6.1 %collective-permute-done.42 = f32[3,1,32,1024]{3,2,1,0:T(8,128)S(1)} collective-permute-done((f32[3,1,32,1024]{3,2,1,0:T(8,128)S(1)}, f32[3,1,32,1024]{3,2,1,0:T(8,128)S(1)}, u32[]{:S(2)}, u32[]{:S(2)}) %collective-permute-start.42) | collective-permute-done | bytes 393248 | tf_op jit(solution)/shard_map/ppermute | solution.py:100
  214.4 3.5 %collective-permute-start.41 = (bf16[64,2048]{1,0:T(8,128)(2,1)S(1)}, bf16[64,2048]{1,0:T(8,128)(2,1)S(1)}, u32[]{:S(2)}, u32[]{:S(2)}) collective-permute-start(bf16[64,2048]{1,0:T(8,128)(2,1)S(1)} %slice.84), channel_id=1, source_target_pairs={{8,0},{16,8},{24,16},{28,24},{20,28},{12,20},{4,12},{0,4},{9,1},{1... | collective-permute-start | bytes 786440 | tf_op jit(solution)/shard_map/ppermute | solution.py:80
  219.7 3.2 %collective-permute-done.45 = bf16[2,1,32,1024]{3,2,0,1:T(8,128)(2,1)S(1)} collective-permute-done((bf16[2,1,32,1024]{3,2,0,1:T(8,128)(2,1)S(1)}, bf16[2,1,32,1024]{3,2,0,1:T(8,128)(2,1)S(1)}, u32[]{:S(2)}, u32[]{:S(2)}) %collective-permute-start.45) | collective-permute-done | bytes 131104 | tf_op jit(solution)/shard_map/ppermute | solution.py:100
  223.0 3.5 %collective-permute-start.46 = (bf16[32,1024]{1,0:T(8,128)(2,1)S(1)}, bf16[32,1024]{1,0:T(8,128)(2,1)S(1)}, u32[]{:S(2)}, u32[]{:S(2)}) collective-permute-start(bf16[32,1024]{1,0:T(8,128)(2,1)S(1)} %get-tuple-element.152), channel_id=1, source_target_pairs={{0,12},{1,13},{2,14},{3,15},{8,4},{9,5},{10,6},{11,7},{16,0},{17,1... | collective-permute-start | bytes 196616 | tf_op jit(solution)/shard_map/ppermute | solution.py:197
  229.0 4.7 %collective-permute-start.53 = (bf16[32,1024]{1,0:T(8,128)(2,1)S(1)}, bf16[32,1024]{1,0:T(8,128)(2,1)S(1)}, u32[]{:S(2)}, u32[]{:S(2)}) collective-permute-start(bf16[32,1024]{1,0:T(8,128)(2,1)S(1)} %get-tuple-element.148), channel_id=1, source_target_pairs={{0,28},{1,29},{2,30},{3,31},{8,20},{9,21},{10,22},{11,23},{16,12},... | collective-permute-start | bytes 196616 | tf_op jit(solution)/shard_map/ppermute | solution.py:197
  234.1 3.4 %collective-permute-start.50 = (bf16[32,1024]{1,0:T(8,128)(2,1)S(1)}, bf16[32,1024]{1,0:T(8,128)(2,1)S(1)}, u32[]{:S(2)}, u32[]{:S(2)}) collective-permute-start(bf16[32,1024]{1,0:T(8,128)(2,1)S(1)} %get-tuple-element.150), channel_id=1, source_target_pairs={{0,20},{1,21},{2,22},{3,23},{8,12},{9,13},{10,14},{11,15},{16,4},{... | collective-permute-start | bytes 196616 | tf_op jit(solution)/shard_map/ppermute | solution.py:197
  238.5 3.5 %collective-permute-done.54.refs_8_ = bf16[32,1024]{1,0:T(8,128)(2,1)S(1)} collective-permute-done((bf16[32,1024]{1,0:T(8,128)(2,1)S(1)}, bf16[32,1024]{1,0:T(8,128)(2,1)S(1)}, u32[]{:S(2)}, u32[]{:S(2)}) %collective-permute-start.54) | collective-permute-done | bytes 65568 | tf_op jit(solution)/shard_map/ppermute | solution.py:197
  (209 shorter events, 84.7 us)
Async XLA Ops:
  0.0 15.9 %collective-permute-start = (bf16[128,2048]{1,0:T(8,128)(2,1)}, bf16[128,2048]{1,0:T(8,128)(2,1)S(1)}, u32[]{:S(2)}, u32[]{:S(2)}) collective-permute-start(bf16[128,2048]{1,0:T(8,128)(2,1)} %param.7), channel_id=1, source_target_pairs={{0,8},{8,16},{16,24},{24,28},{28,20},{20,12},{12,4},{4,0},{1,9},{9... | collective-permute-start | bytes 1572872 | tf_op jit(solution)/shard_map/ppermute | solution.py:80
  3.0 23.3 %collective-permute-start.2 = (bf16[128,2048]{1,0:T(8,128)(2,1)}, bf16[128,2048]{1,0:T(8,128)(2,1)S(1)}, u32[]{:S(2)}, u32[]{:S(2)}) collective-permute-start(bf16[128,2048]{1,0:T(8,128)(2,1)} %param.9), channel_id=1, source_target_pairs={{0,8},{8,16},{16,24},{24,28},{28,20},{20,12},{12,4},{4,0},{1,9},{9... | collective-permute-start | bytes 1572872 | tf_op jit(solution)/shard_map/ppermute | solution.py:80
  5.1 22.8 %collective-permute-start.3 = (bf16[128,2048]{1,0:T(8,128)(2,1)}, bf16[128,2048]{1,0:T(8,128)(2,1)S(1)}, u32[]{:S(2)}, u32[]{:S(2)}) collective-permute-start(bf16[128,2048]{1,0:T(8,128)(2,1)} %param.9), channel_id=1, source_target_pairs={{8,0},{16,8},{24,16},{28,24},{20,28},{12,20},{4,12},{0,4},{9,1},{1... | collective-permute-start | bytes 1572872 | tf_op jit(solution)/shard_map/ppermute | solution.py:80
  29.9 21.7 %collective-permute-start.6 = (bf16[128,2048]{1,0:T(8,128)(2,1)S(1)}, bf16[128,2048]{1,0:T(8,128)(2,1)S(1)}, u32[]{:S(2)}, u32[]{:S(2)}) collective-permute-start(bf16[128,2048]{1,0:T(8,128)(2,1)S(1)} %collective-permute-done.2), channel_id=1, source_target_pairs={{0,8},{8,16},{16,24},{24,28},{28,20},{20,12},{12,4},{4,0},{1,9},{9... | collective-permute-start | bytes 1572872 | tf_op jit(solution)/shard_map/ppermute | solution.py:80
  31.5 21.4 %collective-permute-start.7 = (bf16[128,2048]{1,0:T(8,128)(2,1)S(1)}, bf16[128,2048]{1,0:T(8,128)(2,1)S(1)}, u32[]{:S(2)}, u32[]{:S(2)}) collective-permute-start(bf16[128,2048]{1,0:T(8,128)(2,1)S(1)} %collective-permute-done.3), channel_id=1, source_target_pairs={{8,0},{16,8},{24,16},{28,24},{20,28},{12,20},{4,12},{0,4},{9,1},{1... | collective-permute-start | bytes 1572872 | tf_op jit(solution)/shard_map/ppermute | solution.py:80
  52.9 18.1 %collective-permute-start.8 = (bf16[128,2048]{1,0:T(8,128)(2,1)}, bf16[128,2048]{1,0:T(8,128)(2,1)S(1)}, u32[]{:S(2)}, u32[]{:S(2)}) collective-permute-start(bf16[128,2048]{1,0:T(8,128)(2,1)} %collective-permute-done.4), channel_id=1, source_target_pairs={{0,8},{8,16},{16,24},{24,28},{28,20},{20,12},{12,4},{4,0},{1,9},{9... | collective-permute-start | bytes 1572872 | tf_op jit(solution)/shard_map/ppermute | solution.py:80
  54.9 20.7 %collective-permute-start.10 = (bf16[128,2048]{1,0:T(8,128)(2,1)S(1)}, bf16[128,2048]{1,0:T(8,128)(2,1)S(1)}, u32[]{:S(2)}, u32[]{:S(2)}) collective-permute-start(bf16[128,2048]{1,0:T(8,128)(2,1)S(1)} %collective-permute-done.6), channel_id=1, source_target_pairs={{0,8},{8,16},{16,24},{24,28},{28,20},{20,12},{12,4},{4,0},{1,9},{9... | collective-permute-start | bytes 1572872 | tf_op jit(solution)/shard_map/ppermute | solution.py:80
  56.5 20.4 %collective-permute-start.11 = (bf16[128,2048]{1,0:T(8,128)(2,1)S(1)}, bf16[128,2048]{1,0:T(8,128)(2,1)S(1)}, u32[]{:S(2)}, u32[]{:S(2)}) collective-permute-start(bf16[128,2048]{1,0:T(8,128)(2,1)S(1)} %collective-permute-done.7), channel_id=1, source_target_pairs={{8,0},{16,8},{24,16},{28,24},{20,28},{12,20},{4,12},{0,4},{9,1},{1... | collective-permute-start | bytes 1572872 | tf_op jit(solution)/shard_map/ppermute | solution.py:80
  87.7 16.1 %collective-permute-start.21 = (bf16[128,2048]{1,0:T(8,128)(2,1)S(1)}, bf16[128,2048]{1,0:T(8,128)(2,1)S(1)}, u32[]{:S(2)}, u32[]{:S(2)}) collective-permute-start(bf16[128,2048]{1,0:T(8,128)(2,1)S(1)} %copy-done.7), channel_id=1, source_target_pairs={{0,8},{8,16},{16,24},{24,28},{28,20},{20,12},{12,4},{4,0},{1,9},{9... | collective-permute-start | bytes 1572872 | tf_op jit(solution)/shard_map/ppermute | solution.py:80
  116.1 16.6 %collective-permute-start.28 = (bf16[64,2048]{1,0:T(8,128)(2,1)S(1)}, bf16[64,2048]{1,0:T(8,128)(2,1)S(1)}, u32[]{:S(2)}, u32[]{:S(2)}) collective-permute-start(bf16[64,2048]{1,0:T(8,128)(2,1)S(1)} %slice.76), channel_id=1, source_target_pairs={{0,8},{8,16},{16,24},{24,28},{28,20},{20,12},{12,4},{4,0},{1,9},{9... | collective-permute-start | bytes 786440 | tf_op jit(solution)/shard_map/ppermute | solution.py:80
  128.6 28.1 %collective-permute-start.24 = (bf16[128,2048]{1,0:T(8,128)(2,1)S(1)}, bf16[128,2048]{1,0:T(8,128)(2,1)S(1)}, u32[]{:S(2)}, u32[]{:S(2)}) collective-permute-start(bf16[128,2048]{1,0:T(8,128)(2,1)S(1)} %copy-done), channel_id=1, source_target_pairs={{0,8},{8,16},{16,24},{24,28},{28,20},{20,12},{12,4},{4,0},{1,9},{9... | collective-permute-start | bytes 1572872 | tf_op jit(solution)/shard_map/ppermute | solution.py:80
  128.7 28.0 %collective-permute-start.25 = (bf16[128,2048]{1,0:T(8,128)(2,1)S(1)}, bf16[128,2048]{1,0:T(8,128)(2,1)S(1)}, u32[]{:S(2)}, u32[]{:S(2)}) collective-permute-start(bf16[128,2048]{1,0:T(8,128)(2,1)S(1)} %copy-done), channel_id=1, source_target_pairs={{8,0},{16,8},{24,16},{28,24},{20,28},{12,20},{4,12},{0,4},{9,1},{1... | collective-permute-start | bytes 1572872 | tf_op jit(solution)/shard_map/ppermute | solution.py:80
  130.7 26.0 %collective-permute-start.26 = (bf16[128,2048]{1,0:T(8,128)(2,1)S(1)}, bf16[128,2048]{1,0:T(8,128)(2,1)S(1)}, u32[]{:S(2)}, u32[]{:S(2)}) collective-permute-start(bf16[128,2048]{1,0:T(8,128)(2,1)S(1)} %copy-done.9), channel_id=1, source_target_pairs={{0,8},{8,16},{16,24},{24,28},{28,20},{20,12},{12,4},{4,0},{1,9},{9... | collective-permute-start | bytes 1572872 | tf_op jit(solution)/shard_map/ppermute | solution.py:80
  130.8 26.0 %collective-permute-start.27 = (bf16[128,2048]{1,0:T(8,128)(2,1)S(1)}, bf16[128,2048]{1,0:T(8,128)(2,1)S(1)}, u32[]{:S(2)}, u32[]{:S(2)}) collective-permute-start(bf16[128,2048]{1,0:T(8,128)(2,1)S(1)} %copy-done.11), channel_id=1, source_target_pairs={{8,0},{16,8},{24,16},{28,24},{20,28},{12,20},{4,12},{0,4},{9,1},{1... | collective-permute-start | bytes 1572872 | tf_op jit(solution)/shard_map/ppermute | solution.py:80
  132.7 24.0 %collective-permute-start.29 = (bf16[64,2048]{1,0:T(8,128)(2,1)S(1)}, bf16[64,2048]{1,0:T(8,128)(2,1)S(1)}, u32[]{:S(2)}, u32[]{:S(2)}) collective-permute-start(bf16[64,2048]{1,0:T(8,128)(2,1)S(1)} %slice.77), channel_id=1, source_target_pairs={{8,0},{16,8},{24,16},{28,24},{20,28},{12,20},{4,12},{0,4},{9,1},{1... | collective-permute-start | bytes 786440 | tf_op jit(solution)/shard_map/ppermute | solution.py:80
  156.7 25.1 %collective-permute-start.30 = (bf16[128,2048]{1,0:T(8,128)(2,1)S(1)}, bf16[128,2048]{1,0:T(8,128)(2,1)S(1)}, u32[]{:S(2)}, u32[]{:S(2)}) collective-permute-start(bf16[128,2048]{1,0:T(8,128)(2,1)S(1)} %collective-permute-done.24), channel_id=1, source_target_pairs={{0,8},{8,16},{16,24},{24,28},{28,20},{20,12},{12,4},{4,0},{1,9},{9... | collective-permute-start | bytes 1572872 | tf_op jit(solution)/shard_map/ppermute | solution.py:80
  156.8 25.1 %collective-permute-start.31 = (bf16[128,2048]{1,0:T(8,128)(2,1)S(1)}, bf16[128,2048]{1,0:T(8,128)(2,1)S(1)}, u32[]{:S(2)}, u32[]{:S(2)}) collective-permute-start(bf16[128,2048]{1,0:T(8,128)(2,1)S(1)} %collective-permute-done.25), channel_id=1, source_target_pairs={{8,0},{16,8},{24,16},{28,24},{20,28},{12,20},{4,12},{0,4},{9,1},{1... | collective-permute-start | bytes 1572872 | tf_op jit(solution)/shard_map/ppermute | solution.py:80
  159.3 21.1 %collective-permute-start.32 = (bf16[128,2048]{1,0:T(8,128)(2,1)S(1)}, bf16[128,2048]{1,0:T(8,128)(2,1)S(1)}, u32[]{:S(2)}, u32[]{:S(2)}) collective-permute-start(bf16[128,2048]{1,0:T(8,128)(2,1)S(1)} %collective-permute-done.26), channel_id=1, source_target_pairs={{0,8},{8,16},{16,24},{24,28},{28,20},{20,12},{12,4},{4,0},{1,9},{9... | collective-permute-start | bytes 1572872 | tf_op jit(solution)/shard_map/ppermute | solution.py:80
  159.3 21.1 %collective-permute-start.33 = (bf16[128,2048]{1,0:T(8,128)(2,1)S(1)}, bf16[128,2048]{1,0:T(8,128)(2,1)S(1)}, u32[]{:S(2)}, u32[]{:S(2)}) collective-permute-start(bf16[128,2048]{1,0:T(8,128)(2,1)S(1)} %collective-permute-done.27), channel_id=1, source_target_pairs={{8,0},{16,8},{24,16},{28,24},{20,28},{12,20},{4,12},{0,4},{9,1},{1... | collective-permute-start | bytes 1572872 | tf_op jit(solution)/shard_map/ppermute | solution.py:80
  163.5 19.8 %collective-permute-start.34 = (f32[3,2,32,1024]{3,2,1,0:T(8,128)S(1)}, f32[3,2,32,1024]{3,2,1,0:T(8,128)S(1)}, u32[]{:S(2)}, u32[]{:S(2)}) collective-permute-start(f32[3,2,32,1024]{3,2,1,0:T(8,128)S(1)} %dynamic-slice_bitcast_fusion), channel_id=1, source_target_pairs={{0,1},{1,0},{2,3},{3,2},{4,5},{5,4},{6,7},{7,6},{8,9},{9,8},{10,11... | collective-permute-start | bytes 2359304 | tf_op jit(solution)/shard_map/ppermute | solution.py:100
  183.4 30.6 %collective-permute-start.35 = (bf16[128,2048]{1,0:T(8,128)(2,1)S(1)}, bf16[128,2048]{1,0:T(8,128)(2,1)S(1)}, u32[]{:S(2)}, u32[]{:S(2)}) collective-permute-start(bf16[128,2048]{1,0:T(8,128)(2,1)S(1)} %collective-permute-done.30), channel_id=1, source_target_pairs={{0,8},{8,16},{16,24},{24,28},{28,20},{20,12},{12,4},{4,0},{1,9},{9... | collective-permute-start | bytes 1572872 | tf_op jit(solution)/shard_map/ppermute | solution.py:80
  184.3 29.7 %collective-permute-start.36 = (bf16[128,2048]{1,0:T(8,128)(2,1)S(1)}, bf16[128,2048]{1,0:T(8,128)(2,1)S(1)}, u32[]{:S(2)}, u32[]{:S(2)}) collective-permute-start(bf16[128,2048]{1,0:T(8,128)(2,1)S(1)} %collective-permute-done.31), channel_id=1, source_target_pairs={{8,0},{16,8},{24,16},{28,24},{20,28},{12,20},{4,12},{0,4},{9,1},{1... | collective-permute-start | bytes 1572872 | tf_op jit(solution)/shard_map/ppermute | solution.py:80
  186.2 15.5 %collective-permute-start.37 = (bf16[64,2048]{1,0:T(8,128)(2,1)S(1)}, bf16[64,2048]{1,0:T(8,128)(2,1)S(1)}, u32[]{:S(2)}, u32[]{:S(2)}) collective-permute-start(bf16[64,2048]{1,0:T(8,128)(2,1)S(1)} %slice.81), channel_id=1, source_target_pairs={{0,8},{8,16},{16,24},{24,28},{28,20},{20,12},{12,4},{4,0},{1,9},{9... | collective-permute-start | bytes 786440 | tf_op jit(solution)/shard_map/ppermute | solution.py:80
  190.0 24.0 %collective-permute-start.39 = (f32[2,2,32,1024]{3,2,0,1:T(8,128)S(1)}, f32[2,2,32,1024]{3,2,0,1:T(8,128)S(1)}, u32[]{:S(2)}, u32[]{:S(2)}) collective-permute-start(f32[2,2,32,1024]{3,2,0,1:T(8,128)S(1)} %bitcast.193), channel_id=1, source_target_pairs={{0,1},{1,0},{2,3},{3,2},{4,5},{5,4},{6,7},{7,6},{8,9},{9,8},{10,11... | collective-permute-start | bytes 1572872 | tf_op jit(solution)/shard_map/ppermute | solution.py:100
  (59 other events, 597.1 us)

commit v12 on v11

--- a/solution.py
+++ b/solution.py
@@ -133,6 +133,8 @@
         attn.hop()
         (mid if hop == last else low).hop()
         sum_cores(multiply_pairs(hop - 1))
+    low.ends, attn.ends = tie(low.ends, attn.ends)
+    low.hop()
     attn.slots[last], pair_sums = tie(attn.ends, pair_sums)
     sum_cores(multiply_pairs(last))
 
@@ -167,7 +169,7 @@
         name="add_residual",
     )(*arrived, residual)
 
-    own_top, low.ends, mid.ends = tie(own_top, low.ends, mid.ends)
+    own_top, low.slots[last] = tie(own_top, low.slots[last])
     top = Gather(own_top, 0)
     cuts = [0] + list(range(3, groups, 2)) + [groups]
     chunks = [offsets[low_cut:high_cut] for low_cut, high_cut in zip(cuts, cuts[1:])]
@@ -196,12 +198,12 @@
         ]
         return lax.ppermute(part.astype(jnp.bfloat16), ("dp", "tensor"), moves)
 
-    def add_x(total, dtype):
+    def add_x(total):
         half = xs // 2
         while half:
             total = total.reshape((total.shape[0], 2, half) + total.shape[-2:])
             side = bit_of_x(half)
-            sent = lax.dynamic_index_in_dim(total, 1 - side, 1, keepdims=False).astype(dtype)
+            sent = lax.dynamic_index_in_dim(total, 1 - side, 1, keepdims=False).astype(jnp.bfloat16)
             total = lax.dynamic_index_in_dim(total, side, 1, keepdims=False) + swap(sent, 2 * half).astype(jnp.float32)
             half //= 2
         return total.reshape(total.shape[0], rows, width)
@@ -217,24 +219,28 @@
 
     cored, deep_sum, summed = None, None, None
     for hop in range(1, last + 1):
-        top.ends, mid.ends, low.ends, cored, deep_sum = tie(top.ends, mid.ends, low.ends, cored, deep_sum)
-        if hop == 2:
-            low.slots[last] = low.ends
+        if hop < last:
+            top.ends, mid.ends, cored, deep_sum = tie(top.ends, mid.ends, cored, deep_sum)
+        else:
+            top.ends, cored, deep_sum = tie(top.ends, cored, deep_sum)
         top.hop()
-        if mid.hops < last:
+        if hop < last - 1:
             mid.hop()
-        if hop == 1:
-            low.hop()
         if hop > 2:
-            summed = add_x(cored, jnp.float32 if hop == 3 else jnp.bfloat16)
+            summed = add_x(cored)
+            if hop == last - 1:
+                mid.ends, summed = tie(mid.ends, summed)
+                mid.hop()
             if hop < last:
                 send_all(chunks[hop - 3], summed)
         if hop > 1:
             cored = add_cores(multiply(chunks[hop - 2], deep_sum))
-        deep_sum = multiply_deep(chunks[hop - 1])
+        if hop < last:
+            deep_sum = multiply_deep(chunks[hop - 1])
+    deep_sum = multiply_deep(chunks[-1])
     top.slots[last], deep_sum, owned, summed = tie(top.ends, deep_sum, owned, summed)
     send_all(chunks[-3], summed)
-    send_all(chunks[-2], add_x(cored, jnp.bfloat16))
+    send_all(chunks[-2], add_x(cored))
     add_halves(chunks[-1], add_cores(multiply(chunks[-1], deep_sum)))
     parts = [part for k in offsets for part in owned[k]]
     counts = [len(owned[k]) for k in offsets]

time: 247 us -> 240 us (0.972)
  waiting for transfers between devices: 137 us -> 120 us
  matrix products: 27.5 us -> 37.6 us
    ppermute x16, waiting for transfers between devices: 39.7 us -> 18.8 us  [hop(): lax.ppermute(ends[1], 'dp', down)]
    ppermute x16, waiting for transfers between devices: 68.4 us -> 84.7 us  [hop(): lax.ppermute(ends[0], 'dp', up)]
    dot_general x16, matrix products: 27.5 us -> 37.6 us  [product(): jnp.dot(rows_in, weight, preferred_element_type=jnp.float32)]
    ppermute x13, waiting for transfers between devices: 20 us -> 11.8 us  [swap(): return lax.ppermute(values, 'tensor', [(t, t ^ bit) for t in range(owners)])]
    ppermute x16, starting transfers between devices: 25.5 us -> 20.5 us  [hop(): lax.ppermute(ends[0], 'dp', up)]
    ppermute x13, starting transfers between devices: 3.99 us -> 8.97 us  [swap(): return lax.ppermute(values, 'tensor', [(t, t ^ bit) for t in range(owners)])]
    ppermute x16, starting transfers between devices: 17.7 us -> 13.4 us  [hop(): lax.ppermute(ends[1], 'dp', down)]
    ppermute x2, starting transfers between devices: 5.95 us -> 9.75 us  [local(): arrived.append(lax.ppermute(held, ('dp', 'tensor'), moves))]
  transfers between devices with their start and end apart: 55 -> 55, of which waited for: 25 -> 25; matrix products, arithmetic and copies ran while one was open for 13% -> 19% of each run, Pallas kernels for 0% -> 1%
where the time goes in v12:
time: 240 us
  waiting for transfers between devices  120 us (50%)
  starting transfers between devices  67 us (28%)
  matrix products  37.6 us (16%)
  other arithmetic  5.16 us (2%)
  local copies, waits for them, and re-layouts  4.79 us (2%)
  Pallas kernels  4.41 us (2%)
    ppermute x16, waiting for transfers between devices, hop(): lax.ppermute(ends[0], 'dp', up)  84.7 us
    dot_general x16, matrix products, product(): jnp.dot(rows_in, weight, preferred_element_type=jnp.float32)  37.6 us
    ppermute x16, starting transfers between devices, hop(): lax.ppermute(ends[0], 'dp', up)  20.5 us
    ppermute x16, waiting for transfers between devices, hop(): lax.ppermute(ends[1], 'dp', down)  18.8 us
    ppermute x8, starting transfers between devices, send(): return lax.ppermute(part.astype(jnp.bfloat16), ('dp', 'tensor'), moves)  14.4 us
    ppermute x16, starting transfers between devices, hop(): lax.ppermute(ends[1], 'dp', down)  13.4 us
    ppermute x13, waiting for transfers between devices, swap(): return lax.ppermute(values, 'tensor', [(t, t ^ bit) for t in range(owners)])  11.8 us
    ppermute x2, starting transfers between devices, local(): arrived.append(lax.ppermute(held, ('dp', 'tensor'), moves))  9.75 us
  transfers between devices with their start and end apart: 55, of which 25 were waited for; matrix products, arithmetic and copies ran while one was open for 19% of the time, Pallas kernels for 1%

profile of v12, /device:TPU:0, one launch (start us, length us, event | category | flops | bytes accessed | tf_op | source)
XLA Modules:
  0.0 239.6 jit_solution(9580190847308660511)
XLA Ops:
  0.0 3.0 %collective-permute-start = (bf16[128,2048]{1,0:T(8,128)(2,1)}, bf16[128,2048]{1,0:T(8,128)(2,1)}, u32[]{:S(2)}, u32[]{:S(2)}) collective-permute-start(bf16[128,2048]{1,0:T(8,128)(2,1)} %param.7), channel_id=1, source_target_pairs={{0,8},{8,16},{16,24},{24,28},{28,20},{20,12},{12,4},{4,0},{1,9},{9... | collective-permute-start | bytes 1572872 | tf_op jit(solution)/shard_map/ppermute | solution.py:80
  5.1 11.0 %collective-permute-done = bf16[128,2048]{1,0:T(8,128)(2,1)} collective-permute-done((bf16[128,2048]{1,0:T(8,128)(2,1)}, bf16[128,2048]{1,0:T(8,128)(2,1)}, u32[]{:S(2)}, u32[]{:S(2)}) %collective-permute-start) | collective-permute-done | bytes 524320 | tf_op jit(solution)/shard_map/ppermute | solution.py:80
  18.1 8.2 %collective-permute-done.2 = bf16[128,2048]{1,0:T(8,128)(2,1)S(1)} collective-permute-done((bf16[128,2048]{1,0:T(8,128)(2,1)}, bf16[128,2048]{1,0:T(8,128)(2,1)S(1)}, u32[]{:S(2)}, u32[]{:S(2)}) %collective-permute-start.2) | collective-permute-done | bytes 524320 | tf_op jit(solution)/shard_map/ppermute | solution.py:80
  31.9 11.0 %collective-permute-done.4 = bf16[128,2048]{1,0:T(8,128)(2,1)S(1)} collective-permute-done((bf16[128,2048]{1,0:T(8,128)(2,1)}, bf16[128,2048]{1,0:T(8,128)(2,1)S(1)}, u32[]{:S(2)}, u32[]{:S(2)}) %collective-permute-start.4) | collective-permute-done | bytes 524320 | tf_op jit(solution)/shard_map/ppermute | solution.py:80
  44.3 3.6 %fusion.63 = f32[256,1024]{1,0:T(8,128)S(1)} fusion(bf16[2048,1024]{1,0:T(8,128)(2,1)} %param.11, bf16[128,2048]{1,0:T(8,128)(2,1)S(1)} %collective-permute-done.5, bf16[128,2048]{1,0:T(8,128)(2,1)S(1)} %collective-permute-done.4), kind=kOutput, calls=%fused_computation.48 | convolution fusion | flops 1075838976 | bytes 6291456 | tf_op jit(solution)/shard_map/dot_general | solution.py:104
  48.1 3.8 %collective-permute-done.6 = bf16[128,2048]{1,0:T(8,128)(2,1)} collective-permute-done((bf16[128,2048]{1,0:T(8,128)(2,1)S(1)}, bf16[128,2048]{1,0:T(8,128)(2,1)}, u32[]{:S(2)}, u32[]{:S(2)}) %collective-permute-start.6) | collective-permute-done | bytes 524320 | tf_op jit(solution)/shard_map/ppermute | solution.py:80
  57.1 11.1 %collective-permute-done.8 = bf16[128,2048]{1,0:T(8,128)(2,1)} collective-permute-done((bf16[128,2048]{1,0:T(8,128)(2,1)}, bf16[128,2048]{1,0:T(8,128)(2,1)}, u32[]{:S(2)}, u32[]{:S(2)}) %collective-permute-start.8) | collective-permute-done | bytes 524320 | tf_op jit(solution)/shard_map/ppermute | solution.py:80
  69.7 6.0 %collective-permute-done.10 = bf16[128,2048]{1,0:T(8,128)(2,1)S(1)} collective-permute-done((bf16[128,2048]{1,0:T(8,128)(2,1)}, bf16[128,2048]{1,0:T(8,128)(2,1)S(1)}, u32[]{:S(2)}, u32[]{:S(2)}) %collective-permute-start.10) | collective-permute-done | bytes 524320 | tf_op jit(solution)/shard_map/ppermute | solution.py:80
  81.1 4.0 %fusion.67 = f32[256,1024]{1,0:T(8,128)S(1)} fusion(bf16[2048,1024]{1,0:T(8,128)(2,1)} %param.11, bf16[128,2048]{1,0:T(8,128)(2,1)} %collective-permute-done, bf16[128,2048]{1,0:T(8,128)(2,1)} %collective-permute-done.9), kind=kOutput, calls=%fused_computation.52 | convolution fusion | flops 1075838976 | bytes 6291456 | tf_op jit(solution)/shard_map/dot_general | solution.py:104
  85.3 2.4 %fusion.71 = f32[256,1024]{1,0:T(8,128)S(1)} fusion(bf16[2048,1024]{1,0:T(8,128)(2,1)S(1)} %copy-done.20, bf16[128,2048]{1,0:T(8,128)(2,1)} %collective-permute-done.8, bf16[128,2048]{1,0:T(8,128)(2,1)S(1)} %copy-done.23), kind=kOutput, calls=%fused_computation.56 | convolution fusion | flops 1075838976 | bytes 6291456 | tf_op jit(solution)/shard_map/dot_general | solution.py:104
  97.6 7.9 %collective-permute-done.21 = bf16[128,2048]{1,0:T(8,128)(2,1)S(1)} collective-permute-done((bf16[128,2048]{1,0:T(8,128)(2,1)S(1)}, bf16[128,2048]{1,0:T(8,128)(2,1)S(1)}, u32[]{:S(2)}, u32[]{:S(2)}) %collective-permute-start.21) | collective-permute-done | bytes 524320 | tf_op jit(solution)/shard_map/ppermute | solution.py:80
  108.8 6.0 %collective-permute-done.17 = bf16[1,128,1024]{2,1,0:T(8,128)(2,1)S(1)} collective-permute-done((bf16[1,128,1024]{2,1,0:T(8,128)(2,1)S(1)}, bf16[1,128,1024]{2,1,0:T(8,128)(2,1)S(1)}, u32[]{:S(2)}, u32[]{:S(2)}) %collective-permute-start.17) | collective-permute-done | bytes 262176 | tf_op jit(solution)/shard_map/ppermute | solution.py:100
  117.9 7.9 %collective-permute-start.23 = (bf16[128,1024]{1,0:T(8,128)(2,1)S(1)}, bf16[128,1024]{1,0:T(8,128)(2,1)}, u32[]{:S(2)}, u32[]{:S(2)}) collective-permute-start(bf16[128,1024]{1,0:T(8,128)(2,1)S(1)} %fusion.97), channel_id=1, source_target_pairs={{0,28},{1,0},{2,12},{3,16},{8,21},{9,9},{10,5},{11,25},{16,14},{17... | collective-permute-start | bytes 786440 | tf_op jit(solution)/shard_map/ppermute | solution.py:163
  125.9 5.2 %fusion.12 = f32[3,128,1024]{2,1,0:T(8,128)} fusion(bf16[3,128,2048]{2,1,0:T(8,128)(2,1)S(1)} %bitcast.173, bf16[3,2048,1024]{2,1,0:T(8,128)(2,1)} %param.12), kind=kOutput, calls=%fused_computation.12 | convolution fusion | flops 1610612736 | bytes 7340032 | tf_op jit(solution)/shard_map/dot_general | solution.py:104
  138.0 4.5 %fusion.36 = f32[3,128,1024]{2,1,0:T(8,128)S(1)} fusion(f32[3,128,1024]{2,1,0:T(8,128)} %fusion.12, bf16[3,128,2048]{2,1,0:T(8,128)(2,1)S(1)} %bitcast.172, bf16[3,2048,1024]{2,1,0:T(8,128)(2,1)} %param.12), kind=kOutput, calls=%fused_computation.39 | convolution fusion | flops 1611005952 | bytes 8912896 | tf_op jit(solution)/shard_map/dot_general | solution.py:104
  142.5 3.2 %fusion.22 = f32[128,1024]{1,0:T(8,128)S(1)} fusion(bf16[3,2048,1024]{2,1,0:T(8,128)(2,1)} %param.12, bf16[64,2048]{1,0:T(8,128)(2,1)} %collective-permute-done.25, bf16[64,2048]{1,0:T(8,128)(2,1)} %collective-permute-done.24), kind=kOutput, calls=%fused_computation.22 | convolution fusion | flops 537919488 | bytes 5242880 | tf_op jit(solution)/shard_map/dot_general | solution.py:104
  145.7 3.2 %collective-permute-done.26 = bf16[128,2048]{1,0:T(8,128)(2,1)S(1)} collective-permute-done((bf16[128,2048]{1,0:T(8,128)(2,1)}, bf16[128,2048]{1,0:T(8,128)(2,1)S(1)}, u32[]{:S(2)}, u32[]{:S(2)}) %collective-permute-start.26) | collective-permute-done | bytes 524320 | tf_op jit(solution)/shard_map/ppermute | solution.py:80
  150.8 9.1 %collective-permute-done.28 = bf16[128,2048]{1,0:T(8,128)(2,1)S(1)} collective-permute-done((bf16[128,2048]{1,0:T(8,128)(2,1)S(1)}, bf16[128,2048]{1,0:T(8,128)(2,1)S(1)}, u32[]{:S(2)}, u32[]{:S(2)}) %collective-permute-start.28) | collective-permute-done | bytes 524320 | tf_op jit(solution)/shard_map/ppermute | solution.py:80
  164.2 4.2 %fusion.39 = f32[3,128,1024]{2,1,0:T(8,128)S(1)} fusion(f32[3,128,1024]{2,1,0:T(8,128)S(1)} %fusion.36, bf16[3,128,2048]{2,1,0:T(8,128)(2,1)S(1)} %bitcast.175, bf16[3,2048,1024]{2,1,0:T(8,128)(2,1)} %param.12), kind=kOutput, calls=%fused_computation.40 | convolution fusion | flops 1611005952 | bytes 8912896 | tf_op jit(solution)/shard_map/dot_general | solution.py:104
  171.4 13.4 %collective-permute-done.32 = bf16[128,2048]{1,0:T(8,128)(2,1)S(1)} collective-permute-done((bf16[128,2048]{1,0:T(8,128)(2,1)S(1)}, bf16[128,2048]{1,0:T(8,128)(2,1)S(1)}, u32[]{:S(2)}, u32[]{:S(2)}) %collective-permute-start.32) | collective-permute-done | bytes 524320 | tf_op jit(solution)/shard_map/ppermute | solution.py:80
  192.6 3.1 %collective-permute-done.40 = bf16[3,1,32,1024]{3,2,0,1:T(8,128)(2,1)S(1)} collective-permute-done((bf16[3,1,32,1024]{3,2,0,1:T(8,128)(2,1)S(1)}, bf16[3,1,32,1024]{3,2,0,1:T(8,128)(2,1)S(1)}, u32[]{:S(2)}, u32[]{:S(2)}) %collective-permute-start.40) | collective-permute-done | bytes 196640 | tf_op jit(solution)/shard_map/ppermute | solution.py:100
  198.6 8.0 %collective-permute-done.42 = bf16[64,2048]{1,0:T(8,128)(2,1)S(1)} collective-permute-done((bf16[64,2048]{1,0:T(8,128)(2,1)S(1)}, bf16[64,2048]{1,0:T(8,128)(2,1)S(1)}, u32[]{:S(2)}, u32[]{:S(2)}) %collective-permute-start.42) | collective-permute-done | bytes 262176 | tf_op jit(solution)/shard_map/ppermute | solution.py:80
  216.8 2.4 collective-permute-start.46
  222.8 3.5 %collective-permute-start.53 = (bf16[32,1024]{1,0:T(8,128)(2,1)S(1)}, bf16[32,1024]{1,0:T(8,128)(2,1)S(1)}, u32[]{:S(2)}, u32[]{:S(2)}) collective-permute-start(bf16[32,1024]{1,0:T(8,128)(2,1)S(1)} %get-tuple-element.150), channel_id=1, source_target_pairs={{0,28},{1,29},{2,30},{3,31},{8,20},{9,21},{10,22},{11,23},{16,12},... | collective-permute-start | bytes 196616 | tf_op jit(solution)/shard_map/ppermute | solution.py:199
  (213 shorter events, 93.0 us)
Async XLA Ops:
  0.0 16.0 %collective-permute-start = (bf16[128,2048]{1,0:T(8,128)(2,1)}, bf16[128,2048]{1,0:T(8,128)(2,1)}, u32[]{:S(2)}, u32[]{:S(2)}) collective-permute-start(bf16[128,2048]{1,0:T(8,128)(2,1)} %param.7), channel_id=1, source_target_pairs={{0,8},{8,16},{16,24},{24,28},{28,20},{20,12},{12,4},{4,0},{1,9},{9... | collective-permute-start | bytes 1572872 | tf_op jit(solution)/shard_map/ppermute | solution.py:80
  3.0 23.3 %collective-permute-start.2 = (bf16[128,2048]{1,0:T(8,128)(2,1)}, bf16[128,2048]{1,0:T(8,128)(2,1)S(1)}, u32[]{:S(2)}, u32[]{:S(2)}) collective-permute-start(bf16[128,2048]{1,0:T(8,128)(2,1)} %param.9), channel_id=1, source_target_pairs={{0,8},{8,16},{16,24},{24,28},{28,20},{20,12},{12,4},{4,0},{1,9},{9... | collective-permute-start | bytes 1572872 | tf_op jit(solution)/shard_map/ppermute | solution.py:80
  5.1 22.8 %collective-permute-start.3 = (bf16[128,2048]{1,0:T(8,128)(2,1)}, bf16[128,2048]{1,0:T(8,128)(2,1)S(1)}, u32[]{:S(2)}, u32[]{:S(2)}) collective-permute-start(bf16[128,2048]{1,0:T(8,128)(2,1)} %param.9), channel_id=1, source_target_pairs={{8,0},{16,8},{24,16},{28,24},{20,28},{12,20},{4,12},{0,4},{9,1},{1... | collective-permute-start | bytes 1572872 | tf_op jit(solution)/shard_map/ppermute | solution.py:80
  27.9 15.1 %collective-permute-start.4 = (bf16[128,2048]{1,0:T(8,128)(2,1)}, bf16[128,2048]{1,0:T(8,128)(2,1)S(1)}, u32[]{:S(2)}, u32[]{:S(2)}) collective-permute-start(bf16[128,2048]{1,0:T(8,128)(2,1)} %collective-permute-done), channel_id=1, source_target_pairs={{0,8},{8,16},{16,24},{24,28},{28,20},{20,12},{12,4},{4,0},{1,9},{9... | collective-permute-start | bytes 1572872 | tf_op jit(solution)/shard_map/ppermute | solution.py:80
  29.9 22.0 %collective-permute-start.6 = (bf16[128,2048]{1,0:T(8,128)(2,1)S(1)}, bf16[128,2048]{1,0:T(8,128)(2,1)}, u32[]{:S(2)}, u32[]{:S(2)}) collective-permute-start(bf16[128,2048]{1,0:T(8,128)(2,1)S(1)} %collective-permute-done.2), channel_id=1, source_target_pairs={{0,8},{8,16},{16,24},{24,28},{28,20},{20,12},{12,4},{4,0},{1,9},{9... | collective-permute-start | bytes 1572872 | tf_op jit(solution)/shard_map/ppermute | solution.py:80
  31.5 21.5 %collective-permute-start.7 = (bf16[128,2048]{1,0:T(8,128)(2,1)S(1)}, bf16[128,2048]{1,0:T(8,128)(2,1)}, u32[]{:S(2)}, u32[]{:S(2)}) collective-permute-start(bf16[128,2048]{1,0:T(8,128)(2,1)S(1)} %collective-permute-done.3), channel_id=1, source_target_pairs={{8,0},{16,8},{24,16},{28,24},{20,28},{12,20},{4,12},{0,4},{9,1},{1... | collective-permute-start | bytes 1572872 | tf_op jit(solution)/shard_map/ppermute | solution.py:80
  53.0 15.2 %collective-permute-start.8 = (bf16[128,2048]{1,0:T(8,128)(2,1)}, bf16[128,2048]{1,0:T(8,128)(2,1)}, u32[]{:S(2)}, u32[]{:S(2)}) collective-permute-start(bf16[128,2048]{1,0:T(8,128)(2,1)} %copy-done.24), channel_id=1, source_target_pairs={{0,8},{8,16},{16,24},{24,28},{28,20},{20,12},{12,4},{4,0},{1,9},{9... | collective-permute-start | bytes 1572872 | tf_op jit(solution)/shard_map/ppermute | solution.py:80
  54.5 15.2 %collective-permute-start.9 = (bf16[128,2048]{1,0:T(8,128)(2,1)}, bf16[128,2048]{1,0:T(8,128)(2,1)}, u32[]{:S(2)}, u32[]{:S(2)}) collective-permute-start(bf16[128,2048]{1,0:T(8,128)(2,1)} %copy-done.25), channel_id=1, source_target_pairs={{8,0},{16,8},{24,16},{28,24},{20,28},{12,20},{4,12},{0,4},{9,1},{1... | collective-permute-start | bytes 1572872 | tf_op jit(solution)/shard_map/ppermute | solution.py:80
  55.0 20.7 %collective-permute-start.10 = (bf16[128,2048]{1,0:T(8,128)(2,1)}, bf16[128,2048]{1,0:T(8,128)(2,1)S(1)}, u32[]{:S(2)}, u32[]{:S(2)}) collective-permute-start(bf16[128,2048]{1,0:T(8,128)(2,1)} %collective-permute-done.6), channel_id=1, source_target_pairs={{0,8},{8,16},{16,24},{24,28},{28,20},{20,12},{12,4},{4,0},{1,9},{9... | collective-permute-start | bytes 1572872 | tf_op jit(solution)/shard_map/ppermute | solution.py:80
  56.6 20.4 %collective-permute-start.11 = (bf16[128,2048]{1,0:T(8,128)(2,1)}, bf16[128,2048]{1,0:T(8,128)(2,1)S(1)}, u32[]{:S(2)}, u32[]{:S(2)}) collective-permute-start(bf16[128,2048]{1,0:T(8,128)(2,1)} %collective-permute-done.7), channel_id=1, source_target_pairs={{8,0},{16,8},{24,16},{28,24},{20,28},{12,20},{4,12},{0,4},{9,1},{1... | collective-permute-start | bytes 1572872 | tf_op jit(solution)/shard_map/ppermute | solution.py:80
  95.4 38.5 %collective-permute-start.24 = (bf16[64,2048]{1,0:T(8,128)(2,1)S(1)}, bf16[64,2048]{1,0:T(8,128)(2,1)}, u32[]{:S(2)}, u32[]{:S(2)}) collective-permute-start(bf16[64,2048]{1,0:T(8,128)(2,1)S(1)} %slice.73), channel_id=1, source_target_pairs={{0,8},{8,16},{16,24},{24,28},{28,20},{20,12},{12,4},{4,0},{1,9},{9... | collective-permute-start | bytes 786440 | tf_op jit(solution)/shard_map/ppermute | solution.py:80
  96.9 37.0 %collective-permute-start.25 = (bf16[64,2048]{1,0:T(8,128)(2,1)S(1)}, bf16[64,2048]{1,0:T(8,128)(2,1)}, u32[]{:S(2)}, u32[]{:S(2)}) collective-permute-start(bf16[64,2048]{1,0:T(8,128)(2,1)S(1)} %slice.74), channel_id=1, source_target_pairs={{8,0},{16,8},{24,16},{28,24},{20,28},{12,20},{4,12},{0,4},{9,1},{1... | collective-permute-start | bytes 786440 | tf_op jit(solution)/shard_map/ppermute | solution.py:80
  114.9 16.2 %collective-permute-start.18 = (bf16[128,1024]{1,0:T(8,128)(2,1)S(1)}, bf16[128,1024]{1,0:T(8,128)(2,1)S(1)}, u32[]{:S(2)}, u32[]{:S(2)}) collective-permute-start(bf16[128,1024]{1,0:T(8,128)(2,1)S(1)} %fusion.98), channel_id=1, source_target_pairs={{0,24},{1,4},{2,8},{3,20},{8,29},{9,1},{10,17},{11,13},{16,22},{17... | collective-permute-start | bytes 786440 | tf_op jit(solution)/shard_map/ppermute | solution.py:163
  135.7 15.1 %collective-permute-start.27 = (bf16[128,2048]{1,0:T(8,128)(2,1)}, bf16[128,2048]{1,0:T(8,128)(2,1)S(1)}, u32[]{:S(2)}, u32[]{:S(2)}) collective-permute-start(bf16[128,2048]{1,0:T(8,128)(2,1)} %add_residual.1), channel_id=1, source_target_pairs={{8,0},{16,8},{24,16},{28,24},{20,28},{12,20},{4,12},{0,4},{9,1},{1... | collective-permute-start | bytes 1572872 | tf_op jit(solution)/shard_map/ppermute | solution.py:80
  136.0 24.0 %collective-permute-start.28 = (bf16[128,2048]{1,0:T(8,128)(2,1)S(1)}, bf16[128,2048]{1,0:T(8,128)(2,1)S(1)}, u32[]{:S(2)}, u32[]{:S(2)}) collective-permute-start(bf16[128,2048]{1,0:T(8,128)(2,1)S(1)} %collective-permute-done.21), channel_id=1, source_target_pairs={{0,8},{8,16},{16,24},{24,28},{28,20},{20,12},{12,4},{4,0},{1,9},{9... | collective-permute-start | bytes 1572872 | tf_op jit(solution)/shard_map/ppermute | solution.py:80
  137.8 22.1 %collective-permute-start.29 = (bf16[128,2048]{1,0:T(8,128)(2,1)S(1)}, bf16[128,2048]{1,0:T(8,128)(2,1)S(1)}, u32[]{:S(2)}, u32[]{:S(2)}) collective-permute-start(bf16[128,2048]{1,0:T(8,128)(2,1)S(1)} %copy-done.6), channel_id=1, source_target_pairs={{8,0},{16,8},{24,16},{28,24},{20,28},{12,20},{4,12},{0,4},{9,1},{1... | collective-permute-start | bytes 1572872 | tf_op jit(solution)/shard_map/ppermute | solution.py:80
  159.9 26.3 %collective-permute-start.30 = (bf16[128,2048]{1,0:T(8,128)(2,1)S(1)}, bf16[128,2048]{1,0:T(8,128)(2,1)S(1)}, u32[]{:S(2)}, u32[]{:S(2)}) collective-permute-start(bf16[128,2048]{1,0:T(8,128)(2,1)S(1)} %collective-permute-done.26), channel_id=1, source_target_pairs={{0,8},{8,16},{16,24},{24,28},{28,20},{20,12},{12,4},{4,0},{1,9},{9... | collective-permute-start | bytes 1572872 | tf_op jit(solution)/shard_map/ppermute | solution.py:80
  159.9 26.3 %collective-permute-start.31 = (bf16[128,2048]{1,0:T(8,128)(2,1)S(1)}, bf16[128,2048]{1,0:T(8,128)(2,1)S(1)}, u32[]{:S(2)}, u32[]{:S(2)}) collective-permute-start(bf16[128,2048]{1,0:T(8,128)(2,1)S(1)} %collective-permute-done.27), channel_id=1, source_target_pairs={{8,0},{16,8},{24,16},{28,24},{20,28},{12,20},{4,12},{0,4},{9,1},{1... | collective-permute-start | bytes 1572872 | tf_op jit(solution)/shard_map/ppermute | solution.py:80
  161.9 22.9 %collective-permute-start.32 = (bf16[128,2048]{1,0:T(8,128)(2,1)S(1)}, bf16[128,2048]{1,0:T(8,128)(2,1)S(1)}, u32[]{:S(2)}, u32[]{:S(2)}) collective-permute-start(bf16[128,2048]{1,0:T(8,128)(2,1)S(1)} %collective-permute-done.28), channel_id=1, source_target_pairs={{0,8},{8,16},{16,24},{24,28},{28,20},{20,12},{12,4},{4,0},{1,9},{9... | collective-permute-start | bytes 1572872 | tf_op jit(solution)/shard_map/ppermute | solution.py:80
  162.0 22.9 %collective-permute-start.33 = (bf16[128,2048]{1,0:T(8,128)(2,1)S(1)}, bf16[128,2048]{1,0:T(8,128)(2,1)S(1)}, u32[]{:S(2)}, u32[]{:S(2)}) collective-permute-start(bf16[128,2048]{1,0:T(8,128)(2,1)S(1)} %collective-permute-done.29), channel_id=1, source_target_pairs={{8,0},{16,8},{24,16},{28,24},{20,28},{12,20},{4,12},{0,4},{9,1},{1... | collective-permute-start | bytes 1572872 | tf_op jit(solution)/shard_map/ppermute | solution.py:80
  168.5 19.1 %collective-permute-start.34 = (f32[3,2,32,1024]{3,2,0,1:T(8,128)S(1)}, f32[3,2,32,1024]{3,2,0,1:T(8,128)S(1)}, u32[]{:S(2)}, u32[]{:S(2)}) collective-permute-start(f32[3,2,32,1024]{3,2,0,1:T(8,128)S(1)} %bitcast.191), channel_id=1, source_target_pairs={{0,1},{1,0},{2,3},{3,2},{4,5},{5,4},{6,7},{7,6},{8,9},{9,8},{10,11... | collective-permute-start | bytes 2359304 | tf_op jit(solution)/shard_map/ppermute | solution.py:100
  187.8 21.7 %collective-permute-start.35 = (bf16[128,2048]{1,0:T(8,128)(2,1)S(1)}, bf16[128,2048]{1,0:T(8,128)(2,1)S(1)}, u32[]{:S(2)}, u32[]{:S(2)}) collective-permute-start(bf16[128,2048]{1,0:T(8,128)(2,1)S(1)} %collective-permute-done.30), channel_id=1, source_target_pairs={{0,8},{8,16},{16,24},{24,28},{28,20},{20,12},{12,4},{4,0},{1,9},{9... | collective-permute-start | bytes 1572872 | tf_op jit(solution)/shard_map/ppermute | solution.py:80
  188.1 21.4 %collective-permute-start.36 = (bf16[128,2048]{1,0:T(8,128)(2,1)S(1)}, bf16[128,2048]{1,0:T(8,128)(2,1)S(1)}, u32[]{:S(2)}, u32[]{:S(2)}) collective-permute-start(bf16[128,2048]{1,0:T(8,128)(2,1)S(1)} %collective-permute-done.31), channel_id=1, source_target_pairs={{8,0},{16,8},{24,16},{28,24},{20,28},{12,20},{4,12},{0,4},{9,1},{1... | collective-permute-start | bytes 1572872 | tf_op jit(solution)/shard_map/ppermute | solution.py:80
  192.5 16.9 %collective-permute-start.37 = (f32[2,2,32,1024]{3,2,0,1:T(8,128)S(1)}, f32[2,2,32,1024]{3,2,0,1:T(8,128)S(1)}, u32[]{:S(2)}, u32[]{:S(2)}) collective-permute-start(f32[2,2,32,1024]{3,2,0,1:T(8,128)S(1)} %bitcast.194), channel_id=1, source_target_pairs={{0,1},{1,0},{2,3},{3,2},{4,5},{5,4},{6,7},{7,6},{8,9},{9,8},{10,11... | collective-permute-start | bytes 1572872 | tf_op jit(solution)/shard_map/ppermute | solution.py:100
  (60 other events, 531.9 us)

commit v13 on v12

--- a/solution.py
+++ b/solution.py
@@ -133,8 +133,6 @@
         attn.hop()
         (mid if hop == last else low).hop()
         sum_cores(multiply_pairs(hop - 1))
-    low.ends, attn.ends = tie(low.ends, attn.ends)
-    low.hop()
     attn.slots[last], pair_sums = tie(attn.ends, pair_sums)
     sum_cores(multiply_pairs(last))
 
@@ -154,7 +152,8 @@
     for kind in classes:
         held = sum_xs(pair_sums[kind]).astype(jnp.bfloat16)
         if kind == classes[-1]:
-            held, mid.ends = tie(held, mid.ends)
+            held, mid.ends, low.ends = tie(held, mid.ends, low.ends)
+            low.hop()
         moves = [
             (d * owners + t, ring[(p - kept[kind][t]) % groups] * owners + d // per_owner)
             for p, d in enumerate(ring)

time: 240 us -> 230 us (0.958)
  waiting for transfers between devices: 120 us -> 115 us
    ppermute x16, waiting for transfers between devices: 84.7 us -> 70.5 us  [hop(): lax.ppermute(ends[0], 'dp', up)]
    ppermute x16, waiting for transfers between devices: 18.8 us -> 28.9 us  [hop(): lax.ppermute(ends[1], 'dp', down)]
  transfers between devices with their start and end apart: 55 -> 55, of which waited for: 25 -> 26; matrix products, arithmetic and copies ran while one was open for 19% -> 19% of each run, Pallas kernels for 1% -> 1%
where the time goes in v13:
time: 230 us; the launch traced here: 229 us
  waiting for transfers between devices  115 us (50%)
  starting transfers between devices  65 us (28%)
  matrix products  35.8 us (16%)
  other arithmetic  5 us (2%)
  Pallas kernels  4.41 us (2%)
  local copies, waits for them, and re-layouts  2.9 us (1%)
    ppermute x16, waiting for transfers between devices, hop(): lax.ppermute(ends[0], 'dp', up)  70.5 us
    dot_general x16, matrix products, product(): jnp.dot(rows_in, weight, preferred_element_type=jnp.float32)  35.8 us
    ppermute x16, waiting for transfers between devices, hop(): lax.ppermute(ends[1], 'dp', down)  28.9 us
    ppermute x16, starting transfers between devices, hop(): lax.ppermute(ends[0], 'dp', up)  21 us
    ppermute x8, starting transfers between devices, send(): return lax.ppermute(part.astype(jnp.bfloat16), ('dp', 'tensor'), moves)  14.3 us
    ppermute x16, starting transfers between devices, hop(): lax.ppermute(ends[1], 'dp', down)  12.8 us
    ppermute x13, waiting for transfers between devices, swap(): return lax.ppermute(values, 'tensor', [(t, t ^ bit) for t in range(owners)])  10.4 us
    ppermute x2, starting transfers between devices, local(): arrived.append(lax.ppermute(held, ('dp', 'tensor'), moves))  8.88 us
  transfers between devices with their start and end apart: 55, of which 26 were waited for; matrix products, arithmetic and copies ran while one was open for 19% of the time, Pallas kernels for 1%

profile of v13, /device:TPU:0, one launch (start us, length us, event | category | flops | bytes accessed | tf_op | source)
XLA Modules:
  0.0 229.2 jit_solution(15739531859347215432)
XLA Ops:
  0.0 3.0 %collective-permute-start = (bf16[128,2048]{1,0:T(8,128)(2,1)}, bf16[128,2048]{1,0:T(8,128)(2,1)}, u32[]{:S(2)}, u32[]{:S(2)}) collective-permute-start(bf16[128,2048]{1,0:T(8,128)(2,1)} %param.7), channel_id=1, source_target_pairs={{0,8},{8,16},{16,24},{24,28},{28,20},{20,12},{12,4},{4,0},{1,9},{9... | collective-permute-start | bytes 1572872 | tf_op jit(solution)/shard_map/ppermute | solution.py:80
  5.1 11.0 %collective-permute-done = bf16[128,2048]{1,0:T(8,128)(2,1)} collective-permute-done((bf16[128,2048]{1,0:T(8,128)(2,1)}, bf16[128,2048]{1,0:T(8,128)(2,1)}, u32[]{:S(2)}, u32[]{:S(2)}) %collective-permute-start) | collective-permute-done | bytes 524320 | tf_op jit(solution)/shard_map/ppermute | solution.py:80
  18.2 8.1 %collective-permute-done.2 = bf16[128,2048]{1,0:T(8,128)(2,1)S(1)} collective-permute-done((bf16[128,2048]{1,0:T(8,128)(2,1)}, bf16[128,2048]{1,0:T(8,128)(2,1)S(1)}, u32[]{:S(2)}, u32[]{:S(2)}) %collective-permute-start.2) | collective-permute-done | bytes 524320 | tf_op jit(solution)/shard_map/ppermute | solution.py:80
  33.1 9.9 %collective-permute-done.4 = bf16[128,2048]{1,0:T(8,128)(2,1)} collective-permute-done((bf16[128,2048]{1,0:T(8,128)(2,1)}, bf16[128,2048]{1,0:T(8,128)(2,1)}, u32[]{:S(2)}, u32[]{:S(2)}) %collective-permute-start.4) | collective-permute-done | bytes 524320 | tf_op jit(solution)/shard_map/ppermute | solution.py:80
  44.6 7.2 %collective-permute-done.6 = bf16[128,2048]{1,0:T(8,128)(2,1)S(1)} collective-permute-done((bf16[128,2048]{1,0:T(8,128)(2,1)S(1)}, bf16[128,2048]{1,0:T(8,128)(2,1)S(1)}, u32[]{:S(2)}, u32[]{:S(2)}) %collective-permute-start.6) | collective-permute-done | bytes 524320 | tf_op jit(solution)/shard_map/ppermute | solution.py:80
  57.2 3.8 %fusion.63 = f32[256,1024]{1,0:T(8,128)S(1)} fusion(bf16[2048,1024]{1,0:T(8,128)(2,1)} %param.11, bf16[128,2048]{1,0:T(8,128)(2,1)} %collective-permute-done.5, bf16[128,2048]{1,0:T(8,128)(2,1)} %collective-permute-done.4), kind=kOutput, calls=%fused_computation.48 | convolution fusion | flops 1075838976 | bytes 6291456 | tf_op jit(solution)/shard_map/dot_general | solution.py:104
  61.1 8.7 %collective-permute-done.9 = bf16[128,2048]{1,0:T(8,128)(2,1)S(1)} collective-permute-done((bf16[128,2048]{1,0:T(8,128)(2,1)}, bf16[128,2048]{1,0:T(8,128)(2,1)S(1)}, u32[]{:S(2)}, u32[]{:S(2)}) %collective-permute-start.9) | collective-permute-done | bytes 524320 | tf_op jit(solution)/shard_map/ppermute | solution.py:80
  81.6 5.0 %collective-permute-done.13 = bf16[64,2048]{1,0:T(8,128)(2,1)S(1)} collective-permute-done((bf16[64,2048]{1,0:T(8,128)(2,1)S(1)}, bf16[64,2048]{1,0:T(8,128)(2,1)S(1)}, u32[]{:S(2)}, u32[]{:S(2)}) %collective-permute-start.13) | collective-permute-done | bytes 262176 | tf_op jit(solution)/shard_map/ppermute | solution.py:80
  92.2 3.9 %collective-permute-done.21 = bf16[128,2048]{1,0:T(8,128)(2,1)S(1)} collective-permute-done((bf16[128,2048]{1,0:T(8,128)(2,1)S(1)}, bf16[128,2048]{1,0:T(8,128)(2,1)S(1)}, u32[]{:S(2)}, u32[]{:S(2)}) %collective-permute-start.21) | collective-permute-done | bytes 524320 | tf_op jit(solution)/shard_map/ppermute | solution.py:80
  100.6 4.4 %collective-permute-done.20 = bf16[1,128,1024]{2,1,0:T(8,128)(2,1)S(1)} collective-permute-done((bf16[1,128,1024]{2,1,0:T(8,128)(2,1)S(1)}, bf16[1,128,1024]{2,1,0:T(8,128)(2,1)S(1)}, u32[]{:S(2)}, u32[]{:S(2)}) %collective-permute-start.20) | collective-permute-done | bytes 262176 | tf_op jit(solution)/shard_map/ppermute | solution.py:100
  105.2 8.2 %collective-permute-start.23 = (bf16[128,1024]{1,0:T(8,128)(2,1)S(1)}, bf16[128,1024]{1,0:T(8,128)(2,1)}, u32[]{:S(2)}, u32[]{:S(2)}) collective-permute-start(bf16[128,1024]{1,0:T(8,128)(2,1)S(1)} %fusion.97), channel_id=1, source_target_pairs={{0,28},{1,0},{2,12},{3,16},{8,21},{9,9},{10,5},{11,25},{16,14},{17... | collective-permute-start | bytes 786440 | tf_op jit(solution)/shard_map/ppermute | solution.py:162
  116.2 5.2 %fusion.12 = f32[3,128,1024]{2,1,0:T(8,128)} fusion(bf16[3,128,2048]{2,1,0:T(8,128)(2,1)S(1)} %bitcast.173, bf16[3,2048,1024]{2,1,0:T(8,128)(2,1)} %param.12), kind=kOutput, calls=%fused_computation.12 | convolution fusion | flops 1610612736 | bytes 7340032 | tf_op jit(solution)/shard_map/dot_general | solution.py:104
  127.6 4.5 %fusion.36 = f32[3,128,1024]{2,1,0:T(8,128)S(1)} fusion(f32[3,128,1024]{2,1,0:T(8,128)} %fusion.12, bf16[3,128,2048]{2,1,0:T(8,128)(2,1)S(1)} %bitcast.172, bf16[3,2048,1024]{2,1,0:T(8,128)(2,1)} %param.12), kind=kOutput, calls=%fused_computation.39 | convolution fusion | flops 1611005952 | bytes 8912896 | tf_op jit(solution)/shard_map/dot_general | solution.py:104
  132.1 3.2 %fusion.22 = f32[128,1024]{1,0:T(8,128)S(1)} fusion(bf16[3,2048,1024]{2,1,0:T(8,128)(2,1)} %param.12, bf16[64,2048]{1,0:T(8,128)(2,1)} %collective-permute-done.25, bf16[64,2048]{1,0:T(8,128)(2,1)} %collective-permute-done.24), kind=kOutput, calls=%fused_computation.22 | convolution fusion | flops 537919488 | bytes 5242880 | tf_op jit(solution)/shard_map/dot_general | solution.py:104
  135.3 3.2 %collective-permute-done.26 = bf16[128,2048]{1,0:T(8,128)(2,1)S(1)} collective-permute-done((bf16[128,2048]{1,0:T(8,128)(2,1)}, bf16[128,2048]{1,0:T(8,128)(2,1)S(1)}, u32[]{:S(2)}, u32[]{:S(2)}) %collective-permute-start.26) | collective-permute-done | bytes 524320 | tf_op jit(solution)/shard_map/ppermute | solution.py:80
  140.5 8.6 %collective-permute-done.28 = bf16[128,2048]{1,0:T(8,128)(2,1)S(1)} collective-permute-done((bf16[128,2048]{1,0:T(8,128)(2,1)S(1)}, bf16[128,2048]{1,0:T(8,128)(2,1)S(1)}, u32[]{:S(2)}, u32[]{:S(2)}) %collective-permute-start.28) | collective-permute-done | bytes 524320 | tf_op jit(solution)/shard_map/ppermute | solution.py:80
  153.3 4.2 %fusion.39 = f32[3,128,1024]{2,1,0:T(8,128)S(1)} fusion(f32[3,128,1024]{2,1,0:T(8,128)S(1)} %fusion.36, bf16[3,128,2048]{2,1,0:T(8,128)(2,1)S(1)} %bitcast.175, bf16[3,2048,1024]{2,1,0:T(8,128)(2,1)} %param.12), kind=kOutput, calls=%fused_computation.40 | convolution fusion | flops 1611005952 | bytes 8912896 | tf_op jit(solution)/shard_map/dot_general | solution.py:104
  160.5 13.7 %collective-permute-done.32 = bf16[128,2048]{1,0:T(8,128)(2,1)S(1)} collective-permute-done((bf16[128,2048]{1,0:T(8,128)(2,1)S(1)}, bf16[128,2048]{1,0:T(8,128)(2,1)S(1)}, u32[]{:S(2)}, u32[]{:S(2)}) %collective-permute-start.32) | collective-permute-done | bytes 524320 | tf_op jit(solution)/shard_map/ppermute | solution.py:80
  182.3 2.6 %collective-permute-done.40 = bf16[3,1,32,1024]{3,2,0,1:T(8,128)(2,1)S(1)} collective-permute-done((bf16[3,1,32,1024]{3,2,0,1:T(8,128)(2,1)S(1)}, bf16[3,1,32,1024]{3,2,0,1:T(8,128)(2,1)S(1)}, u32[]{:S(2)}, u32[]{:S(2)}) %collective-permute-start.40) | collective-permute-done | bytes 196640 | tf_op jit(solution)/shard_map/ppermute | solution.py:100
  187.9 8.0 %collective-permute-done.42 = bf16[64,2048]{1,0:T(8,128)(2,1)S(1)} collective-permute-done((bf16[64,2048]{1,0:T(8,128)(2,1)S(1)}, bf16[64,2048]{1,0:T(8,128)(2,1)S(1)}, u32[]{:S(2)}, u32[]{:S(2)}) %collective-permute-start.42) | collective-permute-done | bytes 262176 | tf_op jit(solution)/shard_map/ppermute | solution.py:80
  206.0 2.8 %collective-permute-start.46 = (bf16[32,1024]{1,0:T(8,128)(2,1)S(1)}, bf16[32,1024]{1,0:T(8,128)(2,1)S(1)}, u32[]{:S(2)}, u32[]{:S(2)}) collective-permute-start(bf16[32,1024]{1,0:T(8,128)(2,1)S(1)} %get-tuple-element.150), channel_id=1, source_target_pairs={{0,12},{1,13},{2,14},{3,15},{8,4},{9,5},{10,6},{11,7},{16,0},{17,1... | collective-permute-start | bytes 196616 | tf_op jit(solution)/shard_map/ppermute | solution.py:198
  211.7 4.4 %collective-permute-start.53 = (bf16[32,1024]{1,0:T(8,128)(2,1)S(1)}, bf16[32,1024]{1,0:T(8,128)(2,1)S(1)}, u32[]{:S(2)}, u32[]{:S(2)}) collective-permute-start(bf16[32,1024]{1,0:T(8,128)(2,1)S(1)} %get-tuple-element.146), channel_id=1, source_target_pairs={{0,28},{1,29},{2,30},{3,31},{8,20},{9,21},{10,22},{11,23},{16,12},... | collective-permute-start | bytes 196616 | tf_op jit(solution)/shard_map/ppermute | solution.py:198
  216.9 2.8 %collective-permute-start.50 = (bf16[32,1024]{1,0:T(8,128)(2,1)S(1)}, bf16[32,1024]{1,0:T(8,128)(2,1)S(1)}, u32[]{:S(2)}, u32[]{:S(2)}) collective-permute-start(bf16[32,1024]{1,0:T(8,128)(2,1)S(1)} %get-tuple-element.148), channel_id=1, source_target_pairs={{0,20},{1,21},{2,22},{3,23},{8,12},{9,13},{10,14},{11,15},{16,4},{... | collective-permute-start | bytes 196616 | tf_op jit(solution)/shard_map/ppermute | solution.py:198
  220.9 3.4 %collective-permute-done.54.refs_8_ = bf16[32,1024]{1,0:T(8,128)(2,1)S(1)} collective-permute-done((bf16[32,1024]{1,0:T(8,128)(2,1)S(1)}, bf16[32,1024]{1,0:T(8,128)(2,1)S(1)}, u32[]{:S(2)}, u32[]{:S(2)}) %collective-permute-start.54) | collective-permute-done | bytes 65568 | tf_op jit(solution)/shard_map/ppermute | solution.py:198
  (189 shorter events, 88.9 us)
Async XLA Ops:
  0.0 16.0 %collective-permute-start = (bf16[128,2048]{1,0:T(8,128)(2,1)}, bf16[128,2048]{1,0:T(8,128)(2,1)}, u32[]{:S(2)}, u32[]{:S(2)}) collective-permute-start(bf16[128,2048]{1,0:T(8,128)(2,1)} %param.7), channel_id=1, source_target_pairs={{0,8},{8,16},{16,24},{24,28},{28,20},{20,12},{12,4},{4,0},{1,9},{9... | collective-permute-start | bytes 1572872 | tf_op jit(solution)/shard_map/ppermute | solution.py:80
  3.0 23.3 %collective-permute-start.2 = (bf16[128,2048]{1,0:T(8,128)(2,1)}, bf16[128,2048]{1,0:T(8,128)(2,1)S(1)}, u32[]{:S(2)}, u32[]{:S(2)}) collective-permute-start(bf16[128,2048]{1,0:T(8,128)(2,1)} %param.9), channel_id=1, source_target_pairs={{0,8},{8,16},{16,24},{24,28},{28,20},{20,12},{12,4},{4,0},{1,9},{9... | collective-permute-start | bytes 1572872 | tf_op jit(solution)/shard_map/ppermute | solution.py:80
  5.1 22.8 %collective-permute-start.3 = (bf16[128,2048]{1,0:T(8,128)(2,1)}, bf16[128,2048]{1,0:T(8,128)(2,1)S(1)}, u32[]{:S(2)}, u32[]{:S(2)}) collective-permute-start(bf16[128,2048]{1,0:T(8,128)(2,1)} %param.9), channel_id=1, source_target_pairs={{8,0},{16,8},{24,16},{28,24},{20,28},{12,20},{4,12},{0,4},{9,1},{1... | collective-permute-start | bytes 1572872 | tf_op jit(solution)/shard_map/ppermute | solution.py:80
  29.9 21.9 %collective-permute-start.6 = (bf16[128,2048]{1,0:T(8,128)(2,1)S(1)}, bf16[128,2048]{1,0:T(8,128)(2,1)S(1)}, u32[]{:S(2)}, u32[]{:S(2)}) collective-permute-start(bf16[128,2048]{1,0:T(8,128)(2,1)S(1)} %collective-permute-done.2), channel_id=1, source_target_pairs={{0,8},{8,16},{16,24},{24,28},{28,20},{20,12},{12,4},{4,0},{1,9},{9... | collective-permute-start | bytes 1572872 | tf_op jit(solution)/shard_map/ppermute | solution.py:80
  31.5 21.7 %collective-permute-start.7 = (bf16[128,2048]{1,0:T(8,128)(2,1)S(1)}, bf16[128,2048]{1,0:T(8,128)(2,1)}, u32[]{:S(2)}, u32[]{:S(2)}) collective-permute-start(bf16[128,2048]{1,0:T(8,128)(2,1)S(1)} %collective-permute-done.3), channel_id=1, source_target_pairs={{8,0},{16,8},{24,16},{28,24},{20,28},{12,20},{4,12},{0,4},{9,1},{1... | collective-permute-start | bytes 1572872 | tf_op jit(solution)/shard_map/ppermute | solution.py:80
  53.2 19.1 %collective-permute-start.8 = (bf16[128,2048]{1,0:T(8,128)(2,1)}, bf16[128,2048]{1,0:T(8,128)(2,1)S(1)}, u32[]{:S(2)}, u32[]{:S(2)}) collective-permute-start(bf16[128,2048]{1,0:T(8,128)(2,1)} %collective-permute-done.4), channel_id=1, source_target_pairs={{0,8},{8,16},{16,24},{24,28},{28,20},{20,12},{12,4},{4,0},{1,9},{9... | collective-permute-start | bytes 1572872 | tf_op jit(solution)/shard_map/ppermute | solution.py:80
  55.2 21.3 %collective-permute-start.10 = (bf16[128,2048]{1,0:T(8,128)(2,1)S(1)}, bf16[128,2048]{1,0:T(8,128)(2,1)S(1)}, u32[]{:S(2)}, u32[]{:S(2)}) collective-permute-start(bf16[128,2048]{1,0:T(8,128)(2,1)S(1)} %collective-permute-done.6), channel_id=1, source_target_pairs={{0,8},{8,16},{16,24},{24,28},{28,20},{20,12},{12,4},{4,0},{1,9},{9... | collective-permute-start | bytes 1572872 | tf_op jit(solution)/shard_map/ppermute | solution.py:80
  56.8 20.4 %collective-permute-start.11 = (bf16[128,2048]{1,0:T(8,128)(2,1)}, bf16[128,2048]{1,0:T(8,128)(2,1)S(1)}, u32[]{:S(2)}, u32[]{:S(2)}) collective-permute-start(bf16[128,2048]{1,0:T(8,128)(2,1)} %collective-permute-done.7), channel_id=1, source_target_pairs={{8,0},{16,8},{24,16},{28,24},{20,28},{12,20},{4,12},{0,4},{9,1},{1... | collective-permute-start | bytes 1572872 | tf_op jit(solution)/shard_map/ppermute | solution.py:80
  61.1 15.3 %collective-permute-start.12 = (f32[128,1024]{1,0:T(8,128)S(1)}, f32[128,1024]{1,0:T(8,128)S(1)}, u32[]{:S(2)}, u32[]{:S(2)}) collective-permute-start(f32[128,1024]{1,0:T(8,128)S(1)} %dynamic-slice_bitcast_fusion.4), channel_id=1, source_target_pairs={{0,1},{1,0},{2,3},{3,2},{4,5},{5,4},{6,7},{7,6},{8,9},{9,8},{10,11... | collective-permute-start | bytes 1572872 | tf_op jit(solution)/shard_map/ppermute | solution.py:100
  79.4 16.7 %collective-permute-start.21 = (bf16[128,2048]{1,0:T(8,128)(2,1)S(1)}, bf16[128,2048]{1,0:T(8,128)(2,1)S(1)}, u32[]{:S(2)}, u32[]{:S(2)}) collective-permute-start(bf16[128,2048]{1,0:T(8,128)(2,1)S(1)} %copy-done.2), channel_id=1, source_target_pairs={{0,8},{8,16},{16,24},{24,28},{28,20},{20,12},{12,4},{4,0},{1,9},{9... | collective-permute-start | bytes 1572872 | tf_op jit(solution)/shard_map/ppermute | solution.py:80
  80.9 16.5 %collective-permute-start.22 = (bf16[128,2048]{1,0:T(8,128)(2,1)S(1)}, bf16[128,2048]{1,0:T(8,128)(2,1)S(1)}, u32[]{:S(2)}, u32[]{:S(2)}) collective-permute-start(bf16[128,2048]{1,0:T(8,128)(2,1)S(1)} %copy-done.2), channel_id=1, source_target_pairs={{8,0},{16,8},{24,16},{28,24},{20,28},{12,20},{4,12},{0,4},{9,1},{1... | collective-permute-start | bytes 1572872 | tf_op jit(solution)/shard_map/ppermute | solution.py:80
  99.9 21.5 %collective-permute-start.18 = (bf16[128,1024]{1,0:T(8,128)(2,1)S(1)}, bf16[128,1024]{1,0:T(8,128)(2,1)}, u32[]{:S(2)}, u32[]{:S(2)}) collective-permute-start(bf16[128,1024]{1,0:T(8,128)(2,1)S(1)} %fusion.98), channel_id=1, source_target_pairs={{0,24},{1,4},{2,8},{3,20},{8,29},{9,1},{10,17},{11,13},{16,22},{17... | collective-permute-start | bytes 786440 | tf_op jit(solution)/shard_map/ppermute | solution.py:162
  105.2 16.2 %collective-permute-start.23 = (bf16[128,1024]{1,0:T(8,128)(2,1)S(1)}, bf16[128,1024]{1,0:T(8,128)(2,1)}, u32[]{:S(2)}, u32[]{:S(2)}) collective-permute-start(bf16[128,1024]{1,0:T(8,128)(2,1)S(1)} %fusion.97), channel_id=1, source_target_pairs={{0,28},{1,0},{2,12},{3,16},{8,21},{9,9},{10,5},{11,25},{16,14},{17... | collective-permute-start | bytes 786440 | tf_op jit(solution)/shard_map/ppermute | solution.py:162
  124.8 15.7 %collective-permute-start.27 = (bf16[128,2048]{1,0:T(8,128)(2,1)}, bf16[128,2048]{1,0:T(8,128)(2,1)S(1)}, u32[]{:S(2)}, u32[]{:S(2)}) collective-permute-start(bf16[128,2048]{1,0:T(8,128)(2,1)} %add_residual.1), channel_id=1, source_target_pairs={{8,0},{16,8},{24,16},{28,24},{20,28},{12,20},{4,12},{0,4},{9,1},{1... | collective-permute-start | bytes 1572872 | tf_op jit(solution)/shard_map/ppermute | solution.py:80
  125.6 23.5 %collective-permute-start.28 = (bf16[128,2048]{1,0:T(8,128)(2,1)S(1)}, bf16[128,2048]{1,0:T(8,128)(2,1)S(1)}, u32[]{:S(2)}, u32[]{:S(2)}) collective-permute-start(bf16[128,2048]{1,0:T(8,128)(2,1)S(1)} %collective-permute-done.21), channel_id=1, source_target_pairs={{0,8},{8,16},{16,24},{24,28},{28,20},{20,12},{12,4},{4,0},{1,9},{9... | collective-permute-start | bytes 1572872 | tf_op jit(solution)/shard_map/ppermute | solution.py:80
  127.4 21.7 %collective-permute-start.29 = (bf16[128,2048]{1,0:T(8,128)(2,1)}, bf16[128,2048]{1,0:T(8,128)(2,1)S(1)}, u32[]{:S(2)}, u32[]{:S(2)}) collective-permute-start(bf16[128,2048]{1,0:T(8,128)(2,1)} %copy-done.3), channel_id=1, source_target_pairs={{8,0},{16,8},{24,16},{28,24},{20,28},{12,20},{4,12},{0,4},{9,1},{1... | collective-permute-start | bytes 1572872 | tf_op jit(solution)/shard_map/ppermute | solution.py:80
  149.1 26.5 %collective-permute-start.30 = (bf16[128,2048]{1,0:T(8,128)(2,1)S(1)}, bf16[128,2048]{1,0:T(8,128)(2,1)S(1)}, u32[]{:S(2)}, u32[]{:S(2)}) collective-permute-start(bf16[128,2048]{1,0:T(8,128)(2,1)S(1)} %collective-permute-done.26), channel_id=1, source_target_pairs={{0,8},{8,16},{16,24},{24,28},{28,20},{20,12},{12,4},{4,0},{1,9},{9... | collective-permute-start | bytes 1572872 | tf_op jit(solution)/shard_map/ppermute | solution.py:80
  150.0 25.6 %collective-permute-start.31 = (bf16[128,2048]{1,0:T(8,128)(2,1)S(1)}, bf16[128,2048]{1,0:T(8,128)(2,1)S(1)}, u32[]{:S(2)}, u32[]{:S(2)}) collective-permute-start(bf16[128,2048]{1,0:T(8,128)(2,1)S(1)} %collective-permute-done.27), channel_id=1, source_target_pairs={{8,0},{16,8},{24,16},{28,24},{20,28},{12,20},{4,12},{0,4},{9,1},{1... | collective-permute-start | bytes 1572872 | tf_op jit(solution)/shard_map/ppermute | solution.py:80
  151.1 23.1 %collective-permute-start.32 = (bf16[128,2048]{1,0:T(8,128)(2,1)S(1)}, bf16[128,2048]{1,0:T(8,128)(2,1)S(1)}, u32[]{:S(2)}, u32[]{:S(2)}) collective-permute-start(bf16[128,2048]{1,0:T(8,128)(2,1)S(1)} %collective-permute-done.28), channel_id=1, source_target_pairs={{0,8},{8,16},{16,24},{24,28},{28,20},{20,12},{12,4},{4,0},{1,9},{9... | collective-permute-start | bytes 1572872 | tf_op jit(solution)/shard_map/ppermute | solution.py:80
  152.0 22.2 %collective-permute-start.33 = (bf16[128,2048]{1,0:T(8,128)(2,1)S(1)}, bf16[128,2048]{1,0:T(8,128)(2,1)S(1)}, u32[]{:S(2)}, u32[]{:S(2)}) collective-permute-start(bf16[128,2048]{1,0:T(8,128)(2,1)S(1)} %collective-permute-done.29), channel_id=1, source_target_pairs={{8,0},{16,8},{24,16},{28,24},{20,28},{12,20},{4,12},{0,4},{9,1},{1... | collective-permute-start | bytes 1572872 | tf_op jit(solution)/shard_map/ppermute | solution.py:80
  157.7 19.3 %collective-permute-start.34 = (f32[3,2,32,1024]{3,2,0,1:T(8,128)S(1)}, f32[3,2,32,1024]{3,2,0,1:T(8,128)S(1)}, u32[]{:S(2)}, u32[]{:S(2)}) collective-permute-start(f32[3,2,32,1024]{3,2,0,1:T(8,128)S(1)} %bitcast.191), channel_id=1, source_target_pairs={{0,1},{1,0},{2,3},{3,2},{4,5},{5,4},{6,7},{7,6},{8,9},{9,8},{10,11... | collective-permute-start | bytes 2359304 | tf_op jit(solution)/shard_map/ppermute | solution.py:100
  177.1 21.6 %collective-permute-start.35 = (bf16[128,2048]{1,0:T(8,128)(2,1)S(1)}, bf16[128,2048]{1,0:T(8,128)(2,1)S(1)}, u32[]{:S(2)}, u32[]{:S(2)}) collective-permute-start(bf16[128,2048]{1,0:T(8,128)(2,1)S(1)} %collective-permute-done.30), channel_id=1, source_target_pairs={{0,8},{8,16},{16,24},{24,28},{28,20},{20,12},{12,4},{4,0},{1,9},{9... | collective-permute-start | bytes 1572872 | tf_op jit(solution)/shard_map/ppermute | solution.py:80
  177.8 20.9 %collective-permute-start.36 = (bf16[128,2048]{1,0:T(8,128)(2,1)S(1)}, bf16[128,2048]{1,0:T(8,128)(2,1)S(1)}, u32[]{:S(2)}, u32[]{:S(2)}) collective-permute-start(bf16[128,2048]{1,0:T(8,128)(2,1)S(1)} %collective-permute-done.31), channel_id=1, source_target_pairs={{8,0},{16,8},{24,16},{28,24},{20,28},{12,20},{4,12},{0,4},{9,1},{1... | collective-permute-start | bytes 1572872 | tf_op jit(solution)/shard_map/ppermute | solution.py:80
  182.3 16.3 %collective-permute-start.37 = (f32[2,2,32,1024]{3,2,0,1:T(8,128)S(1)}, f32[2,2,32,1024]{3,2,0,1:T(8,128)S(1)}, u32[]{:S(2)}, u32[]{:S(2)}) collective-permute-start(f32[2,2,32,1024]{3,2,0,1:T(8,128)S(1)} %bitcast.194), channel_id=1, source_target_pairs={{0,1},{1,0},{2,3},{3,2},{4,5},{5,4},{6,7},{7,6},{8,9},{9,8},{10,11... | collective-permute-start | bytes 1572872 | tf_op jit(solution)/shard_map/ppermute | solution.py:100
  (48 other events, 449.4 us)

commit v14 on v13

--- a/solution.py
+++ b/solution.py
@@ -128,10 +128,13 @@
 
     low = Gather(low_hidden, 0)
     mid = Gather(mid_hidden, 0)
+    first_low = None
     for hop in range(1, last + 1):
-        attn.ends, low.ends, mid.ends, pair_sums = tie(attn.ends, low.ends, mid.ends, pair_sums)
+        attn.ends, low.ends, mid.ends, pair_sums, first_low = tie(attn.ends, low.ends, mid.ends, pair_sums, first_low)
         attn.hop()
         (mid if hop == last else low).hop()
+        if hop == 2:
+            first_low = product([low.slots[k] for k in offsets[:3]], join_weight[0])
         sum_cores(multiply_pairs(hop - 1))
     attn.slots[last], pair_sums = tie(attn.ends, pair_sums)
     sum_cores(multiply_pairs(last))
@@ -175,7 +178,7 @@
     owned = {}
 
     def multiply_deep(part):
-        total = product([low.slots[k] for k in part], join_weight[0])
+        total = first_low if part == chunks[0] else product([low.slots[k] for k in part], join_weight[0])
         return total + product([mid.slots[k] for k in part], join_weight[1])
 
     def multiply(part, deep_sum):
@@ -227,7 +230,7 @@
             mid.hop()
         if hop > 2:
             summed = add_x(cored)
-            if hop == last - 1:
+            if hop == last:
                 mid.ends, summed = tie(mid.ends, summed)
                 mid.hop()
             if hop < last:
@@ -237,7 +240,7 @@
         if hop < last:
             deep_sum = multiply_deep(chunks[hop - 1])
     deep_sum = multiply_deep(chunks[-1])
-    top.slots[last], deep_sum, owned, summed = tie(top.ends, deep_sum, owned, summed)
+    top.slots[last], owned, summed = tie(top.ends, owned, summed)
     send_all(chunks[-3], summed)
     send_all(chunks[-2], add_x(cored))
     add_halves(chunks[-1], add_cores(multiply(chunks[-1], deep_sum)))

time: 230 us -> 235 us (1.022)
  matrix products: 35.8 us -> 28.8 us
  local copies, waits for them, and re-layouts: 2.9 us -> 9.67 us
  other arithmetic: 5 us -> 9.85 us
    dot_general x16, matrix products: 35.8 us -> 28.8 us  [product(): jnp.dot(rows_in, weight, preferred_element_type=jnp.float32)]
    ppermute x13, waiting for transfers between devices: 10.4 us -> 14.5 us  [swap(): return lax.ppermute(values, 'tensor', [(t, t ^ bit) for t in range(owners)])]
    ppermute x16, waiting for transfers between devices: 28.9 us -> 25.2 us  [hop(): lax.ppermute(ends[1], 'dp', down)]
    add x3, other arithmetic: 0.21 us -> 3.63 us  [sum_cores(): pick(products, core) + swap(pick(products, 1 - core), 1)]
    ppermute x2, starting transfers between devices: 8.88 us -> 5.58 us  [local(): arrived.append(lax.ppermute(held, ('dp', 'tensor'), moves))]
    squeeze x4, local copies, waits for them, and re-layouts: 0.18 us -> 2.71 us  [pick(): return lax.dynamic_index_in_dim(values, index, 0, keepdims=False)]
  transfers between devices with their start and end apart: 55 -> 55, of which waited for: 26 -> 27; matrix products, arithmetic and copies ran while one was open for 19% -> 19% of each run, Pallas kernels for 1% -> 1%
where the time goes in v14:
time: 235 us
  waiting for transfers between devices  117 us (50%)
  starting transfers between devices  64.1 us (27%)
  matrix products  28.8 us (12%)
  other arithmetic  9.85 us (4%)
  local copies, waits for them, and re-layouts  9.67 us (4%)
  Pallas kernels  4.41 us (2%)
    ppermute x16, waiting for transfers between devices, hop(): lax.ppermute(ends[0], 'dp', up)  70.8 us
    dot_general x16, matrix products, product(): jnp.dot(rows_in, weight, preferred_element_type=jnp.float32)  28.8 us
    ppermute x16, waiting for transfers between devices, hop(): lax.ppermute(ends[1], 'dp', down)  25.2 us
    ppermute x16, starting transfers between devices, hop(): lax.ppermute(ends[0], 'dp', up)  21.3 us
    ppermute x8, starting transfers between devices, send(): return lax.ppermute(part.astype(jnp.bfloat16), ('dp', 'tensor'), moves)  15.1 us
    ppermute x13, waiting for transfers between devices, swap(): return lax.ppermute(values, 'tensor', [(t, t ^ bit) for t in range(owners)])  14.5 us
    ppermute x16, starting transfers between devices, hop(): lax.ppermute(ends[1], 'dp', down)  13.8 us
    ppermute x13, starting transfers between devices, swap(): return lax.ppermute(values, 'tensor', [(t, t ^ bit) for t in range(owners)])  8.29 us
  transfers between devices with their start and end apart: 55, of which 27 were waited for; matrix products, arithmetic and copies ran while one was open for 19% of the time, Pallas kernels for 1%

profile of v14, /device:TPU:0, one launch (start us, length us, event | category | flops | bytes accessed | tf_op | source)
XLA Modules:
  0.0 234.5 jit_solution(6914823030535045523)
XLA Ops:
  0.0 3.0 %collective-permute-start = (bf16[128,2048]{1,0:T(8,128)(2,1)}, bf16[128,2048]{1,0:T(8,128)(2,1)}, u32[]{:S(2)}, u32[]{:S(2)}) collective-permute-start(bf16[128,2048]{1,0:T(8,128)(2,1)} %param.7), channel_id=1, source_target_pairs={{0,8},{8,16},{16,24},{24,28},{28,20},{20,12},{12,4},{4,0},{1,9},{9... | collective-permute-start | bytes 1572872 | tf_op jit(solution)/shard_map/ppermute | solution.py:80
  5.1 11.0 %collective-permute-done = bf16[128,2048]{1,0:T(8,128)(2,1)} collective-permute-done((bf16[128,2048]{1,0:T(8,128)(2,1)}, bf16[128,2048]{1,0:T(8,128)(2,1)}, u32[]{:S(2)}, u32[]{:S(2)}) %collective-permute-start) | collective-permute-done | bytes 524320 | tf_op jit(solution)/shard_map/ppermute | solution.py:80
  18.1 8.2 %collective-permute-done.2 = bf16[128,2048]{1,0:T(8,128)(2,1)S(1)} collective-permute-done((bf16[128,2048]{1,0:T(8,128)(2,1)}, bf16[128,2048]{1,0:T(8,128)(2,1)S(1)}, u32[]{:S(2)}, u32[]{:S(2)}) %collective-permute-start.2) | collective-permute-done | bytes 524320 | tf_op jit(solution)/shard_map/ppermute | solution.py:80
  33.1 4.1 %fusion.20 = f32[3,128,1024]{2,1,0:T(8,128)S(1)} fusion(bf16[3,128,2048]{2,1,0:T(8,128)(2,1)S(1)} %bitcast.163, bf16[3,2048,1024]{2,1,0:T(8,128)(2,1)} %param.12), kind=kOutput, calls=%fused_computation.20 | convolution fusion | flops 1610612736 | bytes 7340032 | tf_op jit(solution)/shard_map/dot_general | solution.py:104
  37.2 5.7 %collective-permute-done.4 = bf16[128,2048]{1,0:T(8,128)(2,1)S(1)} collective-permute-done((bf16[128,2048]{1,0:T(8,128)(2,1)}, bf16[128,2048]{1,0:T(8,128)(2,1)S(1)}, u32[]{:S(2)}, u32[]{:S(2)}) %collective-permute-start.4) | collective-permute-done | bytes 524320 | tf_op jit(solution)/shard_map/ppermute | solution.py:80
  44.3 7.6 %collective-permute-done.6 = bf16[128,2048]{1,0:T(8,128)(2,1)} collective-permute-done((bf16[128,2048]{1,0:T(8,128)(2,1)S(1)}, bf16[128,2048]{1,0:T(8,128)(2,1)}, u32[]{:S(2)}, u32[]{:S(2)}) %collective-permute-start.6) | collective-permute-done | bytes 524320 | tf_op jit(solution)/shard_map/ppermute | solution.py:80
  59.5 9.9 %collective-permute-done.9 = bf16[128,2048]{1,0:T(8,128)(2,1)S(1)} collective-permute-done((bf16[128,2048]{1,0:T(8,128)(2,1)S(1)}, bf16[128,2048]{1,0:T(8,128)(2,1)S(1)}, u32[]{:S(2)}, u32[]{:S(2)}) %collective-permute-start.9) | collective-permute-done | bytes 524320 | tf_op jit(solution)/shard_map/ppermute | solution.py:80
  84.8 2.9 %collective-permute-done.13 = bf16[64,2048]{1,0:T(8,128)(2,1)S(1)} collective-permute-done((bf16[64,2048]{1,0:T(8,128)(2,1)S(1)}, bf16[64,2048]{1,0:T(8,128)(2,1)S(1)}, u32[]{:S(2)}, u32[]{:S(2)}) %collective-permute-start.13) | collective-permute-done | bytes 262176 | tf_op jit(solution)/shard_map/ppermute | solution.py:80
  99.1 5.9 %collective-permute-done.17 = bf16[1,128,1024]{2,1,0:T(8,128)(2,1)S(1)} collective-permute-done((bf16[1,128,1024]{2,1,0:T(8,128)(2,1)S(1)}, bf16[1,128,1024]{2,1,0:T(8,128)(2,1)S(1)}, u32[]{:S(2)}, u32[]{:S(2)}) %collective-permute-start.17) | collective-permute-done | bytes 262176 | tf_op jit(solution)/shard_map/ppermute | solution.py:100
  105.7 4.0 %collective-permute-done.20 = bf16[1,128,1024]{2,1,0:T(8,128)(2,1)S(1)} collective-permute-done((bf16[1,128,1024]{2,1,0:T(8,128)(2,1)S(1)}, bf16[1,128,1024]{2,1,0:T(8,128)(2,1)S(1)}, u32[]{:S(2)}, u32[]{:S(2)}) %collective-permute-start.20) | collective-permute-done | bytes 262176 | tf_op jit(solution)/shard_map/ppermute | solution.py:100
  109.8 5.1 %collective-permute-start.23 = (bf16[128,1024]{1,0:T(8,128)(2,1)S(1)}, bf16[128,1024]{1,0:T(8,128)(2,1)}, u32[]{:S(2)}, u32[]{:S(2)}) collective-permute-start(bf16[128,1024]{1,0:T(8,128)(2,1)S(1)} %fusion.85), channel_id=1, source_target_pairs={{0,28},{1,0},{2,12},{3,16},{8,21},{9,9},{10,5},{11,25},{16,14},{17... | collective-permute-start | bytes 786440 | tf_op jit(solution)/shard_map/ppermute | solution.py:165
  121.0 3.1 %collective-permute-done.24 = bf16[64,2048]{1,0:T(8,128)(2,1)} collective-permute-done((bf16[64,2048]{1,0:T(8,128)(2,1)S(1)}, bf16[64,2048]{1,0:T(8,128)(2,1)}, u32[]{:S(2)}, u32[]{:S(2)}) %collective-permute-start.24) | collective-permute-done | bytes 262176 | tf_op jit(solution)/shard_map/ppermute | solution.py:80
  124.1 3.0 %collective-permute-done.25 = bf16[64,2048]{1,0:T(8,128)(2,1)} collective-permute-done((bf16[64,2048]{1,0:T(8,128)(2,1)}, bf16[64,2048]{1,0:T(8,128)(2,1)}, u32[]{:S(2)}, u32[]{:S(2)}) %collective-permute-start.25) | collective-permute-done | bytes 262176 | tf_op jit(solution)/shard_map/ppermute | solution.py:80
  131.7 4.1 %fusion.12 = f32[3,128,1024]{2,1,0:T(8,128)S(1)} fusion(bf16[3,128,2048]{2,1,0:T(8,128)(2,1)S(1)} %bitcast.161, bf16[3,2048,1024]{2,1,0:T(8,128)(2,1)} %param.12), kind=kOutput, calls=%fused_computation.12 | convolution fusion | flops 1610612736 | bytes 7340032 | tf_op jit(solution)/shard_map/dot_general | solution.py:104
  136.1 3.2 %fusion.22 = f32[128,1024]{1,0:T(8,128)S(1)} fusion(bf16[3,2048,1024]{2,1,0:T(8,128)(2,1)} %param.12, bf16[64,2048]{1,0:T(8,128)(2,1)} %collective-permute-done.25, bf16[64,2048]{1,0:T(8,128)(2,1)} %collective-permute-done.24), kind=kOutput, calls=%fused_computation.22 | convolution fusion | flops 537919488 | bytes 5242880 | tf_op jit(solution)/shard_map/dot_general | solution.py:104
  139.3 3.0 %collective-permute-done.26 = bf16[128,2048]{1,0:T(8,128)(2,1)S(1)} collective-permute-done((bf16[128,2048]{1,0:T(8,128)(2,1)}, bf16[128,2048]{1,0:T(8,128)(2,1)S(1)}, u32[]{:S(2)}, u32[]{:S(2)}) %collective-permute-start.26) | collective-permute-done | bytes 524320 | tf_op jit(solution)/shard_map/ppermute | solution.py:80
  144.7 8.5 %collective-permute-done.28 = bf16[128,2048]{1,0:T(8,128)(2,1)S(1)} collective-permute-done((bf16[128,2048]{1,0:T(8,128)(2,1)}, bf16[128,2048]{1,0:T(8,128)(2,1)S(1)}, u32[]{:S(2)}, u32[]{:S(2)}) %collective-permute-start.28) | collective-permute-done | bytes 524320 | tf_op jit(solution)/shard_map/ppermute | solution.py:80
  162.7 16.4 %collective-permute-done.32 = bf16[128,2048]{1,0:T(8,128)(2,1)S(1)} collective-permute-done((bf16[128,2048]{1,0:T(8,128)(2,1)S(1)}, bf16[128,2048]{1,0:T(8,128)(2,1)S(1)}, u32[]{:S(2)}, u32[]{:S(2)}) %collective-permute-start.32) | collective-permute-done | bytes 524320 | tf_op jit(solution)/shard_map/ppermute | solution.py:80
  193.4 3.2 %collective-permute-done.35 = bf16[128,2048]{1,0:T(8,128)(2,1)S(1)} collective-permute-done((bf16[128,2048]{1,0:T(8,128)(2,1)S(1)}, bf16[128,2048]{1,0:T(8,128)(2,1)S(1)}, u32[]{:S(2)}, u32[]{:S(2)}) %collective-permute-start.35) | collective-permute-done | bytes 524320 | tf_op jit(solution)/shard_map/ppermute | solution.py:80
  206.1 3.0 %collective-permute-start.44 = (bf16[32,1024]{1,0:T(8,128)(2,1)S(1)}, bf16[32,1024]{1,0:T(8,128)(2,1)S(1)}, u32[]{:S(2)}, u32[]{:S(2)}) collective-permute-start(bf16[32,1024]{1,0:T(8,128)(2,1)S(1)} %get-tuple-element.152), channel_id=1, source_target_pairs={{0,12},{1,13},{2,14},{3,15},{8,4},{9,5},{10,6},{11,7},{16,0},{17,1... | collective-permute-start | bytes 196616 | tf_op jit(solution)/shard_map/ppermute | solution.py:201
  215.2 4.2 %collective-permute-start.48 = (bf16[32,1024]{1,0:T(8,128)(2,1)S(1)}, bf16[32,1024]{1,0:T(8,128)(2,1)S(1)}, u32[]{:S(2)}, u32[]{:S(2)}) collective-permute-start(bf16[32,1024]{1,0:T(8,128)(2,1)S(1)} %get-tuple-element.150), channel_id=1, source_target_pairs={{0,20},{1,21},{2,22},{3,23},{8,12},{9,13},{10,14},{11,15},{16,4},{... | collective-permute-start | bytes 196616 | tf_op jit(solution)/shard_map/ppermute | solution.py:201
  219.8 3.9 %collective-permute-start.53 = (bf16[32,1024]{1,0:T(8,128)(2,1)S(1)}, bf16[32,1024]{1,0:T(8,128)(2,1)S(1)}, u32[]{:S(2)}, u32[]{:S(2)}) collective-permute-start(bf16[32,1024]{1,0:T(8,128)(2,1)S(1)} %get-tuple-element.148), channel_id=1, source_target_pairs={{0,28},{1,29},{2,30},{3,31},{8,20},{9,21},{10,22},{11,23},{16,12},... | collective-permute-start | bytes 196616 | tf_op jit(solution)/shard_map/ppermute | solution.py:201
  225.4 2.8 %collective-permute-done.49.refs_6_ = bf16[32,1024]{1,0:T(8,128)(2,1)S(1)} collective-permute-done((bf16[32,1024]{1,0:T(8,128)(2,1)S(1)}, bf16[32,1024]{1,0:T(8,128)(2,1)S(1)}, u32[]{:S(2)}, u32[]{:S(2)}) %collective-permute-start.49) | collective-permute-done | bytes 65568 | tf_op jit(solution)/shard_map/ppermute | solution.py:201
  228.2 3.4 %collective-permute-done.54.refs_8_ = bf16[32,1024]{1,0:T(8,128)(2,1)S(1)} collective-permute-done((bf16[32,1024]{1,0:T(8,128)(2,1)S(1)}, bf16[32,1024]{1,0:T(8,128)(2,1)S(1)}, u32[]{:S(2)}, u32[]{:S(2)}) %collective-permute-start.54) | collective-permute-done | bytes 65568 | tf_op jit(solution)/shard_map/ppermute | solution.py:201
  (212 shorter events, 104.4 us)
Async XLA Ops:
  0.0 16.0 %collective-permute-start = (bf16[128,2048]{1,0:T(8,128)(2,1)}, bf16[128,2048]{1,0:T(8,128)(2,1)}, u32[]{:S(2)}, u32[]{:S(2)}) collective-permute-start(bf16[128,2048]{1,0:T(8,128)(2,1)} %param.7), channel_id=1, source_target_pairs={{0,8},{8,16},{16,24},{24,28},{28,20},{20,12},{12,4},{4,0},{1,9},{9... | collective-permute-start | bytes 1572872 | tf_op jit(solution)/shard_map/ppermute | solution.py:80
  3.0 15.1 %collective-permute-start.1 = (bf16[128,2048]{1,0:T(8,128)(2,1)}, bf16[128,2048]{1,0:T(8,128)(2,1)S(1)}, u32[]{:S(2)}, u32[]{:S(2)}) collective-permute-start(bf16[128,2048]{1,0:T(8,128)(2,1)} %param.7), channel_id=1, source_target_pairs={{8,0},{16,8},{24,16},{28,24},{20,28},{12,20},{4,12},{0,4},{9,1},{1... | collective-permute-start | bytes 1572872 | tf_op jit(solution)/shard_map/ppermute | solution.py:80
  3.0 23.3 %collective-permute-start.2 = (bf16[128,2048]{1,0:T(8,128)(2,1)}, bf16[128,2048]{1,0:T(8,128)(2,1)S(1)}, u32[]{:S(2)}, u32[]{:S(2)}) collective-permute-start(bf16[128,2048]{1,0:T(8,128)(2,1)} %param.9), channel_id=1, source_target_pairs={{0,8},{8,16},{16,24},{24,28},{28,20},{20,12},{12,4},{4,0},{1,9},{9... | collective-permute-start | bytes 1572872 | tf_op jit(solution)/shard_map/ppermute | solution.py:80
  5.1 22.8 %collective-permute-start.3 = (bf16[128,2048]{1,0:T(8,128)(2,1)}, bf16[128,2048]{1,0:T(8,128)(2,1)S(1)}, u32[]{:S(2)}, u32[]{:S(2)}) collective-permute-start(bf16[128,2048]{1,0:T(8,128)(2,1)} %param.9), channel_id=1, source_target_pairs={{8,0},{16,8},{24,16},{28,24},{20,28},{12,20},{4,12},{0,4},{9,1},{1... | collective-permute-start | bytes 1572872 | tf_op jit(solution)/shard_map/ppermute | solution.py:80
  27.9 15.1 %collective-permute-start.4 = (bf16[128,2048]{1,0:T(8,128)(2,1)}, bf16[128,2048]{1,0:T(8,128)(2,1)S(1)}, u32[]{:S(2)}, u32[]{:S(2)}) collective-permute-start(bf16[128,2048]{1,0:T(8,128)(2,1)} %collective-permute-done), channel_id=1, source_target_pairs={{0,8},{8,16},{16,24},{24,28},{28,20},{20,12},{12,4},{4,0},{1,9},{9... | collective-permute-start | bytes 1572872 | tf_op jit(solution)/shard_map/ppermute | solution.py:80
  29.9 22.0 %collective-permute-start.6 = (bf16[128,2048]{1,0:T(8,128)(2,1)S(1)}, bf16[128,2048]{1,0:T(8,128)(2,1)}, u32[]{:S(2)}, u32[]{:S(2)}) collective-permute-start(bf16[128,2048]{1,0:T(8,128)(2,1)S(1)} %collective-permute-done.2), channel_id=1, source_target_pairs={{0,8},{8,16},{16,24},{24,28},{28,20},{20,12},{12,4},{4,0},{1,9},{9... | collective-permute-start | bytes 1572872 | tf_op jit(solution)/shard_map/ppermute | solution.py:80
  31.5 21.5 %collective-permute-start.7 = (bf16[128,2048]{1,0:T(8,128)(2,1)S(1)}, bf16[128,2048]{1,0:T(8,128)(2,1)}, u32[]{:S(2)}, u32[]{:S(2)}) collective-permute-start(bf16[128,2048]{1,0:T(8,128)(2,1)S(1)} %collective-permute-done.3), channel_id=1, source_target_pairs={{8,0},{16,8},{24,16},{28,24},{20,28},{12,20},{4,12},{0,4},{9,1},{1... | collective-permute-start | bytes 1572872 | tf_op jit(solution)/shard_map/ppermute | solution.py:80
  53.0 19.9 %collective-permute-start.8 = (bf16[128,2048]{1,0:T(8,128)(2,1)S(1)}, bf16[128,2048]{1,0:T(8,128)(2,1)S(1)}, u32[]{:S(2)}, u32[]{:S(2)}) collective-permute-start(bf16[128,2048]{1,0:T(8,128)(2,1)S(1)} %collective-permute-done.4), channel_id=1, source_target_pairs={{0,8},{8,16},{16,24},{24,28},{28,20},{20,12},{12,4},{4,0},{1,9},{9... | collective-permute-start | bytes 1572872 | tf_op jit(solution)/shard_map/ppermute | solution.py:80
  55.0 22.9 %collective-permute-start.10 = (bf16[128,2048]{1,0:T(8,128)(2,1)}, bf16[128,2048]{1,0:T(8,128)(2,1)S(1)}, u32[]{:S(2)}, u32[]{:S(2)}) collective-permute-start(bf16[128,2048]{1,0:T(8,128)(2,1)} %collective-permute-done.6), channel_id=1, source_target_pairs={{0,8},{8,16},{16,24},{24,28},{28,20},{20,12},{12,4},{4,0},{1,9},{9... | collective-permute-start | bytes 1572872 | tf_op jit(solution)/shard_map/ppermute | solution.py:80
  56.6 21.3 %collective-permute-start.11 = (bf16[128,2048]{1,0:T(8,128)(2,1)}, bf16[128,2048]{1,0:T(8,128)(2,1)S(1)}, u32[]{:S(2)}, u32[]{:S(2)}) collective-permute-start(bf16[128,2048]{1,0:T(8,128)(2,1)} %collective-permute-done.7), channel_id=1, source_target_pairs={{8,0},{16,8},{24,16},{28,24},{20,28},{12,20},{4,12},{0,4},{9,1},{1... | collective-permute-start | bytes 1572872 | tf_op jit(solution)/shard_map/ppermute | solution.py:80
  59.3 17.2 %collective-permute-start.12 = (f32[128,1024]{1,0:T(8,128)}, f32[128,1024]{1,0:T(8,128)}, u32[]{:S(2)}, u32[]{:S(2)}) collective-permute-start(f32[128,1024]{1,0:T(8,128)} %dynamic-slice_bitcast_fusion.5), channel_id=1, source_target_pairs={{0,1},{1,0},{2,3},{3,2},{4,5},{5,4},{6,7},{7,6},{8,9},{9,8},{10,11... | collective-permute-start | bytes 1572872 | tf_op jit(solution)/shard_map/ppermute | solution.py:100
  93.7 16.0 %collective-permute-start.21 = (bf16[128,2048]{1,0:T(8,128)(2,1)S(1)}, bf16[128,2048]{1,0:T(8,128)(2,1)S(1)}, u32[]{:S(2)}, u32[]{:S(2)}) collective-permute-start(bf16[128,2048]{1,0:T(8,128)(2,1)S(1)} %copy-done.7), channel_id=1, source_target_pairs={{0,8},{8,16},{16,24},{24,28},{28,20},{20,12},{12,4},{4,0},{1,9},{9... | collective-permute-start | bytes 1572872 | tf_op jit(solution)/shard_map/ppermute | solution.py:80
  94.3 15.5 %collective-permute-start.22 = (bf16[128,2048]{1,0:T(8,128)(2,1)S(1)}, bf16[128,2048]{1,0:T(8,128)(2,1)S(1)}, u32[]{:S(2)}, u32[]{:S(2)}) collective-permute-start(bf16[128,2048]{1,0:T(8,128)(2,1)S(1)} %copy-done.7), channel_id=1, source_target_pairs={{8,0},{16,8},{24,16},{28,24},{20,28},{12,20},{4,12},{0,4},{9,1},{1... | collective-permute-start | bytes 1572872 | tf_op jit(solution)/shard_map/ppermute | solution.py:80
  127.1 15.2 %collective-permute-start.26 = (bf16[128,2048]{1,0:T(8,128)(2,1)}, bf16[128,2048]{1,0:T(8,128)(2,1)S(1)}, u32[]{:S(2)}, u32[]{:S(2)}) collective-permute-start(bf16[128,2048]{1,0:T(8,128)(2,1)} %add_residual.1), channel_id=1, source_target_pairs={{0,8},{8,16},{16,24},{24,28},{28,20},{20,12},{12,4},{4,0},{1,9},{9... | collective-permute-start | bytes 1572872 | tf_op jit(solution)/shard_map/ppermute | solution.py:80
  129.6 15.1 %collective-permute-start.27 = (bf16[128,2048]{1,0:T(8,128)(2,1)}, bf16[128,2048]{1,0:T(8,128)(2,1)S(1)}, u32[]{:S(2)}, u32[]{:S(2)}) collective-permute-start(bf16[128,2048]{1,0:T(8,128)(2,1)} %add_residual.1), channel_id=1, source_target_pairs={{8,0},{16,8},{24,16},{28,24},{20,28},{12,20},{4,12},{0,4},{9,1},{1... | collective-permute-start | bytes 1572872 | tf_op jit(solution)/shard_map/ppermute | solution.py:80
  129.6 23.6 %collective-permute-start.28 = (bf16[128,2048]{1,0:T(8,128)(2,1)}, bf16[128,2048]{1,0:T(8,128)(2,1)S(1)}, u32[]{:S(2)}, u32[]{:S(2)}) collective-permute-start(bf16[128,2048]{1,0:T(8,128)(2,1)} %copy-done.8), channel_id=1, source_target_pairs={{0,8},{8,16},{16,24},{24,28},{28,20},{20,12},{12,4},{4,0},{1,9},{9... | collective-permute-start | bytes 1572872 | tf_op jit(solution)/shard_map/ppermute | solution.py:80
  131.6 21.6 %collective-permute-start.29 = (bf16[128,2048]{1,0:T(8,128)(2,1)}, bf16[128,2048]{1,0:T(8,128)(2,1)S(1)}, u32[]{:S(2)}, u32[]{:S(2)}) collective-permute-start(bf16[128,2048]{1,0:T(8,128)(2,1)} %copy-done.9), channel_id=1, source_target_pairs={{8,0},{16,8},{24,16},{28,24},{20,28},{12,20},{4,12},{0,4},{9,1},{1... | collective-permute-start | bytes 1572872 | tf_op jit(solution)/shard_map/ppermute | solution.py:80
  153.2 27.2 %collective-permute-start.30 = (bf16[128,2048]{1,0:T(8,128)(2,1)S(1)}, bf16[128,2048]{1,0:T(8,128)(2,1)S(1)}, u32[]{:S(2)}, u32[]{:S(2)}) collective-permute-start(bf16[128,2048]{1,0:T(8,128)(2,1)S(1)} %collective-permute-done.26), channel_id=1, source_target_pairs={{0,8},{8,16},{16,24},{24,28},{28,20},{20,12},{12,4},{4,0},{1,9},{9... | collective-permute-start | bytes 1572872 | tf_op jit(solution)/shard_map/ppermute | solution.py:80
  153.6 26.9 %collective-permute-start.31 = (bf16[128,2048]{1,0:T(8,128)(2,1)S(1)}, bf16[128,2048]{1,0:T(8,128)(2,1)S(1)}, u32[]{:S(2)}, u32[]{:S(2)}) collective-permute-start(bf16[128,2048]{1,0:T(8,128)(2,1)S(1)} %collective-permute-done.27), channel_id=1, source_target_pairs={{8,0},{16,8},{24,16},{28,24},{20,28},{12,20},{4,12},{0,4},{9,1},{1... | collective-permute-start | bytes 1572872 | tf_op jit(solution)/shard_map/ppermute | solution.py:80
  155.6 23.5 %collective-permute-start.32 = (bf16[128,2048]{1,0:T(8,128)(2,1)S(1)}, bf16[128,2048]{1,0:T(8,128)(2,1)S(1)}, u32[]{:S(2)}, u32[]{:S(2)}) collective-permute-start(bf16[128,2048]{1,0:T(8,128)(2,1)S(1)} %collective-permute-done.28), channel_id=1, source_target_pairs={{0,8},{8,16},{16,24},{24,28},{28,20},{20,12},{12,4},{4,0},{1,9},{9... | collective-permute-start | bytes 1572872 | tf_op jit(solution)/shard_map/ppermute | solution.py:80
  155.6 23.4 %collective-permute-start.33 = (bf16[128,2048]{1,0:T(8,128)(2,1)S(1)}, bf16[128,2048]{1,0:T(8,128)(2,1)S(1)}, u32[]{:S(2)}, u32[]{:S(2)}) collective-permute-start(bf16[128,2048]{1,0:T(8,128)(2,1)S(1)} %collective-permute-done.29), channel_id=1, source_target_pairs={{8,0},{16,8},{24,16},{28,24},{20,28},{12,20},{4,12},{0,4},{9,1},{1... | collective-permute-start | bytes 1572872 | tf_op jit(solution)/shard_map/ppermute | solution.py:80
  159.9 22.0 %collective-permute-start.34 = (f32[3,2,32,1024]{3,2,1,0:T(8,128)S(1)}, f32[3,2,32,1024]{3,2,1,0:T(8,128)S(1)}, u32[]{:S(2)}, u32[]{:S(2)}) collective-permute-start(f32[3,2,32,1024]{3,2,1,0:T(8,128)S(1)} %dynamic-slice_bitcast_fusion), channel_id=1, source_target_pairs={{0,1},{1,0},{2,3},{3,2},{4,5},{5,4},{6,7},{7,6},{8,9},{9,8},{10,11... | collective-permute-start | bytes 2359304 | tf_op jit(solution)/shard_map/ppermute | solution.py:100
  206.1 17.6 %collective-permute-start.44 = (bf16[32,1024]{1,0:T(8,128)(2,1)S(1)}, bf16[32,1024]{1,0:T(8,128)(2,1)S(1)}, u32[]{:S(2)}, u32[]{:S(2)}) collective-permute-start(bf16[32,1024]{1,0:T(8,128)(2,1)S(1)} %get-tuple-element.152), channel_id=1, source_target_pairs={{0,12},{1,13},{2,14},{3,15},{8,4},{9,5},{10,6},{11,7},{16,0},{17,1... | collective-permute-start | bytes 196616 | tf_op jit(solution)/shard_map/ppermute | solution.py:201
  209.1 16.3 %collective-permute-start.45 = (bf16[32,1024]{1,0:T(8,128)(2,1)S(1)}, bf16[32,1024]{1,0:T(8,128)(2,1)S(1)}, u32[]{:S(2)}, u32[]{:S(2)}) collective-permute-start(bf16[32,1024]{1,0:T(8,128)(2,1)S(1)} %get-tuple-element.151), channel_id=1, source_target_pairs={{0,16},{1,17},{2,18},{3,19},{8,24},{9,25},{10,26},{11,27},{16,28},... | collective-permute-start | bytes 196616 | tf_op jit(solution)/shard_map/ppermute | solution.py:201
  (60 other events, 547.3 us)

commit v15 on v13

--- a/solution.py
+++ b/solution.py
@@ -218,18 +218,12 @@
 
     cored, deep_sum, summed = None, None, None
     for hop in range(1, last + 1):
-        if hop < last:
-            top.ends, mid.ends, cored, deep_sum = tie(top.ends, mid.ends, cored, deep_sum)
-        else:
-            top.ends, cored, deep_sum = tie(top.ends, cored, deep_sum)
+        top.ends, mid.ends, cored, deep_sum = tie(top.ends, mid.ends, cored, deep_sum)
         top.hop()
-        if hop < last - 1:
+        if hop != last - 1:
             mid.hop()
         if hop > 2:
             summed = add_x(cored)
-            if hop == last - 1:
-                mid.ends, summed = tie(mid.ends, summed)
-                mid.hop()
             if hop < last:
                 send_all(chunks[hop - 3], summed)
         if hop > 1:
@@ -237,7 +231,7 @@
         if hop < last:
             deep_sum = multiply_deep(chunks[hop - 1])
     deep_sum = multiply_deep(chunks[-1])
-    top.slots[last], deep_sum, owned, summed = tie(top.ends, deep_sum, owned, summed)
+    top.slots[last], owned, summed = tie(top.ends, owned, summed)
     send_all(chunks[-3], summed)
     send_all(chunks[-2], add_x(cored))
     add_halves(chunks[-1], add_cores(multiply(chunks[-1], deep_sum)))

time: 230 us -> 230 us (level)
    ppermute x16, waiting for transfers between devices: 28.9 us -> 25.6 us  [hop(): lax.ppermute(ends[1], 'dp', down)]
    ppermute x16, waiting for transfers between devices: 70.5 us -> 73.6 us  [hop(): lax.ppermute(ends[0], 'dp', up)]
  transfers between devices with their start and end apart: 55 -> 55, of which waited for: 26 -> 28; matrix products, arithmetic and copies ran while one was open for 19% -> 19% of each run, Pallas kernels for 1% -> 1%
where the time goes in v15:
time: 230 us; the launch traced here: 229 us
  waiting for transfers between devices  116 us (50%)
  starting transfers between devices  64 us (28%)
  matrix products  35.8 us (16%)
  other arithmetic  5.02 us (2%)
  Pallas kernels  4.41 us (2%)
  local copies, waits for them, and re-layouts  2.74 us (1%)
    ppermute x16, waiting for transfers between devices, hop(): lax.ppermute(ends[0], 'dp', up)  73.6 us
    dot_general x16, matrix products, product(): jnp.dot(rows_in, weight, preferred_element_type=jnp.float32)  35.8 us
    ppermute x16, waiting for transfers between devices, hop(): lax.ppermute(ends[1], 'dp', down)  25.6 us
    ppermute x16, starting transfers between devices, hop(): lax.ppermute(ends[0], 'dp', up)  21 us
    ppermute x8, starting transfers between devices, send(): return lax.ppermute(part.astype(jnp.bfloat16), ('dp', 'tensor'), moves)  13.8 us
    ppermute x16, starting transfers between devices, hop(): lax.ppermute(ends[1], 'dp', down)  12.8 us
    ppermute x13, waiting for transfers between devices, swap(): return lax.ppermute(values, 'tensor', [(t, t ^ bit) for t in range(owners)])  10.9 us
    ppermute x2, starting transfers between devices, local(): arrived.append(lax.ppermute(held, ('dp', 'tensor'), moves))  8.88 us
  transfers between devices with their start and end apart: 55, of which 28 were waited for; matrix products, arithmetic and copies ran while one was open for 19% of the time, Pallas kernels for 1%

profile of v15, /device:TPU:0, one launch (start us, length us, event | category | flops | bytes accessed | tf_op | source)
XLA Modules:
  0.0 229.2 jit_solution(15067312635684614307)
XLA Ops:
  0.0 3.0 %collective-permute-start = (bf16[128,2048]{1,0:T(8,128)(2,1)}, bf16[128,2048]{1,0:T(8,128)(2,1)}, u32[]{:S(2)}, u32[]{:S(2)}) collective-permute-start(bf16[128,2048]{1,0:T(8,128)(2,1)} %param.7), channel_id=1, source_target_pairs={{0,8},{8,16},{16,24},{24,28},{28,20},{20,12},{12,4},{4,0},{1,9},{9... | collective-permute-start | bytes 1572872 | tf_op jit(solution)/shard_map/ppermute | solution.py:80
  5.1 11.0 %collective-permute-done = bf16[128,2048]{1,0:T(8,128)(2,1)} collective-permute-done((bf16[128,2048]{1,0:T(8,128)(2,1)}, bf16[128,2048]{1,0:T(8,128)(2,1)}, u32[]{:S(2)}, u32[]{:S(2)}) %collective-permute-start) | collective-permute-done | bytes 524320 | tf_op jit(solution)/shard_map/ppermute | solution.py:80
  18.2 8.1 %collective-permute-done.2 = bf16[128,2048]{1,0:T(8,128)(2,1)S(1)} collective-permute-done((bf16[128,2048]{1,0:T(8,128)(2,1)}, bf16[128,2048]{1,0:T(8,128)(2,1)S(1)}, u32[]{:S(2)}, u32[]{:S(2)}) %collective-permute-start.2) | collective-permute-done | bytes 524320 | tf_op jit(solution)/shard_map/ppermute | solution.py:80
  33.1 9.9 %collective-permute-done.4 = bf16[128,2048]{1,0:T(8,128)(2,1)} collective-permute-done((bf16[128,2048]{1,0:T(8,128)(2,1)}, bf16[128,2048]{1,0:T(8,128)(2,1)}, u32[]{:S(2)}, u32[]{:S(2)}) %collective-permute-start.4) | collective-permute-done | bytes 524320 | tf_op jit(solution)/shard_map/ppermute | solution.py:80
  44.6 7.2 %collective-permute-done.6 = bf16[128,2048]{1,0:T(8,128)(2,1)S(1)} collective-permute-done((bf16[128,2048]{1,0:T(8,128)(2,1)S(1)}, bf16[128,2048]{1,0:T(8,128)(2,1)S(1)}, u32[]{:S(2)}, u32[]{:S(2)}) %collective-permute-start.6) | collective-permute-done | bytes 524320 | tf_op jit(solution)/shard_map/ppermute | solution.py:80
  57.2 3.8 %fusion.60 = f32[256,1024]{1,0:T(8,128)S(1)} fusion(bf16[2048,1024]{1,0:T(8,128)(2,1)} %param.11, bf16[128,2048]{1,0:T(8,128)(2,1)} %collective-permute-done.5, bf16[128,2048]{1,0:T(8,128)(2,1)} %collective-permute-done.4), kind=kOutput, calls=%fused_computation.47 | convolution fusion | flops 1075838976 | bytes 6291456 | tf_op jit(solution)/shard_map/dot_general | solution.py:104
  61.1 8.7 %collective-permute-done.9 = bf16[128,2048]{1,0:T(8,128)(2,1)S(1)} collective-permute-done((bf16[128,2048]{1,0:T(8,128)(2,1)}, bf16[128,2048]{1,0:T(8,128)(2,1)S(1)}, u32[]{:S(2)}, u32[]{:S(2)}) %collective-permute-start.9) | collective-permute-done | bytes 524320 | tf_op jit(solution)/shard_map/ppermute | solution.py:80
  81.6 5.0 %collective-permute-done.13 = bf16[64,2048]{1,0:T(8,128)(2,1)S(1)} collective-permute-done((bf16[64,2048]{1,0:T(8,128)(2,1)S(1)}, bf16[64,2048]{1,0:T(8,128)(2,1)S(1)}, u32[]{:S(2)}, u32[]{:S(2)}) %collective-permute-start.13) | collective-permute-done | bytes 262176 | tf_op jit(solution)/shard_map/ppermute | solution.py:80
  92.2 3.9 %collective-permute-done.21 = bf16[128,2048]{1,0:T(8,128)(2,1)S(1)} collective-permute-done((bf16[128,2048]{1,0:T(8,128)(2,1)S(1)}, bf16[128,2048]{1,0:T(8,128)(2,1)S(1)}, u32[]{:S(2)}, u32[]{:S(2)}) %collective-permute-start.21) | collective-permute-done | bytes 524320 | tf_op jit(solution)/shard_map/ppermute | solution.py:80
  100.6 4.4 %collective-permute-done.20 = bf16[1,128,1024]{2,1,0:T(8,128)(2,1)S(1)} collective-permute-done((bf16[1,128,1024]{2,1,0:T(8,128)(2,1)S(1)}, bf16[1,128,1024]{2,1,0:T(8,128)(2,1)S(1)}, u32[]{:S(2)}, u32[]{:S(2)}) %collective-permute-start.20) | collective-permute-done | bytes 262176 | tf_op jit(solution)/shard_map/ppermute | solution.py:100
  105.2 8.2 %collective-permute-start.23 = (bf16[128,1024]{1,0:T(8,128)(2,1)S(1)}, bf16[128,1024]{1,0:T(8,128)(2,1)}, u32[]{:S(2)}, u32[]{:S(2)}) collective-permute-start(bf16[128,1024]{1,0:T(8,128)(2,1)S(1)} %fusion.88), channel_id=1, source_target_pairs={{0,28},{1,0},{2,12},{3,16},{8,21},{9,9},{10,5},{11,25},{16,14},{17... | collective-permute-start | bytes 786440 | tf_op jit(solution)/shard_map/ppermute | solution.py:162
  116.2 5.2 %fusion.12 = f32[3,128,1024]{2,1,0:T(8,128)} fusion(bf16[3,128,2048]{2,1,0:T(8,128)(2,1)S(1)} %bitcast.162, bf16[3,2048,1024]{2,1,0:T(8,128)(2,1)} %param.12), kind=kOutput, calls=%fused_computation.12 | convolution fusion | flops 1610612736 | bytes 7340032 | tf_op jit(solution)/shard_map/dot_general | solution.py:104
  127.6 4.5 %fusion.36 = f32[3,128,1024]{2,1,0:T(8,128)S(1)} fusion(f32[3,128,1024]{2,1,0:T(8,128)} %fusion.12, bf16[3,128,2048]{2,1,0:T(8,128)(2,1)S(1)} %bitcast.161, bf16[3,2048,1024]{2,1,0:T(8,128)(2,1)} %param.12), kind=kOutput, calls=%fused_computation.39 | convolution fusion | flops 1611005952 | bytes 8912896 | tf_op jit(solution)/shard_map/dot_general | solution.py:104
  132.1 3.2 %fusion.22 = f32[128,1024]{1,0:T(8,128)S(1)} fusion(bf16[3,2048,1024]{2,1,0:T(8,128)(2,1)} %param.12, bf16[64,2048]{1,0:T(8,128)(2,1)} %collective-permute-done.25, bf16[64,2048]{1,0:T(8,128)(2,1)} %collective-permute-done.24), kind=kOutput, calls=%fused_computation.22 | convolution fusion | flops 537919488 | bytes 5242880 | tf_op jit(solution)/shard_map/dot_general | solution.py:104
  135.3 3.2 %collective-permute-done.26 = bf16[128,2048]{1,0:T(8,128)(2,1)S(1)} collective-permute-done((bf16[128,2048]{1,0:T(8,128)(2,1)}, bf16[128,2048]{1,0:T(8,128)(2,1)S(1)}, u32[]{:S(2)}, u32[]{:S(2)}) %collective-permute-start.26) | collective-permute-done | bytes 524320 | tf_op jit(solution)/shard_map/ppermute | solution.py:80
  140.5 8.6 %collective-permute-done.28 = bf16[128,2048]{1,0:T(8,128)(2,1)S(1)} collective-permute-done((bf16[128,2048]{1,0:T(8,128)(2,1)S(1)}, bf16[128,2048]{1,0:T(8,128)(2,1)S(1)}, u32[]{:S(2)}, u32[]{:S(2)}) %collective-permute-start.28) | collective-permute-done | bytes 524320 | tf_op jit(solution)/shard_map/ppermute | solution.py:80
  153.3 4.2 %fusion.39 = f32[3,128,1024]{2,1,0:T(8,128)S(1)} fusion(f32[3,128,1024]{2,1,0:T(8,128)S(1)} %fusion.36, bf16[3,128,2048]{2,1,0:T(8,128)(2,1)S(1)} %bitcast.165, bf16[3,2048,1024]{2,1,0:T(8,128)(2,1)} %param.12), kind=kOutput, calls=%fused_computation.40 | convolution fusion | flops 1611005952 | bytes 8912896 | tf_op jit(solution)/shard_map/dot_general | solution.py:104
  160.4 13.8 %collective-permute-done.32 = bf16[128,2048]{1,0:T(8,128)(2,1)S(1)} collective-permute-done((bf16[128,2048]{1,0:T(8,128)(2,1)S(1)}, bf16[128,2048]{1,0:T(8,128)(2,1)S(1)}, u32[]{:S(2)}, u32[]{:S(2)}) %collective-permute-start.32) | collective-permute-done | bytes 524320 | tf_op jit(solution)/shard_map/ppermute | solution.py:80
  187.9 3.0 %collective-permute-done.35 = bf16[128,2048]{1,0:T(8,128)(2,1)S(1)} collective-permute-done((bf16[128,2048]{1,0:T(8,128)(2,1)S(1)}, bf16[128,2048]{1,0:T(8,128)(2,1)S(1)}, u32[]{:S(2)}, u32[]{:S(2)}) %collective-permute-start.35) | collective-permute-done | bytes 524320 | tf_op jit(solution)/shard_map/ppermute | solution.py:80
  204.1 4.6 %collective-permute-done.51 = bf16[64,2048]{1,0:T(8,128)(2,1)S(1)} collective-permute-done((bf16[64,2048]{1,0:T(8,128)(2,1)S(1)}, bf16[64,2048]{1,0:T(8,128)(2,1)S(1)}, u32[]{:S(2)}, u32[]{:S(2)}) %collective-permute-start.51) | collective-permute-done | bytes 262176 | tf_op jit(solution)/shard_map/ppermute | solution.py:80
  211.2 3.5 %collective-permute-start.53 = (bf16[32,1024]{1,0:T(8,128)(2,1)S(1)}, bf16[32,1024]{1,0:T(8,128)(2,1)S(1)}, u32[]{:S(2)}, u32[]{:S(2)}) collective-permute-start(bf16[32,1024]{1,0:T(8,128)(2,1)S(1)} %get-tuple-element.142), channel_id=1, source_target_pairs={{0,28},{1,29},{2,30},{3,31},{8,20},{9,21},{10,22},{11,23},{16,12},... | collective-permute-start | bytes 196616 | tf_op jit(solution)/shard_map/ppermute | solution.py:198
  216.1 3.4 %collective-permute-start.48 = (bf16[32,1024]{1,0:T(8,128)(2,1)S(1)}, bf16[32,1024]{1,0:T(8,128)(2,1)S(1)}, u32[]{:S(2)}, u32[]{:S(2)}) collective-permute-start(bf16[32,1024]{1,0:T(8,128)(2,1)S(1)} %get-tuple-element.144), channel_id=1, source_target_pairs={{0,20},{1,21},{2,22},{3,23},{8,12},{9,13},{10,14},{11,15},{16,4},{... | collective-permute-start | bytes 196616 | tf_op jit(solution)/shard_map/ppermute | solution.py:198
  220.0 2.9 %collective-permute-done.54.refs_8_ = bf16[32,1024]{1,0:T(8,128)(2,1)S(1)} collective-permute-done((bf16[32,1024]{1,0:T(8,128)(2,1)S(1)}, bf16[32,1024]{1,0:T(8,128)(2,1)S(1)}, u32[]{:S(2)}, u32[]{:S(2)}) %collective-permute-start.54) | collective-permute-done | bytes 65568 | tf_op jit(solution)/shard_map/ppermute | solution.py:198
  223.0 3.3 %collective-permute-done.49.refs_6_ = bf16[32,1024]{1,0:T(8,128)(2,1)S(1)} collective-permute-done((bf16[32,1024]{1,0:T(8,128)(2,1)S(1)}, bf16[32,1024]{1,0:T(8,128)(2,1)S(1)}, u32[]{:S(2)}, u32[]{:S(2)}) %collective-permute-start.49) | collective-permute-done | bytes 65568 | tf_op jit(solution)/shard_map/ppermute | solution.py:198
  (187 shorter events, 92.0 us)
Async XLA Ops:
  0.0 16.0 %collective-permute-start = (bf16[128,2048]{1,0:T(8,128)(2,1)}, bf16[128,2048]{1,0:T(8,128)(2,1)}, u32[]{:S(2)}, u32[]{:S(2)}) collective-permute-start(bf16[128,2048]{1,0:T(8,128)(2,1)} %param.7), channel_id=1, source_target_pairs={{0,8},{8,16},{16,24},{24,28},{28,20},{20,12},{12,4},{4,0},{1,9},{9... | collective-permute-start | bytes 1572872 | tf_op jit(solution)/shard_map/ppermute | solution.py:80
  3.0 23.3 %collective-permute-start.2 = (bf16[128,2048]{1,0:T(8,128)(2,1)}, bf16[128,2048]{1,0:T(8,128)(2,1)S(1)}, u32[]{:S(2)}, u32[]{:S(2)}) collective-permute-start(bf16[128,2048]{1,0:T(8,128)(2,1)} %param.9), channel_id=1, source_target_pairs={{0,8},{8,16},{16,24},{24,28},{28,20},{20,12},{12,4},{4,0},{1,9},{9... | collective-permute-start | bytes 1572872 | tf_op jit(solution)/shard_map/ppermute | solution.py:80
  5.1 22.8 %collective-permute-start.3 = (bf16[128,2048]{1,0:T(8,128)(2,1)}, bf16[128,2048]{1,0:T(8,128)(2,1)S(1)}, u32[]{:S(2)}, u32[]{:S(2)}) collective-permute-start(bf16[128,2048]{1,0:T(8,128)(2,1)} %param.9), channel_id=1, source_target_pairs={{8,0},{16,8},{24,16},{28,24},{20,28},{12,20},{4,12},{0,4},{9,1},{1... | collective-permute-start | bytes 1572872 | tf_op jit(solution)/shard_map/ppermute | solution.py:80
  27.9 15.2 %collective-permute-start.4 = (bf16[128,2048]{1,0:T(8,128)(2,1)}, bf16[128,2048]{1,0:T(8,128)(2,1)}, u32[]{:S(2)}, u32[]{:S(2)}) collective-permute-start(bf16[128,2048]{1,0:T(8,128)(2,1)} %collective-permute-done), channel_id=1, source_target_pairs={{0,8},{8,16},{16,24},{24,28},{28,20},{20,12},{12,4},{4,0},{1,9},{9... | collective-permute-start | bytes 1572872 | tf_op jit(solution)/shard_map/ppermute | solution.py:80
  29.9 21.9 %collective-permute-start.6 = (bf16[128,2048]{1,0:T(8,128)(2,1)S(1)}, bf16[128,2048]{1,0:T(8,128)(2,1)S(1)}, u32[]{:S(2)}, u32[]{:S(2)}) collective-permute-start(bf16[128,2048]{1,0:T(8,128)(2,1)S(1)} %collective-permute-done.2), channel_id=1, source_target_pairs={{0,8},{8,16},{16,24},{24,28},{28,20},{20,12},{12,4},{4,0},{1,9},{9... | collective-permute-start | bytes 1572872 | tf_op jit(solution)/shard_map/ppermute | solution.py:80
  31.5 21.7 %collective-permute-start.7 = (bf16[128,2048]{1,0:T(8,128)(2,1)S(1)}, bf16[128,2048]{1,0:T(8,128)(2,1)}, u32[]{:S(2)}, u32[]{:S(2)}) collective-permute-start(bf16[128,2048]{1,0:T(8,128)(2,1)S(1)} %collective-permute-done.3), channel_id=1, source_target_pairs={{8,0},{16,8},{24,16},{28,24},{20,28},{12,20},{4,12},{0,4},{9,1},{1... | collective-permute-start | bytes 1572872 | tf_op jit(solution)/shard_map/ppermute | solution.py:80
  53.2 19.1 %collective-permute-start.8 = (bf16[128,2048]{1,0:T(8,128)(2,1)}, bf16[128,2048]{1,0:T(8,128)(2,1)S(1)}, u32[]{:S(2)}, u32[]{:S(2)}) collective-permute-start(bf16[128,2048]{1,0:T(8,128)(2,1)} %collective-permute-done.4), channel_id=1, source_target_pairs={{0,8},{8,16},{16,24},{24,28},{28,20},{20,12},{12,4},{4,0},{1,9},{9... | collective-permute-start | bytes 1572872 | tf_op jit(solution)/shard_map/ppermute | solution.py:80
  55.2 21.3 %collective-permute-start.10 = (bf16[128,2048]{1,0:T(8,128)(2,1)S(1)}, bf16[128,2048]{1,0:T(8,128)(2,1)S(1)}, u32[]{:S(2)}, u32[]{:S(2)}) collective-permute-start(bf16[128,2048]{1,0:T(8,128)(2,1)S(1)} %collective-permute-done.6), channel_id=1, source_target_pairs={{0,8},{8,16},{16,24},{24,28},{28,20},{20,12},{12,4},{4,0},{1,9},{9... | collective-permute-start | bytes 1572872 | tf_op jit(solution)/shard_map/ppermute | solution.py:80
  56.8 20.4 %collective-permute-start.11 = (bf16[128,2048]{1,0:T(8,128)(2,1)}, bf16[128,2048]{1,0:T(8,128)(2,1)S(1)}, u32[]{:S(2)}, u32[]{:S(2)}) collective-permute-start(bf16[128,2048]{1,0:T(8,128)(2,1)} %collective-permute-done.7), channel_id=1, source_target_pairs={{8,0},{16,8},{24,16},{28,24},{20,28},{12,20},{4,12},{0,4},{9,1},{1... | collective-permute-start | bytes 1572872 | tf_op jit(solution)/shard_map/ppermute | solution.py:80
  61.1 15.3 %collective-permute-start.12 = (f32[128,1024]{1,0:T(8,128)S(1)}, f32[128,1024]{1,0:T(8,128)S(1)}, u32[]{:S(2)}, u32[]{:S(2)}) collective-permute-start(f32[128,1024]{1,0:T(8,128)S(1)} %dynamic-slice_bitcast_fusion.5), channel_id=1, source_target_pairs={{0,1},{1,0},{2,3},{3,2},{4,5},{5,4},{6,7},{7,6},{8,9},{9,8},{10,11... | collective-permute-start | bytes 1572872 | tf_op jit(solution)/shard_map/ppermute | solution.py:100
  79.4 16.7 %collective-permute-start.21 = (bf16[128,2048]{1,0:T(8,128)(2,1)S(1)}, bf16[128,2048]{1,0:T(8,128)(2,1)S(1)}, u32[]{:S(2)}, u32[]{:S(2)}) collective-permute-start(bf16[128,2048]{1,0:T(8,128)(2,1)S(1)} %copy-done.2), channel_id=1, source_target_pairs={{0,8},{8,16},{16,24},{24,28},{28,20},{20,12},{12,4},{4,0},{1,9},{9... | collective-permute-start | bytes 1572872 | tf_op jit(solution)/shard_map/ppermute | solution.py:80
  80.9 16.5 %collective-permute-start.22 = (bf16[128,2048]{1,0:T(8,128)(2,1)S(1)}, bf16[128,2048]{1,0:T(8,128)(2,1)S(1)}, u32[]{:S(2)}, u32[]{:S(2)}) collective-permute-start(bf16[128,2048]{1,0:T(8,128)(2,1)S(1)} %copy-done.2), channel_id=1, source_target_pairs={{8,0},{16,8},{24,16},{28,24},{20,28},{12,20},{4,12},{0,4},{9,1},{1... | collective-permute-start | bytes 1572872 | tf_op jit(solution)/shard_map/ppermute | solution.py:80
  99.9 21.5 %collective-permute-start.18 = (bf16[128,1024]{1,0:T(8,128)(2,1)S(1)}, bf16[128,1024]{1,0:T(8,128)(2,1)}, u32[]{:S(2)}, u32[]{:S(2)}) collective-permute-start(bf16[128,1024]{1,0:T(8,128)(2,1)S(1)} %fusion.89), channel_id=1, source_target_pairs={{0,24},{1,4},{2,8},{3,20},{8,29},{9,1},{10,17},{11,13},{16,22},{17... | collective-permute-start | bytes 786440 | tf_op jit(solution)/shard_map/ppermute | solution.py:162
  105.2 16.2 %collective-permute-start.23 = (bf16[128,1024]{1,0:T(8,128)(2,1)S(1)}, bf16[128,1024]{1,0:T(8,128)(2,1)}, u32[]{:S(2)}, u32[]{:S(2)}) collective-permute-start(bf16[128,1024]{1,0:T(8,128)(2,1)S(1)} %fusion.88), channel_id=1, source_target_pairs={{0,28},{1,0},{2,12},{3,16},{8,21},{9,9},{10,5},{11,25},{16,14},{17... | collective-permute-start | bytes 786440 | tf_op jit(solution)/shard_map/ppermute | solution.py:162
  124.8 15.7 %collective-permute-start.27 = (bf16[128,2048]{1,0:T(8,128)(2,1)}, bf16[128,2048]{1,0:T(8,128)(2,1)S(1)}, u32[]{:S(2)}, u32[]{:S(2)}) collective-permute-start(bf16[128,2048]{1,0:T(8,128)(2,1)} %add_residual.1), channel_id=1, source_target_pairs={{8,0},{16,8},{24,16},{28,24},{20,28},{12,20},{4,12},{0,4},{9,1},{1... | collective-permute-start | bytes 1572872 | tf_op jit(solution)/shard_map/ppermute | solution.py:80
  125.6 23.5 %collective-permute-start.28 = (bf16[128,2048]{1,0:T(8,128)(2,1)S(1)}, bf16[128,2048]{1,0:T(8,128)(2,1)S(1)}, u32[]{:S(2)}, u32[]{:S(2)}) collective-permute-start(bf16[128,2048]{1,0:T(8,128)(2,1)S(1)} %collective-permute-done.21), channel_id=1, source_target_pairs={{0,8},{8,16},{16,24},{24,28},{28,20},{20,12},{12,4},{4,0},{1,9},{9... | collective-permute-start | bytes 1572872 | tf_op jit(solution)/shard_map/ppermute | solution.py:80
  127.4 21.7 %collective-permute-start.29 = (bf16[128,2048]{1,0:T(8,128)(2,1)}, bf16[128,2048]{1,0:T(8,128)(2,1)S(1)}, u32[]{:S(2)}, u32[]{:S(2)}) collective-permute-start(bf16[128,2048]{1,0:T(8,128)(2,1)} %copy-done.3), channel_id=1, source_target_pairs={{8,0},{16,8},{24,16},{28,24},{20,28},{12,20},{4,12},{0,4},{9,1},{1... | collective-permute-start | bytes 1572872 | tf_op jit(solution)/shard_map/ppermute | solution.py:80
  149.1 26.5 %collective-permute-start.30 = (bf16[128,2048]{1,0:T(8,128)(2,1)S(1)}, bf16[128,2048]{1,0:T(8,128)(2,1)S(1)}, u32[]{:S(2)}, u32[]{:S(2)}) collective-permute-start(bf16[128,2048]{1,0:T(8,128)(2,1)S(1)} %collective-permute-done.26), channel_id=1, source_target_pairs={{0,8},{8,16},{16,24},{24,28},{28,20},{20,12},{12,4},{4,0},{1,9},{9... | collective-permute-start | bytes 1572872 | tf_op jit(solution)/shard_map/ppermute | solution.py:80
  150.0 25.6 %collective-permute-start.31 = (bf16[128,2048]{1,0:T(8,128)(2,1)S(1)}, bf16[128,2048]{1,0:T(8,128)(2,1)S(1)}, u32[]{:S(2)}, u32[]{:S(2)}) collective-permute-start(bf16[128,2048]{1,0:T(8,128)(2,1)S(1)} %collective-permute-done.27), channel_id=1, source_target_pairs={{8,0},{16,8},{24,16},{28,24},{20,28},{12,20},{4,12},{0,4},{9,1},{1... | collective-permute-start | bytes 1572872 | tf_op jit(solution)/shard_map/ppermute | solution.py:80
  151.1 23.1 %collective-permute-start.32 = (bf16[128,2048]{1,0:T(8,128)(2,1)S(1)}, bf16[128,2048]{1,0:T(8,128)(2,1)S(1)}, u32[]{:S(2)}, u32[]{:S(2)}) collective-permute-start(bf16[128,2048]{1,0:T(8,128)(2,1)S(1)} %collective-permute-done.28), channel_id=1, source_target_pairs={{0,8},{8,16},{16,24},{24,28},{28,20},{20,12},{12,4},{4,0},{1,9},{9... | collective-permute-start | bytes 1572872 | tf_op jit(solution)/shard_map/ppermute | solution.py:80
  152.0 22.2 %collective-permute-start.33 = (bf16[128,2048]{1,0:T(8,128)(2,1)S(1)}, bf16[128,2048]{1,0:T(8,128)(2,1)S(1)}, u32[]{:S(2)}, u32[]{:S(2)}) collective-permute-start(bf16[128,2048]{1,0:T(8,128)(2,1)S(1)} %collective-permute-done.29), channel_id=1, source_target_pairs={{8,0},{16,8},{24,16},{28,24},{20,28},{12,20},{4,12},{0,4},{9,1},{1... | collective-permute-start | bytes 1572872 | tf_op jit(solution)/shard_map/ppermute | solution.py:80
  157.5 19.4 %collective-permute-start.34 = (f32[3,2,32,1024]{3,2,1,0:T(8,128)S(1)}, f32[3,2,32,1024]{3,2,1,0:T(8,128)S(1)}, u32[]{:S(2)}, u32[]{:S(2)}) collective-permute-start(f32[3,2,32,1024]{3,2,1,0:T(8,128)S(1)} %dynamic-slice_bitcast_fusion), channel_id=1, source_target_pairs={{0,1},{1,0},{2,3},{3,2},{4,5},{5,4},{6,7},{7,6},{8,9},{9,8},{10,11... | collective-permute-start | bytes 2359304 | tf_op jit(solution)/shard_map/ppermute | solution.py:100
  200.3 19.2 %collective-permute-start.44 = (bf16[32,1024]{1,0:T(8,128)(2,1)S(1)}, bf16[32,1024]{1,0:T(8,128)(2,1)S(1)}, u32[]{:S(2)}, u32[]{:S(2)}) collective-permute-start(bf16[32,1024]{1,0:T(8,128)(2,1)S(1)} %get-tuple-element.146), channel_id=1, source_target_pairs={{0,12},{1,13},{2,14},{3,15},{8,4},{9,5},{10,6},{11,7},{16,0},{17,1... | collective-permute-start | bytes 196616 | tf_op jit(solution)/shard_map/ppermute | solution.py:198
  203.2 16.8 %collective-permute-start.45 = (bf16[32,1024]{1,0:T(8,128)(2,1)S(1)}, bf16[32,1024]{1,0:T(8,128)(2,1)S(1)}, u32[]{:S(2)}, u32[]{:S(2)}) collective-permute-start(bf16[32,1024]{1,0:T(8,128)(2,1)S(1)} %get-tuple-element.145), channel_id=1, source_target_pairs={{0,16},{1,17},{2,18},{3,19},{8,24},{9,25},{10,26},{11,27},{16,28},... | collective-permute-start | bytes 196616 | tf_op jit(solution)/shard_map/ppermute | solution.py:198
  (48 other events, 463.9 us)

commit v16 on v15

--- a/solution.py
+++ b/solution.py
@@ -218,20 +218,20 @@
 
     cored, deep_sum, summed = None, None, None
     for hop in range(1, last + 1):
-        top.ends, mid.ends, cored, deep_sum = tie(top.ends, mid.ends, cored, deep_sum)
+        top.ends, mid.ends, cored, deep_sum, summed = tie(top.ends, mid.ends, cored, deep_sum, summed)
         top.hop()
         if hop != last - 1:
             mid.hop()
+        if hop > 3:
+            send_all(chunks[hop - 4], summed)
         if hop > 2:
             summed = add_x(cored)
-            if hop < last:
-                send_all(chunks[hop - 3], summed)
         if hop > 1:
             cored = add_cores(multiply(chunks[hop - 2], deep_sum))
         if hop < last:
             deep_sum = multiply_deep(chunks[hop - 1])
     deep_sum = multiply_deep(chunks[-1])
-    top.slots[last], owned, summed = tie(top.ends, owned, summed)
+    top.slots[last], summed = tie(top.ends, summed)
     send_all(chunks[-3], summed)
     send_all(chunks[-2], add_x(cored))
     add_halves(chunks[-1], add_cores(multiply(chunks[-1], deep_sum)))

time: 230 us -> 236 us (1.026)
  waiting for transfers between devices: 116 us -> 122 us
    ppermute x16, waiting for transfers between devices: 73.6 us -> 89.9 us  [hop(): lax.ppermute(ends[0], 'dp', up)]
    ppermute x16, waiting for transfers between devices: 25.6 us -> 14.9 us  [hop(): lax.ppermute(ends[1], 'dp', down)]
    ppermute x8, waiting for transfers between devices: 6.29 us -> 3.71 us  [send(): return lax.ppermute(part.astype(jnp.bfloat16), ('dp', 'tensor'), moves)]
  transfers between devices with their start and end apart: 55 -> 55, of which waited for: 28 -> 31; matrix products, arithmetic and copies ran while one was open for 19% -> 18% of each run, Pallas kernels for 1% -> 1%
where the time goes in v16:
time: 236 us; the launch traced here: 235 us
  waiting for transfers between devices  122 us (52%)
  starting transfers between devices  64.6 us (27%)
  matrix products  35.8 us (15%)
  other arithmetic  5.02 us (2%)
  Pallas kernels  4.41 us (2%)
  local copies, waits for them, and re-layouts  2.94 us (1%)
    ppermute x16, waiting for transfers between devices, hop(): lax.ppermute(ends[0], 'dp', up)  89.9 us
    dot_general x16, matrix products, product(): jnp.dot(rows_in, weight, preferred_element_type=jnp.float32)  35.8 us
    ppermute x16, starting transfers between devices, hop(): lax.ppermute(ends[0], 'dp', up)  22.7 us
    ppermute x16, waiting for transfers between devices, hop(): lax.ppermute(ends[1], 'dp', down)  14.9 us
    ppermute x8, starting transfers between devices, send(): return lax.ppermute(part.astype(jnp.bfloat16), ('dp', 'tensor'), moves)  14.7 us
    ppermute x13, waiting for transfers between devices, swap(): return lax.ppermute(values, 'tensor', [(t, t ^ bit) for t in range(owners)])  13.1 us
    ppermute x16, starting transfers between devices, hop(): lax.ppermute(ends[1], 'dp', down)  11.6 us
    ppermute x2, starting transfers between devices, local(): arrived.append(lax.ppermute(held, ('dp', 'tensor'), moves))  8.88 us
  transfers between devices with their start and end apart: 55, of which 31 were waited for; matrix products, arithmetic and copies ran while one was open for 18% of the time, Pallas kernels for 1%

profile of v16, /device:TPU:0, one launch (start us, length us, event | category | flops | bytes accessed | tf_op | source)
XLA Modules:
  0.0 235.2 jit_solution(4891918684429907270)
XLA Ops:
  0.0 3.0 %collective-permute-start = (bf16[128,2048]{1,0:T(8,128)(2,1)}, bf16[128,2048]{1,0:T(8,128)(2,1)}, u32[]{:S(2)}, u32[]{:S(2)}) collective-permute-start(bf16[128,2048]{1,0:T(8,128)(2,1)} %param.7), channel_id=1, source_target_pairs={{0,8},{8,16},{16,24},{24,28},{28,20},{20,12},{12,4},{4,0},{1,9},{9... | collective-permute-start | bytes 1572872 | tf_op jit(solution)/shard_map/ppermute | solution.py:80
  5.1 11.0 %collective-permute-done = bf16[128,2048]{1,0:T(8,128)(2,1)} collective-permute-done((bf16[128,2048]{1,0:T(8,128)(2,1)}, bf16[128,2048]{1,0:T(8,128)(2,1)}, u32[]{:S(2)}, u32[]{:S(2)}) %collective-permute-start) | collective-permute-done | bytes 524320 | tf_op jit(solution)/shard_map/ppermute | solution.py:80
  18.2 8.1 %collective-permute-done.2 = bf16[128,2048]{1,0:T(8,128)(2,1)S(1)} collective-permute-done((bf16[128,2048]{1,0:T(8,128)(2,1)}, bf16[128,2048]{1,0:T(8,128)(2,1)S(1)}, u32[]{:S(2)}, u32[]{:S(2)}) %collective-permute-start.2) | collective-permute-done | bytes 524320 | tf_op jit(solution)/shard_map/ppermute | solution.py:80
  33.1 9.9 %collective-permute-done.4 = bf16[128,2048]{1,0:T(8,128)(2,1)} collective-permute-done((bf16[128,2048]{1,0:T(8,128)(2,1)}, bf16[128,2048]{1,0:T(8,128)(2,1)}, u32[]{:S(2)}, u32[]{:S(2)}) %collective-permute-start.4) | collective-permute-done | bytes 524320 | tf_op jit(solution)/shard_map/ppermute | solution.py:80
  44.6 7.2 %collective-permute-done.6 = bf16[128,2048]{1,0:T(8,128)(2,1)S(1)} collective-permute-done((bf16[128,2048]{1,0:T(8,128)(2,1)S(1)}, bf16[128,2048]{1,0:T(8,128)(2,1)S(1)}, u32[]{:S(2)}, u32[]{:S(2)}) %collective-permute-start.6) | collective-permute-done | bytes 524320 | tf_op jit(solution)/shard_map/ppermute | solution.py:80
  57.2 3.8 %fusion.60 = f32[256,1024]{1,0:T(8,128)S(1)} fusion(bf16[2048,1024]{1,0:T(8,128)(2,1)} %param.11, bf16[128,2048]{1,0:T(8,128)(2,1)} %collective-permute-done.5, bf16[128,2048]{1,0:T(8,128)(2,1)} %collective-permute-done.4), kind=kOutput, calls=%fused_computation.47 | convolution fusion | flops 1075838976 | bytes 6291456 | tf_op jit(solution)/shard_map/dot_general | solution.py:104
  61.1 7.1 %collective-permute-done.8 = bf16[128,2048]{1,0:T(8,128)(2,1)S(1)} collective-permute-done((bf16[128,2048]{1,0:T(8,128)(2,1)}, bf16[128,2048]{1,0:T(8,128)(2,1)S(1)}, u32[]{:S(2)}, u32[]{:S(2)}) %collective-permute-start.8) | collective-permute-done | bytes 524320 | tf_op jit(solution)/shard_map/ppermute | solution.py:80
  81.6 4.9 %collective-permute-done.13 = bf16[64,2048]{1,0:T(8,128)(2,1)S(1)} collective-permute-done((bf16[64,2048]{1,0:T(8,128)(2,1)S(1)}, bf16[64,2048]{1,0:T(8,128)(2,1)S(1)}, u32[]{:S(2)}, u32[]{:S(2)}) %collective-permute-start.13) | collective-permute-done | bytes 262176 | tf_op jit(solution)/shard_map/ppermute | solution.py:80
  100.6 4.4 %collective-permute-done.20 = bf16[1,128,1024]{2,1,0:T(8,128)(2,1)S(1)} collective-permute-done((bf16[1,128,1024]{2,1,0:T(8,128)(2,1)S(1)}, bf16[1,128,1024]{2,1,0:T(8,128)(2,1)S(1)}, u32[]{:S(2)}, u32[]{:S(2)}) %collective-permute-start.20) | collective-permute-done | bytes 262176 | tf_op jit(solution)/shard_map/ppermute | solution.py:100
  105.2 8.2 %collective-permute-start.23 = (bf16[128,1024]{1,0:T(8,128)(2,1)S(1)}, bf16[128,1024]{1,0:T(8,128)(2,1)}, u32[]{:S(2)}, u32[]{:S(2)}) collective-permute-start(bf16[128,1024]{1,0:T(8,128)(2,1)S(1)} %fusion.89), channel_id=1, source_target_pairs={{0,28},{1,0},{2,12},{3,16},{8,21},{9,9},{10,5},{11,25},{16,14},{17... | collective-permute-start | bytes 786440 | tf_op jit(solution)/shard_map/ppermute | solution.py:162
  116.2 5.2 %fusion.12 = f32[3,128,1024]{2,1,0:T(8,128)} fusion(bf16[3,128,2048]{2,1,0:T(8,128)(2,1)S(1)} %bitcast.163, bf16[3,2048,1024]{2,1,0:T(8,128)(2,1)} %param.12), kind=kOutput, calls=%fused_computation.12 | convolution fusion | flops 1610612736 | bytes 7340032 | tf_op jit(solution)/shard_map/dot_general | solution.py:104
  125.6 4.5 %fusion.36 = f32[3,128,1024]{2,1,0:T(8,128)S(1)} fusion(f32[3,128,1024]{2,1,0:T(8,128)} %fusion.12, bf16[3,128,2048]{2,1,0:T(8,128)(2,1)S(1)} %bitcast.162, bf16[3,2048,1024]{2,1,0:T(8,128)(2,1)} %param.12), kind=kOutput, calls=%fused_computation.39 | convolution fusion | flops 1611005952 | bytes 8912896 | tf_op jit(solution)/shard_map/dot_general | solution.py:104
  132.2 3.2 %fusion.22 = f32[128,1024]{1,0:T(8,128)S(1)} fusion(bf16[3,2048,1024]{2,1,0:T(8,128)(2,1)} %param.12, bf16[64,2048]{1,0:T(8,128)(2,1)} %collective-permute-done.25, bf16[64,2048]{1,0:T(8,128)(2,1)} %collective-permute-done.24), kind=kOutput, calls=%fused_computation.22 | convolution fusion | flops 537919488 | bytes 5242880 | tf_op jit(solution)/shard_map/dot_general | solution.py:104
  135.4 2.7 %collective-permute-done.28 = bf16[128,2048]{1,0:T(8,128)(2,1)S(1)} collective-permute-done((bf16[128,2048]{1,0:T(8,128)(2,1)S(1)}, bf16[128,2048]{1,0:T(8,128)(2,1)S(1)}, u32[]{:S(2)}, u32[]{:S(2)}) %collective-permute-start.28) | collective-permute-done | bytes 524320 | tf_op jit(solution)/shard_map/ppermute | solution.py:80
  140.3 3.6 %fusion.10 = f32[2,128,1024]{2,1,0:T(8,128)S(1)} fusion(bf16[2,128,2048]{2,1,0:T(8,128)(2,1)S(1)} %bitcast.171, bf16[3,2048,1024]{2,1,0:T(8,128)(2,1)} %param.12), kind=kOutput, calls=%fused_computation.10 | convolution fusion | flops 1073741824 | bytes 6291456 | tf_op jit(solution)/shard_map/dot_general | solution.py:104
  143.9 5.4 %collective-permute-done.26 = bf16[128,2048]{1,0:T(8,128)(2,1)S(1)} collective-permute-done((bf16[128,2048]{1,0:T(8,128)(2,1)S(1)}, bf16[128,2048]{1,0:T(8,128)(2,1)S(1)}, u32[]{:S(2)}, u32[]{:S(2)}) %collective-permute-start.26) | collective-permute-done | bytes 524320 | tf_op jit(solution)/shard_map/ppermute | solution.py:80
  157.5 6.9 %collective-permute-done.32 = bf16[128,2048]{1,0:T(8,128)(2,1)S(1)} collective-permute-done((bf16[128,2048]{1,0:T(8,128)(2,1)S(1)}, bf16[128,2048]{1,0:T(8,128)(2,1)S(1)}, u32[]{:S(2)}, u32[]{:S(2)}) %collective-permute-start.32) | collective-permute-done | bytes 524320 | tf_op jit(solution)/shard_map/ppermute | solution.py:80
  165.0 10.1 %collective-permute-done.30 = bf16[128,2048]{1,0:T(8,128)(2,1)S(1)} collective-permute-done((bf16[128,2048]{1,0:T(8,128)(2,1)S(1)}, bf16[128,2048]{1,0:T(8,128)(2,1)S(1)}, u32[]{:S(2)}, u32[]{:S(2)}) %collective-permute-start.30) | collective-permute-done | bytes 524320 | tf_op jit(solution)/shard_map/ppermute | solution.py:80
  183.2 9.3 %collective-permute-done.35 = bf16[128,2048]{1,0:T(8,128)(2,1)S(1)} collective-permute-done((bf16[128,2048]{1,0:T(8,128)(2,1)S(1)}, bf16[128,2048]{1,0:T(8,128)(2,1)S(1)}, u32[]{:S(2)}, u32[]{:S(2)}) %collective-permute-start.35) | collective-permute-done | bytes 524320 | tf_op jit(solution)/shard_map/ppermute | solution.py:80
  200.6 3.4 %collective-permute-done.41 = bf16[64,2048]{1,0:T(8,128)(2,1)S(1)} collective-permute-done((bf16[64,2048]{1,0:T(8,128)(2,1)S(1)}, bf16[64,2048]{1,0:T(8,128)(2,1)S(1)}, u32[]{:S(2)}, u32[]{:S(2)}) %collective-permute-start.41) | collective-permute-done | bytes 262176 | tf_op jit(solution)/shard_map/ppermute | solution.py:80
  214.4 5.0 %collective-permute-done.47 = bf16[2,1,32,1024]{3,2,1,0:T(8,128)(2,1)S(1)} collective-permute-done((bf16[2,1,32,1024]{3,2,1,0:T(8,128)(2,1)S(1)}, bf16[2,1,32,1024]{3,2,1,0:T(8,128)(2,1)S(1)}, u32[]{:S(2)}, u32[]{:S(2)}) %collective-permute-start.47) | collective-permute-done | bytes 131104 | tf_op jit(solution)/shard_map/ppermute | solution.py:100
  219.4 3.6 %collective-permute-start.53 = (bf16[32,1024]{1,0:T(8,128)(2,1)S(1)}, bf16[32,1024]{1,0:T(8,128)(2,1)S(1)}, u32[]{:S(2)}, u32[]{:S(2)}) collective-permute-start(bf16[32,1024]{1,0:T(8,128)(2,1)S(1)} %get-tuple-element.138), channel_id=1, source_target_pairs={{0,28},{1,29},{2,30},{3,31},{8,20},{9,21},{10,22},{11,23},{16,12},... | collective-permute-start | bytes 196616 | tf_op jit(solution)/shard_map/ppermute | solution.py:198
  225.0 2.8 %collective-permute-start.49 = (bf16[32,1024]{1,0:T(8,128)(2,1)S(1)}, bf16[32,1024]{1,0:T(8,128)(2,1)S(1)}, u32[]{:S(2)}, u32[]{:S(2)}) collective-permute-start(bf16[32,1024]{1,0:T(8,128)(2,1)S(1)} %get-tuple-element.139), channel_id=1, source_target_pairs={{0,24},{1,25},{2,26},{3,27},{8,28},{9,29},{10,30},{11,31},{16,20},... | collective-permute-start | bytes 196616 | tf_op jit(solution)/shard_map/ppermute | solution.py:198
  228.6 2.6 %collective-permute-done.54.refs_8_ = bf16[32,1024]{1,0:T(8,128)(2,1)S(1)} collective-permute-done((bf16[32,1024]{1,0:T(8,128)(2,1)S(1)}, bf16[32,1024]{1,0:T(8,128)(2,1)S(1)}, u32[]{:S(2)}, u32[]{:S(2)}) %collective-permute-start.54) | collective-permute-done | bytes 65568 | tf_op jit(solution)/shard_map/ppermute | solution.py:198
  (189 shorter events, 98.4 us)
Async XLA Ops:
  0.0 16.0 %collective-permute-start = (bf16[128,2048]{1,0:T(8,128)(2,1)}, bf16[128,2048]{1,0:T(8,128)(2,1)}, u32[]{:S(2)}, u32[]{:S(2)}) collective-permute-start(bf16[128,2048]{1,0:T(8,128)(2,1)} %param.7), channel_id=1, source_target_pairs={{0,8},{8,16},{16,24},{24,28},{28,20},{20,12},{12,4},{4,0},{1,9},{9... | collective-permute-start | bytes 1572872 | tf_op jit(solution)/shard_map/ppermute | solution.py:80
  3.0 15.2 %collective-permute-start.1 = (bf16[128,2048]{1,0:T(8,128)(2,1)}, bf16[128,2048]{1,0:T(8,128)(2,1)}, u32[]{:S(2)}, u32[]{:S(2)}) collective-permute-start(bf16[128,2048]{1,0:T(8,128)(2,1)} %param.7), channel_id=1, source_target_pairs={{8,0},{16,8},{24,16},{28,24},{20,28},{12,20},{4,12},{0,4},{9,1},{1... | collective-permute-start | bytes 1572872 | tf_op jit(solution)/shard_map/ppermute | solution.py:80
  3.0 23.3 %collective-permute-start.2 = (bf16[128,2048]{1,0:T(8,128)(2,1)}, bf16[128,2048]{1,0:T(8,128)(2,1)S(1)}, u32[]{:S(2)}, u32[]{:S(2)}) collective-permute-start(bf16[128,2048]{1,0:T(8,128)(2,1)} %param.9), channel_id=1, source_target_pairs={{0,8},{8,16},{16,24},{24,28},{28,20},{20,12},{12,4},{4,0},{1,9},{9... | collective-permute-start | bytes 1572872 | tf_op jit(solution)/shard_map/ppermute | solution.py:80
  5.1 22.8 %collective-permute-start.3 = (bf16[128,2048]{1,0:T(8,128)(2,1)}, bf16[128,2048]{1,0:T(8,128)(2,1)S(1)}, u32[]{:S(2)}, u32[]{:S(2)}) collective-permute-start(bf16[128,2048]{1,0:T(8,128)(2,1)} %param.9), channel_id=1, source_target_pairs={{8,0},{16,8},{24,16},{28,24},{20,28},{12,20},{4,12},{0,4},{9,1},{1... | collective-permute-start | bytes 1572872 | tf_op jit(solution)/shard_map/ppermute | solution.py:80
  27.9 15.2 %collective-permute-start.4 = (bf16[128,2048]{1,0:T(8,128)(2,1)}, bf16[128,2048]{1,0:T(8,128)(2,1)}, u32[]{:S(2)}, u32[]{:S(2)}) collective-permute-start(bf16[128,2048]{1,0:T(8,128)(2,1)} %collective-permute-done), channel_id=1, source_target_pairs={{0,8},{8,16},{16,24},{24,28},{28,20},{20,12},{12,4},{4,0},{1,9},{9... | collective-permute-start | bytes 1572872 | tf_op jit(solution)/shard_map/ppermute | solution.py:80
  29.4 15.2 %collective-permute-start.5 = (bf16[128,2048]{1,0:T(8,128)(2,1)}, bf16[128,2048]{1,0:T(8,128)(2,1)}, u32[]{:S(2)}, u32[]{:S(2)}) collective-permute-start(bf16[128,2048]{1,0:T(8,128)(2,1)} %collective-permute-done.1), channel_id=1, source_target_pairs={{8,0},{16,8},{24,16},{28,24},{20,28},{12,20},{4,12},{0,4},{9,1},{1... | collective-permute-start | bytes 1572872 | tf_op jit(solution)/shard_map/ppermute | solution.py:80
  29.9 21.9 %collective-permute-start.6 = (bf16[128,2048]{1,0:T(8,128)(2,1)S(1)}, bf16[128,2048]{1,0:T(8,128)(2,1)S(1)}, u32[]{:S(2)}, u32[]{:S(2)}) collective-permute-start(bf16[128,2048]{1,0:T(8,128)(2,1)S(1)} %collective-permute-done.2), channel_id=1, source_target_pairs={{0,8},{8,16},{16,24},{24,28},{28,20},{20,12},{12,4},{4,0},{1,9},{9... | collective-permute-start | bytes 1572872 | tf_op jit(solution)/shard_map/ppermute | solution.py:80
  31.5 21.7 %collective-permute-start.7 = (bf16[128,2048]{1,0:T(8,128)(2,1)S(1)}, bf16[128,2048]{1,0:T(8,128)(2,1)}, u32[]{:S(2)}, u32[]{:S(2)}) collective-permute-start(bf16[128,2048]{1,0:T(8,128)(2,1)S(1)} %collective-permute-done.3), channel_id=1, source_target_pairs={{8,0},{16,8},{24,16},{28,24},{20,28},{12,20},{4,12},{0,4},{9,1},{1... | collective-permute-start | bytes 1572872 | tf_op jit(solution)/shard_map/ppermute | solution.py:80
  53.2 15.1 %collective-permute-start.8 = (bf16[128,2048]{1,0:T(8,128)(2,1)}, bf16[128,2048]{1,0:T(8,128)(2,1)S(1)}, u32[]{:S(2)}, u32[]{:S(2)}) collective-permute-start(bf16[128,2048]{1,0:T(8,128)(2,1)} %collective-permute-done.4), channel_id=1, source_target_pairs={{0,8},{8,16},{16,24},{24,28},{28,20},{20,12},{12,4},{4,0},{1,9},{9... | collective-permute-start | bytes 1572872 | tf_op jit(solution)/shard_map/ppermute | solution.py:80
  54.8 16.0 %collective-permute-start.9 = (bf16[128,2048]{1,0:T(8,128)(2,1)}, bf16[128,2048]{1,0:T(8,128)(2,1)S(1)}, u32[]{:S(2)}, u32[]{:S(2)}) collective-permute-start(bf16[128,2048]{1,0:T(8,128)(2,1)} %collective-permute-done.5), channel_id=1, source_target_pairs={{8,0},{16,8},{24,16},{28,24},{20,28},{12,20},{4,12},{0,4},{9,1},{1... | collective-permute-start | bytes 1572872 | tf_op jit(solution)/shard_map/ppermute | solution.py:80
  55.2 20.7 %collective-permute-start.10 = (bf16[128,2048]{1,0:T(8,128)(2,1)S(1)}, bf16[128,2048]{1,0:T(8,128)(2,1)S(1)}, u32[]{:S(2)}, u32[]{:S(2)}) collective-permute-start(bf16[128,2048]{1,0:T(8,128)(2,1)S(1)} %collective-permute-done.6), channel_id=1, source_target_pairs={{0,8},{8,16},{16,24},{24,28},{28,20},{20,12},{12,4},{4,0},{1,9},{9... | collective-permute-start | bytes 1572872 | tf_op jit(solution)/shard_map/ppermute | solution.py:80
  56.8 20.4 %collective-permute-start.11 = (bf16[128,2048]{1,0:T(8,128)(2,1)}, bf16[128,2048]{1,0:T(8,128)(2,1)S(1)}, u32[]{:S(2)}, u32[]{:S(2)}) collective-permute-start(bf16[128,2048]{1,0:T(8,128)(2,1)} %collective-permute-done.7), channel_id=1, source_target_pairs={{8,0},{16,8},{24,16},{28,24},{20,28},{12,20},{4,12},{0,4},{9,1},{1... | collective-permute-start | bytes 1572872 | tf_op jit(solution)/shard_map/ppermute | solution.py:80
  79.4 15.1 %collective-permute-start.21 = (bf16[128,2048]{1,0:T(8,128)(2,1)S(1)}, bf16[128,2048]{1,0:T(8,128)(2,1)S(1)}, u32[]{:S(2)}, u32[]{:S(2)}) collective-permute-start(bf16[128,2048]{1,0:T(8,128)(2,1)S(1)} %copy-done.2), channel_id=1, source_target_pairs={{0,8},{8,16},{16,24},{24,28},{28,20},{20,12},{12,4},{4,0},{1,9},{9... | collective-permute-start | bytes 1572872 | tf_op jit(solution)/shard_map/ppermute | solution.py:80
  99.9 21.5 %collective-permute-start.18 = (bf16[128,1024]{1,0:T(8,128)(2,1)S(1)}, bf16[128,1024]{1,0:T(8,128)(2,1)}, u32[]{:S(2)}, u32[]{:S(2)}) collective-permute-start(bf16[128,1024]{1,0:T(8,128)(2,1)S(1)} %fusion.90), channel_id=1, source_target_pairs={{0,24},{1,4},{2,8},{3,20},{8,29},{9,1},{10,17},{11,13},{16,22},{17... | collective-permute-start | bytes 786440 | tf_op jit(solution)/shard_map/ppermute | solution.py:162
  105.2 16.2 %collective-permute-start.23 = (bf16[128,1024]{1,0:T(8,128)(2,1)S(1)}, bf16[128,1024]{1,0:T(8,128)(2,1)}, u32[]{:S(2)}, u32[]{:S(2)}) collective-permute-start(bf16[128,1024]{1,0:T(8,128)(2,1)S(1)} %fusion.89), channel_id=1, source_target_pairs={{0,28},{1,0},{2,12},{3,16},{8,21},{9,9},{10,5},{11,25},{16,14},{17... | collective-permute-start | bytes 786440 | tf_op jit(solution)/shard_map/ppermute | solution.py:162
  130.1 19.2 %collective-permute-start.26 = (bf16[128,2048]{1,0:T(8,128)(2,1)S(1)}, bf16[128,2048]{1,0:T(8,128)(2,1)S(1)}, u32[]{:S(2)}, u32[]{:S(2)}) collective-permute-start(bf16[128,2048]{1,0:T(8,128)(2,1)S(1)} %copy-done), channel_id=1, source_target_pairs={{0,8},{8,16},{16,24},{24,28},{28,20},{20,12},{12,4},{4,0},{1,9},{9... | collective-permute-start | bytes 1572872 | tf_op jit(solution)/shard_map/ppermute | solution.py:80
  132.0 17.3 %collective-permute-start.27 = (bf16[128,2048]{1,0:T(8,128)(2,1)S(1)}, bf16[128,2048]{1,0:T(8,128)(2,1)S(1)}, u32[]{:S(2)}, u32[]{:S(2)}) collective-permute-start(bf16[128,2048]{1,0:T(8,128)(2,1)S(1)} %copy-done), channel_id=1, source_target_pairs={{8,0},{16,8},{24,16},{28,24},{20,28},{12,20},{4,12},{0,4},{9,1},{1... | collective-permute-start | bytes 1572872 | tf_op jit(solution)/shard_map/ppermute | solution.py:80
  149.3 15.1 %collective-permute-start.32 = (bf16[128,2048]{1,0:T(8,128)(2,1)S(1)}, bf16[128,2048]{1,0:T(8,128)(2,1)S(1)}, u32[]{:S(2)}, u32[]{:S(2)}) collective-permute-start(bf16[128,2048]{1,0:T(8,128)(2,1)S(1)} %collective-permute-done.28), channel_id=1, source_target_pairs={{0,8},{8,16},{16,24},{24,28},{28,20},{20,12},{12,4},{4,0},{1,9},{9... | collective-permute-start | bytes 1572872 | tf_op jit(solution)/shard_map/ppermute | solution.py:80
  154.0 22.5 %collective-permute-start.34 = (f32[3,2,32,1024]{3,2,0,1:T(8,128)S(1)}, f32[3,2,32,1024]{3,2,0,1:T(8,128)S(1)}, u32[]{:S(2)}, u32[]{:S(2)}) collective-permute-start(f32[3,2,32,1024]{3,2,0,1:T(8,128)S(1)} %bitcast.181), channel_id=1, source_target_pairs={{0,1},{1,0},{2,3},{3,2},{4,5},{5,4},{6,7},{7,6},{8,9},{9,8},{10,11... | collective-permute-start | bytes 2359304 | tf_op jit(solution)/shard_map/ppermute | solution.py:100
  154.1 21.1 %collective-permute-start.30 = (bf16[128,2048]{1,0:T(8,128)(2,1)S(1)}, bf16[128,2048]{1,0:T(8,128)(2,1)S(1)}, u32[]{:S(2)}, u32[]{:S(2)}) collective-permute-start(bf16[128,2048]{1,0:T(8,128)(2,1)S(1)} %collective-permute-done.26), channel_id=1, source_target_pairs={{0,8},{8,16},{16,24},{24,28},{28,20},{20,12},{12,4},{4,0},{1,9},{9... | collective-permute-start | bytes 1572872 | tf_op jit(solution)/shard_map/ppermute | solution.py:80
  154.5 20.6 %collective-permute-start.31 = (bf16[128,2048]{1,0:T(8,128)(2,1)S(1)}, bf16[128,2048]{1,0:T(8,128)(2,1)S(1)}, u32[]{:S(2)}, u32[]{:S(2)}) collective-permute-start(bf16[128,2048]{1,0:T(8,128)(2,1)S(1)} %collective-permute-done.27), channel_id=1, source_target_pairs={{8,0},{16,8},{24,16},{28,24},{20,28},{12,20},{4,12},{0,4},{9,1},{1... | collective-permute-start | bytes 1572872 | tf_op jit(solution)/shard_map/ppermute | solution.py:80
  204.0 19.1 %collective-permute-start.39 = (bf16[32,1024]{1,0:T(8,128)(2,1)S(1)}, bf16[32,1024]{1,0:T(8,128)(2,1)S(1)}, u32[]{:S(2)}, u32[]{:S(2)}) collective-permute-start(bf16[32,1024]{1,0:T(8,128)(2,1)S(1)} %get-tuple-element.136), channel_id=1, source_target_pairs={{0,4},{1,5},{2,6},{3,7},{8,0},{9,1},{10,2},{11,3},{16,8},{17,9},{1... | collective-permute-start | bytes 196616 | tf_op jit(solution)/shard_map/ppermute | solution.py:198
  205.7 18.3 %collective-permute-start.40 = (bf16[32,1024]{1,0:T(8,128)(2,1)S(1)}, bf16[32,1024]{1,0:T(8,128)(2,1)S(1)}, u32[]{:S(2)}, u32[]{:S(2)}) collective-permute-start(bf16[32,1024]{1,0:T(8,128)(2,1)S(1)} %get-tuple-element.135), channel_id=1, source_target_pairs={{0,8},{1,9},{2,10},{3,11},{8,16},{9,17},{10,18},{11,19},{16,24},{1... | collective-permute-start | bytes 196616 | tf_op jit(solution)/shard_map/ppermute | solution.py:198
  212.6 15.9 %collective-permute-start.45 = (bf16[32,1024]{1,0:T(8,128)(2,1)S(1)}, bf16[32,1024]{1,0:T(8,128)(2,1)S(1)}, u32[]{:S(2)}, u32[]{:S(2)}) collective-permute-start(bf16[32,1024]{1,0:T(8,128)(2,1)S(1)} %get-tuple-element.141), channel_id=1, source_target_pairs={{0,16},{1,17},{2,18},{3,19},{8,24},{9,25},{10,26},{11,27},{16,28},... | collective-permute-start | bytes 196616 | tf_op jit(solution)/shard_map/ppermute | solution.py:198
  (48 other events, 458.8 us)

commit v17 on v8

--- a/solution.py
+++ b/solution.py
@@ -229,7 +229,7 @@
         deep_sum = multiply_deep(chunks[hop - 1])
     for n, total in cored.items():
         add_x(chunks[n], total, jnp.bfloat16)
-    early = {k: owned[k] for part in chunks[:-2] for k in part}
+    early = {k: owned[k] for part in chunks[:-3] for k in part}
     top.slots[last], early, deep_sum = tie(top.ends, early, deep_sum)
     owned.update(early)
     add_halves(chunks[-1], add_cores(multiply(chunks[-1], deep_sum)))

time: 229 us -> 228 us (level)
    ppermute x13, waiting for transfers between devices: 7.52 us -> 10.9 us  [swap(): return lax.ppermute(values, 'tensor', [(t, t ^ bit) for t in range(owners)])]
    ppermute x8, waiting for transfers between devices: 7.54 us -> 4.88 us  [send(): return lax.ppermute(part.astype(jnp.bfloat16), ('dp', 'tensor'), moves)]
  transfers between devices with their start and end apart: 55 -> 55, of which waited for: 33 -> 30; matrix products, arithmetic and copies ran while one was open for 17% -> 17% of each run, Pallas kernels for 1% -> 1%
where the time goes in v17:
time: 228 us; the launch traced here: 227 us
  waiting for transfers between devices  115 us (50%)
  starting transfers between devices  66.8 us (29%)
  matrix products  33.8 us (15%)
  Pallas kernels  4.41 us (2%)
  other arithmetic  4.1 us (2%)
  local copies, waits for them, and re-layouts  2.7 us (1%)
    ppermute x16, waiting for transfers between devices, hop(): lax.ppermute(ends[0], 'dp', up)  84.2 us
    dot_general x16, matrix products, product(): jnp.dot(rows_in, weight, preferred_element_type=jnp.float32)  33.8 us
    ppermute x16, starting transfers between devices, hop(): lax.ppermute(ends[0], 'dp', up)  20.6 us
    ppermute x16, starting transfers between devices, hop(): lax.ppermute(ends[1], 'dp', down)  14.6 us
    ppermute x8, starting transfers between devices, send(): return lax.ppermute(part.astype(jnp.bfloat16), ('dp', 'tensor'), moves)  13.8 us
    ppermute x16, waiting for transfers between devices, hop(): lax.ppermute(ends[1], 'dp', down)  13.3 us
    ppermute x2, starting transfers between devices, local(): arrived.append(lax.ppermute(held, ('dp', 'tensor'), moves))  12.3 us
    ppermute x13, waiting for transfers between devices, swap(): return lax.ppermute(values, 'tensor', [(t, t ^ bit) for t in range(owners)])  10.9 us
  transfers between devices with their start and end apart: 55, of which 30 were waited for; matrix products, arithmetic and copies ran while one was open for 17% of the time, Pallas kernels for 1%

profile of v17, /device:TPU:0, one launch (start us, length us, event | category | flops | bytes accessed | tf_op | source)
XLA Modules:
  0.0 227.4 jit_solution(18408412159849561213)
XLA Ops:
  0.0 3.0 %collective-permute-start = (bf16[128,2048]{1,0:T(8,128)(2,1)}, bf16[128,2048]{1,0:T(8,128)(2,1)S(1)}, u32[]{:S(2)}, u32[]{:S(2)}) collective-permute-start(bf16[128,2048]{1,0:T(8,128)(2,1)} %param.7), channel_id=1, source_target_pairs={{0,8},{8,16},{16,24},{24,28},{28,20},{20,12},{12,4},{4,0},{1,9},{9... | collective-permute-start | bytes 1572872 | tf_op jit(solution)/shard_map/ppermute | solution.py:80
  5.1 10.9 %collective-permute-done = bf16[128,2048]{1,0:T(8,128)(2,1)S(1)} collective-permute-done((bf16[128,2048]{1,0:T(8,128)(2,1)}, bf16[128,2048]{1,0:T(8,128)(2,1)S(1)}, u32[]{:S(2)}, u32[]{:S(2)}) %collective-permute-start) | collective-permute-done | bytes 524320 | tf_op jit(solution)/shard_map/ppermute | solution.py:80
  18.1 8.2 %collective-permute-done.2 = bf16[128,2048]{1,0:T(8,128)(2,1)S(1)} collective-permute-done((bf16[128,2048]{1,0:T(8,128)(2,1)}, bf16[128,2048]{1,0:T(8,128)(2,1)S(1)}, u32[]{:S(2)}, u32[]{:S(2)}) %collective-permute-start.2) | collective-permute-done | bytes 524320 | tf_op jit(solution)/shard_map/ppermute | solution.py:80
  31.9 10.9 %collective-permute-done.4 = bf16[128,2048]{1,0:T(8,128)(2,1)} collective-permute-done((bf16[128,2048]{1,0:T(8,128)(2,1)S(1)}, bf16[128,2048]{1,0:T(8,128)(2,1)}, u32[]{:S(2)}, u32[]{:S(2)}) %collective-permute-start.4) | collective-permute-done | bytes 524320 | tf_op jit(solution)/shard_map/ppermute | solution.py:80
  44.4 7.2 %collective-permute-done.6 = bf16[128,2048]{1,0:T(8,128)(2,1)S(1)} collective-permute-done((bf16[128,2048]{1,0:T(8,128)(2,1)S(1)}, bf16[128,2048]{1,0:T(8,128)(2,1)S(1)}, u32[]{:S(2)}, u32[]{:S(2)}) %collective-permute-start.6) | collective-permute-done | bytes 524320 | tf_op jit(solution)/shard_map/ppermute | solution.py:80
  58.4 3.8 %fusion.63 = f32[256,1024]{1,0:T(8,128)S(1)} fusion(bf16[2048,1024]{1,0:T(8,128)(2,1)} %param.11, bf16[128,2048]{1,0:T(8,128)(2,1)} %collective-permute-done.5, bf16[128,2048]{1,0:T(8,128)(2,1)} %collective-permute-done.4), kind=kOutput, calls=%fused_computation.48 | convolution fusion | flops 1075838976 | bytes 6291456 | tf_op jit(solution)/shard_map/dot_general | solution.py:104
  62.2 5.8 %collective-permute-done.8 = bf16[128,2048]{1,0:T(8,128)(2,1)S(1)} collective-permute-done((bf16[128,2048]{1,0:T(8,128)(2,1)}, bf16[128,2048]{1,0:T(8,128)(2,1)S(1)}, u32[]{:S(2)}, u32[]{:S(2)}) %collective-permute-start.8) | collective-permute-done | bytes 524320 | tf_op jit(solution)/shard_map/ppermute | solution.py:80
  72.5 3.2 %collective-permute-done.10 = bf16[128,2048]{1,0:T(8,128)(2,1)S(1)} collective-permute-done((bf16[128,2048]{1,0:T(8,128)(2,1)S(1)}, bf16[128,2048]{1,0:T(8,128)(2,1)S(1)}, u32[]{:S(2)}, u32[]{:S(2)}) %collective-permute-start.10) | collective-permute-done | bytes 524320 | tf_op jit(solution)/shard_map/ppermute | solution.py:80
  80.8 4.9 %collective-permute-done.12 = bf16[64,2048]{1,0:T(8,128)(2,1)S(1)} collective-permute-done((bf16[64,2048]{1,0:T(8,128)(2,1)S(1)}, bf16[64,2048]{1,0:T(8,128)(2,1)S(1)}, u32[]{:S(2)}, u32[]{:S(2)}) %collective-permute-start.12) | collective-permute-done | bytes 262176 | tf_op jit(solution)/shard_map/ppermute | solution.py:80
  93.6 4.6 %collective-permute-done.18 = bf16[128,2048]{1,0:T(8,128)(2,1)S(1)} collective-permute-done((bf16[128,2048]{1,0:T(8,128)(2,1)S(1)}, bf16[128,2048]{1,0:T(8,128)(2,1)S(1)}, u32[]{:S(2)}, u32[]{:S(2)}) %collective-permute-start.18) | collective-permute-done | bytes 524320 | tf_op jit(solution)/shard_map/ppermute | solution.py:80
  101.2 3.6 %collective-permute-done.17 = bf16[1,128,1024]{2,1,0:T(8,128)(2,1)S(1)} collective-permute-done((bf16[1,128,1024]{2,1,0:T(8,128)(2,1)S(1)}, bf16[1,128,1024]{2,1,0:T(8,128)(2,1)S(1)}, u32[]{:S(2)}, u32[]{:S(2)}) %collective-permute-start.17) | collective-permute-done | bytes 262176 | tf_op jit(solution)/shard_map/ppermute | solution.py:100
  107.8 10.1 %collective-permute-start.23 = (bf16[128,1024]{1,0:T(8,128)(2,1)S(1)}, bf16[128,1024]{1,0:T(8,128)(2,1)}, u32[]{:S(2)}, u32[]{:S(2)}) collective-permute-start(bf16[128,1024]{1,0:T(8,128)(2,1)S(1)} %fusion.95), channel_id=1, source_target_pairs={{0,28},{1,0},{2,12},{3,16},{8,21},{9,9},{10,5},{11,25},{16,14},{17... | collective-permute-start | bytes 786440 | tf_op jit(solution)/shard_map/ppermute | solution.py:165
  117.9 5.1 %fusion.12 = f32[3,128,1024]{2,1,0:T(8,128)} fusion(bf16[3,128,2048]{2,1,0:T(8,128)(2,1)S(1)} %bitcast.173, bf16[3,2048,1024]{2,1,0:T(8,128)(2,1)} %param.12), kind=kOutput, calls=%fused_computation.12 | convolution fusion | flops 1610612736 | bytes 7340032 | tf_op jit(solution)/shard_map/dot_general | solution.py:104
  128.8 4.5 %fusion.36 = f32[3,128,1024]{2,1,0:T(8,128)S(1)} fusion(f32[3,128,1024]{2,1,0:T(8,128)} %fusion.12, bf16[3,128,2048]{2,1,0:T(8,128)(2,1)S(1)} %bitcast.170, bf16[3,2048,1024]{2,1,0:T(8,128)(2,1)} %param.12), kind=kOutput, calls=%fused_computation.39 | convolution fusion | flops 1611005952 | bytes 8912896 | tf_op jit(solution)/shard_map/dot_general | solution.py:104
  135.4 3.2 %fusion.22 = f32[128,1024]{1,0:T(8,128)S(1)} fusion(bf16[3,2048,1024]{2,1,0:T(8,128)(2,1)} %param.12, bf16[64,2048]{1,0:T(8,128)(2,1)} %collective-permute-done.25, bf16[64,2048]{1,0:T(8,128)(2,1)} %collective-permute-done.24), kind=kOutput, calls=%fused_computation.22 | convolution fusion | flops 537919488 | bytes 5242880 | tf_op jit(solution)/shard_map/dot_general | solution.py:104
  138.6 3.0 %collective-permute-done.28 = bf16[128,2048]{1,0:T(8,128)(2,1)S(1)} collective-permute-done((bf16[128,2048]{1,0:T(8,128)(2,1)S(1)}, bf16[128,2048]{1,0:T(8,128)(2,1)S(1)}, u32[]{:S(2)}, u32[]{:S(2)}) %collective-permute-start.28) | collective-permute-done | bytes 524320 | tf_op jit(solution)/shard_map/ppermute | solution.py:80
  141.7 3.6 %fusion.10 = f32[2,128,1024]{2,1,0:T(8,128)S(1)} fusion(bf16[2,128,2048]{2,1,0:T(8,128)(2,1)S(1)} %bitcast.179, bf16[3,2048,1024]{2,1,0:T(8,128)(2,1)} %param.12), kind=kOutput, calls=%fused_computation.10 | convolution fusion | flops 1073741824 | bytes 6291456 | tf_op jit(solution)/shard_map/dot_general | solution.py:104
  145.4 4.9 %collective-permute-done.26 = bf16[128,2048]{1,0:T(8,128)(2,1)S(1)} collective-permute-done((bf16[128,2048]{1,0:T(8,128)(2,1)S(1)}, bf16[128,2048]{1,0:T(8,128)(2,1)S(1)}, u32[]{:S(2)}, u32[]{:S(2)}) %collective-permute-start.26) | collective-permute-done | bytes 524320 | tf_op jit(solution)/shard_map/ppermute | solution.py:80
  158.0 7.2 %collective-permute-done.32 = bf16[128,2048]{1,0:T(8,128)(2,1)S(1)} collective-permute-done((bf16[128,2048]{1,0:T(8,128)(2,1)S(1)}, bf16[128,2048]{1,0:T(8,128)(2,1)S(1)}, u32[]{:S(2)}, u32[]{:S(2)}) %collective-permute-start.32) | collective-permute-done | bytes 524320 | tf_op jit(solution)/shard_map/ppermute | solution.py:80
  166.8 7.1 %collective-permute-done.30 = bf16[128,2048]{1,0:T(8,128)(2,1)S(1)} collective-permute-done((bf16[128,2048]{1,0:T(8,128)(2,1)S(1)}, bf16[128,2048]{1,0:T(8,128)(2,1)S(1)}, u32[]{:S(2)}, u32[]{:S(2)}) %collective-permute-start.30) | collective-permute-done | bytes 524320 | tf_op jit(solution)/shard_map/ppermute | solution.py:80
  189.9 6.4 %collective-permute-done.35 = bf16[128,2048]{1,0:T(8,128)(2,1)S(1)} collective-permute-done((bf16[128,2048]{1,0:T(8,128)(2,1)S(1)}, bf16[128,2048]{1,0:T(8,128)(2,1)S(1)}, u32[]{:S(2)}, u32[]{:S(2)}) %collective-permute-start.35) | collective-permute-done | bytes 524320 | tf_op jit(solution)/shard_map/ppermute | solution.py:80
  201.7 3.5 %collective-permute-done.45 = bf16[2,1,32,1024]{3,2,1,0:T(8,128)(2,1)S(1)} collective-permute-done((bf16[2,1,32,1024]{3,2,1,0:T(8,128)(2,1)S(1)}, bf16[2,1,32,1024]{3,2,1,0:T(8,128)(2,1)S(1)}, u32[]{:S(2)}, u32[]{:S(2)}) %collective-permute-start.45) | collective-permute-done | bytes 131104 | tf_op jit(solution)/shard_map/ppermute | solution.py:100
  210.7 2.9 %collective-permute-start.53 = (bf16[32,1024]{1,0:T(8,128)(2,1)S(1)}, bf16[32,1024]{1,0:T(8,128)(2,1)S(1)}, u32[]{:S(2)}, u32[]{:S(2)}) collective-permute-start(bf16[32,1024]{1,0:T(8,128)(2,1)S(1)} %get-tuple-element.146), channel_id=1, source_target_pairs={{0,28},{1,29},{2,30},{3,31},{8,20},{9,21},{10,22},{11,23},{16,12},... | collective-permute-start | bytes 196616 | tf_op jit(solution)/shard_map/ppermute | solution.py:201
  216.6 3.0 %collective-permute-start.51 = (bf16[32,1024]{1,0:T(8,128)(2,1)S(1)}, bf16[32,1024]{1,0:T(8,128)(2,1)S(1)}, u32[]{:S(2)}, u32[]{:S(2)}) collective-permute-start(bf16[32,1024]{1,0:T(8,128)(2,1)S(1)} %get-tuple-element.147), channel_id=1, source_target_pairs={{0,24},{1,25},{2,26},{3,27},{8,28},{9,29},{10,30},{11,31},{16,20},... | collective-permute-start | bytes 196616 | tf_op jit(solution)/shard_map/ppermute | solution.py:201
  (200 shorter events, 96.0 us)
Async XLA Ops:
  0.0 15.9 %collective-permute-start = (bf16[128,2048]{1,0:T(8,128)(2,1)}, bf16[128,2048]{1,0:T(8,128)(2,1)S(1)}, u32[]{:S(2)}, u32[]{:S(2)}) collective-permute-start(bf16[128,2048]{1,0:T(8,128)(2,1)} %param.7), channel_id=1, source_target_pairs={{0,8},{8,16},{16,24},{24,28},{28,20},{20,12},{12,4},{4,0},{1,9},{9... | collective-permute-start | bytes 1572872 | tf_op jit(solution)/shard_map/ppermute | solution.py:80
  3.0 15.1 %collective-permute-start.1 = (bf16[128,2048]{1,0:T(8,128)(2,1)}, bf16[128,2048]{1,0:T(8,128)(2,1)S(1)}, u32[]{:S(2)}, u32[]{:S(2)}) collective-permute-start(bf16[128,2048]{1,0:T(8,128)(2,1)} %param.7), channel_id=1, source_target_pairs={{8,0},{16,8},{24,16},{28,24},{20,28},{12,20},{4,12},{0,4},{9,1},{1... | collective-permute-start | bytes 1572872 | tf_op jit(solution)/shard_map/ppermute | solution.py:80
  3.0 23.3 %collective-permute-start.2 = (bf16[128,2048]{1,0:T(8,128)(2,1)}, bf16[128,2048]{1,0:T(8,128)(2,1)S(1)}, u32[]{:S(2)}, u32[]{:S(2)}) collective-permute-start(bf16[128,2048]{1,0:T(8,128)(2,1)} %param.9), channel_id=1, source_target_pairs={{0,8},{8,16},{16,24},{24,28},{28,20},{20,12},{12,4},{4,0},{1,9},{9... | collective-permute-start | bytes 1572872 | tf_op jit(solution)/shard_map/ppermute | solution.py:80
  5.1 22.8 %collective-permute-start.3 = (bf16[128,2048]{1,0:T(8,128)(2,1)}, bf16[128,2048]{1,0:T(8,128)(2,1)S(1)}, u32[]{:S(2)}, u32[]{:S(2)}) collective-permute-start(bf16[128,2048]{1,0:T(8,128)(2,1)} %param.9), channel_id=1, source_target_pairs={{8,0},{16,8},{24,16},{28,24},{20,28},{12,20},{4,12},{0,4},{9,1},{1... | collective-permute-start | bytes 1572872 | tf_op jit(solution)/shard_map/ppermute | solution.py:80
  27.9 15.0 %collective-permute-start.4 = (bf16[128,2048]{1,0:T(8,128)(2,1)S(1)}, bf16[128,2048]{1,0:T(8,128)(2,1)}, u32[]{:S(2)}, u32[]{:S(2)}) collective-permute-start(bf16[128,2048]{1,0:T(8,128)(2,1)S(1)} %collective-permute-done), channel_id=1, source_target_pairs={{0,8},{8,16},{16,24},{24,28},{28,20},{20,12},{12,4},{4,0},{1,9},{9... | collective-permute-start | bytes 1572872 | tf_op jit(solution)/shard_map/ppermute | solution.py:80
  29.9 21.7 %collective-permute-start.6 = (bf16[128,2048]{1,0:T(8,128)(2,1)S(1)}, bf16[128,2048]{1,0:T(8,128)(2,1)S(1)}, u32[]{:S(2)}, u32[]{:S(2)}) collective-permute-start(bf16[128,2048]{1,0:T(8,128)(2,1)S(1)} %collective-permute-done.2), channel_id=1, source_target_pairs={{0,8},{8,16},{16,24},{24,28},{28,20},{20,12},{12,4},{4,0},{1,9},{9... | collective-permute-start | bytes 1572872 | tf_op jit(solution)/shard_map/ppermute | solution.py:80
  31.5 21.4 %collective-permute-start.7 = (bf16[128,2048]{1,0:T(8,128)(2,1)S(1)}, bf16[128,2048]{1,0:T(8,128)(2,1)S(1)}, u32[]{:S(2)}, u32[]{:S(2)}) collective-permute-start(bf16[128,2048]{1,0:T(8,128)(2,1)S(1)} %collective-permute-done.3), channel_id=1, source_target_pairs={{8,0},{16,8},{24,16},{28,24},{20,28},{12,20},{4,12},{0,4},{9,1},{1... | collective-permute-start | bytes 1572872 | tf_op jit(solution)/shard_map/ppermute | solution.py:80
  52.9 15.1 %collective-permute-start.8 = (bf16[128,2048]{1,0:T(8,128)(2,1)}, bf16[128,2048]{1,0:T(8,128)(2,1)S(1)}, u32[]{:S(2)}, u32[]{:S(2)}) collective-permute-start(bf16[128,2048]{1,0:T(8,128)(2,1)} %collective-permute-done.4), channel_id=1, source_target_pairs={{0,8},{8,16},{16,24},{24,28},{28,20},{20,12},{12,4},{4,0},{1,9},{9... | collective-permute-start | bytes 1572872 | tf_op jit(solution)/shard_map/ppermute | solution.py:80
  55.9 15.1 %collective-permute-start.9 = (bf16[128,2048]{1,0:T(8,128)(2,1)}, bf16[128,2048]{1,0:T(8,128)(2,1)S(1)}, u32[]{:S(2)}, u32[]{:S(2)}) collective-permute-start(bf16[128,2048]{1,0:T(8,128)(2,1)} %collective-permute-done.5), channel_id=1, source_target_pairs={{8,0},{16,8},{24,16},{28,24},{20,28},{12,20},{4,12},{0,4},{9,1},{1... | collective-permute-start | bytes 1572872 | tf_op jit(solution)/shard_map/ppermute | solution.py:80
  56.4 19.3 %collective-permute-start.10 = (bf16[128,2048]{1,0:T(8,128)(2,1)S(1)}, bf16[128,2048]{1,0:T(8,128)(2,1)S(1)}, u32[]{:S(2)}, u32[]{:S(2)}) collective-permute-start(bf16[128,2048]{1,0:T(8,128)(2,1)S(1)} %collective-permute-done.6), channel_id=1, source_target_pairs={{0,8},{8,16},{16,24},{24,28},{28,20},{20,12},{12,4},{4,0},{1,9},{9... | collective-permute-start | bytes 1572872 | tf_op jit(solution)/shard_map/ppermute | solution.py:80
  58.0 20.4 %collective-permute-start.11 = (bf16[128,2048]{1,0:T(8,128)(2,1)S(1)}, bf16[128,2048]{1,0:T(8,128)(2,1)S(1)}, u32[]{:S(2)}, u32[]{:S(2)}) collective-permute-start(bf16[128,2048]{1,0:T(8,128)(2,1)S(1)} %collective-permute-done.7), channel_id=1, source_target_pairs={{8,0},{16,8},{24,16},{28,24},{20,28},{12,20},{4,12},{0,4},{9,1},{1... | collective-permute-start | bytes 1572872 | tf_op jit(solution)/shard_map/ppermute | solution.py:80
  69.3 18.7 %collective-permute-start.16 = (f32[128,1024]{1,0:T(8,128)S(1)}, f32[128,1024]{1,0:T(8,128)S(1)}, u32[]{:S(2)}, u32[]{:S(2)}) collective-permute-start(f32[128,1024]{1,0:T(8,128)S(1)} %dynamic-slice_bitcast_fusion.4), channel_id=1, source_target_pairs={{0,1},{1,0},{2,3},{3,2},{4,5},{5,4},{6,7},{7,6},{8,9},{9,8},{10,11... | collective-permute-start | bytes 1572872 | tf_op jit(solution)/shard_map/ppermute | solution.py:100
  72.4 15.7 %collective-permute-start.15 = (f32[128,1024]{1,0:T(8,128)S(1)}, f32[128,1024]{1,0:T(8,128)S(1)}, u32[]{:S(2)}, u32[]{:S(2)}) collective-permute-start(f32[128,1024]{1,0:T(8,128)S(1)} %dynamic-slice_bitcast_fusion.5), channel_id=1, source_target_pairs={{0,1},{1,0},{2,3},{3,2},{4,5},{5,4},{6,7},{7,6},{8,9},{9,8},{10,11... | collective-permute-start | bytes 1572872 | tf_op jit(solution)/shard_map/ppermute | solution.py:100
  90.7 36.0 %collective-permute-start.24 = (bf16[64,2048]{1,0:T(8,128)(2,1)S(1)}, bf16[64,2048]{1,0:T(8,128)(2,1)}, u32[]{:S(2)}, u32[]{:S(2)}) collective-permute-start(bf16[64,2048]{1,0:T(8,128)(2,1)S(1)} %slice.78), channel_id=1, source_target_pairs={{0,8},{8,16},{16,24},{24,28},{28,20},{20,12},{12,4},{4,0},{1,9},{9... | collective-permute-start | bytes 786440 | tf_op jit(solution)/shard_map/ppermute | solution.py:80
  93.5 33.3 %collective-permute-start.25 = (bf16[64,2048]{1,0:T(8,128)(2,1)}, bf16[64,2048]{1,0:T(8,128)(2,1)}, u32[]{:S(2)}, u32[]{:S(2)}) collective-permute-start(bf16[64,2048]{1,0:T(8,128)(2,1)} %slice.79), channel_id=1, source_target_pairs={{8,0},{16,8},{24,16},{28,24},{20,28},{12,20},{4,12},{0,4},{9,1},{1... | collective-permute-start | bytes 786440 | tf_op jit(solution)/shard_map/ppermute | solution.py:80
  105.0 18.1 %collective-permute-start.20 = (bf16[128,1024]{1,0:T(8,128)(2,1)S(1)}, bf16[128,1024]{1,0:T(8,128)(2,1)}, u32[]{:S(2)}, u32[]{:S(2)}) collective-permute-start(bf16[128,1024]{1,0:T(8,128)(2,1)S(1)} %fusion.96), channel_id=1, source_target_pairs={{0,24},{1,4},{2,8},{3,20},{8,29},{9,1},{10,17},{11,13},{16,22},{17... | collective-permute-start | bytes 786440 | tf_op jit(solution)/shard_map/ppermute | solution.py:165
  107.8 16.8 %collective-permute-start.23 = (bf16[128,1024]{1,0:T(8,128)(2,1)S(1)}, bf16[128,1024]{1,0:T(8,128)(2,1)}, u32[]{:S(2)}, u32[]{:S(2)}) collective-permute-start(bf16[128,1024]{1,0:T(8,128)(2,1)S(1)} %fusion.95), channel_id=1, source_target_pairs={{0,28},{1,0},{2,12},{3,16},{8,21},{9,9},{10,5},{11,25},{16,14},{17... | collective-permute-start | bytes 786440 | tf_op jit(solution)/shard_map/ppermute | solution.py:165
  133.3 17.0 %collective-permute-start.26 = (bf16[128,2048]{1,0:T(8,128)(2,1)S(1)}, bf16[128,2048]{1,0:T(8,128)(2,1)S(1)}, u32[]{:S(2)}, u32[]{:S(2)}) collective-permute-start(bf16[128,2048]{1,0:T(8,128)(2,1)S(1)} %copy-done), channel_id=1, source_target_pairs={{0,8},{8,16},{16,24},{24,28},{28,20},{20,12},{12,4},{4,0},{1,9},{9... | collective-permute-start | bytes 1572872 | tf_op jit(solution)/shard_map/ppermute | solution.py:80
  133.4 16.9 %collective-permute-start.27 = (bf16[128,2048]{1,0:T(8,128)(2,1)S(1)}, bf16[128,2048]{1,0:T(8,128)(2,1)S(1)}, u32[]{:S(2)}, u32[]{:S(2)}) collective-permute-start(bf16[128,2048]{1,0:T(8,128)(2,1)S(1)} %copy-done), channel_id=1, source_target_pairs={{8,0},{16,8},{24,16},{28,24},{20,28},{12,20},{4,12},{0,4},{9,1},{1... | collective-permute-start | bytes 1572872 | tf_op jit(solution)/shard_map/ppermute | solution.py:80
  154.5 20.8 %collective-permute-start.34 = (f32[3,2,32,1024]{3,2,1,0:T(8,128)S(1)}, f32[3,2,32,1024]{3,2,1,0:T(8,128)S(1)}, u32[]{:S(2)}, u32[]{:S(2)}) collective-permute-start(f32[3,2,32,1024]{3,2,1,0:T(8,128)S(1)} %dynamic-slice_bitcast_fusion), channel_id=1, source_target_pairs={{0,1},{1,0},{2,3},{3,2},{4,5},{5,4},{6,7},{7,6},{8,9},{9,8},{10,11... | collective-permute-start | bytes 2359304 | tf_op jit(solution)/shard_map/ppermute | solution.py:100
  154.5 19.4 %collective-permute-start.30 = (bf16[128,2048]{1,0:T(8,128)(2,1)S(1)}, bf16[128,2048]{1,0:T(8,128)(2,1)S(1)}, u32[]{:S(2)}, u32[]{:S(2)}) collective-permute-start(bf16[128,2048]{1,0:T(8,128)(2,1)S(1)} %collective-permute-done.26), channel_id=1, source_target_pairs={{0,8},{8,16},{16,24},{24,28},{28,20},{20,12},{12,4},{4,0},{1,9},{9... | collective-permute-start | bytes 1572872 | tf_op jit(solution)/shard_map/ppermute | solution.py:80
  154.8 19.1 %collective-permute-start.31 = (bf16[128,2048]{1,0:T(8,128)(2,1)S(1)}, bf16[128,2048]{1,0:T(8,128)(2,1)S(1)}, u32[]{:S(2)}, u32[]{:S(2)}) collective-permute-start(bf16[128,2048]{1,0:T(8,128)(2,1)S(1)} %collective-permute-done.27), channel_id=1, source_target_pairs={{8,0},{16,8},{24,16},{28,24},{20,28},{12,20},{4,12},{0,4},{9,1},{1... | collective-permute-start | bytes 1572872 | tf_op jit(solution)/shard_map/ppermute | solution.py:80
  187.1 18.2 %collective-permute-start.43 = (bf16[32,1024]{1,0:T(8,128)(2,1)S(1)}, bf16[32,1024]{1,0:T(8,128)(2,1)S(1)}, u32[]{:S(2)}, u32[]{:S(2)}) collective-permute-start(bf16[32,1024]{1,0:T(8,128)(2,1)S(1)} %get-tuple-element.144), channel_id=1, source_target_pairs={{0,8},{1,9},{2,10},{3,11},{8,16},{9,17},{10,18},{11,19},{16,24},{1... | collective-permute-start | bytes 196616 | tf_op jit(solution)/shard_map/ppermute | solution.py:201
  188.5 16.9 %collective-permute-start.44 = (bf16[32,1024]{1,0:T(8,128)(2,1)S(1)}, bf16[32,1024]{1,0:T(8,128)(2,1)S(1)}, u32[]{:S(2)}, u32[]{:S(2)}) collective-permute-start(bf16[32,1024]{1,0:T(8,128)(2,1)S(1)} %get-tuple-element.143), channel_id=1, source_target_pairs={{0,4},{1,5},{2,6},{3,7},{8,0},{9,1},{10,2},{11,3},{16,8},{17,9},{1... | collective-permute-start | bytes 196616 | tf_op jit(solution)/shard_map/ppermute | solution.py:201
  (55 other events, 562.0 us)
